TPU v7x, 32 devices: a whole 2x2x4 slice. The times are simulated.
32 devices in a mesh: dir: 2 (over core), seq: 16 (over z, y, x).
Axes of the slice: x: 2, y: 2, z: 4, core: 2. Of those that a mesh axis runs over, the one named last changes fastest.
Arguments:
- tokens: bfloat16 [16384, 512], P('seq'), may hold values from -6 to 6
- segment_ids: int32 [16384], P('seq'), may hold values from 0 to 3, never falling along the last dimension, each value on 1 to 8192 neighbouring positions
- norm_gain: float32 [2, 512], replicated, may hold values from 0.5 to 1.5
- norm_bias: float32 [2, 512], replicated, may hold values from -3 to 3
- input_matrix: bfloat16 [2, 2, 512, 768], P(None, 'dir'), may hold values from -0.25 to 0.25
- output_matrix: bfloat16 [2, 2, 768, 512], P(None, 'dir'), may hold values from -0.21875 to 0.21875
- rate_params: float32 [2, 2, 384], P(None, 'dir'), may hold values from -9 to 3, as said below
- turn_params: float32 [2, 2, 2, 384], P(None, 'dir'), may hold values from -810 to 810, as said below
- skip_weight: float32 [2, 512], replicated, may hold values from -4 to 4
- glu_weight: bfloat16 [2, 512, 512], replicated, may hold values from -0.25 to 0.25
- glu_bias: float32 [2, 512], replicated, may hold values from -3 to 3
- cotangent: float32 [16384, 512], P('seq'), may hold values from -6 to 6
Outputs:
- block_output: float32 [16384, 512], P('seq')
- tokens_grad: float32 [16384, 512], P('seq')
- norm_gain_grad: float32 [2, 512], replicated
- norm_bias_grad: float32 [2, 512], replicated
- input_matrix_grad: float32 [2, 2, 512, 768], P(None, 'dir')
- output_matrix_grad: float32 [2, 2, 768, 512], P(None, 'dir')
- rate_params_grad: float32 [2, 2, 384], P(None, 'dir')
- turn_params_grad: float32 [2, 2, 2, 384], P(None, 'dir')
- skip_weight_grad: float32 [2, 512], replicated
- glu_weight_grad: float32 [2, 512, 512], replicated
- glu_bias_grad: float32 [2, 512], replicated
Inputs may be any that keep to these rules, and one draw needn't show every extreme that they name: `segment_ids`: ids never fall along the tokens; one id covers 1 to 8192 consecutive tokens. For every direction and state the damping exp(rate_params[l,s] + turn_params[l,s,1]) lies between 2e-5 and 0.035. exp(turn_params[l,s,1]) lies between 0.0024 and 0.14.
All inputs are finite; a program needn't handle non-finite values.
Results may differ from a plain program's by a relative error of at most 0.017.
Values may be sent and summed in bfloat16 or wider, within the bound.
No kernel may reach another device: no remote copies, remote signals or barrier semaphores. Data moves between devices by JAX's collectives and lax.ppermute only.
A program may use at most 192 MiB of HBM per device.

v0:
```python
import jax
import jax.numpy as jnp
from jax import lax
from jax.sharding import PartitionSpec as P

LAYERS = 2
LENGTH = 16384


eps = 1e-05
inv_root_two = 0.7071067811865476
inv_root_two_pi = 0.3989422804014327


def entering(value, axis, join, neutral, backward):
    count, mine = (lax.axis_size(axis), lax.axis_index(axis))
    pieces = jax.tree.map(lambda part: lax.all_gather(part, axis), value)
    if backward:
        pieces = jax.tree.map(lambda part: part[::-1], pieces)
        mine = count - 1 - mine
    so_far = jax.tree.map(
        lambda part, zero: jnp.full_like(part, 0) + jnp.asarray(zero, part.dtype), value, neutral
    )

    def hop(position, so_far):
        longer = join(so_far, jax.tree.map(lambda part: part[position], pieces))
        return jax.tree.map(lambda new, old: jnp.where(position < mine, new, old), longer, so_far)

    return lax.fori_loop(0, count - 1, hop, so_far)


def padded(cells, sides, width):
    for axis, dim in sides:
        count = lax.axis_size(axis)
        ends = count - 1
        head = lax.slice_in_dim(cells, 0, width, axis=dim)
        tail = lax.slice_in_dim(cells, cells.shape[dim] - width, cells.shape[dim], axis=dim)
        cells = jnp.concatenate(
            [
                lax.ppermute(tail, axis, [(i, (i + 1) % count) for i in range(ends)]),
                cells,
                lax.ppermute(head, axis, [((i + 1) % count, i) for i in range(ends)]),
            ],
            axis=dim,
        )
    return cells


def decay_terms(log_rate, turn):
    frequency = turn[0]
    log_step = turn[1]
    step_size = jnp.exp(log_step)
    damping = jnp.exp(log_rate + log_step)
    magnitude = jnp.exp(-damping)
    rotation = frequency * step_size
    decay_re = magnitude * jnp.cos(rotation)
    decay_im = magnitude * jnp.sin(rotation)
    scaling = jnp.sqrt(-jnp.expm1(-2.0 * damping))
    return (decay_re, decay_im, scaling)


def combine_steps(earlier, following):
    first_re, first_im, value_re, value_im = earlier
    second_re, second_im, added_re, added_im = following
    return (
        first_re * second_re - first_im * second_im,
        first_re * second_im + first_im * second_re,
        second_re * value_re - second_im * value_im + added_re,
        second_re * value_im + second_im * value_re + added_im,
    )


def orient(values, flipped):
    return jnp.where(flipped, jnp.flip(values, 0), values)


def sweep_chain(factor_re, factor_im, drive_re, drive_im, upward):
    product_re, product_im, local_re, local_im = lax.associative_scan(
        combine_steps, (factor_re, factor_im, drive_re, drive_im), axis=0
    )
    unit_factor = jnp.ones_like(product_re[-1])
    nothing = jnp.zeros_like(product_re[-1])
    from_below = entering(
        (product_re[-1], product_im[-1], local_re[-1], local_im[-1]),
        "seq",
        combine_steps,
        (unit_factor, nothing, nothing, nothing),
        False,
    )
    from_above = entering(
        (product_re[-1], product_im[-1], local_re[-1], local_im[-1]),
        "seq",
        combine_steps,
        (unit_factor, nothing, nothing, nothing),
        True,
    )
    carry_re = jnp.where(upward, from_below[2], from_above[2])
    carry_im = jnp.where(upward, from_below[3], from_above[3])
    states_re = local_re + product_re * carry_re - product_im * carry_im
    states_im = local_im + product_re * carry_im + product_im * carry_re
    return (states_re, states_im, carry_re, carry_im)


def body(
    tokens,
    segment_ids,
    norm_gain,
    norm_bias,
    input_matrix,
    output_matrix,
    rate_params,
    turn_params,
    skip_weight,
    glu_weight,
    glu_bias,
    cotangent,
):
    tok_rows = tokens.shape[0]
    state_count = rate_params.shape[2]
    row_devices = LENGTH // tok_rows
    direction = lax.axis_index("dir")
    reversed_side = direction == 1
    forward_side = direction == 0
    shifted_ids = segment_ids + 1
    padded_ids = padded(shifted_ids, (("seq", 0),), 1)
    seq_place = lax.axis_index("seq")
    differs = (padded_ids[1:] != padded_ids[:-1]).astype(jnp.float32)
    row_first = jnp.where(seq_place % row_devices == 0, 1.0, differs[0])
    row_next = jnp.where((seq_place + 1) % row_devices == 0, 1.0, differs[tok_rows])
    starts = jnp.concatenate([row_first[None], differs[1:tok_rows], row_next[None]])
    resets = orient(starts, reversed_side)
    keep_ahead = (1.0 - resets[:-1])[:, None]
    keep_behind = (1.0 - resets[1:])[:, None]
    residual = tokens.astype(jnp.float32)
    kept_layers = []
    for layer_index in range(LAYERS):
        average = jnp.mean(residual, 1, keepdims=True)
        centred = residual - average
        inv_scale = lax.rsqrt(jnp.mean(centred * centred, 1, keepdims=True) + eps)
        normed = centred * inv_scale
        mixed = normed * norm_gain[layer_index] + norm_bias[layer_index]
        mixed_low = mixed.astype(jnp.bfloat16)
        decay_re, decay_im, scaling = decay_terms(
            rate_params[layer_index, 0], turn_params[layer_index, 0]
        )
        projected = orient(
            jnp.dot(mixed_low, input_matrix[layer_index, 0], preferred_element_type=jnp.float32),
            reversed_side,
        )
        states_re, states_im, carry_re, carry_im = sweep_chain(
            keep_ahead * decay_re,
            keep_ahead * decay_im,
            projected[:, :state_count] * scaling,
            projected[:, state_count:] * scaling,
            forward_side,
        )
        states_low = orient(jnp.concatenate([states_re, states_im], 1), reversed_side).astype(
            jnp.bfloat16
        )
        side_out = jnp.dot(
            states_low, output_matrix[layer_index, 0], preferred_element_type=jnp.float32
        )
        mixed_rows = mixed
        residual_rows = residual
        summed = lax.psum(side_out.astype(jnp.bfloat16), "dir").astype(jnp.float32)
        combined = summed + skip_weight[layer_index] * mixed_rows
        activation = jax.nn.gelu(combined, approximate=False)
        activation_low = activation.astype(jnp.bfloat16)
        gate_logit = (
            jnp.dot(activation_low, glu_weight[layer_index], preferred_element_type=jnp.float32)
            + glu_bias[layer_index]
        )
        gate_value = jax.nn.sigmoid(gate_logit)
        new_rows = residual_rows + activation * gate_value
        residual = new_rows
        kept_layers.append(
            (
                normed,
                inv_scale,
                mixed_low,
                projected,
                states_re,
                states_im,
                carry_re,
                carry_im,
                states_low,
                combined,
                activation,
                activation_low,
                gate_value,
                decay_re,
                decay_im,
                scaling,
                mixed_rows,
            )
        )
    grad_rows = cotangent
    gain_list = []
    shift_list = []
    in_list = []
    out_list = []
    rate_list = []
    turn_list = []
    skip_list = []
    weight_list = []
    bias_list = []
    for layer_index in reversed(range(LAYERS)):
        (
            normed,
            inv_scale,
            mixed_low,
            projected,
            states_re,
            states_im,
            carry_re,
            carry_im,
            states_low,
            combined,
            activation,
            activation_low,
            gate_value,
            decay_re,
            decay_im,
            scaling,
            mixed_rows,
        ) = kept_layers[layer_index]
        gate_grad = grad_rows * activation * gate_value * (1.0 - gate_value)
        gate_grad_low = gate_grad.astype(jnp.bfloat16)
        weight_grad = jnp.einsum(
            "ti,tj->ij", activation_low, gate_grad_low, preferred_element_type=jnp.float32
        )
        bias_grad = jnp.sum(gate_grad, 0)
        activation_grad = grad_rows * gate_value + jnp.einsum(
            "tj,ij->ti", gate_grad_low, glu_weight[layer_index], preferred_element_type=jnp.float32
        )
        normal_cdf = 0.5 * (1.0 + jax.scipy.special.erf(combined * inv_root_two))
        gelu_slope = normal_cdf + combined * jnp.exp(-0.5 * combined * combined) * inv_root_two_pi
        combined_grad = activation_grad * gelu_slope
        skip_grad = jnp.sum(combined_grad * mixed_rows, 0)
        combined_low = combined_grad.astype(jnp.bfloat16)
        out_grad = jnp.einsum(
            "tk,th->kh", states_low, combined_low, preferred_element_type=jnp.float32
        )
        state_grad = orient(
            jnp.einsum(
                "th,kh->tk",
                combined_low,
                output_matrix[layer_index, 0],
                preferred_element_type=jnp.float32,
            ),
            reversed_side,
        )
        chained = sweep_chain(
            jnp.flip(keep_behind * decay_re, 0),
            jnp.flip(-keep_behind * decay_im, 0),
            jnp.flip(state_grad[:, :state_count], 0),
            jnp.flip(state_grad[:, state_count:], 0),
            reversed_side,
        )
        adjoint_re = jnp.flip(chained[0], 0)
        adjoint_im = jnp.flip(chained[1], 0)
        previous_re = jnp.concatenate([carry_re[None], states_re[:-1]], 0)
        previous_im = jnp.concatenate([carry_im[None], states_im[:-1]], 0)
        decay_grad_re = jnp.sum(
            keep_ahead * (adjoint_re * previous_re + adjoint_im * previous_im), 0
        )
        decay_grad_im = jnp.sum(
            keep_ahead * (adjoint_im * previous_re - adjoint_re * previous_im), 0
        )
        scaling_grad = jnp.sum(
            adjoint_re * projected[:, :state_count] + adjoint_im * projected[:, state_count:], 0
        )
        terms_out, pullback = jax.vjp(
            decay_terms, rate_params[layer_index, 0], turn_params[layer_index, 0]
        )
        rate_grad, turn_grad = pullback((decay_grad_re, decay_grad_im, scaling_grad))
        projected_low = orient(
            jnp.concatenate([adjoint_re * scaling, adjoint_im * scaling], 1), reversed_side
        ).astype(jnp.bfloat16)
        in_grad = jnp.einsum(
            "th,tk->hk", mixed_low, projected_low, preferred_element_type=jnp.float32
        )
        mixed_scan = jnp.einsum(
            "tk,hk->th",
            projected_low,
            input_matrix[layer_index, 0],
            preferred_element_type=jnp.float32,
        )
        mixed_grad = (
            lax.psum(mixed_scan.astype(jnp.bfloat16), "dir").astype(jnp.float32)
            + combined_grad * skip_weight[layer_index]
        )
        gain_grad = jnp.sum(mixed_grad * normed, 0)
        shift_grad = jnp.sum(mixed_grad, 0)
        normed_grad = mixed_grad * norm_gain[layer_index]
        grad_rows = grad_rows + inv_scale * (
            normed_grad
            - jnp.mean(normed_grad, 1, keepdims=True)
            - normed * jnp.mean(normed_grad * normed, 1, keepdims=True)
        )
        gain_list.insert(0, gain_grad)
        shift_list.insert(0, shift_grad)
        in_list.insert(0, in_grad)
        out_list.insert(0, out_grad)
        rate_list.insert(0, rate_grad)
        turn_list.insert(0, turn_grad)
        skip_list.insert(0, skip_grad)
        weight_list.insert(0, weight_grad)
        bias_list.insert(0, bias_grad)
    gain_all = jnp.stack(gain_list)
    shift_all = jnp.stack(shift_list)
    in_all = jnp.stack(in_list)[:, None]
    out_all = jnp.stack(out_list)[:, None]
    rate_all = jnp.stack(rate_list)[:, None]
    turn_all = jnp.stack(turn_list)[:, None]
    skip_all = jnp.stack(skip_list)
    weight_all = jnp.stack(weight_list)
    bias_all = jnp.stack(bias_list)
    totals = lax.psum(
        (gain_all, shift_all, in_all, out_all, rate_all, turn_all, skip_all, weight_all, bias_all),
        "seq",
    )
    return (
        residual,
        grad_rows,
        totals[0],
        totals[1],
        totals[2],
        totals[3],
        totals[4],
        totals[5],
        totals[6],
        totals[7],
        totals[8],
    )


def solution(mesh):
    return jax.shard_map(
        body,
        mesh=mesh,
        in_specs=(
            P("seq", None),
            P("seq"),
            P(),
            P(),
            P(None, "dir", None, None),
            P(None, "dir", None, None),
            P(None, "dir", None),
            P(None, "dir", None, None),
            P(),
            P(),
            P(),
            P("seq", None),
        ),
        out_specs=(
            P("seq", None),
            P("seq", None),
            P(),
            P(),
            P(None, "dir", None, None),
            P(None, "dir", None, None),
            P(None, "dir", None),
            P(None, "dir", None, None),
            P(),
            P(),
            P(),
        ),
        check_vma=False,
    )
```

profile of v0, /device:TPU:1, one launch (start us, length us, event | category | flops | bytes accessed | tf_op | source)
XLA Modules:
  0.0 2155.7 jit_solution(10453649057490216775)
XLA Ops:
  22.9 24.5 %rev.98 = f32[1024,768]{1,0:T(8,128)} reverse(f32[1024,768]{1,0:T(8,128)} %fusion.57), dimensions={0} | reverse | bytes 6291456 | tf_op jit(solution)/shard_map/jit(_flip)/rev | solution.py:74
  197.4 5.2 pad.1062
  203.6 5.1 pad.1064
  208.8 5.2 pad.1063
  214.7 34.7 %all-gather = f32[16,1,384]{2,1,0:T(1,128)S(1)} all-gather(f32[1,1,384]{2,1,0:T(1,128)S(1)} %add_bitcast_fusion.17), channel_id=1, replica_groups=mesh['dir'=2,'seq'=16] {'seq'}, dimensions={0}, use_global_device_ids=true | all-gather | bytes 26112 | tf_op jit(solution)/shard_map/all_gather | solution.py:17
  253.5 28.6 %all-gather.1 = f32[16,1,384]{2,1,0:T(1,128)S(1)} all-gather(f32[1,1,384]{2,1,0:T(1,128)S(1)} %add_bitcast_fusion.16), channel_id=1, replica_groups=mesh['dir'=2,'seq'=16] {'seq'}, dimensions={0}, use_global_device_ids=true | all-gather | bytes 26112 | tf_op jit(solution)/shard_map/all_gather | solution.py:17
  287.5 5.2 pad.1025
  293.4 30.6 %all-gather.2 = f32[16,1,384]{2,1,0:T(1,128)S(1)} all-gather(f32[1,1,384]{2,1,0:T(1,128)S(1)} %add_bitcast_fusion.15), channel_id=1, replica_groups=mesh['dir'=2,'seq'=16] {'seq'}, dimensions={0}, use_global_device_ids=true | all-gather | bytes 26112 | tf_op jit(solution)/shard_map/all_gather | solution.py:17
  329.2 28.6 %all-gather.3 = f32[16,1,384]{2,1,0:T(1,128)S(1)} all-gather(f32[1,1,384]{2,1,0:T(1,128)S(1)} %add_bitcast_fusion.14), channel_id=1, replica_groups=mesh['dir'=2,'seq'=16] {'seq'}, dimensions={0}, use_global_device_ids=true | all-gather | bytes 26112 | tf_op jit(solution)/shard_map/all_gather | solution.py:17
  359.4 22.6 %while.129 = (s32[]{:T(128)}, f32[384]{0:T(512)S(1)}, f32[384]{0:T(512)S(1)}, s32[]{:T(128)}, f32[16,384]{1,0:T(8,128)S(1)}, /*index=5*/f32[16,384]{1,0:T(8,128)...) while((s32[]{:T(128)}, f32[384]{0:T(512)S(1)}, f32[384]{0:T(512)S(1)}, ...), condition=%wide.region_5.6_spmd.clone, body=%wide.region_4.5_spmd.clone.sunk | while | flops 4612 | bytes 24713 | solution.py:29
  382.0 5.3 multiply_subtract_fusion.3
  389.8 23.1 %rev.104 = bf16[1024,768]{1,0:T(8,128)(2,1)} reverse(bf16[1024,768]{1,0:T(8,128)(2,1)} %pad_maximum_fusion), dimensions={0} | reverse | bytes 3145728 | tf_op jit(solution)/shard_map/jit(_flip)/rev | solution.py:74
  421.1 5.2 slice.2839
  444.8 19.7 all-reduce.332.cloned.1.call-done
  464.6 7.1 fusion.19
  477.5 15.3 rev.105
  590.9 5.2 pad.1144
  596.1 5.1 pad.1143
  602.0 34.1 %all-gather.4 = f32[16,1,384]{2,1,0:T(1,128)S(1)} all-gather(f32[1,1,384]{2,1,0:T(1,128)S(1)} %add_bitcast_fusion.13), channel_id=1, replica_groups=mesh['dir'=2,'seq'=16] {'seq'}, dimensions={0}, use_global_device_ids=true | all-gather | bytes 26112 | tf_op jit(solution)/shard_map/all_gather | solution.py:17
  639.2 28.6 %all-gather.5 = f32[16,1,384]{2,1,0:T(1,128)S(1)} all-gather(f32[1,1,384]{2,1,0:T(1,128)S(1)} %add_bitcast_fusion.12), channel_id=1, replica_groups=mesh['dir'=2,'seq'=16] {'seq'}, dimensions={0}, use_global_device_ids=true | all-gather | bytes 26112 | tf_op jit(solution)/shard_map/all_gather | solution.py:17
  675.0 5.2 pad.1105
  681.0 30.3 %all-gather.6 = f32[16,1,384]{2,1,0:T(1,128)S(1)} all-gather(f32[1,1,384]{2,1,0:T(1,128)S(1)} %add_bitcast_fusion.11), channel_id=1, replica_groups=mesh['dir'=2,'seq'=16] {'seq'}, dimensions={0}, use_global_device_ids=true | all-gather | bytes 26112 | tf_op jit(solution)/shard_map/all_gather | solution.py:17
  713.7 29.0 %all-gather.7 = f32[16,1,384]{2,1,0:T(1,128)S(1)} all-gather(f32[1,1,384]{2,1,0:T(1,128)S(1)} %add_bitcast_fusion.10), channel_id=1, replica_groups=mesh['dir'=2,'seq'=16] {'seq'}, dimensions={0}, use_global_device_ids=true | all-gather | bytes 26112 | tf_op jit(solution)/shard_map/all_gather | solution.py:17
  746.3 5.3 multiply_subtract_fusion.2
  753.1 23.2 %rev.110 = bf16[1024,768]{1,0:T(8,128)(2,1)} reverse(bf16[1024,768]{1,0:T(8,128)(2,1)} %pad_maximum_fusion.1), dimensions={0} | reverse | bytes 3145728 | tf_op jit(solution)/shard_map/jit(_flip)/rev | solution.py:74
  814.9 7.2 slice.3191
  834.1 6.8 slice.3251
  868.8 7.2 fusion.21
  885.4 24.5 %rev.111 = f32[1024,768]{1,0:T(8,128)} reverse(f32[1024,768]{1,0:T(8,128)} %fusion.47), dimensions={0} | reverse | bytes 6291456 | tf_op jit(solution)/shard_map/jit(_flip)/rev | solution.py:74
  942.7 6.8 slice.3043
  953.4 6.9 slice.3048
  1069.8 7.1 slice.3240
  1161.1 5.2 pad.1222
  1167.2 5.2 pad.1224
  1172.4 5.2 pad.1223
  1178.3 29.7 %all-gather.8 = f32[16,1,384]{2,1,0:T(1,128)S(1)} all-gather(f32[1,1,384]{2,1,0:T(1,128)S(1)} %add_bitcast_fusion.9), channel_id=1, replica_groups=mesh['dir'=2,'seq'=16] {'seq'}, dimensions={0}, use_global_device_ids=true | all-gather | bytes 26112 | tf_op jit(solution)/shard_map/all_gather | solution.py:17
  1212.0 28.9 %all-gather.9 = f32[16,1,384]{2,1,0:T(1,128)S(1)} all-gather(f32[1,1,384]{2,1,0:T(1,128)S(1)} %add_bitcast_fusion.8), channel_id=1, replica_groups=mesh['dir'=2,'seq'=16] {'seq'}, dimensions={0}, use_global_device_ids=true | all-gather | bytes 26112 | tf_op jit(solution)/shard_map/all_gather | solution.py:17
  1245.3 5.1 pad.1185
  1251.2 30.1 %all-gather.10 = f32[16,1,384]{2,1,0:T(1,128)S(1)} all-gather(f32[1,1,384]{2,1,0:T(1,128)S(1)} %add_bitcast_fusion.7), channel_id=1, replica_groups=mesh['dir'=2,'seq'=16] {'seq'}, dimensions={0}, use_global_device_ids=true | all-gather | bytes 26112 | tf_op jit(solution)/shard_map/all_gather | solution.py:17
  1285.2 28.8 %all-gather.11 = f32[16,1,384]{2,1,0:T(1,128)S(1)} all-gather(f32[1,1,384]{2,1,0:T(1,128)S(1)} %add_bitcast_fusion.6), channel_id=1, replica_groups=mesh['dir'=2,'seq'=16] {'seq'}, dimensions={0}, use_global_device_ids=true | all-gather | bytes 26112 | tf_op jit(solution)/shard_map/all_gather | solution.py:17
  1317.2 7.0 multiply_subtract_fusion.1
  1324.2 12.8 rev.116
  1337.0 12.8 rev.117
  1354.1 23.0 %rev.118 = bf16[1024,768]{1,0:T(8,128)(2,1)} reverse(bf16[1024,768]{1,0:T(8,128)(2,1)} %pad_maximum_fusion.2), dimensions={0} | reverse | bytes 3145728 | tf_op jit(solution)/shard_map/jit(_flip)/rev | solution.py:74
  1390.7 66.1 %all-reduce.336.cloned.1.call-done = bf16[1024,512]{1,0:T(8,128)(2,1)} async-done(((bf16[1024,512]{1,0:T(8,128)(2,1)}), bf16[1024,512]{1,0:T(8,128)(2,1)}) %all-reduce.336.cloned.1.call-update) | async-done | bytes 1048592 | tf_op jit(solution)/shard_map/psum | solution.py:290
  1461.5 5.8 fusion.114
  1474.9 15.3 rev.119
  1507.9 6.9 slice.3249
  1616.2 5.1 pad.1304
  1621.3 5.2 pad.1303
  1627.2 33.8 %all-gather.12 = f32[16,1,384]{2,1,0:T(1,128)S(1)} all-gather(f32[1,1,384]{2,1,0:T(1,128)S(1)} %add_bitcast_fusion.5), channel_id=1, replica_groups=mesh['dir'=2,'seq'=16] {'seq'}, dimensions={0}, use_global_device_ids=true | all-gather | bytes 26112 | tf_op jit(solution)/shard_map/all_gather | solution.py:17
  1661.0 5.2 pad.1305
  1667.0 28.7 %all-gather.13 = f32[16,1,384]{2,1,0:T(1,128)S(1)} all-gather(f32[1,1,384]{2,1,0:T(1,128)S(1)} %add_bitcast_fusion.4), channel_id=1, replica_groups=mesh['dir'=2,'seq'=16] {'seq'}, dimensions={0}, use_global_device_ids=true | all-gather | bytes 26112 | tf_op jit(solution)/shard_map/all_gather | solution.py:17
  1708.7 30.4 %all-gather.14 = f32[16,1,384]{2,1,0:T(1,128)S(1)} all-gather(f32[1,1,384]{2,1,0:T(1,128)S(1)} %add_bitcast_fusion.3), channel_id=1, replica_groups=mesh['dir'=2,'seq'=16] {'seq'}, dimensions={0}, use_global_device_ids=true | all-gather | bytes 26112 | tf_op jit(solution)/shard_map/all_gather | solution.py:17
  1739.2 5.1 pad.1307
  1745.0 28.6 %all-gather.15 = f32[16,1,384]{2,1,0:T(1,128)S(1)} all-gather(f32[1,1,384]{2,1,0:T(1,128)S(1)} %add_bitcast_fusion.2), channel_id=1, replica_groups=mesh['dir'=2,'seq'=16] {'seq'}, dimensions={0}, use_global_device_ids=true | all-gather | bytes 26112 | tf_op jit(solution)/shard_map/all_gather | solution.py:17
  1776.8 6.1 multiply_subtract_fusion
  1782.8 10.2 rev.124
  1793.1 10.4 rev.125
  1807.2 19.0 rev.126
  1842.5 6.9 multiply_reduce_fusion.9
  1849.7 23.9 %all-reduce.338.cloned.1.call-done = bf16[1024,512]{1,0:T(8,128)(2,1)} async-done(((bf16[1024,512]{1,0:T(8,128)(2,1)}), bf16[1024,512]{1,0:T(8,128)(2,1)}) %all-reduce.338.cloned.1.call-update) | async-done | bytes 1048592 | tf_op jit(solution)/shard_map/psum | solution.py:290
  1877.9 66.7 %all-reduce.324 = (f32[2,512]{1,0:T(2,128)}, f32[2,512]{1,0:T(2,128)}, f32[2,1,384]{2,0,1:T(2,128)S(1)}, f32[2,1,2,384]{3,2,1,0:T(2,128)}, f32[2,512]{1,0:T(2,128)}, /*index=5*/f32[2,512]{1,0:T(2,128)}) all-reduce(f32[2,512]{1,0:T(2,128)S(1)} %pad_maximum_fusion.137, ...), channel_id=1, replica_groups=mesh['dir'=2,'seq'=16] {'seq'}, use_global_device_ids=true, to_apply=%region_30.31 | all-reduce | flops 6400 | bytes 51200 | tf_op jit(solution)/shard_map/psum | solution.py:319
  1948.3 192.7 %all-reduce.340.cloned.1.call-done = (f32[2,1,512,768]{3,2,0,1:T(8,128)}, f32[2,1,768,512]{3,2,0,1:T(8,128)}, f32[2,512,512]{2,1,0:T(8,128)}) async-done(((f32[2,1,512,768]{3,2,0,1:T(8,128)}, f32[2,1,768,512]{3,2,0,1:T(8,128)}, f32[2,512,512]{2,1,0:T(8,128)}), (f32[2,1,512,768]{3,2,0,1:T(8,128)}, f32[2,1,768,512]{3,2,0,1:T(8,128)}, f32[2,512,512]{2,1,0:T(8,128)})) %all-reduce.340.cloned.1.call-update) | async-done | bytes 8388624 | tf_op jit(solution)/shard_map/psum | solution.py:319
  (2441 shorter events, 896.5 us)
Async XLA Ops:
  7.2 457.3 %all-reduce.332.cloned.1.call-start = ((), (), s32[]{:S(2)}) async-start(), calls=%async_computation | async-start | bytes 2097152 | tf_op jit(solution)/shard_map/psum | solution.py:165
  8.6 67.2 %collective-permute-start.1 = (s32[1]{0:T(128)}, s32[1]{0:T(128)}, u32[]{:S(2)}, u32[]{:S(2)}) collective-permute-start(s32[1]{0:T(128)} %get-tuple-element.2071), channel_id=1, source_target_pairs={{0,1},{1,2},{2,3},{3,4},{4,5},{5,6},{6,7},{7,8},{8,9},{9,10},{10,1... | collective-permute-start | bytes 20 | tf_op jit(solution)/shard_map/ppermute | solution.py:40
  13.2 64.0 %collective-permute-start = (s32[1]{0:T(128)}, s32[1]{0:T(128)}, u32[]{:S(2)}, u32[]{:S(2)}) collective-permute-start(s32[1]{0:T(128)} %get-tuple-element.2072), channel_id=1, source_target_pairs={{1,0},{2,1},{3,2},{4,3},{5,4},{6,5},{7,6},{8,7},{9,8},{10,9},{11,1... | collective-permute-start | bytes 20 | tf_op jit(solution)/shard_map/ppermute | solution.py:42
  16.0 448.6 %copy-start.200 = (f32[1024]{0:T(1024)}, f32[1024]{0:T(1024)S(1)}, u32[]{:S(2)}) copy-start(f32[1024]{0:T(1024)S(1)} %broadcast_multiply_fusion.17) | copy-start | bytes 12292
  17.7 446.9 %copy-start.214 = (f32[1024]{0:T(1024)}, f32[1024]{0:T(1024)S(1)}, u32[]{:S(2)}) copy-start(f32[1024]{0:T(1024)S(1)} %add_rsqrt_fusion.1) | copy-start | bytes 12292
  194.7 133.7 %copy-start.71 = (f32[1024,384]{1,0:T(8,128)}, f32[1024,384]{1,0:T(8,128)S(1)}, u32[]{:S(2)}) copy-start(f32[1024,384]{1,0:T(8,128)S(1)} %pad.1066) | copy-start | bytes 4718596
  203.6 45.8 %copy-start.103 = (f32[512,384]{1,0:T(8,128)S(1)}, f32[512,384]{1,0:T(8,128)}, u32[]{:S(2)}) copy-start(f32[512,384]{1,0:T(8,128)} %add.2773) | copy-start | bytes 2359300
  287.5 37.7 %copy-start.102 = (f32[512,384]{1,0:T(8,128)S(1)}, f32[512,384]{1,0:T(8,128)}, u32[]{:S(2)}) copy-start(f32[512,384]{1,0:T(8,128)} %add.2744) | copy-start | bytes 2359300
  387.4 25.6 %copy-start.15 = (f32[1024,384]{1,0:T(8,128)}, f32[1024,384]{1,0:T(8,128)S(1)}, u32[]{:S(2)}) copy-start(f32[1024,384]{1,0:T(8,128)S(1)} %get-tuple-element.1614) | copy-start | bytes 4718596
  418.5 450.3 %all-reduce.334.cloned.1.call-start = ((), (), s32[]{:S(2)}) async-start(), calls=%async_computation.1 | async-start | bytes 2097152 | tf_op jit(solution)/shard_map/psum | solution.py:165
  419.2 45.3 %copy-start.236 = (f32[1,512]{1,0:T(1,128)}, f32[1,512]{1,0:T(1,128)S(1)}, u32[]{:S(2)}) copy-start(f32[1,512]{1,0:T(1,128)S(1)} %get-tuple-element.2056) | copy-start | bytes 6148
  434.5 30.1 %copy-start.224 = (f32[1,512]{1,0:T(1,128)S(1)}, f32[1,512]{1,0:T(1,128)}, u32[]{:S(2)}) copy-start(f32[1,512]{1,0:T(1,128)} %copy-done.223) | copy-start | bytes 6148
  434.5 30.1 %copy-start.232 = (f32[1,512]{1,0:T(1,128)S(1)}, f32[1,512]{1,0:T(1,128)}, u32[]{:S(2)}) copy-start(f32[1,512]{1,0:T(1,128)} %copy-done.231) | copy-start | bytes 6148
  584.2 129.5 %copy-start.70 = (f32[1024,384]{1,0:T(8,128)}, f32[1024,384]{1,0:T(8,128)S(1)}, u32[]{:S(2)}) copy-start(f32[1024,384]{1,0:T(8,128)S(1)} %pad.1146) | copy-start | bytes 4718596
  588.3 13.0 copy-start.72
  596.1 71.7 %copy-start.267 = (f32[1,384]{1,0:T(1,128)S(1)}, f32[1,384]{1,0:T(1,128)}, u32[]{:S(2)}) copy-start(f32[1,384]{1,0:T(1,128)} %slice.3585) | copy-start | bytes 4612
  638.4 41.9 %copy-start.73 = (f32[1024,384]{1,0:T(8,128)}, f32[1024,384]{1,0:T(8,128)S(1)}, u32[]{:S(2)}) copy-start(f32[1024,384]{1,0:T(8,128)S(1)} %pad.1145) | copy-start | bytes 4718596
  675.0 68.1 %copy-start.213 = (f32[384]{0:T(512)S(1)}, f32[384]{0:T(512)}, u32[]{:S(2)}) copy-start(f32[384]{0:T(512)} %custom-call.4) | copy-start | bytes 4612
  713.7 32.6 %copy-start.74 = (f32[1024,384]{1,0:T(8,128)}, f32[1024,384]{1,0:T(8,128)S(1)}, u32[]{:S(2)}) copy-start(f32[1024,384]{1,0:T(8,128)S(1)} %pad.1147) | copy-start | bytes 4718596
  751.6 24.7 %copy-start.17 = (f32[1024,384]{1,0:T(8,128)}, f32[1024,384]{1,0:T(8,128)S(1)}, u32[]{:S(2)}) copy-start(f32[1024,384]{1,0:T(8,128)S(1)} %get-tuple-element.1612) | copy-start | bytes 4718596
  751.6 24.7 %copy-start.18 = (f32[1024,384]{1,0:T(8,128)}, f32[1024,384]{1,0:T(8,128)S(1)}, u32[]{:S(2)}) copy-start(f32[1024,384]{1,0:T(8,128)S(1)} %get-tuple-element.1613) | copy-start | bytes 4718596
  781.3 675.5 %all-reduce.336.cloned.1.call-start = ((), (), s32[]{:S(2)}) async-start(), calls=%async_computation.2 | async-start | bytes 2097152 | tf_op jit(solution)/shard_map/psum | solution.py:290
  812.1 13.9 copy-start.107
  814.9 15.1 copy-start.112
  826.0 14.9 copy-start.106
  829.9 14.9 copy-start.108
  840.9 12.0 copy-start.105
  856.8 12.0 copy-start.217
  856.8 12.0 copy-start.227
  856.8 12.0 copy-start.250
  856.8 12.0 copy-start.252
  876.1 509.3 %copy-start.2 = (f32[1024,512]{1,0:T(8,128)}, f32[1024,512]{1,0:T(8,128)S(1)}, u32[]{:S(2)}) copy-start(f32[1024,512]{1,0:T(8,128)S(1)} %fusion.21) | copy-start | bytes 6291460
  1031.5 34.1 %copy-start.98 = (f32[511,384]{1,0:T(8,128)S(1)}, f32[511,384]{1,0:T(8,128)}, u32[]{:S(2)}) copy-start(f32[511,384]{1,0:T(8,128)} %slice.3195) | copy-start | bytes 2354692
  1062.7 15.2 copy-start.296
  1065.2 13.6 copy-start.219
  1065.2 13.6 copy-start.220
  1065.2 12.0 copy-start.229
  1065.2 12.1 copy-start.297
  1065.6 15.4 copy-start.197
  1086.2 15.1 copy-start.128
  1167.2 40.8 %copy-start.104 = (f32[512,384]{1,0:T(8,128)S(1)}, f32[512,384]{1,0:T(8,128)}, u32[]{:S(2)}) copy-start(f32[512,384]{1,0:T(8,128)} %add.3031) | copy-start | bytes 2359300
  1172.4 68.6 %copy-start.287 = (f32[1,384]{1,0:T(1,128)S(1)}, f32[1,384]{1,0:T(1,128)}, u32[]{:S(2)}) copy-start(f32[1,384]{1,0:T(1,128)} %get-tuple-element.1648) | copy-start | bytes 4612
  1245.3 36.0 %copy-start.101 = (f32[512,384]{1,0:T(8,128)S(1)}, f32[512,384]{1,0:T(8,128)}, u32[]{:S(2)}) copy-start(f32[512,384]{1,0:T(8,128)} %add.3002) | copy-start | bytes 2359300
  1245.3 68.8 %copy-start.211 = (f32[384]{0:T(512)S(1)}, f32[384]{0:T(512)}, u32[]{:S(2)}) copy-start(f32[384]{0:T(512)} %custom-call.9) | copy-start | bytes 4612
  1245.3 68.8 %copy-start.212 = (f32[384]{0:T(512)S(1)}, f32[384]{0:T(512)}, u32[]{:S(2)}) copy-start(f32[384]{0:T(512)} %custom-call.8) | copy-start | bytes 4612
  1250.4 65.2 %copy-start.210 = (f32[384]{0:T(512)S(1)}, f32[384]{0:T(512)}, u32[]{:S(2)}) copy-start(f32[384]{0:T(512)} %custom-call.10) | copy-start | bytes 4612
  1337.0 12.8 copy-start.240
  1380.9 492.7 %all-reduce.338.cloned.1.call-start = ((), (), s32[]{:S(2)}) async-start(), calls=%async_computation.3 | async-start | bytes 2097152 | tf_op jit(solution)/shard_map/psum | solution.py:290
  1388.1 68.6 %copy-start.253 = (f32[1,512]{1,0:T(1,128)S(1)}, f32[1,512]{1,0:T(1,128)}, u32[]{:S(2)}) copy-start(f32[1,512]{1,0:T(1,128)} %get-tuple-element.2055) | copy-start | bytes 6148
  1390.7 70.9 %copy-start.1 = (f32[1024,512]{1,0:T(8,128)S(1)}, f32[1024,512]{1,0:T(8,128)}, u32[]{:S(2)}) copy-start(f32[1024,512]{1,0:T(8,128)} %copy-done) | copy-start | bytes 6291460
  1621.3 74.5 %copy-start.288 = (f32[1,384]{1,0:T(1,128)S(1)}, f32[1,384]{1,0:T(1,128)}, u32[]{:S(2)}) copy-start(f32[1,384]{1,0:T(1,128)} %get-tuple-element.1640) | copy-start | bytes 4612
  1702.9 70.8 %copy-start.208 = (f32[384]{0:T(512)S(1)}, f32[384]{0:T(512)}, u32[]{:S(2)}) copy-start(f32[384]{0:T(512)} %custom-call.13) | copy-start | bytes 4612
  1702.9 70.8 %copy-start.209 = (f32[384]{0:T(512)S(1)}, f32[384]{0:T(512)}, u32[]{:S(2)}) copy-start(f32[384]{0:T(512)} %custom-call.12) | copy-start | bytes 4612
  1708.0 67.2 %copy-start.206 = (f32[384]{0:T(512)S(1)}, f32[384]{0:T(512)}, u32[]{:S(2)}) copy-start(f32[384]{0:T(512)} %custom-call.15) | copy-start | bytes 4612
  1708.0 67.2 %copy-start.207 = (f32[384]{0:T(512)S(1)}, f32[384]{0:T(512)}, u32[]{:S(2)}) copy-start(f32[384]{0:T(512)} %custom-call.14) | copy-start | bytes 4612
  1807.2 19.0 copy-start.43
  1807.2 19.0 copy-start.45
  1829.8 311.2 %all-reduce.340.cloned.1.call-start = ((), (), s32[]{:S(2)}) async-start(), calls=%async_computation.4 | async-start | bytes 16777216 | tf_op jit(solution)/shard_map/psum | solution.py:319
  1842.5 31.1 %copy-start.238 = (f32[1,512]{1,0:T(1,128)S(1)}, f32[1,512]{1,0:T(1,128)}, u32[]{:S(2)}) copy-start(f32[1,512]{1,0:T(1,128)} %copy-done.236) | copy-start | bytes 6148
  1849.7 28.2 %copy-start.260 = (f32[512]{0:T(512)S(1)}, f32[512]{0:T(512)}, u32[]{:S(2)}) copy-start(f32[512]{0:T(512)} %get-tuple-element.1389) | copy-start | bytes 6148
  1849.7 28.2 %copy-start.259 = (f32[512]{0:T(512)S(1)}, f32[512]{0:T(512)}, u32[]{:S(2)}) copy-start(f32[512]{0:T(512)} %get-tuple-element.1399) | copy-start | bytes 6148
  1849.7 28.2 %copy-start.258 = (f32[512]{0:T(512)S(1)}, f32[512]{0:T(512)}, u32[]{:S(2)}) copy-start(f32[512]{0:T(512)} %get-tuple-element.1395) | copy-start | bytes 6148
  1849.7 95.5 %copy-start.14 = (bf16[1024,512]{1,0:T(8,128)(2,1)S(1)}, bf16[1024,512]{1,0:T(8,128)(2,1)}, u32[]{:S(2)}) copy-start(bf16[1024,512]{1,0:T(8,128)(2,1)} %param.28) | copy-start | bytes 3145732
  1849.7 95.5 %copy-start.20 = (f32[1024,512]{1,0:T(8,128)S(1)}, f32[1024,512]{1,0:T(8,128)}, u32[]{:S(2)}) copy-start(f32[1024,512]{1,0:T(8,128)} %copy-done.19) | copy-start | bytes 6291460
  (271 other events, 961.7 us)
Sparse Core Ops, SparseCore 0:
  418.6 45.8 all-reduce.331
  781.4 47.4 all-reduce.333
  1381.0 75.6 all-reduce.335
  1829.9 43.6 all-reduce.337
  1880.5 260.4 all-reduce.339
where the time goes:
time: 2190 us; the launch traced here: 2160 us
  local copies, waits for them, and re-layouts  963 us (44%)
  blocking collectives  550 us (25%)
  waiting for transfers between devices  302 us (14%)
  other arithmetic  267 us (12%)
  matrix products  39.3 us (2%)
  between operations  24.5 us (1%)
    all_gather x16, blocking collectives, entering(): pieces = jax.tree.map(lambda part: lax.all_gather(part, axis), value)  484 us
    slice x578, local copies, waits for them, and re-layouts, sweep_chain(): lax.associative_scan(combine_steps, (factor_re, factor_im, drive_re, driv...  451 us
    pad x288, local copies, waits for them, and re-layouts, sweep_chain(): lax.associative_scan(combine_steps, (factor_re, factor_im, drive_re, driv...  217 us
    psum x1, waiting for transfers between devices, body(): lax.psum((gain_all, shift_all, in_all, out_all, rate_all, turn_all, skip_...  193 us
    rev x8, local copies, waits for them, and re-layouts, orient(): return jnp.where(flipped, jnp.flip(values, 0), values)  168 us
    psum x2, waiting for transfers between devices, body(): lax.psum(mixed_scan.astype(jnp.bfloat16), 'dir').astype(jnp.float32)  89.9 us
    psum x1, blocking collectives, body(): lax.psum((gain_all, shift_all, in_all, out_all, rate_all, turn_all, skip_...  66.7 us
    add x144, other arithmetic, sweep_chain(): lax.associative_scan(combine_steps, (factor_re, factor_im, drive_re, driv...  58.4 us
  transfers between devices with their start and end apart: 7, of which 4 were waited for; matrix products, arithmetic and copies ran while one was open for 10% of the time, Pallas kernels for 0%

commit v1 on v0

v1 whole, which is shorter than its diff:
```python
import functools

import jax
import jax.numpy as jnp
from jax import lax
from jax.experimental import pallas as pl
from jax.experimental.pallas import tpu as pltpu
from jax.sharding import PartitionSpec as P

LENGTH = 16384
LONGEST_RUN = 8192

eps = 1e-05
inv_root_two = 0.7071067811865476
inv_root_two_pi = 0.3989422804014327

f32 = jnp.float32
bf16 = jnp.bfloat16


LANES = 128
ELEMENT_ROWS = 32
UNROLL = 4


def core_place(row_devices):
    core = lax.axis_index("dir")
    return core, lax.rem(lax.axis_index("seq"), row_devices) * 2 + core


def dot(a, b):
    return jnp.dot(a, b, preferred_element_type=f32)


def dot_nt(a, b):
    return lax.dot_general(a, b, (((1,), (1,)), ((), ())), preferred_element_type=f32)


def dot_tn(a, b):
    return lax.dot_general(a, b, (((0,), (0,)), ((), ())), preferred_element_type=f32)


def squared(re, im, times):
    for _ in range(times):
        re, im = re * re - im * im, 2.0 * re * im
    return re, im


def over_blocks(rows, step, init=()):
    def one(i, carry):
        return step(pl.multiple_of(i * ELEMENT_ROWS, ELEMENT_ROWS), carry)

    return lax.fori_loop(0, rows // ELEMENT_ROWS, one, init)


def fold(values):
    total = values[0:8]
    for start in range(8, values.shape[0], 8):
        total = total + values[start : start + 8]
    return total


class Lanes:
    def __init__(self, rows_ref, tiles_ref, layer, adjoint, spans, rows):
        states = rows_ref.shape[2]
        self.states = states
        self.rows_ref, self.layer = rows_ref, layer
        flip = -1.0 if adjoint else 1.0
        self.step = []
        self.run = []
        self.block = []
        for side in range(2):
            row = 8 * side
            re = rows_ref[layer, row : row + 1, :]
            im = rows_ref[layer, row + 1 : row + 2, :] * flip
            self.step.append((jnp.broadcast_to(re, (8, states)), jnp.broadcast_to(im, (8, states))))
            self.run.append(squared(re, im, (spans - 1).bit_length()))
            thirds = states // LANES
            tile_re = tiles_ref[layer, 8 * side : 8 * side + thirds, :]
            tile_im = tiles_ref[layer, 8 * side + thirds : 8 * side + 2 * thirds, :] * flip
            self.block.append(squared(tile_re, tile_im, (rows - 1).bit_length()))

    def scaling(self, side):
        row = self.rows_ref[self.layer, 8 * side + 2 : 8 * side + 3, :]
        return jnp.concatenate([row, row], 1)


def sweep(first_forward, drives, masks, lanes, init, visit=None, totals=()):
    states = lanes.states
    span = drives[0].shape[0] // 8

    def step(i, carry):
        values, sums = carry
        up = pl.multiple_of(i * 8, 8)
        down = pl.multiple_of((span - 1 - i) * 8, 8)
        places = (jnp.where(first_forward, up, down), jnp.where(first_forward, down, up))
        new = []
        for side in range(2):
            rows = pl.ds(pl.multiple_of(places[side], 8), 8)
            keep = masks[side][rows, :]
            keep = jnp.concatenate([keep] * (states // LANES), 1)
            step_re, step_im = lanes.step[side]
            step_re, step_im = step_re * keep, step_im * keep
            re, im = values[side]
            drive_re = drives[side][rows, :states]
            drive_im = drives[side][rows, states:]
            re, im = (
                step_re * re - step_im * im + drive_re,
                step_re * im + step_im * re + drive_im,
            )
            new.append((re, im))
            if visit is not None:
                sums = visit(side, rows, re, im, sums)
        return tuple(new), sums

    return lax.fori_loop(0, span, step, (init, totals), unroll=UNROLL)


def run_chain(first_up, lanes, side, ends, whole, start, places):
    states = lanes.states
    power_re, power_im = lanes.run[side]
    re, im = start
    for i in range(8):
        s = jnp.where(first_up, i, 7 - i)
        row = pl.ds(s, 1)
        if places is not None:
            places[row, :states] = re
            places[row, states:] = im
        passes = whole[row, :]
        passes = jnp.concatenate([passes] * (states // LANES), 1)
        pass_re, pass_im = power_re * passes, power_im * passes
        end_re, end_im = ends[row, :states], ends[row, states:]
        re, im = (end_re + pass_re * re - pass_im * im, end_im + pass_re * im + pass_im * re)
    return re, im


def first_pass(running_up, drives, masks, wholes, lanes, ids_ref, ends, payload):
    states = lanes.states
    thirds = states // LANES
    nothing = jnp.zeros((8, states), f32)
    zero = (nothing, nothing)
    values, _ = sweep(running_up, drives, masks, lanes, (zero, zero))
    payload[...] = jnp.zeros_like(payload)
    for side in range(2):
        ends[side][:, :states] = values[side][0]
        ends[side][:, states:] = values[side][1]
        upward = running_up if side == 0 else jnp.logical_not(running_up)
        start = jnp.zeros((1, states), f32)
        re, im = run_chain(upward, lanes, side, ends[side], wholes[side], (start, start), None)
        base = jnp.where(upward, 0, 8)
        for i in range(thirds):
            payload[pl.ds(base + i, 1), :] = re[:, LANES * i : LANES * (i + 1)]
            payload[pl.ds(base + thirds + i, 1), :] = im[:, LANES * i : LANES * (i + 1)]
        payload[8 * side + 6 : 8 * side + 8, :] = ids_ref[0:2, :]


def entering(upward, place, lanes, side, gathered, ids_ref, small):
    states = lanes.states
    thirds = states // LANES
    count = gathered.shape[0]
    rows = lanes.token_rows
    block_re, block_im = lanes.block[side]
    re = jnp.zeros((thirds, LANES), f32)
    im = jnp.zeros((thirds, LANES), f32)
    base = jnp.where(upward, 0, 8)
    key = jnp.where(upward, ids_ref[0:1, :], ids_ref[1:2, :])
    for distance in range(min(count - 1, LONGEST_RUN // rows), 0, -1):
        source = jnp.where(upward, place - distance, place + distance)
        inside = jnp.logical_and(source >= 0, source < count)
        source = jnp.clip(source, 0, count - 1)
        sent_re = gathered[source, pl.ds(base, thirds), :]
        sent_im = gathered[source, pl.ds(base + thirds, thirds), :]
        sent_key = gathered[source, pl.ds(jnp.where(upward, base + 7, base + 6), 1), :]
        joined = jnp.where(jnp.logical_and(sent_key == key, inside), 1.0, 0.0)
        re, im = (
            joined * sent_re + block_re * re - block_im * im,
            joined * sent_im + block_re * im + block_im * re,
        )
    small[0:thirds, :] = re
    small[thirds : 2 * thirds, :] = im
    wide_re = jnp.concatenate([small[i : i + 1, :] for i in range(thirds)], 1)
    wide_im = jnp.concatenate([small[thirds + i : thirds + i + 1, :] for i in range(thirds)], 1)
    return wide_re, wide_im


def second_starts(running_up, place, lanes, gathered, ids_ref, ends, wholes, places, small):
    init = []
    states = lanes.states
    for side in range(2):
        upward = running_up if side == 0 else jnp.logical_not(running_up)
        start = entering(upward, place, lanes, side, gathered, ids_ref, small)
        run_chain(upward, lanes, side, ends[side], wholes[side], start, places)
        init.append((places[:, :states], places[:, states:]))
    return tuple(init)


def make_lanes(rows_ref, tiles_ref, layer, adjoint, token_rows):
    lanes = Lanes(rows_ref, tiles_ref, layer, adjoint, token_rows // 8, token_rows)
    lanes.token_rows = token_rows
    return lanes


def standardise(x):
    width = x.shape[1]
    average = jnp.sum(x, 1, keepdims=True) * (1.0 / width)
    centred = x - average
    inv_scale = lax.rsqrt(jnp.sum(centred * centred, 1, keepdims=True) * (1.0 / width) + eps)
    return centred * inv_scale, inv_scale


def fill_columns(columns, values):
    for i in range(columns.shape[0]):
        columns[i] = values[:, i * LANES : (i + 1) * LANES].astype(columns.dtype)


def tile_order(columns, first, count, span):
    tiles = [
        jnp.concatenate([columns[i, pl.ds(first + j, 8, stride=span), :] for i in range(columns.shape[0])], 1)
        for j in range(count)
    ]
    return jnp.concatenate(tiles, 0)


def store_token_order(columns, first, values, span):
    for j in range(values.shape[0] // 8):
        for i in range(columns.shape[0]):
            columns[i, pl.ds(first + j, 8, stride=span), :] = values[8 * j : 8 * j + 8, i * LANES : (i + 1) * LANES]


def join_columns(out, columns):
    for i in range(columns.shape[0]):
        out[:, i * LANES : (i + 1) * LANES] = columns[i]


def one_minus_exp(x):
    series = jnp.ones_like(x)
    for term in range(12, 1, -1):
        series = 1.0 - x * (1.0 / term) * series
    return jnp.where(x < 0.5, x * series, 1.0 - jnp.exp(-x))


def table_rows(table, layer, base, rate, turn):
    frequency = turn[layer, 0, 0:1, :]
    log_step = turn[layer, 0, 1:2, :]
    step_size = jnp.exp(log_step)
    damping = jnp.exp(rate[layer, 0:1, :] + log_step)
    magnitude = jnp.exp(-damping)
    rotation = frequency * step_size
    square = magnitude * magnitude
    rows = (
        magnitude * jnp.cos(rotation), magnitude * jnp.sin(rotation), jnp.sqrt(one_minus_exp(2.0 * damping)), damping,
        step_size, rotation, square,
    )
    for i, row in enumerate(rows):
        table[layer, base + i : base + i + 1, :] = row


def open_kernel(
    row_devices,
    tokens,
    segments,
    gain,
    bias,
    rate,
    turn,
    in_own,
    x_out,
    normed_out,
    inv_out,
    mixed_out,
    drive_out,
    keep_own,
    keep_oth,
    whole_out,
    table,
    ids,
    natural,
    rows8,
):
    core, _ = core_place(row_devices)
    rows = x_out.shape[0]
    span = rows // 8
    base = pl.multiple_of(core * rows, rows)
    fill_columns(natural, tokens[pl.ds(base, rows), :].astype(f32))
    table[...] = jnp.zeros_like(table)
    for layer in range(table.shape[0]):
        table_rows(table, layer, 0, rate, turn)

    number = segments[...].astype(f32)
    count = number.shape[0]
    lane = lax.broadcasted_iota(jnp.int32, number.shape, 1)
    row = lax.broadcasted_iota(jnp.int32, number.shape, 0)
    back = pltpu.roll(number, 1, 1)
    back = jnp.where(lane == 0, pltpu.roll(back, 1, 0), back)
    ahead = pltpu.roll(number, LANES - 1, 1)
    ahead = jnp.where(lane == LANES - 1, pltpu.roll(ahead, count - 1, 0), ahead)
    edge_first = jnp.logical_and(lane == 0, row == 0)
    edge_last = jnp.logical_and(lane == LANES - 1, row == count - 1)
    up_keep = jnp.where(jnp.logical_or(number == back, edge_first), 1.0, 0.0)
    down_keep = jnp.where(jnp.logical_or(number == ahead, edge_last), 1.0, 0.0)
    per = LANES // span
    used = 8 // per
    for side, out in ((0, keep_own), (1, keep_oth)):
        rows8[0:count, :] = jnp.where(core == side, up_keep, down_keep)
        half = rows8[pl.ds(core * used, used), :]
        runs = jnp.concatenate([half[s // per : s // per + 1] for s in range(8)], 0)
        place = lax.broadcasted_iota(jnp.int32, (8, LANES), 1)
        sub = lax.broadcasted_iota(jnp.int32, (8, LANES), 0)
        first = lax.rem(sub, per) * span
        inside = jnp.logical_and(place >= first, place < first + span)
        least = jnp.min(jnp.where(inside, runs, 1.0), 1, keepdims=True)
        whole_out[side] = jnp.broadcast_to(least, (8, LANES))
        step = lax.broadcasted_iota(jnp.int32, (span, 8, LANES), 0)
        spread = jnp.where(step == (place - first)[None], runs[None], 0.0)
        spread = spread.reshape(span * 8, LANES).astype(bf16)
        out[...] = dot(spread, jnp.ones((LANES, LANES), bf16))
    rows8[0:count, :] = number
    first_row = rows8[pl.ds(core * used, 1), :]
    last_row = rows8[pl.ds(core * used + used - 1, 1), :]
    ids[...] = jnp.zeros_like(ids)
    ids[0:1, :] = jnp.broadcast_to(first_row[:, 0:1], (1, LANES))
    ids[1:2, :] = jnp.broadcast_to(last_row[:, LANES - 1 : LANES], (1, LANES))

    def element(start, carry):
        x = tile_order(natural, start // 8, ELEMENT_ROWS // 8, span)
        normed, inv_scale = standardise(x)
        block = pl.ds(start, ELEMENT_ROWS)
        x_out[block, :] = x
        normed_out[block, :] = normed
        inv_out[block, :] = jnp.broadcast_to(inv_scale, (ELEMENT_ROWS, LANES))
        mixed_out[block, :] = (normed * gain[0:1, :] + bias[0:1, :]).astype(bf16)
        return carry

    over_blocks(rows, element)
    scale = table[0, 2:3, :]
    drive_out[...] = dot(mixed_out[...], in_own[0, 0]) * jnp.concatenate([scale, scale], 1)


def open_second_kernel(
    row_devices,
    mixed_low,
    in_oth,
    rate,
    turn,
    table_in,
    drive_own,
    keep_own,
    keep_oth,
    whole,
    ids,
    drive_oth,
    ends_own,
    ends_oth,
    payload,
    table,
    tiles,
):
    core, _ = core_place(row_devices)
    table[...] = table_in[...]
    tiles[...] = jnp.zeros_like(tiles)
    thirds = table.shape[2] // LANES
    for layer in range(table.shape[0]):
        table_rows(table, layer, 8, rate, turn)
        for side in range(2):
            for part in range(2):
                for i in range(thirds):
                    at = 8 * side + part * thirds + i
                    tiles[layer, at : at + 1, :] = table[
                        layer, 8 * side + part : 8 * side + part + 1, i * LANES : (i + 1) * LANES
                    ]
    scale = table[0, 10:11, :]
    drive_oth[...] = dot(mixed_low[...], in_oth[0, 0]) * jnp.concatenate([scale, scale], 1)
    rows = drive_own.shape[0]
    lanes = make_lanes(table, tiles, 0, False, rows)
    first_pass(
        core == 0,
        (drive_own, drive_oth),
        (keep_own, keep_oth),
        (whole.at[0], whole.at[1]),
        lanes,
        ids,
        (ends_own, ends_oth),
        payload,
    )


def forward_states(layer, info, gathered, ends, drives, masks, whole, rows_ref, tiles_ref, ids, states, lows, places, small):
    rows = drives[0].shape[0]
    lanes = make_lanes(rows_ref, tiles_ref, layer, False, rows)
    core, place = info
    running_up = core == 0
    init = second_starts(
        running_up, place, lanes, gathered, ids, ends, (whole.at[0], whole.at[1]), places, small
    )
    width = lanes.states

    def visit(side, where, re, im, sums):
        states[side][where, :width] = re
        states[side][where, width:] = im
        return sums

    sweep(running_up, drives, masks, lanes, init, visit)
    for side in range(2):
        lows[side][...] = states[side][...].astype(bf16)


def mid_kernel(
    row_devices,
    gathered,
    ends_own,
    ends_oth,
    drive_own,
    drive_oth,
    keep_own,
    keep_oth,
    whole,
    rows_ref,
    tiles_ref,
    ids,
    out_own,
    out_oth,
    x_in,
    normed,
    gain,
    bias,
    skip,
    glu,
    glu_bias,
    in_own,
    in_oth,
    low_own,
    low_oth,
    combined_out,
    phi_out,
    sig_out,
    act_low,
    x_out,
    normed_out,
    inv_out,
    mixed_out,
    next_own,
    next_oth,
    next_ends_own,
    next_ends_oth,
    payload,
    places,
    small,
    wide,
    states_own,
    states_oth,
):
    info = core_place(row_devices)
    rows = x_in.shape[0]
    masks = (keep_own, keep_oth)
    forward_states(
        0, info, gathered, (ends_own, ends_oth), (drive_own, drive_oth), masks, whole, rows_ref, tiles_ref,
        ids, (states_own, states_oth), (low_own, low_oth), places, small,
    )
    wide[...] = dot(low_own[...], out_own[0, 0]) + dot(low_oth[...], out_oth[0, 0])

    def element(start, carry):
        block = pl.ds(start, ELEMENT_ROWS)
        mixed = normed[block, :] * gain[0:1, :] + bias[0:1, :]
        combined = wide[block, :] + skip[0:1, :] * mixed
        phi = 0.5 * (1.0 + lax.erf(combined * inv_root_two))
        combined_out[block, :] = combined
        phi_out[block, :] = phi
        act_low[block, :] = (combined * phi).astype(bf16)
        return carry

    over_blocks(rows, element)
    wide[...] = dot(act_low[...], glu[0])

    def element_two(start, carry):
        block = pl.ds(start, ELEMENT_ROWS)
        sig = jax.nn.sigmoid(wide[block, :] + glu_bias[0:1, :])
        sig_out[block, :] = sig
        x = x_in[block, :] + combined_out[block, :] * phi_out[block, :] * sig
        x_out[block, :] = x
        after, inv_scale = standardise(x)
        normed_out[block, :] = after
        inv_out[block, :] = jnp.broadcast_to(inv_scale, (ELEMENT_ROWS, LANES))
        mixed_out[block, :] = (after * gain[1:2, :] + bias[1:2, :]).astype(bf16)
        return carry

    over_blocks(rows, element_two)
    for side, (matrix, out) in enumerate(((in_own, next_own), (in_oth, next_oth))):
        scale = rows_ref[1, 8 * side + 2 : 8 * side + 3, :]
        out[...] = dot(mixed_out[...], matrix[1, 0]) * jnp.concatenate([scale, scale], 1)
    lanes = make_lanes(rows_ref, tiles_ref, 1, False, rows)
    first_pass(
        info[0] == 0,
        (next_own, next_oth),
        masks,
        (whole.at[0], whole.at[1]),
        lanes,
        ids,
        (next_ends_own, next_ends_oth),
        payload,
    )


def backward_half(
    layer, info, grad, combined, phi, sig, normed, gain, bias, skip, glu, out_own, out_oth, masks, whole,
    rows_ref, tiles_ref, ids, gate_low, combined_grad, combined_low, grad_own, grad_oth, ends, payload, sums, wide,
):
    rows = grad.shape[0]
    width = grad.shape[1]
    zero = jnp.zeros((8, width), f32)

    def element(start, carry):
        block = pl.ds(start, ELEMENT_ROWS)
        gate = sig[block, :]
        gate_grad = grad[block, :] * (combined[block, :] * phi[block, :]) * gate * (1.0 - gate)
        gate_low[block, :] = gate_grad.astype(bf16)
        return carry + fold(gate_grad)

    bias_sum = over_blocks(rows, element, zero)
    wide[...] = dot_nt(gate_low[...], glu[layer])

    def element_two(start, carry):
        block = pl.ds(start, ELEMENT_ROWS)
        value = combined[block, :]
        activation_grad = grad[block, :] * sig[block, :] + wide[block, :]
        slope = phi[block, :] + value * (jnp.exp(-0.5 * value * value) * inv_root_two_pi)
        result = activation_grad * slope
        combined_grad[block, :] = result
        combined_low[block, :] = result.astype(bf16)
        mixed = normed[block, :] * gain[layer : layer + 1, :] + bias[layer : layer + 1, :]
        return carry + fold(result * mixed)

    skip_sum = over_blocks(rows, element_two, zero)
    sums[0:1, :] = jnp.sum(bias_sum, 0, keepdims=True)
    sums[1:2, :] = jnp.sum(skip_sum, 0, keepdims=True)
    grad_own[...] = dot_nt(combined_low[...], out_own[layer, 0])
    grad_oth[...] = dot_nt(combined_low[...], out_oth[layer, 0])
    lanes = make_lanes(rows_ref, tiles_ref, layer, True, rows)
    first_pass(
        info[0] == 1,
        (grad_own, grad_oth),
        (masks[1], masks[0]),
        (whole.at[1], whole.at[0]),
        lanes,
        ids,
        ends,
        payload,
    )


def turn_kernel(
    row_devices,
    gathered,
    ends_own,
    ends_oth,
    drive_own,
    drive_oth,
    keep_own,
    keep_oth,
    whole,
    rows_ref,
    tiles_ref,
    ids,
    out_own,
    out_oth,
    x_in,
    normed,
    gain,
    bias,
    skip,
    glu,
    glu_bias,
    cotangent,
    low_own,
    low_oth,
    block_out,
    grad_out,
    act_low,
    gate_low,
    combined_grad,
    combined_low,
    grad_own,
    grad_oth,
    next_ends_own,
    next_ends_oth,
    payload,
    sums,
    places,
    small,
    wide,
    combined,
    phi_rows,
    sig_rows,
    natural,
    natural_out,
    states_own,
    states_oth,
):
    info = core_place(row_devices)
    rows = x_in.shape[0]
    span = rows // 8
    masks = (keep_own, keep_oth)
    forward_states(
        1, info, gathered, (ends_own, ends_oth), (drive_own, drive_oth), masks, whole, rows_ref, tiles_ref,
        ids, (states_own, states_oth), (low_own, low_oth), places, small,
    )
    wide[...] = dot(low_own[...], out_own[1, 0]) + dot(low_oth[...], out_oth[1, 0])

    def element(start, carry):
        block = pl.ds(start, ELEMENT_ROWS)
        mixed = normed[block, :] * gain[1:2, :] + bias[1:2, :]
        value = wide[block, :] + skip[1:2, :] * mixed
        phi = 0.5 * (1.0 + lax.erf(value * inv_root_two))
        combined[block, :] = value
        phi_rows[block, :] = phi
        act_low[block, :] = (value * phi).astype(bf16)
        return carry

    over_blocks(rows, element)
    wide[...] = dot(act_low[...], glu[1])
    base = pl.multiple_of(info[0] * rows, rows)
    fill_columns(natural, cotangent[pl.ds(base, rows), :])

    def element_two(start, carry):
        block = pl.ds(start, ELEMENT_ROWS)
        sig = jax.nn.sigmoid(wide[block, :] + glu_bias[1:2, :])
        sig_rows[block, :] = sig
        result = x_in[block, :] + combined[block, :] * phi_rows[block, :] * sig
        store_token_order(natural_out, start // 8, result, span)
        grad_out[block, :] = tile_order(natural, start // 8, ELEMENT_ROWS // 8, span)
        return carry

    over_blocks(rows, element_two)
    join_columns(block_out, natural_out)
    sums[...] = jnp.zeros_like(sums)
    backward_half(
        1, info, grad_out, combined, phi_rows, sig_rows, normed, gain, bias, skip, glu, out_own, out_oth, masks,
        whole, rows_ref, tiles_ref, ids, gate_low, combined_grad, combined_low, grad_own, grad_oth,
        (next_ends_own, next_ends_oth), payload, sums, wide,
    )


def adjoint_states(
    layer, info, gathered, ends, grads, masks, whole, rows_ref, tiles_ref, ids, states, drives, lows, decay_sums,
    adjoints, places, small,
):
    rows = grads[0].shape[0]
    lanes = make_lanes(rows_ref, tiles_ref, layer, True, rows)
    core, place = info
    running_up = core == 1
    init = second_starts(
        running_up, place, lanes, gathered, ids, ends, (whole.at[1], whole.at[0]), places, small
    )
    width = lanes.states
    zero = jnp.zeros((8, width), f32)
    for side in range(2):
        adjoints[side][...] = states[side][...].astype(f32)

    def visit(side, where, re, im, sums):
        drive_re, drive_im = drives[side][where, :width], drives[side][where, width:]
        moved_re = adjoints[side][where, :width] - drive_re
        moved_im = adjoints[side][where, width:] - drive_im
        adjoints[side][where, :width] = re
        adjoints[side][where, width:] = im
        mine = sums[side]
        mine = (
            mine[0] + (re * moved_re + im * moved_im),
            mine[1] + (im * moved_re - re * moved_im),
            mine[2] + (re * drive_re + im * drive_im),
        )
        return (mine, sums[1]) if side == 0 else (sums[0], mine)

    _, sums = sweep(
        running_up, grads, (masks[1], masks[0]), lanes, init, visit, ((zero, zero, zero), (zero, zero, zero))
    )
    decay_sums[...] = jnp.zeros_like(decay_sums)
    for side in range(2):
        for i in range(3):
            decay_sums[3 * side + i : 3 * side + i + 1, :] = jnp.sum(sums[side][i], 0, keepdims=True)
        lows[side][...] = (adjoints[side][...] * lanes.scaling(side)).astype(bf16)


def norm_backward(
    layer, low_own, low_oth, in_own, in_oth, grad, combined_grad, normed, inv_scale, gain, skip, sums, wide, finish
):
    rows, width = grad.shape
    wide[...] = dot_nt(low_own[...], in_own[layer, 0]) + dot_nt(low_oth[...], in_oth[layer, 0])
    zero = jnp.zeros((8, width), f32)

    def element(start, carry):
        block = pl.ds(start, ELEMENT_ROWS)
        mixed_grad = wide[block, :] + combined_grad[block, :] * skip[layer : layer + 1, :]
        unit = normed[block, :]
        weighted = mixed_grad * unit
        inner = mixed_grad * gain[layer : layer + 1, :]
        mean_one = jnp.sum(inner, 1, keepdims=True) * (1.0 / width)
        mean_two = jnp.sum(weighted * gain[layer : layer + 1, :], 1, keepdims=True) * (1.0 / width)
        spread = jnp.concatenate([inv_scale[block, :]] * (width // LANES), 1)
        finish(start, grad[block, :] + spread * (inner - mean_one - unit * mean_two))
        return carry[0] + fold(weighted), carry[1] + fold(mixed_grad)

    gain_sum, bias_sum = over_blocks(rows, element, (zero, zero))
    sums[2:3, :] = jnp.sum(gain_sum, 0, keepdims=True)
    sums[3:4, :] = jnp.sum(bias_sum, 0, keepdims=True)


def back_kernel(
    row_devices,
    gathered,
    ends_own,
    ends_oth,
    grad_own,
    grad_oth,
    keep_own,
    keep_oth,
    whole,
    rows_ref,
    tiles_ref,
    ids,
    states_own,
    states_oth,
    drive_own,
    drive_oth,
    in_own,
    in_oth,
    out_own,
    out_oth,
    grad_in,
    combined_grad_in,
    normed_in,
    inv_in,
    gain,
    bias,
    skip,
    glu,
    combined,
    phi,
    sig,
    normed,
    low_own,
    low_oth,
    decay_sums,
    grad_out,
    gate_low,
    combined_grad,
    combined_low,
    next_own,
    next_oth,
    next_ends_own,
    next_ends_oth,
    payload,
    sums,
    places,
    small,
    wide,
    adjoint_own,
    adjoint_oth,
):
    info = core_place(row_devices)
    masks = (keep_own, keep_oth)
    adjoint_states(
        1, info, gathered, (ends_own, ends_oth), (grad_own, grad_oth), masks, whole, rows_ref, tiles_ref, ids,
        (states_own, states_oth), (drive_own, drive_oth), (low_own, low_oth), decay_sums,
        (adjoint_own, adjoint_oth), places, small,
    )
    sums[...] = jnp.zeros_like(sums)

    def finish(start, value):
        grad_out[pl.ds(start, ELEMENT_ROWS), :] = value

    norm_backward(
        1, low_own, low_oth, in_own, in_oth, grad_in, combined_grad_in, normed_in, inv_in, gain, skip, sums, wide,
        finish,
    )
    backward_half(
        0, info, grad_out, combined, phi, sig, normed, gain, bias, skip, glu, out_own, out_oth, masks, whole,
        rows_ref, tiles_ref, ids, gate_low, combined_grad, combined_low, next_own, next_oth,
        (next_ends_own, next_ends_oth), payload, sums, wide,
    )


def last_kernel(
    row_devices,
    gathered,
    ends_own,
    ends_oth,
    grad_own,
    grad_oth,
    keep_own,
    keep_oth,
    whole,
    rows_ref,
    tiles_ref,
    ids,
    states_own,
    states_oth,
    drive_own,
    drive_oth,
    mixed_low,
    low_own,
    low_oth,
    decay_sums,
    mine,
    theirs,
    places,
    small,
    adjoint_own,
    adjoint_oth,
):
    info = core_place(row_devices)
    masks = (keep_own, keep_oth)
    adjoint_states(
        0, info, gathered, (ends_own, ends_oth), (grad_own, grad_oth), masks, whole, rows_ref, tiles_ref, ids,
        (states_own, states_oth), (drive_own, drive_oth), (low_own, low_oth), decay_sums,
        (adjoint_own, adjoint_oth), places, small,
    )
    store_columns(mine, 0, dot_tn(mixed_low[...], low_own[...]))
    store_columns(theirs, 0, dot_tn(mixed_low[...], low_oth[...]))


def final_kernel(
    low_own, low_oth, in_own, in_oth, grad_in, combined_grad, normed, inv_scale, gain, skip, out, sums, wide, natural
):
    rows = grad_in.shape[0]
    sums[...] = jnp.zeros_like(sums)

    def finish(start, value):
        store_token_order(natural, start // 8, value, rows // 8)

    norm_backward(
        0, low_own, low_oth, in_own, in_oth, grad_in, combined_grad, normed, inv_scale, gain, skip, sums, wide, finish
    )
    join_columns(out, natural)


def store_columns(out, first, values):
    rows, width = values.shape
    for i in range(width // LANES):
        out[first + i * rows : first + (i + 1) * rows, :] = values[:, i * LANES : (i + 1) * LANES].astype(out.dtype)


def half_rows(core, act_low, gate_low, mine, theirs, first, wide):
    wide[...] = dot_tn(act_low[...], gate_low[...])
    half = wide.shape[0] // 2
    width = wide.shape[1]
    for out, which in ((mine, core), (theirs, 1 - core)):
        rows = pl.ds(pl.multiple_of(which * half, half), half)
        for i in range(width // LANES):
            out[first + i * half : first + (i + 1) * half, :] = wide[rows, i * LANES : (i + 1) * LANES].astype(out.dtype)


def weights_kernel(act_low, gate_low, combined_low, low_own, low_oth, payload_in, mine, theirs, payload, wide):
    payload[...] = payload_in[...]
    core = lax.axis_index("dir")
    store_columns(theirs, 0, dot_tn(low_oth[...], combined_low[...]))
    store_columns(mine, 0, dot_tn(low_own[...], combined_low[...]))
    size = low_own.shape[1] * (combined_low.shape[1] // LANES)
    half_rows(core, act_low, gate_low, mine, theirs, size, wide)


def weights_two_kernel(
    mixed_low, in_low_own, in_low_oth, act_low, gate_low, combined_low, low_own, low_oth, payload_in, mine, theirs,
    payload, wide,
):
    payload[...] = payload_in[...]
    core = lax.axis_index("dir")
    store_columns(theirs, 0, dot_tn(mixed_low[...], in_low_oth[...]))
    store_columns(mine, 0, dot_tn(mixed_low[...], in_low_own[...]))
    size = mixed_low.shape[1] * (in_low_own.shape[1] // LANES)
    store_columns(theirs, size, dot_tn(low_oth[...], combined_low[...]))
    store_columns(mine, size, dot_tn(low_own[...], combined_low[...]))
    size = size + low_own.shape[1] * (combined_low.shape[1] // LANES)
    half_rows(core, act_low, gate_low, mine, theirs, size, wide)


def slot(low_bit, parts):
    return jnp.bitwise_and(jnp.right_shift(lax.axis_index("seq"), low_bit), parts - 1)


def sum_kernel(count, low_bit, *refs):
    sources, outs = refs[:count], refs[count:]
    parts = len(outs)
    rows = outs[0].shape[0]
    mine = slot(low_bit, parts) if parts > 1 else 0
    for k, out in enumerate(outs):
        where = pl.ds(pl.multiple_of(jnp.bitwise_xor(mine, k) * rows, rows), rows) if parts > 1 else slice(None)
        total = sources[0][where, :].astype(f32)
        for source in sources[1:]:
            total = total + source[where, :].astype(f32)
        out[...] = total.astype(out.dtype)


def gather_kernel(low_bit, *refs):
    sources, out = refs[:-1], refs[-1]
    rows = sources[0].shape[0]
    mine = slot(low_bit, len(sources))
    for k, source in enumerate(sources):
        out[pl.ds(pl.multiple_of(jnp.bitwise_xor(mine, k) * rows, rows), rows), :] = source[...]


def join_kernel(mine, theirs, out):
    core = lax.axis_index("dir")
    rows = mine.shape[0]
    out[pl.ds(pl.multiple_of(core * rows, rows), rows), :] = mine[...]
    out[pl.ds(pl.multiple_of((1 - core) * rows, rows), rows), :] = theirs[...]


def matrix_columns(source, first, out):
    rows, width = out.shape
    for i in range(width // LANES):
        out[:, i * LANES : (i + 1) * LANES] = source[first + i * rows : first + (i + 1) * rows, :].astype(f32)


def unpack_kernel(layer_of, olds, gate_rows, *refs):
    refs = list(refs)
    take = lambda n: [refs.pop(0) for _ in range(n)]
    sources = take(4)
    take(olds)
    outs = take(len(layer_of))
    gate_out = take(1 if gate_rows else 0)
    buffers = take(len(layer_of))
    whole, sems = refs
    gather_kernel(0, *sources, whole)
    first = 0
    copies = []
    for i, layer in enumerate(layer_of):
        buffer, out = buffers[i], outs[i]
        matrix_columns(whole, first, buffer)
        first = first + buffer.shape[0] * (buffer.shape[1] // LANES)
        copies.append(pltpu.make_async_copy(buffer, out.at[layer, 0], sems.at[i]))
        copies[-1].start()
    for out in gate_out:
        out[...] = whole[first : first + gate_rows, :]
    for copy in copies:
        copy.wait()


def gate_kernel(mine_early, theirs_early, mine_middle, theirs_middle, out):
    core = lax.axis_index("dir")
    half = out.shape[1] // 2
    width = out.shape[2]
    for layer, mine, theirs in ((1, mine_early, theirs_early), (0, mine_middle, theirs_middle)):
        for source, which in ((mine, core), (theirs, 1 - core)):
            rows = pl.ds(pl.multiple_of(which * half, half), half)
            for i in range(width // LANES):
                out[layer, rows, i * LANES : (i + 1) * LANES] = source[i * half : (i + 1) * half, :].astype(f32)


def small_pack_kernel(sums_turn, sums_back, sums_last, decay_late, decay_early, send, own):
    per = sums_turn.shape[1] // LANES
    thirds = decay_late.shape[1] // LANES
    send[...] = jnp.zeros_like(send)
    own[...] = jnp.zeros_like(own)
    kinds = (
        ((sums_last, 2), (sums_back, 2)),
        ((sums_last, 3), (sums_back, 3)),
        ((sums_back, 1), (sums_turn, 1)),
        ((sums_back, 0), (sums_turn, 0)),
    )
    at = 0
    for kind in kinds:
        for source, row in kind:
            for i in range(per):
                value = source[row : row + 1, i * LANES : (i + 1) * LANES]
                send[at : at + 1, :] = value
                own[at : at + 1, :] = value
                at += 1
    for source in (decay_late, decay_early):
        for term in range(3):
            for i in range(thirds):
                lanes = slice(i * LANES, (i + 1) * LANES)
                own[at : at + 1, :] = source[term : term + 1, lanes]
                send[at : at + 1, :] = source[3 + term : 4 + term, lanes]
                at += 1


def small_kernel(tokens_rows, own, got, table, out):
    layers, _, states = table.shape
    thirds = states // LANES
    out[...] = jnp.zeros_like(out)
    out[0:tokens_rows, :] = own[0:tokens_rows, :] + got[0:tokens_rows, :]
    for layer in range(layers):
        for i in range(thirds):
            lanes = slice(i * LANES, (i + 1) * LANES)
            base = tokens_rows + (layer * 3) * thirds + i
            term_re, term_im, term_scale = (
                own[base + t * thirds : base + t * thirds + 1, :] + got[base + t * thirds : base + t * thirds + 1, :]
                for t in range(3)
            )
            re, im, scale, damping, step_size, rotation, square = (
                table[layer, t : t + 1, lanes] for t in range(7)
            )
            grad_re = (term_re * re - term_im * im) / square
            grad_im = (term_re * im + term_im * re) / square
            grad_scale = term_scale / scale
            grad_damping = grad_scale * square / scale - (grad_re * re + grad_im * im)
            grad_rotation = grad_im * re - grad_re * im
            log_rate = grad_damping * damping
            at = tokens_rows + layer * thirds + i
            out[at : at + 1, :] = log_rate
            at = tokens_rows + layers * thirds + (layer * 2) * thirds + i
            out[at : at + 1, :] = grad_rotation * step_size
            out[at + thirds : at + thirds + 1, :] = log_rate + grad_rotation * rotation


def add_kernel(*refs):
    total = refs[0][...]
    for source in refs[1:-1]:
        total = total + source[...]
    refs[-1][...] = total


def small_out_kernel(*refs):
    sources, (gain, bias, rate, turn, skip, gate) = refs[:-6], refs[-6:]
    layers, width = gain.shape
    per = width // LANES
    thirds = rate.shape[1] // LANES
    total = sources[0][...]
    for source in sources[1:]:
        total = total + source[...]
    at = 0
    for out in (gain, bias, skip, gate):
        for layer in range(layers):
            for i in range(per):
                out[layer : layer + 1, i * LANES : (i + 1) * LANES] = total[at : at + 1]
                at += 1
    for layer in range(layers):
        for i in range(thirds):
            rate[layer : layer + 1, i * LANES : (i + 1) * LANES] = total[at : at + 1]
            at += 1
    for row in range(2 * layers):
        for i in range(thirds):
            turn[row : row + 1, i * LANES : (i + 1) * LANES] = total[at : at + 1]
            at += 1


class Order:
    def __init__(self):
        self.tile = None

    def run(self, kernel, outs, operands, scratch=(), flops=0, name=None, spare=8, after=(), free_outs=0, alias=None,
            semaphores=0):
        whole = pl.BlockSpec(memory_space=pltpu.VMEM)
        free = pl.BlockSpec(memory_space=pl.ANY)
        waits = list(after) + ([] if self.tile is None else [self.tile])
        inputs, results = len(operands), len(outs)
        skipped = len(waits)

        def body(*refs):
            token = refs[skipped + inputs]
            token[...] = jnp.zeros_like(token)
            kernel(*refs[skipped : skipped + inputs], *refs[skipped + inputs + 1 :])

        shapes = [jax.ShapeDtypeStruct((8, LANES), f32)]
        shapes += [jax.ShapeDtypeStruct(shape, dtype) for shape, dtype in outs]
        moved = sum(value.size * value.dtype.itemsize for value in operands)
        held = sum(jnp.dtype(dtype).itemsize * functools.reduce(lambda a, b: a * b, shape) for shape, dtype in scratch)
        specs = [free] * skipped + [whole] * inputs
        aliases = {}
        if alias is not None:
            for operand, out in alias.items():
                specs[skipped + operand] = free
                aliases[skipped + operand] = out + 1
        extra = [pltpu.SemaphoreType.DMA((semaphores,))] if semaphores else []
        results = pl.pallas_call(
            body,
            out_shape=shapes,
            in_specs=specs,
            out_specs=[whole] + [free] * free_outs + [whole] * (results - free_outs),
            scratch_shapes=[pltpu.VMEM(shape, dtype) for shape, dtype in scratch] + extra,
            input_output_aliases=aliases,
            compiler_params=pltpu.CompilerParams(vmem_limit_bytes=held + spare * 2**20),
            cost_estimate=pl.CostEstimate(flops=int(flops), bytes_accessed=int(moved), transcendentals=0),
            name=name,
        )(*waits, *operands)
        self.tile = results[0]
        return results[1:]


def swap(value):
    return lax.ppermute(value, "dir", [(0, 1), (1, 0)])


def across(value, bits):
    count = lax.axis_size("seq")
    return lax.ppermute(value, "seq", [(i, i ^ bits) for i in range(count)])


def beyond(value):
    bit = 4
    while (1 << bit) < lax.axis_size("seq"):
        value = (value.astype(f32) + across(value, 1 << bit).astype(f32)).astype(value.dtype)
        bit += 1
    return value


def exchanged(payload, row_devices):
    count = lax.axis_size("seq")
    group = 2 * row_devices
    groups = None
    if count != row_devices:
        groups = [list(range(i, i + group)) for i in range(0, 2 * count, group)]
    copies = jnp.broadcast_to(payload[None], (group,) + payload.shape)
    return lax.all_to_all(copies, ("seq", "dir"), 0, 0, tiled=True, axis_index_groups=groups)


class Pack:
    def __init__(self, order, name, mine, theirs):
        self.order, self.name = order, name
        self.mine, self.got = mine, swap(theirs)
        self.rows = mine.shape[0]

    def sum(self, sources, parts, low_bit, step, after=()):
        rows = sources[0].shape[0] // parts
        return self.order.run(
            functools.partial(sum_kernel, len(sources), low_bit), [((rows, LANES), bf16)] * parts, sources,
            name=f"{self.name}_{step}", after=after,
        )

    def first(self, after=()):
        self.parts = self.sum([self.mine, self.got], 4, 0, "sum_cores", after)
        self.parts = [self.parts[0]] + [across(self.parts[k], k) for k in (1, 2, 3)]

    def second(self, after=()):
        self.parts = self.sum(self.parts, 4, 2, "sum_plane", after)
        self.parts = [self.parts[0]] + [across(self.parts[k], k << 2) for k in (1, 2, 3)]

    def third(self, after=()):
        (share,) = self.sum(self.parts, 1, 0, "sum_planes", after)
        share = beyond(share)
        self.parts = [share] + [across(share, k << 2) for k in (1, 2, 3)]

    def fourth(self, after=()):
        (quarter,) = self.order.run(
            functools.partial(gather_kernel, 2), [((self.rows // 4, LANES), bf16)], self.parts,
            name=f"{self.name}_gather", after=after,
        )
        self.parts = [quarter] + [across(quarter, k) for k in (1, 2, 3)]


def body(
    tokens,
    segment_ids,
    norm_gain,
    norm_bias,
    input_matrix,
    output_matrix,
    rate_params,
    turn_params,
    skip_weight,
    glu_weight,
    glu_bias,
    cotangent,
):
    chip_rows, width = tokens.shape
    rows = chip_rows // 2
    layers = rate_params.shape[0]
    states = rate_params.shape[2]
    row_devices = LENGTH // chip_rows
    order = Order()
    here = functools.partial

    in_own, out_own = input_matrix, output_matrix
    in_oth = swap(input_matrix)
    rate_oth, turn_oth = swap(rate_params), swap(turn_params)
    out_oth = swap(output_matrix)
    segments = segment_ids.reshape(chip_rows // LANES, LANES)

    full = ((rows, width), f32)
    full_low = ((rows, width), bf16)
    columns = ((width // LANES, rows, LANES), f32)
    wide = ((rows, 2 * states), f32)
    wide_low = ((rows, 2 * states), bf16)
    ends = ((8, 2 * states), f32)
    payload_shape = ((16, LANES), f32)
    narrow = ((rows, LANES), f32)
    tile = ((8, LANES), f32)
    sums_shape = ((8, width), f32)
    decay_shape = ((8, states), f32)
    table_shape = ((layers, 16, states), f32)
    places = ((8, 2 * states), f32)
    one = 2.0 * rows * width * 2 * states
    gate = 2.0 * rows * width * width
    scan = 1e9

    x0, normed0, inv0, mixed0, drive_own0, keep_own, keep_oth, whole, table, ids = order.run(
        here(open_kernel, row_devices),
        [full, full, narrow, full_low, wide, narrow, narrow, ((2, 8, LANES), f32), table_shape, tile],
        [tokens, segments, norm_gain, norm_bias, rate_params, turn_params, in_own],
        [columns, tile],
        flops=one + scan,
        name="open_norm",
    )
    drive_oth0, ends_own, ends_oth, payload, table, tiles = order.run(
        here(open_second_kernel, row_devices),
        [wide, ends, ends, payload_shape, table_shape, ((layers, 16, LANES), f32)],
        [mixed0, in_oth, rate_oth, turn_oth, table, drive_own0, keep_own, keep_oth, whole, ids],
        flops=one + scan,
        name="open_scan",
    )
    gathered = exchanged(payload, row_devices)
    (
        low_own0, low_oth0, combined0, phi0, sig0, act_low0, x1, normed1, inv1, mixed1, drive_own1, drive_oth1,
        ends_own, ends_oth, payload,
    ) = order.run(
        here(mid_kernel, row_devices),
        [wide_low, wide_low, full, full, full, full_low, full, full, narrow, full_low, wide, wide, ends, ends,
         payload_shape],
        [gathered, ends_own, ends_oth, drive_own0, drive_oth0, keep_own, keep_oth, whole, table, tiles,
         ids, out_own, out_oth, x0, normed0, norm_gain, norm_bias, skip_weight, glu_weight, glu_bias, in_own, in_oth],
        [places, tile, full, wide, wide],
        flops=4 * one + gate + 3 * scan,
        name="mid",
    )
    gathered = exchanged(payload, row_devices)
    (
        low_own1, low_oth1, half_out, grad1, act_low1, gate_low1, combined_grad1, combined_low1, grad_own1, grad_oth1,
        ends_own, ends_oth, payload, sums_turn,
    ) = order.run(
        here(turn_kernel, row_devices),
        [wide_low, wide_low, full, full, full_low, full_low, full, full_low, wide, wide, ends, ends, payload_shape,
         sums_shape],
        [gathered, ends_own, ends_oth, drive_own1, drive_oth1, keep_own, keep_oth, whole, table, tiles,
         ids, out_own, out_oth, x1, normed1, norm_gain, norm_bias, skip_weight, glu_weight, glu_bias, cotangent],
        [places, tile, full, full, full, full, columns, columns, wide, wide],
        flops=4 * one + 2 * gate + 4 * scan,
        name="turn",
    )
    in_size = width * (2 * states // LANES)
    out_size = 2 * states * (width // LANES)
    glu_size = width // 2 * (width // LANES)
    pack = ((out_size + glu_size, LANES), bf16)
    mine, theirs, payload = order.run(
        weights_kernel,
        [pack, pack, payload_shape],
        [act_low1, gate_low1, combined_low1, low_own1, low_oth1, payload],
        [((width, width), f32)],
        flops=2 * one + gate,
        name="weights_early",
    )
    gathered = exchanged(payload, row_devices)
    early = Pack(order, "early", mine, theirs)
    early.first(after=[gathered])
    (
        in_low_own1, in_low_oth1, decay_sums1, grad0, gate_low0, combined_grad0, combined_low0, grad_own0, grad_oth0,
        ends_own, ends_oth, payload, sums_back,
    ) = order.run(
        here(back_kernel, row_devices),
        [wide_low, wide_low, decay_shape, full, full_low, full, full_low, wide, wide, ends, ends, payload_shape,
         sums_shape],
        [gathered, ends_own, ends_oth, grad_own1, grad_oth1, keep_own, keep_oth, whole, table, tiles,
         ids, low_own1, low_oth1, drive_own1, drive_oth1, in_own, in_oth, out_own, out_oth, grad1, combined_grad1,
         normed1, inv1, norm_gain, norm_bias, skip_weight, glu_weight, combined0, phi0, sig0, normed0],
        [places, tile, full, wide, wide],
        flops=4 * one + gate + 4 * scan,
        name="back",
    )
    early.second()
    pack = ((in_size + out_size + glu_size, LANES), bf16)
    mine, theirs, payload = order.run(
        weights_two_kernel,
        [pack, pack, payload_shape],
        [mixed1, in_low_own1, in_low_oth1, act_low0, gate_low0, combined_low0, low_own0, low_oth0, payload],
        [((width, width), f32)],
        flops=4 * one + gate,
        name="weights_middle",
    )
    gathered = exchanged(payload, row_devices)
    middle = Pack(order, "middle", mine, theirs)
    middle.first(after=[gathered])
    early.third()
    pack = ((in_size, LANES), bf16)
    in_low_own0, in_low_oth0, decay_sums0, mine, theirs = order.run(
        here(last_kernel, row_devices),
        [wide_low, wide_low, decay_shape, pack, pack],
        [gathered, ends_own, ends_oth, grad_own0, grad_oth0, keep_own, keep_oth, whole, table, tiles,
         ids, low_own0, low_oth0, drive_own0, drive_oth0, mixed0],
        [places, tile, wide, wide],
        flops=2 * one + 2 * scan,
        name="last_scan",
    )
    late = Pack(order, "late", mine, theirs)
    early.fourth()
    half_grad, sums_last = order.run(
        final_kernel,
        [full, sums_shape],
        [in_low_own0, in_low_oth0, in_own, in_oth, grad0, combined_grad0, normed0, inv0, norm_gain, skip_weight],
        [full, columns],
        flops=2 * one + scan,
        name="final_norm",
    )
    late.first()
    token_rows = 4 * layers * (width // LANES)
    small_rows = -(-(token_rows + 3 * layers * (states // LANES)) // 8) * 8
    small = ((small_rows, LANES), f32)
    send, own = order.run(
        small_pack_kernel, [small, small], [sums_turn, sums_back, sums_last, decay_sums0, decay_sums1],
        name="small_pack",
    )
    got = swap(send)
    whole_rows = ((chip_rows, width), f32)
    (block_output,) = order.run(join_kernel, [whole_rows], [half_out, swap(half_out)], name="join_out")
    (tiny,) = order.run(here(small_kernel, token_rows), [small], [own, got, table], name="small_map")
    tiny = [tiny] + [across(tiny, k) for k in (1, 2, 3)]
    middle.second()
    (tokens_grad,) = order.run(join_kernel, [whole_rows], [half_grad, swap(half_grad)], name="join_grad")
    (tiny,) = order.run(add_kernel, [small], tiny, name="small_plane")
    tiny = beyond(tiny)
    tiny = [tiny] + [across(tiny, k << 2) for k in (1, 2, 3)]
    late.second()
    middle.third()
    gain_grad, bias_grad, rate_grad, turn_grad, skip_grad, gate_grad = order.run(
        small_out_kernel,
        [((layers, width), f32), ((layers, width), f32), ((layers, states), f32), ((2 * layers, states), f32),
         ((layers, width), f32), ((layers, width), f32)],
        tiny,
        name="small_out",
    )

    def unpack(pack, shapes, layer_of, old, gate_rows, name):
        held = [value for value in old if value is not None]
        alias = {4 + i: j for i, j in enumerate(j for j, value in enumerate(old) if value is not None)}
        gate_out = [((gate_rows, LANES), bf16)] if gate_rows else []
        return order.run(
            here(unpack_kernel, layer_of, len(held), gate_rows),
            [(shape, f32) for shape in shapes] + gate_out,
            list(pack.parts) + held,
            [(shape[2:], f32) for shape in shapes] + [((pack.rows, LANES), bf16)],
            name=name,
            free_outs=len(shapes),
            alias=alias,
            semaphores=len(shapes),
        )

    in_shape, out_shape = input_matrix.shape, output_matrix.shape
    out_all, gate_early = unpack(early, [out_shape], (1,), [None], glu_size, "unpack_early")
    got_early = swap(gate_early)
    late.third()
    middle.fourth()
    late.fourth()
    in_all, out_all, gate_middle = unpack(
        middle, [in_shape, out_shape], (1, 0), [None, out_all], glu_size, "unpack_middle"
    )
    got_middle = swap(gate_middle)
    (in_all,) = unpack(late, [in_shape], (0,), [in_all], 0, "unpack_late")
    (glu_all,) = order.run(
        gate_kernel, [(glu_weight.shape, f32)], [gate_early, got_early, gate_middle, got_middle], name="unpack_gate"
    )
    return (
        block_output,
        tokens_grad,
        gain_grad,
        bias_grad,
        in_all,
        out_all,
        rate_grad.reshape(rate_params.shape),
        turn_grad.reshape(turn_params.shape),
        skip_grad,
        glu_all,
        gate_grad,
    )


def solution(mesh):
    return jax.shard_map(
        body,
        mesh=mesh,
        in_specs=(
            P("seq", None),
            P("seq"),
            P(),
            P(),
            P(None, "dir", None, None),
            P(None, "dir", None, None),
            P(None, "dir", None),
            P(None, "dir", None, None),
            P(),
            P(),
            P(),
            P("seq", None),
        ),
        out_specs=(
            P("seq", None),
            P("seq", None),
            P(),
            P(),
            P(None, "dir", None, None),
            P(None, "dir", None, None),
            P(None, "dir", None),
            P(None, "dir", None, None),
            P(),
            P(),
            P(),
        ),
        check_vma=False,
    )
```

time: 2190 us -> 270 us (0.12); the launches traced: 2160 us -> 268 us
  local copies, waits for them, and re-layouts: 963 us -> 35.3 us
  blocking collectives: 550 us -> 25.1 us
  other arithmetic: 267 us -> 0 us
  waiting for transfers between devices: 302 us -> 74 us
  starting transfers between devices: 6.22 us -> 73.4 us
  Pallas kernels: 0 us -> 58.9 us
  matrix products: 39.3 us -> 0 us
  between operations: 24.5 us -> 1.46 us
    all_gather x16 -> x0, blocking collectives: 484 us -> none  [entering(): pieces = jax.tree.map(lambda part: lax.all_gather(part, axis), value)]
    slice x588 -> x0, local copies, waits for them, and re-layouts: 456 us -> none  [the longest x578 451 us: sweep_chain(): lax.associative_scan(combine_steps, (factor_re, factor_im, drive_re, driv...]
    psum x5 -> x0, waiting for transfers between devices: 302 us -> none  [the longest x1 193 us: body(): lax.psum((gain_all, shift_all, in_all, out_all, rate_all, turn_all, skip_...]
    rev x28 -> x0, local copies, waits for them, and re-layouts: 218 us -> none  [the longest x8 168 us: orient(): return jnp.where(flipped, jnp.flip(values, 0), values)]
    pad x288 -> x0, local copies, waits for them, and re-layouts: 217 us -> none  [sweep_chain(): lax.associative_scan(combine_steps, (factor_re, factor_im, drive_re, driv...]
    add x242 -> x0, other arithmetic: 98.5 us -> none  [the longest x144 58.4 us: sweep_chain(): lax.associative_scan(combine_steps, (factor_re, factor_im, drive_re, driv...]
    psum x1 -> x0, blocking collectives: 66.7 us -> none  [body(): lax.psum((gain_all, shift_all, in_all, out_all, rate_all, turn_all, skip_...]
    pallas_call x0 -> x31, Pallas kernels: none -> 58.9 us  [run(): pl.pallas_call(body, out_shape=shapes, in_specs=specs, out_specs=[whole]...]
  transfers between devices with their start and end apart: 7 -> 56, of which waited for: 4 -> 20; matrix products, arithmetic and copies ran while one was open for 10% -> 1% of each run, Pallas kernels for 0% -> 11%
where the time goes in v1:
time: 270 us; the launch traced here: 268 us
  waiting for transfers between devices  74 us (27%)
  starting transfers between devices  73.4 us (27%)
  Pallas kernels  58.9 us (22%)
  local copies, waits for them, and re-layouts  35.3 us (13%)
  blocking collectives  25.1 us (9%)
    pallas_call x31, Pallas kernels, run(): pl.pallas_call(body, out_shape=shapes, in_specs=specs, out_specs=[whole]...  58.9 us
    ppermute x42, waiting for transfers between devices, across(): return lax.ppermute(value, 'seq', [(i, i ^ bits) for i in range(count)])  56 us
    ppermute x42, starting transfers between devices, across(): return lax.ppermute(value, 'seq', [(i, i ^ bits) for i in range(count)])  50.7 us
    unnamed x143, local copies, waits for them, and re-layouts  33.2 us
    all_to_all x2, blocking collectives, exchanged(): lax.all_to_all(copies, ('seq', 'dir'), 0, 0, tiled=True, axis_index_group...  25.1 us
    all_to_all x2, waiting for transfers between devices, exchanged(): lax.all_to_all(copies, ('seq', 'dir'), 0, 0, tiled=True, axis_index_group...  17.1 us
    ppermute x12, starting transfers between devices, swap(): return lax.ppermute(value, 'dir', [(0, 1), (1, 0)])  13.1 us
    all_to_all x2, starting transfers between devices, exchanged(): lax.all_to_all(copies, ('seq', 'dir'), 0, 0, tiled=True, axis_index_group...  9.69 us
  transfers between devices with their start and end apart: 56, of which 20 were waited for; matrix products, arithmetic and copies ran while one was open for 1% of the time, Pallas kernels for 11%

profile of v1, /device:TPU:1, one launch (start us, length us, event | category | flops | bytes accessed | tf_op | source)
XLA Modules:
  0.0 268.2 jit_solution(8978891069850940694)
XLA Ops:
  1.7 1.4 copy-done
  4.5 1.2 copy-done.45
  7.8 4.3 %open_norm.1 = (f32[8,128]{1,0:T(8,128)S(1)}, f32[512,512]{1,0:T(8,128)S(1)}, f32[512,512]{1,0:T(8,128)S(1)}, f32[512,128]{1,0:T(8,128)S(1)}, bf16[512,512]{1,0:...) custom-call(bf16[1024,512]{1,0:T(8,128)(2,1)S(1)} %copy-done.45, ...), custom_call_target="tpu_custom_call" | custom-call | flops 1402653184 | bytes 2642944 | tf_op jit(solution)/shard_map/open_norm/pallas_call | solution.py:1064
  14.9 1.2 open_scan.1
  18.0 7.1 %all-to-all-start = ((f32[32,16,128]{2,1,0:T(8,128)}), f32[32,16,128]{2,1,0:T(8,128)}, u32[]{:S(2)}, u32[]{:S(2)}) async-start(f32[32,16,128]{2,1,0:T(8,128)} %broadcast_in_dim.8), calls=%async_computation | async-start | bytes 524288 | tf_op jit(solution)/shard_map/all_to_all | solution.py:1103
  25.2 10.3 %all-to-all-done.refs_1_ = f32[32,16,128]{2,1,0:T(8,128)} async-done(((f32[32,16,128]{2,1,0:T(8,128)}), f32[32,16,128]{2,1,0:T(8,128)}, u32[]{:S(2)}, u32[]{:S(2)}) %all-to-all-start) | async-done | bytes 262176 | tf_op jit(solution)/shard_map/all_to_all | solution.py:1103
  35.5 1.2 copy-done.3
  36.8 1.4 copy-done.8
  38.2 1.2 copy-done.10
  40.4 1.4 copy-done.58
  41.8 1.4 copy-done.61
  43.2 1.2 copy-done.70
  44.4 9.2 %mid.1 = (f32[8,128]{1,0:T(8,128)S(1)}, bf16[512,768]{1,0:T(8,128)(2,1)S(1)}, bf16[512,768]{1,0:T(8,128)(2,1)S(1)}, f32[512,512]{1,0:T(8,128)S(1)}, f32[512,512]...) custom-call(f32[8,128]{1,0:T(8,128)S(1)} %get-tuple-element.169.refs, ...), custom_call_target="tpu_custom_call" | custom-call | flops 4879048192 | bytes 13512704 | tf_op jit(solution)/shard_map/mid/pallas_call | solution.py:1064
  53.7 12.8 %all_to_all.20.refs_1_ = f32[32,16,128]{2,1,0:T(8,128)S(1)} all-to-all(f32[32,16,128]{2,1,0:T(8,128)S(1)} %broadcast_in_dim.9), channel_id=1, replica_groups=mesh['dir'=2,'seq'=16] {'seq','dir'}, dimensions={0} | all-to-all | bytes 524288 | tf_op jit(solution)/shard_map/all_to_all | solution.py:1103
  66.5 9.5 %turn.1 = (f32[8,128]{1,0:T(8,128)S(1)}, bf16[512,768]{1,0:T(8,128)(2,1)S(1)}, bf16[512,768]{1,0:T(8,128)(2,1)S(1)}, f32[512,512]{1,0:T(8,128)S(1)}, f32[512,512...) custom-call(f32[8,128]{1,0:T(8,128)S(1)} %get-tuple-element.178.refs, ...), custom_call_target="tpu_custom_call" | custom-call | flops 6147483648 | bytes 12464128 | tf_op jit(solution)/shard_map/turn/pallas_call | solution.py:1064
  76.0 1.4 weights_early.1
  78.1 12.3 %all_to_all.21.refs_0_.refs_1_ = f32[32,16,128]{2,1,0:T(8,128)S(1)} all-to-all(f32[32,16,128]{2,1,0:T(8,128)S(1)} %broadcast_in_dim.10), channel_id=1, replica_groups=mesh['dir'=2,'seq'=16] {'seq','dir'}, dimensions={0} | all-to-all | bytes 524288 | tf_op jit(solution)/shard_map/all_to_all | solution.py:1103
  91.8 1.6 collective-permute-start.7
  93.4 9.2 %back.1 = (f32[8,128]{1,0:T(8,128)S(1)}, bf16[512,768]{1,0:T(8,128)(2,1)S(1)}, bf16[512,768]{1,0:T(8,128)(2,1)S(1)}, f32[8,384]{1,0:T(8,128)S(1)}, f32[512,512]{...) custom-call(f32[8,128]{1,0:T(8,128)S(1)} %get-tuple-element.197.refs, ...), custom_call_target="tpu_custom_call" | custom-call | flops 5879048192 | bytes 23732224 | tf_op jit(solution)/shard_map/back/pallas_call | solution.py:1064
  107.2 3.4 %weights_middle.1 = (f32[8,128]{1,0:T(8,128)S(1)}, bf16[7168,128]{1,0:T(8,128)(2,1)S(1)}, bf16[7168,128]{1,0:T(8,128)(2,1)}, f32[16,128]{1,0:T(8,128)S(1)}) custom-call(f32[8,128]{1,0:T(8,128)S(1)} %get-tuple-element.213.refs_0_, bf16[512,512]{1,0:T(8,128)(2,1)S(1)} %get-tuple-element.214.refs_1_, bf16[512,768]{1,0:T(8,128)(2,1)S(1)} %get-tuple-element.215.refs_2_, ...), custom_call_target="tpu_custom_call" | custom-call | flops 1879048192 | bytes 5251072 | tf_op jit(solution)/shard_map/weights_middle/pallas_call | solution.py:1064
  110.7 1.2 copy-done.6
  114.3 2.5 all-to-all-start.3
  118.1 2.2 collective-permute-start.10
  120.5 6.8 %all-to-all-done.3.refs_0_.refs_1_ = f32[32,16,128]{2,1,0:T(8,128)S(1)} async-done(((f32[32,16,128]{2,1,0:T(8,128)}), f32[32,16,128]{2,1,0:T(8,128)S(1)}, u32[]{:S(2)}, u32[]{:S(2)}) %all-to-all-start.3) | async-done | bytes 262176 | tf_op jit(solution)/shard_map/all_to_all | solution.py:1103
  127.3 1.5 copy-done.7
  129.5 2.1 middle_sum_cores.1
  132.7 1.4 copy-done.59
  134.1 1.4 copy-done.62
  138.8 2.9 %last_scan.1 = (f32[8,128]{1,0:T(8,128)S(1)}, bf16[512,768]{1,0:T(8,128)(2,1)S(1)}, bf16[512,768]{1,0:T(8,128)(2,1)S(1)}, f32[8,384]{1,0:T(8,128)S(1)}, bf16[307...) custom-call(f32[8,128]{1,0:T(8,128)S(1)} %get-tuple-element.232.refs_0_, ...), custom_call_target="tpu_custom_call" | custom-call | flops 2805306368 | bytes 9302016 | tf_op jit(solution)/shard_map/last_scan/pallas_call | solution.py:1064
  142.3 2.7 collective-permute-start.14
  145.9 1.8 collective-permute-done.14.refs_4_
  147.7 3.4 %collective-permute-done.13.refs_3_ = bf16[256,128]{1,0:T(8,128)(2,1)S(1)} collective-permute-done((bf16[256,128]{1,0:T(8,128)(2,1)S(1)}, bf16[256,128]{1,0:T(8,128)(2,1)S(1)}, u32[]{:S(2)}, u32[]{:S(2)}) %collective-permute-start.13) | collective-permute-done | bytes 65568 | tf_op jit(solution)/shard_map/ppermute | solution.py:1085
  151.1 3.7 %final_norm.1 = (f32[8,128]{1,0:T(8,128)S(1)}, f32[512,512]{1,0:T(8,128)S(1)}, f32[8,512]{1,0:T(8,128)S(1)}) custom-call(f32[8,128]{1,0:T(8,128)S(1)} %get-tuple-element.239.refs_0_, bf16[512,768]{1,0:T(8,128)(2,1)S(1)} %get-tuple-element.240.refs_1_, bf16[512,768]{1,0:T(8,128)(2,1)S(1)} %get-tuple-element.241.refs_2_, ...), custom_call_target="tpu_custom_call" | custom-call | flops 1805306368 | bytes 8134656 | tf_op jit(solution)/shard_map/final_norm/pallas_call | solution.py:1064
  161.2 1.5 join_out.1
  162.7 4.8 %collective-permute-done.18.refs_2_ = bf16[1792,128]{1,0:T(8,128)(2,1)S(1)} collective-permute-done((bf16[1792,128]{1,0:T(8,128)(2,1)S(1)}, bf16[1792,128]{1,0:T(8,128)(2,1)S(1)}, u32[]{:S(2)}, u32[]{:S(2)}) %collective-permute-start.18) | collective-permute-done | bytes 458784 | tf_op jit(solution)/shard_map/ppermute | solution.py:1085
  167.5 2.0 collective-permute-start.24
  169.5 9.6 %collective-permute-start.26 = (bf16[768,128]{1,0:T(8,128)(2,1)S(1)}, bf16[768,128]{1,0:T(8,128)(2,1)S(1)}, u32[]{:S(2)}, u32[]{:S(2)}) collective-permute-start(bf16[768,128]{1,0:T(8,128)(2,1)S(1)} %get-tuple-element.273), channel_id=1, source_target_pairs={{0,2},{1,3},{2,0},{3,1},{4,6},{5,7},{6,4},{7,5},{8,10},{9,11},{10,... | collective-permute-start | bytes 589832 | tf_op jit(solution)/shard_map/ppermute | solution.py:1085
  179.1 3.6 %collective-permute-done.24.refs_4_ = f32[56,128]{1,0:T(8,128)S(1)} collective-permute-done((f32[56,128]{1,0:T(8,128)S(1)}, f32[56,128]{1,0:T(8,128)S(1)}, u32[]{:S(2)}, u32[]{:S(2)}) %collective-permute-start.24) | collective-permute-done | bytes 28704 | tf_op jit(solution)/shard_map/ppermute | solution.py:1085
  185.7 1.2 collective-permute-start.29
  188.5 2.5 collective-permute-done.29.refs_3_
  191.1 1.7 collective-permute-start.35
  193.9 2.0 collective-permute-start.30
  195.9 1.5 join_grad.1
  197.4 6.6 %collective-permute-done.27.refs_4_ = bf16[768,128]{1,0:T(8,128)(2,1)S(1)} collective-permute-done((bf16[768,128]{1,0:T(8,128)(2,1)S(1)}, bf16[768,128]{1,0:T(8,128)(2,1)S(1)}, u32[]{:S(2)}, u32[]{:S(2)}) %collective-permute-start.27) | collective-permute-done | bytes 196640 | tf_op jit(solution)/shard_map/ppermute | solution.py:1085
  203.9 2.5 collective-permute-start.33
  207.5 2.8 %collective-permute-start.40 = (bf16[448,128]{1,0:T(8,128)(2,1)S(1)}, bf16[448,128]{1,0:T(8,128)(2,1)S(1)}, u32[]{:S(2)}, u32[]{:S(2)}) collective-permute-start(bf16[448,128]{1,0:T(8,128)(2,1)S(1)} %get-tuple-element.292.refs_1_), channel_id=1, source_target_pairs={{0,4},{1,5},{2,6},{3,7},{4,0},{5,1},{6,2},{7,3},{8,12},{9,13},{10,... | collective-permute-start | bytes 344072 | tf_op jit(solution)/shard_map/ppermute | solution.py:1085
  211.3 7.8 %collective-permute-done.32.refs_3_ = f32[56,128]{1,0:T(8,128)S(1)} collective-permute-done((f32[56,128]{1,0:T(8,128)S(1)}, f32[56,128]{1,0:T(8,128)S(1)}, u32[]{:S(2)}, u32[]{:S(2)}) %collective-permute-start.32) | collective-permute-done | bytes 28704 | tf_op jit(solution)/shard_map/ppermute | solution.py:1085
  219.1 2.7 %collective-permute-done.31.refs_2_ = f32[56,128]{1,0:T(8,128)S(1)} collective-permute-done((f32[56,128]{1,0:T(8,128)S(1)}, f32[56,128]{1,0:T(8,128)S(1)}, u32[]{:S(2)}, u32[]{:S(2)}) %collective-permute-start.31) | collective-permute-done | bytes 28704 | tf_op jit(solution)/shard_map/ppermute | solution.py:1085
  222.2 1.8 collective-permute-start.39
  224.5 1.4 unpack_early.1
  227.1 1.6 collective-permute-start.48
  228.7 1.7 collective-permute-start.47
  230.4 1.3 collective-permute-start.45
  231.7 3.5 %collective-permute-done.45.refs_4_ = bf16[192,128]{1,0:T(8,128)(2,1)S(1)} collective-permute-done((bf16[192,128]{1,0:T(8,128)(2,1)S(1)}, bf16[192,128]{1,0:T(8,128)(2,1)S(1)}, u32[]{:S(2)}, u32[]{:S(2)}) %collective-permute-start.45) | collective-permute-done | bytes 49184 | tf_op jit(solution)/shard_map/ppermute | solution.py:1085
  235.2 1.3 collective-permute-done.44.refs_3_
  236.5 6.4 %collective-permute-start.52 = (bf16[1024,128]{1,0:T(8,128)(2,1)S(1)}, bf16[1024,128]{1,0:T(8,128)(2,1)S(1)}, u32[]{:S(2)}, u32[]{:S(2)}) collective-permute-start(bf16[1024,128]{1,0:T(8,128)(2,1)S(1)} %get-tuple-element.307.refs_1_), channel_id=1, source_target_pairs={{0,16},{16,0},{1,17},{17,1},{2,18},{18,2},{3,19},{19,3},{4,20},{20... | collective-permute-start | bytes 786440 | tf_op jit(solution)/shard_map/ppermute | solution.py:1080
  243.0 6.7 %collective-permute-done.47.refs_3_ = bf16[1792,128]{1,0:T(8,128)(2,1)S(1)} collective-permute-done((bf16[1792,128]{1,0:T(8,128)(2,1)S(1)}, bf16[1792,128]{1,0:T(8,128)(2,1)S(1)}, u32[]{:S(2)}, u32[]{:S(2)}) %collective-permute-start.47) | collective-permute-done | bytes 458784 | tf_op jit(solution)/shard_map/ppermute | solution.py:1085
  249.6 1.9 unpack_middle.1
  251.6 1.7 collective-permute-start.53
  253.3 1.6 collective-permute-start.51
  257.1 3.6 %collective-permute-done.51.refs_4_ = bf16[768,128]{1,0:T(8,128)(2,1)S(1)} collective-permute-done((bf16[768,128]{1,0:T(8,128)(2,1)S(1)}, bf16[768,128]{1,0:T(8,128)(2,1)S(1)}, u32[]{:S(2)}, u32[]{:S(2)}) %collective-permute-start.51) | collective-permute-done | bytes 196640 | tf_op jit(solution)/shard_map/ppermute | solution.py:1085
  260.7 4.5 %collective-permute-done.50.refs_3_ = bf16[768,128]{1,0:T(8,128)(2,1)S(1)} collective-permute-done((bf16[768,128]{1,0:T(8,128)(2,1)S(1)}, bf16[768,128]{1,0:T(8,128)(2,1)S(1)}, u32[]{:S(2)}, u32[]{:S(2)}) %collective-permute-start.50) | collective-permute-done | bytes 196640 | tf_op jit(solution)/shard_map/ppermute | solution.py:1085
  265.3 1.3 unpack_late.1
  266.6 1.6 unpack_gate.1
  (229 shorter events, 45.4 us)
Async XLA Ops:
  0.6 14.2 %collective-permute-start = (bf16[2,1,512,768]{3,2,1,0:T(8,128)(2,1)}, bf16[2,1,512,768]{3,2,1,0:T(8,128)(2,1)S(1)}, u32[]{:S(2)}, u32[]{:S(2)}) collective-permute-start(bf16[2,1,512,768]{3,2,1,0:T(8,128)(2,1)} %refs_3_.3), channel_id=1, source_target_pairs={{0,16},{16,0},{1,17},{17,1},{2,18},{18,2},{3,19},{19,3},{4,20},{20... | collective-permute-start | bytes 4718600 | tf_op jit(solution)/shard_map/ppermute | solution.py:1080
  0.8 24.4 %collective-permute-start.3 = (bf16[2,1,768,512]{3,2,1,0:T(8,128)(2,1)}, bf16[2,1,768,512]{3,2,1,0:T(8,128)(2,1)}, u32[]{:S(2)}, u32[]{:S(2)}) collective-permute-start(bf16[2,1,768,512]{3,2,1,0:T(8,128)(2,1)} %refs_18_.5), channel_id=1, source_target_pairs={{0,16},{16,0},{1,17},{17,1},{2,18},{18,2},{3,19},{19,3},{4,20},{20... | collective-permute-start | bytes 4718600 | tf_op jit(solution)/shard_map/ppermute | solution.py:1080
  1.2 13.6 %collective-permute-start.1 = (f32[2,1,384]{2,1,0:T(1,128)}, f32[2,1,384]{2,1,0:T(1,128)S(1)}, u32[]{:S(2)}, u32[]{:S(2)}) collective-permute-start(f32[2,1,384]{2,1,0:T(1,128)} %refs_4_.1), channel_id=1, source_target_pairs={{0,16},{16,0},{1,17},{17,1},{2,18},{18,2},{3,19},{19,3},{4,20},{20... | collective-permute-start | bytes 9224 | tf_op jit(solution)/shard_map/ppermute | solution.py:1080
  1.3 13.5 %collective-permute-start.2 = (f32[2,1,2,384]{3,2,1,0:T(2,128)}, f32[2,1,2,384]{3,2,1,0:T(2,128)S(1)}, u32[]{:S(2)}, u32[]{:S(2)}) collective-permute-start(f32[2,1,2,384]{3,2,1,0:T(2,128)} %refs_5_.1), channel_id=1, source_target_pairs={{0,16},{16,0},{1,17},{17,1},{2,18},{18,2},{3,19},{19,3},{4,20},{20... | collective-permute-start | bytes 18440 | tf_op jit(solution)/shard_map/ppermute | solution.py:1080
  14.8 78.6 %copy-start.18 = (f32[512,128]{1,0:T(8,128)}, f32[512,128]{1,0:T(8,128)S(1)}, u32[]{:S(2)}) copy-start(f32[512,128]{1,0:T(8,128)S(1)} %get-tuple-element.165.refs_7_.refs_6_) | copy-start | bytes 786436
  14.8 78.6 %copy-start.36 = (f32[8,128]{1,0:T(8,128)}, f32[8,128]{1,0:T(8,128)S(1)}, u32[]{:S(2)}) copy-start(f32[8,128]{1,0:T(8,128)S(1)} %get-tuple-element.168.refs_10_.refs_11_) | copy-start | bytes 12292
  14.8 20.7 %copy-start.1 = (bf16[2,1,512,768]{3,2,1,0:T(8,128)(2,1)S(1)}, bf16[2,1,512,768]{3,2,1,0:T(8,128)(2,1)}, u32[]{:S(2)}) copy-start(bf16[2,1,512,768]{3,2,1,0:T(8,128)(2,1)} %refs_3_.3) | copy-start | bytes 4718596
  18.0 17.5 %all-to-all-start = ((f32[32,16,128]{2,1,0:T(8,128)}), f32[32,16,128]{2,1,0:T(8,128)}, u32[]{:S(2)}, u32[]{:S(2)}) async-start(f32[32,16,128]{2,1,0:T(8,128)} %broadcast_in_dim.8), calls=%async_computation | async-start | bytes 524288 | tf_op jit(solution)/shard_map/all_to_all | solution.py:1103
  44.4 22.1 %copy-start.9 = (bf16[2,1,768,512]{3,2,1,0:T(8,128)(2,1)S(1)}, bf16[2,1,768,512]{3,2,1,0:T(8,128)(2,1)}, u32[]{:S(2)}) copy-start(bf16[2,1,768,512]{3,2,1,0:T(8,128)(2,1)} %refs_18_.5) | copy-start | bytes 4718596
  44.4 22.1 %copy-start.11 = (bf16[2,512,512]{2,1,0:T(8,128)(2,1)S(1)}, bf16[2,512,512]{2,1,0:T(8,128)(2,1)}, u32[]{:S(2)}) copy-start(bf16[2,512,512]{2,1,0:T(8,128)(2,1)} %refs_27_.1) | copy-start | bytes 3145732
  44.4 22.1 %copy-start.40 = (f32[1024,512]{1,0:T(8,128)S(1)}, f32[1024,512]{1,0:T(8,128)}, u32[]{:S(2)}) copy-start(f32[1024,512]{1,0:T(8,128)} %refs_21_.3) | copy-start | bytes 6291460
  53.6 53.6 %copy-start.63 = (bf16[512,768]{1,0:T(8,128)(2,1)}, bf16[512,768]{1,0:T(8,128)(2,1)S(1)}, u32[]{:S(2)}) copy-start(bf16[512,768]{1,0:T(8,128)(2,1)S(1)} %get-tuple-element.220.refs_7_.refs_12_) | copy-start | bytes 2359300
  53.6 53.6 %copy-start.65 = (bf16[512,768]{1,0:T(8,128)(2,1)}, bf16[512,768]{1,0:T(8,128)(2,1)S(1)}, u32[]{:S(2)}) copy-start(bf16[512,768]{1,0:T(8,128)(2,1)S(1)} %get-tuple-element.221.refs_8_.refs_13_) | copy-start | bytes 2359300
  77.4 13.0 %collective-permute-start.4 = (bf16[4096,128]{1,0:T(8,128)(2,1)S(1)}, bf16[4096,128]{1,0:T(8,128)(2,1)S(1)}, u32[]{:S(2)}, u32[]{:S(2)}) collective-permute-start(bf16[4096,128]{1,0:T(8,128)(2,1)S(1)} %get-tuple-element.196), channel_id=1, source_target_pairs={{0,16},{16,0},{1,17},{17,1},{2,18},{18,2},{3,19},{19,3},{4,20},{20... | collective-permute-start | bytes 3145736 | tf_op jit(solution)/shard_map/ppermute | solution.py:1080
  90.7 13.2 %collective-permute-start.5 = (bf16[1024,128]{1,0:T(8,128)(2,1)S(1)}, bf16[1024,128]{1,0:T(8,128)(2,1)S(1)}, u32[]{:S(2)}, u32[]{:S(2)}) collective-permute-start(bf16[1024,128]{1,0:T(8,128)(2,1)S(1)} %get-tuple-element.210), channel_id=1, source_target_pairs={{0,1},{1,0},{2,3},{3,2},{4,5},{5,4},{6,7},{7,6},{8,9},{9,8},{10,11... | collective-permute-start | bytes 786440 | tf_op jit(solution)/shard_map/ppermute | solution.py:1085
  91.4 13.3 %collective-permute-start.6 = (bf16[1024,128]{1,0:T(8,128)(2,1)S(1)}, bf16[1024,128]{1,0:T(8,128)(2,1)S(1)}, u32[]{:S(2)}, u32[]{:S(2)}) collective-permute-start(bf16[1024,128]{1,0:T(8,128)(2,1)S(1)} %get-tuple-element.211), channel_id=1, source_target_pairs={{0,2},{1,3},{2,0},{3,1},{4,6},{5,7},{6,4},{7,5},{8,10},{9,11},{10,... | collective-permute-start | bytes 786440 | tf_op jit(solution)/shard_map/ppermute | solution.py:1085
  91.8 12.9 %collective-permute-start.7 = (bf16[1024,128]{1,0:T(8,128)(2,1)S(1)}, bf16[1024,128]{1,0:T(8,128)(2,1)S(1)}, u32[]{:S(2)}, u32[]{:S(2)}) collective-permute-start(bf16[1024,128]{1,0:T(8,128)(2,1)S(1)} %get-tuple-element.212), channel_id=1, source_target_pairs={{0,3},{1,2},{2,1},{3,0},{4,7},{5,6},{6,5},{7,4},{8,11},{9,10},{10,... | collective-permute-start | bytes 786440 | tf_op jit(solution)/shard_map/ppermute | solution.py:1085
  112.5 14.8 %collective-permute-start.8 = (bf16[7168,128]{1,0:T(8,128)(2,1)}, bf16[7168,128]{1,0:T(8,128)(2,1)}, u32[]{:S(2)}, u32[]{:S(2)}) collective-permute-start(bf16[7168,128]{1,0:T(8,128)(2,1)} %get-tuple-element.226), channel_id=1, source_target_pairs={{0,16},{16,0},{1,17},{17,1},{2,18},{18,2},{3,19},{19,3},{4,20},{20... | collective-permute-start | bytes 5505032 | tf_op jit(solution)/shard_map/ppermute | solution.py:1080
  114.3 13.0 %all-to-all-start.3 = ((f32[32,16,128]{2,1,0:T(8,128)}), f32[32,16,128]{2,1,0:T(8,128)S(1)}, u32[]{:S(2)}, u32[]{:S(2)}) async-start(f32[32,16,128]{2,1,0:T(8,128)} %broadcast_in_dim.11), calls=%async_computation.3 | async-start | bytes 524288 | tf_op jit(solution)/shard_map/all_to_all | solution.py:1103
  116.9 14.7 %collective-permute-start.9 = (bf16[256,128]{1,0:T(8,128)(2,1)}, bf16[256,128]{1,0:T(8,128)(2,1)}, u32[]{:S(2)}, u32[]{:S(2)}) collective-permute-start(bf16[256,128]{1,0:T(8,128)(2,1)} %copy-done.48), channel_id=1, source_target_pairs={{0,4},{1,5},{2,6},{3,7},{4,0},{5,1},{6,2},{7,3},{8,12},{9,13},{10,... | collective-permute-start | bytes 196616 | tf_op jit(solution)/shard_map/ppermute | solution.py:1085
  118.1 13.6 %collective-permute-start.10 = (bf16[256,128]{1,0:T(8,128)(2,1)}, bf16[256,128]{1,0:T(8,128)(2,1)}, u32[]{:S(2)}, u32[]{:S(2)}) collective-permute-start(bf16[256,128]{1,0:T(8,128)(2,1)} %copy-done.47), channel_id=1, source_target_pairs={{0,8},{1,9},{2,10},{3,11},{4,12},{5,13},{6,14},{7,15},{8,0},{9,1},... | collective-permute-start | bytes 196616 | tf_op jit(solution)/shard_map/ppermute | solution.py:1085
  120.3 11.4 %collective-permute-start.11 = (bf16[256,128]{1,0:T(8,128)(2,1)}, bf16[256,128]{1,0:T(8,128)(2,1)}, u32[]{:S(2)}, u32[]{:S(2)}) collective-permute-start(bf16[256,128]{1,0:T(8,128)(2,1)} %copy-done.46), channel_id=1, source_target_pairs={{0,12},{1,13},{2,14},{3,15},{4,8},{5,9},{6,10},{7,11},{8,4},{9,5},... | collective-permute-start | bytes 196616 | tf_op jit(solution)/shard_map/ppermute | solution.py:1085
  141.7 15.9 %collective-permute-start.15 = (bf16[3072,128]{1,0:T(8,128)(2,1)S(1)}, bf16[3072,128]{1,0:T(8,128)(2,1)S(1)}, u32[]{:S(2)}, u32[]{:S(2)}) collective-permute-start(bf16[3072,128]{1,0:T(8,128)(2,1)S(1)} %get-tuple-element.247), channel_id=1, source_target_pairs={{0,16},{16,0},{1,17},{17,1},{2,18},{18,2},{3,19},{19,3},{4,20},{20... | collective-permute-start | bytes 2359304 | tf_op jit(solution)/shard_map/ppermute | solution.py:1080
  142.0 16.3 %collective-permute-start.16 = (f32[512,512]{1,0:T(8,128)S(1)}, f32[512,512]{1,0:T(8,128)S(1)}, u32[]{:S(2)}, u32[]{:S(2)}) collective-permute-start(f32[512,512]{1,0:T(8,128)S(1)} %copy-done.17), channel_id=1, source_target_pairs={{0,16},{16,0},{1,17},{17,1},{2,18},{18,2},{3,19},{19,3},{4,20},{20... | collective-permute-start | bytes 3145736 | tf_op jit(solution)/shard_map/ppermute | solution.py:1080
  142.3 5.3 %collective-permute-start.14 = (bf16[256,128]{1,0:T(8,128)(2,1)S(1)}, bf16[256,128]{1,0:T(8,128)(2,1)S(1)}, u32[]{:S(2)}, u32[]{:S(2)}) collective-permute-start(bf16[256,128]{1,0:T(8,128)(2,1)S(1)} %get-tuple-element.238.refs_1_), channel_id=1, source_target_pairs={{0,12},{1,13},{2,14},{3,15},{4,8},{5,9},{6,10},{7,11},{8,4},{9,5},... | collective-permute-start | bytes 196616 | tf_op jit(solution)/shard_map/ppermute | solution.py:1085
  145.0 6.0 %collective-permute-start.13 = (bf16[256,128]{1,0:T(8,128)(2,1)S(1)}, bf16[256,128]{1,0:T(8,128)(2,1)S(1)}, u32[]{:S(2)}, u32[]{:S(2)}) collective-permute-start(bf16[256,128]{1,0:T(8,128)(2,1)S(1)} %get-tuple-element.238.refs_1_), channel_id=1, source_target_pairs={{0,8},{1,9},{2,10},{3,11},{4,12},{5,13},{6,14},{7,15},{8,0},{9,1},... | collective-permute-start | bytes 196616 | tf_op jit(solution)/shard_map/ppermute | solution.py:1085
  145.0 6.0 %collective-permute-start.12 = (bf16[256,128]{1,0:T(8,128)(2,1)S(1)}, bf16[256,128]{1,0:T(8,128)(2,1)S(1)}, u32[]{:S(2)}, u32[]{:S(2)}) collective-permute-start(bf16[256,128]{1,0:T(8,128)(2,1)S(1)} %get-tuple-element.238.refs_1_), channel_id=1, source_target_pairs={{0,4},{1,5},{2,6},{3,7},{4,0},{5,1},{6,2},{7,3},{8,12},{9,13},{10,... | collective-permute-start | bytes 196616 | tf_op jit(solution)/shard_map/ppermute | solution.py:1085
  154.9 39.1 %collective-permute-start.21 = (f32[512,512]{1,0:T(8,128)S(1)}, f32[512,512]{1,0:T(8,128)S(1)}, u32[]{:S(2)}, u32[]{:S(2)}) collective-permute-start(f32[512,512]{1,0:T(8,128)S(1)} %get-tuple-element.266.refs_1_), channel_id=1, source_target_pairs={{0,16},{16,0},{1,17},{17,1},{2,18},{18,2},{3,19},{19,3},{4,20},{20... | collective-permute-start | bytes 3145736 | tf_op jit(solution)/shard_map/ppermute | solution.py:1080
  155.4 12.1 %collective-permute-start.18 = (bf16[1792,128]{1,0:T(8,128)(2,1)S(1)}, bf16[1792,128]{1,0:T(8,128)(2,1)S(1)}, u32[]{:S(2)}, u32[]{:S(2)}) collective-permute-start(bf16[1792,128]{1,0:T(8,128)(2,1)S(1)} %get-tuple-element.262), channel_id=1, source_target_pairs={{0,1},{1,0},{2,3},{3,2},{4,5},{5,4},{6,7},{7,6},{8,9},{9,8},{10,11... | collective-permute-start | bytes 1376264 | tf_op jit(solution)/shard_map/ppermute | solution.py:1085
  156.5 13.0 %collective-permute-start.19 = (bf16[1792,128]{1,0:T(8,128)(2,1)S(1)}, bf16[1792,128]{1,0:T(8,128)(2,1)S(1)}, u32[]{:S(2)}, u32[]{:S(2)}) collective-permute-start(bf16[1792,128]{1,0:T(8,128)(2,1)S(1)} %get-tuple-element.263), channel_id=1, source_target_pairs={{0,2},{1,3},{2,0},{3,1},{4,6},{5,7},{6,4},{7,5},{8,10},{9,11},{10,... | collective-permute-start | bytes 1376264 | tf_op jit(solution)/shard_map/ppermute | solution.py:1085
  157.7 21.4 %collective-permute-start.20 = (bf16[1792,128]{1,0:T(8,128)(2,1)S(1)}, bf16[1792,128]{1,0:T(8,128)(2,1)S(1)}, u32[]{:S(2)}, u32[]{:S(2)}) collective-permute-start(bf16[1792,128]{1,0:T(8,128)(2,1)S(1)} %get-tuple-element.264), channel_id=1, source_target_pairs={{0,3},{1,2},{2,1},{3,0},{4,7},{5,6},{6,5},{7,4},{8,11},{9,10},{10,... | collective-permute-start | bytes 1376264 | tf_op jit(solution)/shard_map/ppermute | solution.py:1085
  158.3 1.8 collective-permute-start.17
  160.1 32.6 %collective-permute-start.25 = (bf16[768,128]{1,0:T(8,128)(2,1)S(1)}, bf16[768,128]{1,0:T(8,128)(2,1)S(1)}, u32[]{:S(2)}, u32[]{:S(2)}) collective-permute-start(bf16[768,128]{1,0:T(8,128)(2,1)S(1)} %get-tuple-element.272), channel_id=1, source_target_pairs={{0,1},{1,0},{2,3},{3,2},{4,5},{5,4},{6,7},{7,6},{8,9},{9,8},{10,11... | collective-permute-start | bytes 589832 | tf_op jit(solution)/shard_map/ppermute | solution.py:1085
  167.5 15.2 %collective-permute-start.24 = (f32[56,128]{1,0:T(8,128)S(1)}, f32[56,128]{1,0:T(8,128)S(1)}, u32[]{:S(2)}, u32[]{:S(2)}) collective-permute-start(f32[56,128]{1,0:T(8,128)S(1)} %get-tuple-element.269.refs_1_), channel_id=1, source_target_pairs={{0,3},{1,2},{2,1},{3,0},{4,7},{5,6},{6,5},{7,4},{8,11},{9,10},{10,... | collective-permute-start | bytes 86024 | tf_op jit(solution)/shard_map/ppermute | solution.py:1085
  169.5 23.3 %collective-permute-start.26 = (bf16[768,128]{1,0:T(8,128)(2,1)S(1)}, bf16[768,128]{1,0:T(8,128)(2,1)S(1)}, u32[]{:S(2)}, u32[]{:S(2)}) collective-permute-start(bf16[768,128]{1,0:T(8,128)(2,1)S(1)} %get-tuple-element.273), channel_id=1, source_target_pairs={{0,2},{1,3},{2,0},{3,1},{4,6},{5,7},{6,4},{7,5},{8,10},{9,11},{10,... | collective-permute-start | bytes 589832 | tf_op jit(solution)/shard_map/ppermute | solution.py:1085
  179.0 5.1 %collective-permute-start.23 = (f32[56,128]{1,0:T(8,128)S(1)}, f32[56,128]{1,0:T(8,128)S(1)}, u32[]{:S(2)}, u32[]{:S(2)}) collective-permute-start(f32[56,128]{1,0:T(8,128)S(1)} %get-tuple-element.269.refs_1_), channel_id=1, source_target_pairs={{0,2},{1,3},{2,0},{3,1},{4,6},{5,7},{6,4},{7,5},{8,10},{9,11},{10,... | collective-permute-start | bytes 86024 | tf_op jit(solution)/shard_map/ppermute | solution.py:1085
  182.7 3.0 %collective-permute-start.22 = (f32[56,128]{1,0:T(8,128)S(1)}, f32[56,128]{1,0:T(8,128)S(1)}, u32[]{:S(2)}, u32[]{:S(2)}) collective-permute-start(f32[56,128]{1,0:T(8,128)S(1)} %get-tuple-element.269.refs_1_), channel_id=1, source_target_pairs={{0,1},{1,0},{2,3},{3,2},{4,5},{5,4},{6,7},{7,6},{8,9},{9,8},{10,11... | collective-permute-start | bytes 86024 | tf_op jit(solution)/shard_map/ppermute | solution.py:1085
  184.1 3.7 %collective-permute-start.28 = (bf16[448,128]{1,0:T(8,128)(2,1)S(1)}, bf16[448,128]{1,0:T(8,128)(2,1)S(1)}, u32[]{:S(2)}, u32[]{:S(2)}) collective-permute-start(bf16[448,128]{1,0:T(8,128)(2,1)S(1)} %get-tuple-element.277), channel_id=1, source_target_pairs={{0,4},{1,5},{2,6},{3,7},{4,0},{5,1},{6,2},{7,3},{8,12},{9,13},{10,... | collective-permute-start | bytes 344072 | tf_op jit(solution)/shard_map/ppermute | solution.py:1085
  185.7 5.4 %collective-permute-start.29 = (bf16[448,128]{1,0:T(8,128)(2,1)S(1)}, bf16[448,128]{1,0:T(8,128)(2,1)S(1)}, u32[]{:S(2)}, u32[]{:S(2)}) collective-permute-start(bf16[448,128]{1,0:T(8,128)(2,1)S(1)} %get-tuple-element.278), channel_id=1, source_target_pairs={{0,8},{1,9},{2,10},{3,11},{4,12},{5,13},{6,14},{7,15},{8,0},{9,1},... | collective-permute-start | bytes 344072 | tf_op jit(solution)/shard_map/ppermute | solution.py:1085
  187.8 19.6 %collective-permute-start.36 = (bf16[1024,128]{1,0:T(8,128)(2,1)S(1)}, bf16[1024,128]{1,0:T(8,128)(2,1)S(1)}, u32[]{:S(2)}, u32[]{:S(2)}) collective-permute-start(bf16[1024,128]{1,0:T(8,128)(2,1)S(1)} %get-tuple-element.285.refs_1_), channel_id=1, source_target_pairs={{0,3},{1,2},{2,1},{3,0},{4,7},{5,6},{6,5},{7,4},{8,11},{9,10},{10,... | collective-permute-start | bytes 786440 | tf_op jit(solution)/shard_map/ppermute | solution.py:1085
  191.1 16.4 %collective-permute-start.35 = (bf16[1024,128]{1,0:T(8,128)(2,1)S(1)}, bf16[1024,128]{1,0:T(8,128)(2,1)S(1)}, u32[]{:S(2)}, u32[]{:S(2)}) collective-permute-start(bf16[1024,128]{1,0:T(8,128)(2,1)S(1)} %get-tuple-element.285.refs_1_), channel_id=1, source_target_pairs={{0,2},{1,3},{2,0},{3,1},{4,6},{5,7},{6,4},{7,5},{8,10},{9,11},{10,... | collective-permute-start | bytes 786440 | tf_op jit(solution)/shard_map/ppermute | solution.py:1085
  192.7 17.6 %collective-permute-start.34 = (bf16[1024,128]{1,0:T(8,128)(2,1)S(1)}, bf16[1024,128]{1,0:T(8,128)(2,1)S(1)}, u32[]{:S(2)}, u32[]{:S(2)}) collective-permute-start(bf16[1024,128]{1,0:T(8,128)(2,1)S(1)} %get-tuple-element.285.refs_1_), channel_id=1, source_target_pairs={{0,1},{1,0},{2,3},{3,2},{4,5},{5,4},{6,7},{7,6},{8,9},{9,8},{10,11... | collective-permute-start | bytes 786440 | tf_op jit(solution)/shard_map/ppermute | solution.py:1085
  192.7 11.2 %collective-permute-start.27 = (bf16[768,128]{1,0:T(8,128)(2,1)S(1)}, bf16[768,128]{1,0:T(8,128)(2,1)S(1)}, u32[]{:S(2)}, u32[]{:S(2)}) collective-permute-start(bf16[768,128]{1,0:T(8,128)(2,1)S(1)} %get-tuple-element.274), channel_id=1, source_target_pairs={{0,3},{1,2},{2,1},{3,0},{4,7},{5,6},{6,5},{7,4},{8,11},{9,10},{10,... | collective-permute-start | bytes 589832 | tf_op jit(solution)/shard_map/ppermute | solution.py:1085
  193.9 12.7 %collective-permute-start.30 = (bf16[448,128]{1,0:T(8,128)(2,1)S(1)}, bf16[448,128]{1,0:T(8,128)(2,1)S(1)}, u32[]{:S(2)}, u32[]{:S(2)}) collective-permute-start(bf16[448,128]{1,0:T(8,128)(2,1)S(1)} %get-tuple-element.279), channel_id=1, source_target_pairs={{0,12},{1,13},{2,14},{3,15},{4,8},{5,9},{6,10},{7,11},{8,4},{9,5},... | collective-permute-start | bytes 344072 | tf_op jit(solution)/shard_map/ppermute | solution.py:1085
  203.9 6.4 %collective-permute-start.33 = (f32[56,128]{1,0:T(8,128)S(1)}, f32[56,128]{1,0:T(8,128)S(1)}, u32[]{:S(2)}, u32[]{:S(2)}) collective-permute-start(f32[56,128]{1,0:T(8,128)S(1)} %get-tuple-element.281.refs_1_), channel_id=1, source_target_pairs={{0,12},{1,13},{2,14},{3,15},{4,8},{5,9},{6,10},{7,11},{8,4},{9,5},... | collective-permute-start | bytes 86024 | tf_op jit(solution)/shard_map/ppermute | solution.py:1085
  206.6 20.4 %collective-permute-start.42 = (bf16[448,128]{1,0:T(8,128)(2,1)S(1)}, bf16[448,128]{1,0:T(8,128)(2,1)S(1)}, u32[]{:S(2)}, u32[]{:S(2)}) collective-permute-start(bf16[448,128]{1,0:T(8,128)(2,1)S(1)} %get-tuple-element.292.refs_1_), channel_id=1, source_target_pairs={{0,12},{1,13},{2,14},{3,15},{4,8},{5,9},{6,10},{7,11},{8,4},{9,5},... | collective-permute-start | bytes 344072 | tf_op jit(solution)/shard_map/ppermute | solution.py:1085
  207.5 19.6 %collective-permute-start.41 = (bf16[448,128]{1,0:T(8,128)(2,1)S(1)}, bf16[448,128]{1,0:T(8,128)(2,1)S(1)}, u32[]{:S(2)}, u32[]{:S(2)}) collective-permute-start(bf16[448,128]{1,0:T(8,128)(2,1)S(1)} %get-tuple-element.292.refs_1_), channel_id=1, source_target_pairs={{0,8},{1,9},{2,10},{3,11},{4,12},{5,13},{6,14},{7,15},{8,0},{9,1},... | collective-permute-start | bytes 344072 | tf_op jit(solution)/shard_map/ppermute | solution.py:1085
  207.5 19.6 %collective-permute-start.40 = (bf16[448,128]{1,0:T(8,128)(2,1)S(1)}, bf16[448,128]{1,0:T(8,128)(2,1)S(1)}, u32[]{:S(2)}, u32[]{:S(2)}) collective-permute-start(bf16[448,128]{1,0:T(8,128)(2,1)S(1)} %get-tuple-element.292.refs_1_), channel_id=1, source_target_pairs={{0,4},{1,5},{2,6},{3,7},{4,0},{5,1},{6,2},{7,3},{8,12},{9,13},{10,... | collective-permute-start | bytes 344072 | tf_op jit(solution)/shard_map/ppermute | solution.py:1085
  210.3 8.9 %collective-permute-start.32 = (f32[56,128]{1,0:T(8,128)S(1)}, f32[56,128]{1,0:T(8,128)S(1)}, u32[]{:S(2)}, u32[]{:S(2)}) collective-permute-start(f32[56,128]{1,0:T(8,128)S(1)} %get-tuple-element.281.refs_1_), channel_id=1, source_target_pairs={{0,8},{1,9},{2,10},{3,11},{4,12},{5,13},{6,14},{7,15},{8,0},{9,1},... | collective-permute-start | bytes 86024 | tf_op jit(solution)/shard_map/ppermute | solution.py:1085
  210.3 11.8 %collective-permute-start.37 = (bf16[192,128]{1,0:T(8,128)(2,1)S(1)}, bf16[192,128]{1,0:T(8,128)(2,1)S(1)}, u32[]{:S(2)}, u32[]{:S(2)}) collective-permute-start(bf16[192,128]{1,0:T(8,128)(2,1)S(1)} %get-tuple-element.288), channel_id=1, source_target_pairs={{0,4},{1,5},{2,6},{3,7},{4,0},{5,1},{6,2},{7,3},{8,12},{9,13},{10,... | collective-permute-start | bytes 147464 | tf_op jit(solution)/shard_map/ppermute | solution.py:1085
  219.1 2.7 %collective-permute-start.31 = (f32[56,128]{1,0:T(8,128)S(1)}, f32[56,128]{1,0:T(8,128)S(1)}, u32[]{:S(2)}, u32[]{:S(2)}) collective-permute-start(f32[56,128]{1,0:T(8,128)S(1)} %get-tuple-element.281.refs_1_), channel_id=1, source_target_pairs={{0,4},{1,5},{2,6},{3,7},{4,0},{5,1},{6,2},{7,3},{8,12},{9,13},{10,... | collective-permute-start | bytes 86024 | tf_op jit(solution)/shard_map/ppermute | solution.py:1085
  221.8 4.2 %collective-permute-start.38 = (bf16[192,128]{1,0:T(8,128)(2,1)S(1)}, bf16[192,128]{1,0:T(8,128)(2,1)S(1)}, u32[]{:S(2)}, u32[]{:S(2)}) collective-permute-start(bf16[192,128]{1,0:T(8,128)(2,1)S(1)} %get-tuple-element.289), channel_id=1, source_target_pairs={{0,8},{1,9},{2,10},{3,11},{4,12},{5,13},{6,14},{7,15},{8,0},{9,1},... | collective-permute-start | bytes 147464 | tf_op jit(solution)/shard_map/ppermute | solution.py:1085
  222.2 4.8 %collective-permute-start.39 = (bf16[192,128]{1,0:T(8,128)(2,1)S(1)}, bf16[192,128]{1,0:T(8,128)(2,1)S(1)}, u32[]{:S(2)}, u32[]{:S(2)}) collective-permute-start(bf16[192,128]{1,0:T(8,128)(2,1)S(1)} %get-tuple-element.290), channel_id=1, source_target_pairs={{0,12},{1,13},{2,14},{3,15},{4,8},{5,9},{6,10},{7,11},{8,4},{9,5},... | collective-permute-start | bytes 147464 | tf_op jit(solution)/shard_map/ppermute | solution.py:1085
  227.1 15.9 %collective-permute-start.48 = (bf16[1792,128]{1,0:T(8,128)(2,1)S(1)}, bf16[1792,128]{1,0:T(8,128)(2,1)S(1)}, u32[]{:S(2)}, u32[]{:S(2)}) collective-permute-start(bf16[1792,128]{1,0:T(8,128)(2,1)S(1)} %get-tuple-element.296.refs_1_), channel_id=1, source_target_pairs={{0,3},{1,2},{2,1},{3,0},{4,7},{5,6},{6,5},{7,4},{8,11},{9,10},{10,... | collective-permute-start | bytes 1376264 | tf_op jit(solution)/shard_map/ppermute | solution.py:1085
  228.7 20.9 %collective-permute-start.47 = (bf16[1792,128]{1,0:T(8,128)(2,1)S(1)}, bf16[1792,128]{1,0:T(8,128)(2,1)S(1)}, u32[]{:S(2)}, u32[]{:S(2)}) collective-permute-start(bf16[1792,128]{1,0:T(8,128)(2,1)S(1)} %get-tuple-element.296.refs_1_), channel_id=1, source_target_pairs={{0,2},{1,3},{2,0},{3,1},{4,6},{5,7},{6,4},{7,5},{8,10},{9,11},{10,... | collective-permute-start | bytes 1376264 | tf_op jit(solution)/shard_map/ppermute | solution.py:1085
  230.4 19.2 %collective-permute-start.46 = (bf16[1792,128]{1,0:T(8,128)(2,1)S(1)}, bf16[1792,128]{1,0:T(8,128)(2,1)S(1)}, u32[]{:S(2)}, u32[]{:S(2)}) collective-permute-start(bf16[1792,128]{1,0:T(8,128)(2,1)S(1)} %get-tuple-element.296.refs_1_), channel_id=1, source_target_pairs={{0,1},{1,0},{2,3},{3,2},{4,5},{5,4},{6,7},{7,6},{8,9},{9,8},{10,11... | collective-permute-start | bytes 1376264 | tf_op jit(solution)/shard_map/ppermute | solution.py:1085
  230.4 4.7 %collective-permute-start.45 = (bf16[192,128]{1,0:T(8,128)(2,1)S(1)}, bf16[192,128]{1,0:T(8,128)(2,1)S(1)}, u32[]{:S(2)}, u32[]{:S(2)}) collective-permute-start(bf16[192,128]{1,0:T(8,128)(2,1)S(1)} %get-tuple-element.294.refs_1_), channel_id=1, source_target_pairs={{0,12},{1,13},{2,14},{3,15},{4,8},{5,9},{6,10},{7,11},{8,4},{9,5},... | collective-permute-start | bytes 147464 | tf_op jit(solution)/shard_map/ppermute | solution.py:1085
  231.7 4.8 %collective-permute-start.44 = (bf16[192,128]{1,0:T(8,128)(2,1)S(1)}, bf16[192,128]{1,0:T(8,128)(2,1)S(1)}, u32[]{:S(2)}, u32[]{:S(2)}) collective-permute-start(bf16[192,128]{1,0:T(8,128)(2,1)S(1)} %get-tuple-element.294.refs_1_), channel_id=1, source_target_pairs={{0,8},{1,9},{2,10},{3,11},{4,12},{5,13},{6,14},{7,15},{8,0},{9,1},... | collective-permute-start | bytes 147464 | tf_op jit(solution)/shard_map/ppermute | solution.py:1085
  235.1 7.8 %collective-permute-start.43 = (bf16[192,128]{1,0:T(8,128)(2,1)S(1)}, bf16[192,128]{1,0:T(8,128)(2,1)S(1)}, u32[]{:S(2)}, u32[]{:S(2)}) collective-permute-start(bf16[192,128]{1,0:T(8,128)(2,1)S(1)} %get-tuple-element.294.refs_1_), channel_id=1, source_target_pairs={{0,4},{1,5},{2,6},{3,7},{4,0},{5,1},{6,2},{7,3},{8,12},{9,13},{10,... | collective-permute-start | bytes 147464 | tf_op jit(solution)/shard_map/ppermute | solution.py:1085
  236.5 30.1 %collective-permute-start.52 = (bf16[1024,128]{1,0:T(8,128)(2,1)S(1)}, bf16[1024,128]{1,0:T(8,128)(2,1)S(1)}, u32[]{:S(2)}, u32[]{:S(2)}) collective-permute-start(bf16[1024,128]{1,0:T(8,128)(2,1)S(1)} %get-tuple-element.307.refs_1_), channel_id=1, source_target_pairs={{0,16},{16,0},{1,17},{17,1},{2,18},{18,2},{3,19},{19,3},{4,20},{20... | collective-permute-start | bytes 786440 | tf_op jit(solution)/shard_map/ppermute | solution.py:1080
  251.6 15.0 %collective-permute-start.53 = (bf16[1024,128]{1,0:T(8,128)(2,1)S(1)}, bf16[1024,128]{1,0:T(8,128)(2,1)S(1)}, u32[]{:S(2)}, u32[]{:S(2)}) collective-permute-start(bf16[1024,128]{1,0:T(8,128)(2,1)S(1)} %get-tuple-element.308.refs_3_), channel_id=1, source_target_pairs={{0,16},{16,0},{1,17},{17,1},{2,18},{18,2},{3,19},{19,3},{4,20},{20... | collective-permute-start | bytes 786440 | tf_op jit(solution)/shard_map/ppermute | solution.py:1080
  253.3 7.4 %collective-permute-start.51 = (bf16[768,128]{1,0:T(8,128)(2,1)S(1)}, bf16[768,128]{1,0:T(8,128)(2,1)S(1)}, u32[]{:S(2)}, u32[]{:S(2)}) collective-permute-start(bf16[768,128]{1,0:T(8,128)(2,1)S(1)} %get-tuple-element.299.refs_1_), channel_id=1, source_target_pairs={{0,3},{1,2},{2,1},{3,0},{4,7},{5,6},{6,5},{7,4},{8,11},{9,10},{10,... | collective-permute-start | bytes 589832 | tf_op jit(solution)/shard_map/ppermute | solution.py:1085
  254.9 10.3 %collective-permute-start.50 = (bf16[768,128]{1,0:T(8,128)(2,1)S(1)}, bf16[768,128]{1,0:T(8,128)(2,1)S(1)}, u32[]{:S(2)}, u32[]{:S(2)}) collective-permute-start(bf16[768,128]{1,0:T(8,128)(2,1)S(1)} %get-tuple-element.299.refs_1_), channel_id=1, source_target_pairs={{0,2},{1,3},{2,0},{3,1},{4,6},{5,7},{6,4},{7,5},{8,10},{9,11},{10,... | collective-permute-start | bytes 589832 | tf_op jit(solution)/shard_map/ppermute | solution.py:1085
  255.9 9.3 %collective-permute-start.49 = (bf16[768,128]{1,0:T(8,128)(2,1)S(1)}, bf16[768,128]{1,0:T(8,128)(2,1)S(1)}, u32[]{:S(2)}, u32[]{:S(2)}) collective-permute-start(bf16[768,128]{1,0:T(8,128)(2,1)S(1)} %get-tuple-element.299.refs_1_), channel_id=1, source_target_pairs={{0,1},{1,0},{2,3},{3,2},{4,5},{5,4},{6,7},{7,6},{8,9},{9,8},{10,11... | collective-permute-start | bytes 589832 | tf_op jit(solution)/shard_map/ppermute | solution.py:1085
  (63 other events, 262.5 us)

commit v2 on v1

--- a/solution.py
+++ b/solution.py
@@ -21,6 +21,7 @@
 LANES = 128
 ELEMENT_ROWS = 32
 UNROLL = 4
+RELAY = 50
 
 
 def core_place(row_devices):
@@ -140,7 +141,8 @@
     nothing = jnp.zeros((8, states), f32)
     zero = (nothing, nothing)
     values, _ = sweep(running_up, drives, masks, lanes, (zero, zero))
-    payload[...] = jnp.zeros_like(payload)
+    one = jnp.zeros((16, LANES), f32)
+    payload[0] = one
     for side in range(2):
         ends[side][:, :states] = values[side][0]
         ends[side][:, states:] = values[side][1]
@@ -149,9 +151,12 @@
         re, im = run_chain(upward, lanes, side, ends[side], wholes[side], (start, start), None)
         base = jnp.where(upward, 0, 8)
         for i in range(thirds):
-            payload[pl.ds(base + i, 1), :] = re[:, LANES * i : LANES * (i + 1)]
-            payload[pl.ds(base + thirds + i, 1), :] = im[:, LANES * i : LANES * (i + 1)]
-        payload[8 * side + 6 : 8 * side + 8, :] = ids_ref[0:2, :]
+            payload[0, pl.ds(base + i, 1), :] = re[:, LANES * i : LANES * (i + 1)]
+            payload[0, pl.ds(base + thirds + i, 1), :] = im[:, LANES * i : LANES * (i + 1)]
+        payload[0, 8 * side + 6 : 8 * side + 8, :] = ids_ref[0:2, :]
+    one = payload[0]
+    for i in range(1, payload.shape[0]):
+        payload[i] = one
 
 
 def entering(upward, place, lanes, side, gathered, ids_ref, small):
@@ -574,16 +579,15 @@
     low_oth,
     block_out,
     grad_out,
-    act_low,
-    gate_low,
     combined_grad,
-    combined_low,
     grad_own,
     grad_oth,
     next_ends_own,
     next_ends_oth,
     payload,
     sums,
+    mine,
+    theirs,
     places,
     small,
     wide,
@@ -594,6 +598,9 @@
     natural_out,
     states_own,
     states_oth,
+    act_low,
+    gate_low,
+    combined_low,
 ):
     info = core_place(row_devices)
     rows = x_in.shape[0]
@@ -637,6 +644,7 @@
         whole, rows_ref, tiles_ref, ids, gate_low, combined_grad, combined_low, grad_own, grad_oth,
         (next_ends_own, next_ends_oth), payload, sums, wide,
     )
+    gradient_pack(act_low, gate_low, combined_low, low_own, low_oth, mine, theirs, wide)
 
 
 def adjoint_states(
@@ -705,21 +713,14 @@
 
 def back_kernel(
     row_devices,
-    gathered,
-    ends_own,
-    ends_oth,
-    grad_own,
-    grad_oth,
+    in_low_own,
+    in_low_oth,
     keep_own,
     keep_oth,
     whole,
     rows_ref,
     tiles_ref,
     ids,
-    states_own,
-    states_oth,
-    drive_own,
-    drive_oth,
     in_own,
     in_oth,
     out_own,
@@ -736,39 +737,32 @@
     phi,
     sig,
     normed,
+    act_low,
     low_own,
     low_oth,
-    decay_sums,
     grad_out,
-    gate_low,
     combined_grad,
-    combined_low,
     next_own,
     next_oth,
     next_ends_own,
     next_ends_oth,
     payload,
     sums,
-    places,
-    small,
+    mine,
+    theirs,
     wide,
-    adjoint_own,
-    adjoint_oth,
+    gate_low,
+    combined_low,
 ):
     info = core_place(row_devices)
     masks = (keep_own, keep_oth)
-    adjoint_states(
-        1, info, gathered, (ends_own, ends_oth), (grad_own, grad_oth), masks, whole, rows_ref, tiles_ref, ids,
-        (states_own, states_oth), (drive_own, drive_oth), (low_own, low_oth), decay_sums,
-        (adjoint_own, adjoint_oth), places, small,
-    )
     sums[...] = jnp.zeros_like(sums)
 
     def finish(start, value):
         grad_out[pl.ds(start, ELEMENT_ROWS), :] = value
 
     norm_backward(
-        1, low_own, low_oth, in_own, in_oth, grad_in, combined_grad_in, normed_in, inv_in, gain, skip, sums, wide,
+        1, in_low_own, in_low_oth, in_own, in_oth, grad_in, combined_grad_in, normed_in, inv_in, gain, skip, sums, wide,
         finish,
     )
     backward_half(
@@ -776,9 +770,11 @@
         rows_ref, tiles_ref, ids, gate_low, combined_grad, combined_low, next_own, next_oth,
         (next_ends_own, next_ends_oth), payload, sums, wide,
     )
-
-
-def last_kernel(
+    gradient_pack(act_low, gate_low, combined_low, low_own, low_oth, mine, theirs, wide)
+
+
+def scan_kernel(
+    layer,
     row_devices,
     gathered,
     ends_own,
@@ -809,7 +805,7 @@
     info = core_place(row_devices)
     masks = (keep_own, keep_oth)
     adjoint_states(
-        0, info, gathered, (ends_own, ends_oth), (grad_own, grad_oth), masks, whole, rows_ref, tiles_ref, ids,
+        layer, info, gathered, (ends_own, ends_oth), (grad_own, grad_oth), masks, whole, rows_ref, tiles_ref, ids,
         (states_own, states_oth), (drive_own, drive_oth), (low_own, low_oth), decay_sums,
         (adjoint_own, adjoint_oth), places, small,
     )
@@ -848,53 +844,116 @@
             out[first + i * half : first + (i + 1) * half, :] = wide[rows, i * LANES : (i + 1) * LANES].astype(out.dtype)
 
 
-def weights_kernel(act_low, gate_low, combined_low, low_own, low_oth, payload_in, mine, theirs, payload, wide):
-    payload[...] = payload_in[...]
-    core = lax.axis_index("dir")
+def gradient_pack(act_low, gate_low, combined_low, low_own, low_oth, mine, theirs, wide):
     store_columns(theirs, 0, dot_tn(low_oth[...], combined_low[...]))
     store_columns(mine, 0, dot_tn(low_own[...], combined_low[...]))
     size = low_own.shape[1] * (combined_low.shape[1] // LANES)
-    half_rows(core, act_low, gate_low, mine, theirs, size, wide)
-
-
-def weights_two_kernel(
-    mixed_low, in_low_own, in_low_oth, act_low, gate_low, combined_low, low_own, low_oth, payload_in, mine, theirs,
-    payload, wide,
-):
-    payload[...] = payload_in[...]
-    core = lax.axis_index("dir")
-    store_columns(theirs, 0, dot_tn(mixed_low[...], in_low_oth[...]))
-    store_columns(mine, 0, dot_tn(mixed_low[...], in_low_own[...]))
-    size = mixed_low.shape[1] * (in_low_own.shape[1] // LANES)
-    store_columns(theirs, size, dot_tn(low_oth[...], combined_low[...]))
-    store_columns(mine, size, dot_tn(low_own[...], combined_low[...]))
-    size = size + low_own.shape[1] * (combined_low.shape[1] // LANES)
-    half_rows(core, act_low, gate_low, mine, theirs, size, wide)
+    half_rows(lax.axis_index("dir"), act_low, gate_low, mine, theirs, size, wide)
 
 
 def slot(low_bit, parts):
     return jnp.bitwise_and(jnp.right_shift(lax.axis_index("seq"), low_bit), parts - 1)
 
 
-def sum_kernel(count, low_bit, *refs):
-    sources, outs = refs[:count], refs[count:]
+def paired(values):
+    while len(values) > 1:
+        values = [a + b for a, b in zip(values[::2], values[1::2])]
+    return values[0]
+
+
+def part_rows(index, rows):
+    return pl.ds(pl.multiple_of(index * rows, rows), rows)
+
+
+def sum_parts(groups, outs, low_bit):
     parts = len(outs)
-    rows = outs[0].shape[0]
-    mine = slot(low_bit, parts) if parts > 1 else 0
+    mine = slot(low_bit, parts)
     for k, out in enumerate(outs):
-        where = pl.ds(pl.multiple_of(jnp.bitwise_xor(mine, k) * rows, rows), rows) if parts > 1 else slice(None)
-        total = sources[0][where, :].astype(f32)
-        for source in sources[1:]:
-            total = total + source[where, :].astype(f32)
-        out[...] = total.astype(out.dtype)
-
-
-def gather_kernel(low_bit, *refs):
-    sources, out = refs[:-1], refs[-1]
-    rows = sources[0].shape[0]
+        first = 0
+        for rows, sources in groups:
+            share = rows // parts
+            where = part_rows(jnp.bitwise_xor(mine, k), share)
+            total = paired([source[where, :].astype(f32) for source in sources])
+            out[first : first + share, :] = total.astype(out.dtype)
+            first += share
+
+
+def gather_parts(sizes, sources, low_bit, outs):
     mine = slot(low_bit, len(sources))
     for k, source in enumerate(sources):
-        out[pl.ds(pl.multiple_of(jnp.bitwise_xor(mine, k) * rows, rows), rows), :] = source[...]
+        first = 0
+        for rows, out in zip(sizes, outs):
+            out[part_rows(jnp.bitwise_xor(mine, k), rows), :] = source[first : first + rows, :]
+            first += rows
+
+
+def encode_small(value, outs, first):
+    high = value.astype(bf16)
+    low = (value - high.astype(f32)).astype(bf16)
+    rows = value.shape[0]
+    for out in outs:
+        out[first : first + rows, :] = high
+        out[first + rows : first + 2 * rows, :] = low
+
+
+def decode_small(sources, first, rows):
+    return paired(
+        [
+            source[first : first + rows, :].astype(f32) + source[first + rows : first + 2 * rows, :].astype(f32)
+            for source in sources
+        ]
+    )
+
+
+def early_cores_kernel(mine, got, *outs):
+    sum_parts([(mine.shape[0], [mine, got])], outs, 0)
+
+
+def relay_kernel(payload_in, payload):
+    payload[...] = payload_in[...]
+
+
+def first_plane_kernel(*refs):
+    early, inner, (mine, got), outs = refs[:4], refs[4:8], refs[8:10], refs[10:]
+    sum_parts([(early[0].shape[0], early), (inner[0].shape[0], inner)], outs[:4], 2)
+    sum_parts([(mine.shape[0], [mine, got])], outs[4:], 0)
+
+
+def late_cores_kernel(small_rows, mine, got, sums_turn, sums_back, sums_last, decay_late, decay_early, *outs):
+    pack = outs[:4]
+    small = outs[4]
+    small_pack(sums_turn, sums_back, sums_last, decay_late, decay_early, small)
+    sum_parts([(mine.shape[0], [mine, got])], pack, 0)
+    encode_small(small[...], pack, mine.shape[0] // 4)
+
+
+def planes_kernel(*refs):
+    refs[-1][...] = paired([source[...].astype(f32) for source in refs[:-1]]).astype(bf16)
+
+
+def gather_kernel(sizes, *refs):
+    out = refs[-1]
+    outs = []
+    first = 0
+    for rows in sizes:
+        outs.append(out.at[first : first + 4 * rows])
+        first += 4 * rows
+    gather_parts(sizes, refs[:-1], 2, outs)
+
+
+def second_plane_kernel(small_rows, *refs):
+    outer, late, outs, small = refs[:4], refs[4:8], refs[8:12], refs[12]
+    late_rows = late[0].shape[0] - 2 * small_rows
+    sum_parts([(outer[0].shape[0], outer), (late_rows, late)], outs, 2)
+    small[...] = decode_small(late, late_rows, small_rows)
+    encode_small(small[...], outs, (outer[0].shape[0] + late_rows) // 4)
+
+
+def second_planes_kernel(small_rows, *refs):
+    sources, out, small = refs[:-2], refs[-2], refs[-1]
+    rows = out.shape[0]
+    out[...] = paired([source[0:rows, :].astype(f32) for source in sources]).astype(bf16)
+    small[...] = decode_small(sources, rows, small_rows)
 
 
 def join_kernel(mine, theirs, out):
@@ -910,26 +969,27 @@
         out[:, i * LANES : (i + 1) * LANES] = source[first + i * rows : first + (i + 1) * rows, :].astype(f32)
 
 
-def unpack_kernel(layer_of, olds, gate_rows, *refs):
+def gate_part_kernel(quarter_rows, first, *refs):
+    sources, out, whole = refs[:-2], refs[-2], refs[-1]
+    gather_parts((quarter_rows,), sources, 0, (whole,))
+    out[...] = whole[first : first + out.shape[0], :]
+
+
+def unpack_kernel(layer, olds, sizes, *refs):
     refs = list(refs)
     take = lambda n: [refs.pop(0) for _ in range(n)]
     sources = take(4)
     take(olds)
-    outs = take(len(layer_of))
-    gate_out = take(1 if gate_rows else 0)
-    buffers = take(len(layer_of))
-    whole, sems = refs
-    gather_kernel(0, *sources, whole)
-    first = 0
+    outs = take(2)
+    buffers = take(2)
+    whole = take(2)
+    (sems,) = refs
+    gather_parts(sizes, sources, 0, whole)
     copies = []
-    for i, layer in enumerate(layer_of):
-        buffer, out = buffers[i], outs[i]
-        matrix_columns(whole, first, buffer)
-        first = first + buffer.shape[0] * (buffer.shape[1] // LANES)
-        copies.append(pltpu.make_async_copy(buffer, out.at[layer, 0], sems.at[i]))
+    for i in range(2):
+        matrix_columns(whole[i], 0, buffers[i])
+        copies.append(pltpu.make_async_copy(buffers[i], outs[i].at[layer, 0], sems.at[i]))
         copies[-1].start()
-    for out in gate_out:
-        out[...] = whole[first : first + gate_rows, :]
     for copy in copies:
         copy.wait()
 
@@ -945,11 +1005,10 @@
                 out[layer, rows, i * LANES : (i + 1) * LANES] = source[i * half : (i + 1) * half, :].astype(f32)
 
 
-def small_pack_kernel(sums_turn, sums_back, sums_last, decay_late, decay_early, send, own):
+def small_pack(sums_turn, sums_back, sums_last, decay_late, decay_early, out):
     per = sums_turn.shape[1] // LANES
     thirds = decay_late.shape[1] // LANES
-    send[...] = jnp.zeros_like(send)
-    own[...] = jnp.zeros_like(own)
+    out[...] = jnp.zeros_like(out)
     kinds = (
         ((sums_last, 2), (sums_back, 2)),
         ((sums_last, 3), (sums_back, 3)),
@@ -960,31 +1019,35 @@
     for kind in kinds:
         for source, row in kind:
             for i in range(per):
-                value = source[row : row + 1, i * LANES : (i + 1) * LANES]
-                send[at : at + 1, :] = value
-                own[at : at + 1, :] = value
+                out[at : at + 1, :] = source[row : row + 1, i * LANES : (i + 1) * LANES]
                 at += 1
-    for source in (decay_late, decay_early):
-        for term in range(3):
-            for i in range(thirds):
-                lanes = slice(i * LANES, (i + 1) * LANES)
-                own[at : at + 1, :] = source[term : term + 1, lanes]
-                send[at : at + 1, :] = source[3 + term : 4 + term, lanes]
-                at += 1
-
-
-def small_kernel(tokens_rows, own, got, table, out):
+    for side in range(2):
+        for source in (decay_late, decay_early):
+            for term in range(3):
+                for i in range(thirds):
+                    row = 3 * side + term
+                    out[at : at + 1, :] = source[row : row + 1, i * LANES : (i + 1) * LANES]
+                    at += 1
+
+
+def small_out_kernel(own, got, table, gain, bias, rate, turn, skip, gate):
     layers, _, states = table.shape
     thirds = states // LANES
-    out[...] = jnp.zeros_like(out)
-    out[0:tokens_rows, :] = own[0:tokens_rows, :] + got[0:tokens_rows, :]
+    width = gain.shape[1]
+    per = width // LANES
+    at = 0
+    for out in (gain, bias, skip, gate):
+        for layer in range(layers):
+            for i in range(per):
+                out[layer : layer + 1, i * LANES : (i + 1) * LANES] = own[at : at + 1, :] + got[at : at + 1, :]
+                at += 1
+    other = at + layers * 3 * thirds
     for layer in range(layers):
         for i in range(thirds):
             lanes = slice(i * LANES, (i + 1) * LANES)
-            base = tokens_rows + (layer * 3) * thirds + i
+            rows = [(layer * 3 + t) * thirds + i for t in range(3)]
             term_re, term_im, term_scale = (
-                own[base + t * thirds : base + t * thirds + 1, :] + got[base + t * thirds : base + t * thirds + 1, :]
-                for t in range(3)
+                own[at + row : at + row + 1, :] + got[other + row : other + row + 1, :] for row in rows
             )
             re, im, scale, damping, step_size, rotation, square = (
                 table[layer, t : t + 1, lanes] for t in range(7)
@@ -995,42 +1058,9 @@
             grad_damping = grad_scale * square / scale - (grad_re * re + grad_im * im)
             grad_rotation = grad_im * re - grad_re * im
             log_rate = grad_damping * damping
-            at = tokens_rows + layer * thirds + i
-            out[at : at + 1, :] = log_rate
-            at = tokens_rows + layers * thirds + (layer * 2) * thirds + i
-            out[at : at + 1, :] = grad_rotation * step_size
-            out[at + thirds : at + thirds + 1, :] = log_rate + grad_rotation * rotation
-
-
-def add_kernel(*refs):
-    total = refs[0][...]
-    for source in refs[1:-1]:
-        total = total + source[...]
-    refs[-1][...] = total
-
-
-def small_out_kernel(*refs):
-    sources, (gain, bias, rate, turn, skip, gate) = refs[:-6], refs[-6:]
-    layers, width = gain.shape
-    per = width // LANES
-    thirds = rate.shape[1] // LANES
-    total = sources[0][...]
-    for source in sources[1:]:
-        total = total + source[...]
-    at = 0
-    for out in (gain, bias, skip, gate):
-        for layer in range(layers):
-            for i in range(per):
-                out[layer : layer + 1, i * LANES : (i + 1) * LANES] = total[at : at + 1]
-                at += 1
-    for layer in range(layers):
-        for i in range(thirds):
-            rate[layer : layer + 1, i * LANES : (i + 1) * LANES] = total[at : at + 1]
-            at += 1
-    for row in range(2 * layers):
-        for i in range(thirds):
-            turn[row : row + 1, i * LANES : (i + 1) * LANES] = total[at : at + 1]
-            at += 1
+            rate[layer : layer + 1, lanes] = log_rate
+            turn[2 * layer : 2 * layer + 1, lanes] = grad_rotation * step_size
+            turn[2 * layer + 1 : 2 * layer + 2, lanes] = log_rate + grad_rotation * rotation
 
 
 class Order:
@@ -1038,7 +1068,7 @@
         self.tile = None
 
     def run(self, kernel, outs, operands, scratch=(), flops=0, name=None, spare=8, after=(), free_outs=0, alias=None,
-            semaphores=0):
+            semaphores=0, cost=0):
         whole = pl.BlockSpec(memory_space=pltpu.VMEM)
         free = pl.BlockSpec(memory_space=pl.ANY)
         waits = list(after) + ([] if self.tile is None else [self.tile])
@@ -1052,7 +1082,6 @@
 
         shapes = [jax.ShapeDtypeStruct((8, LANES), f32)]
         shapes += [jax.ShapeDtypeStruct(shape, dtype) for shape, dtype in outs]
-        moved = sum(value.size * value.dtype.itemsize for value in operands)
         held = sum(jnp.dtype(dtype).itemsize * functools.reduce(lambda a, b: a * b, shape) for shape, dtype in scratch)
         specs = [free] * skipped + [whole] * inputs
         aliases = {}
@@ -1069,7 +1098,7 @@
             scratch_shapes=[pltpu.VMEM(shape, dtype) for shape, dtype in scratch] + extra,
             input_output_aliases=aliases,
             compiler_params=pltpu.CompilerParams(vmem_limit_bytes=held + spare * 2**20),
-            cost_estimate=pl.CostEstimate(flops=int(flops), bytes_accessed=int(moved), transcendentals=0),
+            cost_estimate=pl.CostEstimate(flops=int(1 + cost * 1e9), bytes_accessed=int(1 + cost * 3e6), transcendentals=0),
             name=name,
         )(*waits, *operands)
         self.tile = results[0]
@@ -1099,42 +1128,15 @@
     groups = None
     if count != row_devices:
         groups = [list(range(i, i + group)) for i in range(0, 2 * count, group)]
-    copies = jnp.broadcast_to(payload[None], (group,) + payload.shape)
-    return lax.all_to_all(copies, ("seq", "dir"), 0, 0, tiled=True, axis_index_groups=groups)
-
-
-class Pack:
-    def __init__(self, order, name, mine, theirs):
-        self.order, self.name = order, name
-        self.mine, self.got = mine, swap(theirs)
-        self.rows = mine.shape[0]
-
-    def sum(self, sources, parts, low_bit, step, after=()):
-        rows = sources[0].shape[0] // parts
-        return self.order.run(
-            functools.partial(sum_kernel, len(sources), low_bit), [((rows, LANES), bf16)] * parts, sources,
-            name=f"{self.name}_{step}", after=after,
-        )
-
-    def first(self, after=()):
-        self.parts = self.sum([self.mine, self.got], 4, 0, "sum_cores", after)
-        self.parts = [self.parts[0]] + [across(self.parts[k], k) for k in (1, 2, 3)]
-
-    def second(self, after=()):
-        self.parts = self.sum(self.parts, 4, 2, "sum_plane", after)
-        self.parts = [self.parts[0]] + [across(self.parts[k], k << 2) for k in (1, 2, 3)]
-
-    def third(self, after=()):
-        (share,) = self.sum(self.parts, 1, 0, "sum_planes", after)
-        share = beyond(share)
-        self.parts = [share] + [across(share, k << 2) for k in (1, 2, 3)]
-
-    def fourth(self, after=()):
-        (quarter,) = self.order.run(
-            functools.partial(gather_kernel, 2), [((self.rows // 4, LANES), bf16)], self.parts,
-            name=f"{self.name}_gather", after=after,
-        )
-        self.parts = [quarter] + [across(quarter, k) for k in (1, 2, 3)]
+    return lax.all_to_all(payload, ("seq", "dir"), 0, 0, tiled=True, axis_index_groups=groups)
+
+
+def sent(parts, low_bit):
+    return [parts[0]] + [across(parts[k], k << low_bit) for k in (1, 2, 3)]
+
+
+def shared(value, low_bit):
+    return [value] + [across(value, k << low_bit) for k in (1, 2, 3)]
 
 
 def body(
@@ -1171,13 +1173,19 @@
     wide = ((rows, 2 * states), f32)
     wide_low = ((rows, 2 * states), bf16)
     ends = ((8, 2 * states), f32)
-    payload_shape = ((16, LANES), f32)
+    payload_shape = ((2 * row_devices, 16, LANES), f32)
     narrow = ((rows, LANES), f32)
     tile = ((8, LANES), f32)
     sums_shape = ((8, width), f32)
     decay_shape = ((8, states), f32)
     table_shape = ((layers, 16, states), f32)
     places = ((8, 2 * states), f32)
+    in_size = width * (2 * states // LANES)
+    out_size = 2 * states * (width // LANES)
+    glu_size = width // 2 * (width // LANES)
+    outer_size = out_size + glu_size
+    outer_pack = ((outer_size, LANES), bf16)
+    inner_pack = ((in_size, LANES), bf16)
     one = 2.0 * rows * width * 2 * states
     gate = 2.0 * rows * width * width
     scan = 1e9
@@ -1196,6 +1204,7 @@
         [mixed0, in_oth, rate_oth, turn_oth, table, drive_own0, keep_own, keep_oth, whole, ids],
         flops=one + scan,
         name="open_scan",
+        after=[out_oth],
     )
     gathered = exchanged(payload, row_devices)
     (
@@ -1213,137 +1222,148 @@
     )
     gathered = exchanged(payload, row_devices)
     (
-        low_own1, low_oth1, half_out, grad1, act_low1, gate_low1, combined_grad1, combined_low1, grad_own1, grad_oth1,
-        ends_own, ends_oth, payload, sums_turn,
+        low_own1, low_oth1, half_out, grad1, combined_grad1, grad_own1, grad_oth1, ends_own, ends_oth, payload,
+        sums_turn, mine, theirs,
     ) = order.run(
         here(turn_kernel, row_devices),
-        [wide_low, wide_low, full, full, full_low, full_low, full, full_low, wide, wide, ends, ends, payload_shape,
-         sums_shape],
+        [wide_low, wide_low, full, full, full, wide, wide, ends, ends, payload_shape, sums_shape, outer_pack, outer_pack],
         [gathered, ends_own, ends_oth, drive_own1, drive_oth1, keep_own, keep_oth, whole, table, tiles,
          ids, out_own, out_oth, x1, normed1, norm_gain, norm_bias, skip_weight, glu_weight, glu_bias, cotangent],
-        [places, tile, full, full, full, full, columns, columns, wide, wide],
+        [places, tile, full, full, full, full, columns, columns, wide, wide, full_low, full_low, full_low],
         flops=4 * one + 2 * gate + 4 * scan,
         name="turn",
     )
-    in_size = width * (2 * states // LANES)
-    out_size = 2 * states * (width // LANES)
-    glu_size = width // 2 * (width // LANES)
-    pack = ((out_size + glu_size, LANES), bf16)
-    mine, theirs, payload = order.run(
-        weights_kernel,
-        [pack, pack, payload_shape],
-        [act_low1, gate_low1, combined_low1, low_own1, low_oth1, payload],
-        [((width, width), f32)],
-        flops=2 * one + gate,
-        name="weights_early",
-    )
+    got = swap(theirs)
+    got_half = swap(half_out)
     gathered = exchanged(payload, row_devices)
-    early = Pack(order, "early", mine, theirs)
-    early.first(after=[gathered])
+    early = order.run(
+        early_cores_kernel, [((outer_size // 4, LANES), bf16)] * 4, [mine, got], name="early_cores", after=[gathered]
+    )
+    early = sent(early, 0)
+    in_low_own1, in_low_oth1, decay_sums1, mine, theirs = order.run(
+        here(scan_kernel, 1, row_devices),
+        [wide_low, wide_low, decay_shape, inner_pack, inner_pack],
+        [gathered, ends_own, ends_oth, grad_own1, grad_oth1, keep_own, keep_oth, whole, table, tiles,
+         ids, low_own1, low_oth1, drive_own1, drive_oth1, mixed1],
+        [places, tile, wide, wide],
+        name="scan_one",
+    )
+    got = swap(theirs)
     (
-        in_low_own1, in_low_oth1, decay_sums1, grad0, gate_low0, combined_grad0, combined_low0, grad_own0, grad_oth0,
-        ends_own, ends_oth, payload, sums_back,
+        grad0, combined_grad0, grad_own0, grad_oth0, ends_own, ends_oth, payload, sums_back, mine_outer, theirs_outer,
     ) = order.run(
         here(back_kernel, row_devices),
-        [wide_low, wide_low, decay_shape, full, full_low, full, full_low, wide, wide, ends, ends, payload_shape,
-         sums_shape],
-        [gathered, ends_own, ends_oth, grad_own1, grad_oth1, keep_own, keep_oth, whole, table, tiles,
-         ids, low_own1, low_oth1, drive_own1, drive_oth1, in_own, in_oth, out_own, out_oth, grad1, combined_grad1,
-         normed1, inv1, norm_gain, norm_bias, skip_weight, glu_weight, combined0, phi0, sig0, normed0],
-        [places, tile, full, wide, wide],
-        flops=4 * one + gate + 4 * scan,
+        [full, full, wide, wide, ends, ends, payload_shape, sums_shape, outer_pack, outer_pack],
+        [in_low_own1, in_low_oth1, keep_own, keep_oth, whole, table, tiles, ids, in_own, in_oth, out_own, out_oth, grad1,
+         combined_grad1, normed1, inv1, norm_gain, norm_bias, skip_weight, glu_weight, combined0, phi0, sig0, normed0,
+         act_low0, low_own0, low_oth0],
+        [full, full_low, full_low],
         name="back",
     )
-    early.second()
-    pack = ((in_size + out_size + glu_size, LANES), bf16)
-    mine, theirs, payload = order.run(
-        weights_two_kernel,
-        [pack, pack, payload_shape],
-        [mixed1, in_low_own1, in_low_oth1, act_low0, gate_low0, combined_low0, low_own0, low_oth0, payload],
-        [((width, width), f32)],
-        flops=4 * one + gate,
-        name="weights_middle",
-    )
+    got_outer = swap(theirs_outer)
+    (payload,) = order.run(relay_kernel, [payload_shape], [payload], name="relay", after=early[1:] + [got_half], cost=RELAY)
     gathered = exchanged(payload, row_devices)
-    middle = Pack(order, "middle", mine, theirs)
-    middle.first(after=[gathered])
-    early.third()
-    pack = ((in_size, LANES), bf16)
+    inner = order.run(
+        early_cores_kernel, [((in_size // 4, LANES), bf16)] * 4, [mine, got], name="inner_cores", after=[gathered]
+    )
+    inner = sent(inner, 0)
     in_low_own0, in_low_oth0, decay_sums0, mine, theirs = order.run(
-        here(last_kernel, row_devices),
-        [wide_low, wide_low, decay_shape, pack, pack],
+        here(scan_kernel, 0, row_devices),
+        [wide_low, wide_low, decay_shape, inner_pack, inner_pack],
         [gathered, ends_own, ends_oth, grad_own0, grad_oth0, keep_own, keep_oth, whole, table, tiles,
          ids, low_own0, low_oth0, drive_own0, drive_oth0, mixed0],
         [places, tile, wide, wide],
-        flops=2 * one + 2 * scan,
-        name="last_scan",
-    )
-    late = Pack(order, "late", mine, theirs)
-    early.fourth()
+        name="scan_zero",
+    )
+    got = swap(theirs)
+    quarter = (outer_size + in_size) // 4
+    parts = order.run(
+        first_plane_kernel,
+        [((quarter // 4, LANES), bf16)] * 4 + [((outer_size // 4, LANES), bf16)] * 4,
+        early + inner + [mine_outer, got_outer],
+        name="first_plane",
+    )
+    first = sent(parts[:4], 2)
+    outer = sent(parts[4:], 0)
     half_grad, sums_last = order.run(
         final_kernel,
         [full, sums_shape],
         [in_low_own0, in_low_oth0, in_own, in_oth, grad0, combined_grad0, normed0, inv0, norm_gain, skip_weight],
         [full, columns],
-        flops=2 * one + scan,
         name="final_norm",
     )
-    late.first()
-    token_rows = 4 * layers * (width // LANES)
-    small_rows = -(-(token_rows + 3 * layers * (states // LANES)) // 8) * 8
-    small = ((small_rows, LANES), f32)
-    send, own = order.run(
-        small_pack_kernel, [small, small], [sums_turn, sums_back, sums_last, decay_sums0, decay_sums1],
-        name="small_pack",
-    )
-    got = swap(send)
+    small_rows = -(-(4 * layers * (width // LANES) + 6 * layers * (states // LANES)) // 16) * 16
+    *late, _ = order.run(
+        here(late_cores_kernel, small_rows),
+        [((in_size // 4 + 2 * small_rows, LANES), bf16)] * 4 + [((small_rows, LANES), f32)],
+        [mine, got, sums_turn, sums_back, sums_last, decay_sums0, decay_sums1],
+        name="late_cores",
+    )
+    late = sent(late, 0)
+    (share,) = order.run(planes_kernel, [((quarter // 4, LANES), bf16)], first, name="first_planes", after=outer[1:])
+    first = shared(beyond(share), 2)
     whole_rows = ((chip_rows, width), f32)
-    (block_output,) = order.run(join_kernel, [whole_rows], [half_out, swap(half_out)], name="join_out")
-    (tiny,) = order.run(here(small_kernel, token_rows), [small], [own, got, table], name="small_map")
-    tiny = [tiny] + [across(tiny, k) for k in (1, 2, 3)]
-    middle.second()
+    (block_output,) = order.run(join_kernel, [whole_rows], [half_out, got_half], name="join_out")
+    sizes = (outer_size // 16, in_size // 16)
+    (full_quarter,) = order.run(
+        here(gather_kernel, sizes), [((quarter, LANES), bf16)], first, name="first_gather"
+    )
+    first = shared(full_quarter, 0)
     (tokens_grad,) = order.run(join_kernel, [whole_rows], [half_grad, swap(half_grad)], name="join_grad")
-    (tiny,) = order.run(add_kernel, [small], tiny, name="small_plane")
-    tiny = beyond(tiny)
-    tiny = [tiny] + [across(tiny, k << 2) for k in (1, 2, 3)]
-    late.second()
-    middle.third()
+    *second, _ = order.run(
+        here(second_plane_kernel, small_rows),
+        [((quarter // 4 + 2 * small_rows, LANES), bf16)] * 4 + [((small_rows, LANES), f32)],
+        outer + late,
+        name="second_plane",
+    )
+    second = sent(second, 2)
+    share, small = order.run(
+        here(second_planes_kernel, small_rows), [((quarter // 4, LANES), bf16), ((small_rows, LANES), f32)], second,
+        name="second_planes",
+    )
+    second = shared(beyond(share), 2)
+    small = beyond(small)
+    got_small = swap(small)
+    in_shape, out_shape = input_matrix.shape, output_matrix.shape
+
+    def gate_part(quarters, name):
+        (value,) = order.run(
+            here(gate_part_kernel, outer_size // 4, out_size), [((glu_size, LANES), bf16)], quarters,
+            [((outer_size, LANES), bf16)], name=name,
+        )
+        return value
+
+    def unpack(quarters, layer, old, name):
+        return order.run(
+            here(unpack_kernel, layer, len(old), (outer_size // 4, in_size // 4)),
+            [(out_shape, f32), (in_shape, f32)],
+            quarters + old,
+            [(out_shape[2:], f32), (in_shape[2:], f32), outer_pack, inner_pack],
+            name=name,
+            free_outs=2,
+            alias={4 + i: i for i in range(len(old))},
+            semaphores=2,
+        )
+
+    gate_one = gate_part(first, "gate_one")
+    got_one = swap(gate_one)
+    results = unpack(first, 1, [], "unpack_one")
     gain_grad, bias_grad, rate_grad, turn_grad, skip_grad, gate_grad = order.run(
         small_out_kernel,
         [((layers, width), f32), ((layers, width), f32), ((layers, states), f32), ((2 * layers, states), f32),
          ((layers, width), f32), ((layers, width), f32)],
-        tiny,
+        [small, got_small, table],
         name="small_out",
     )
-
-    def unpack(pack, shapes, layer_of, old, gate_rows, name):
-        held = [value for value in old if value is not None]
-        alias = {4 + i: j for i, j in enumerate(j for j, value in enumerate(old) if value is not None)}
-        gate_out = [((gate_rows, LANES), bf16)] if gate_rows else []
-        return order.run(
-            here(unpack_kernel, layer_of, len(held), gate_rows),
-            [(shape, f32) for shape in shapes] + gate_out,
-            list(pack.parts) + held,
-            [(shape[2:], f32) for shape in shapes] + [((pack.rows, LANES), bf16)],
-            name=name,
-            free_outs=len(shapes),
-            alias=alias,
-            semaphores=len(shapes),
-        )
-
-    in_shape, out_shape = input_matrix.shape, output_matrix.shape
-    out_all, gate_early = unpack(early, [out_shape], (1,), [None], glu_size, "unpack_early")
-    got_early = swap(gate_early)
-    late.third()
-    middle.fourth()
-    late.fourth()
-    in_all, out_all, gate_middle = unpack(
-        middle, [in_shape, out_shape], (1, 0), [None, out_all], glu_size, "unpack_middle"
-    )
-    got_middle = swap(gate_middle)
-    (in_all,) = unpack(late, [in_shape], (0,), [in_all], 0, "unpack_late")
+    (full_quarter,) = order.run(
+        here(gather_kernel, sizes), [((quarter, LANES), bf16)], second, name="second_gather"
+    )
+    second = shared(full_quarter, 0)
+    gate_zero = gate_part(second, "gate_zero")
+    got_zero = swap(gate_zero)
+    out_all, in_all = unpack(second, 0, list(results), "unpack_zero")
     (glu_all,) = order.run(
-        gate_kernel, [(glu_weight.shape, f32)], [gate_early, got_early, gate_middle, got_middle], name="unpack_gate"
+        gate_kernel, [(glu_weight.shape, f32)], [gate_one, got_one, gate_zero, got_zero], name="unpack_gate"
     )
     return (
         block_output,

time: 270 us -> 223 us (0.83)
  blocking collectives: 25.1 us -> 55.3 us
  local copies, waits for them, and re-layouts: 35.3 us -> 7.3 us
  waiting for transfers between devices: 74 us -> 49.3 us
  starting transfers between devices: 73.4 us -> 57.9 us
  Pallas kernels: 58.9 us -> 52 us
    all_to_all x2 -> x4, blocking collectives: 25.1 us -> 55.3 us  [exchanged(): lax.all_to_all(payload, ('seq', 'dir'), 0, 0, tiled=True, axis_index_grou...]
    unnamed x143 -> x31, local copies, waits for them, and re-layouts: 33.2 us -> 6.7 us
    all_to_all x2 -> x0, waiting for transfers between devices: 17.1 us -> none  [exchanged(): lax.all_to_all(copies, ('seq', 'dir'), 0, 0, tiled=True, axis_index_group...]
    ppermute x42 -> x30, starting transfers between devices: 50.7 us -> 38.8 us  [across(): return lax.ppermute(value, 'seq', [(i, i ^ bits) for i in range(count)])]
    all_to_all x2 -> x0, starting transfers between devices: 9.69 us -> none  [exchanged(): lax.all_to_all(copies, ('seq', 'dir'), 0, 0, tiled=True, axis_index_group...]
    pallas_call x31 -> x26, Pallas kernels: 58.9 us -> 52 us  [run(): pl.pallas_call(body, out_shape=shapes, in_specs=specs, out_specs=[whole]...]
    ppermute x42 -> x30, waiting for transfers between devices: 56 us -> 49.3 us  [across(): return lax.ppermute(value, 'seq', [(i, i ^ bits) for i in range(count)])]
    ppermute x12 -> x13, starting transfers between devices: 13.1 us -> 19.1 us  [swap(): return lax.ppermute(value, 'dir', [(0, 1), (1, 0)])]
  transfers between devices with their start and end apart: 56 -> 43, of which waited for: 20 -> 11; matrix products, arithmetic and copies ran while one was open for 1% -> 1% of each run, Pallas kernels for 11% -> 14%
where the time goes in v2:
time: 223 us
  starting transfers between devices  57.9 us (26%)
  blocking collectives  55.3 us (25%)
  Pallas kernels  52 us (23%)
  waiting for transfers between devices  49.3 us (22%)
  local copies, waits for them, and re-layouts  7.3 us (3%)
    all_to_all x4, blocking collectives, exchanged(): lax.all_to_all(payload, ('seq', 'dir'), 0, 0, tiled=True, axis_index_grou...  55.3 us
    pallas_call x26, Pallas kernels, run(): pl.pallas_call(body, out_shape=shapes, in_specs=specs, out_specs=[whole]...  52 us
    ppermute x30, waiting for transfers between devices, across(): return lax.ppermute(value, 'seq', [(i, i ^ bits) for i in range(count)])  49.3 us
    ppermute x30, starting transfers between devices, across(): return lax.ppermute(value, 'seq', [(i, i ^ bits) for i in range(count)])  38.8 us
    ppermute x13, starting transfers between devices, swap(): return lax.ppermute(value, 'dir', [(0, 1), (1, 0)])  19.1 us
    unnamed x31, local copies, waits for them, and re-layouts  6.7 us
  transfers between devices with their start and end apart: 43, of which 11 were waited for; matrix products, arithmetic and copies ran while one was open for 1% of the time, Pallas kernels for 14%

profile of v2, /device:TPU:1, one launch (start us, length us, event | category | flops | bytes accessed | tf_op | source)
XLA Modules:
  0.0 222.7 jit_solution(14182351732362289003)
XLA Ops:
  1.7 1.4 copy-done
  3.1 1.2 copy-done.5
  4.4 0.7 copy-done.6
  5.1 0.7 copy-done.8
  5.7 0.7 copy-done.12
  6.4 0.7 copy-done.13
  7.1 0.7 copy-done.14
  7.8 4.3 %open_norm.1 = (f32[8,128]{1,0:T(8,128)S(1)}, f32[512,512]{1,0:T(8,128)S(1)}, f32[512,512]{1,0:T(8,128)S(1)}, f32[512,128]{1,0:T(8,128)S(1)}, bf16[512,512]{1,0:...) custom-call(bf16[1024,512]{1,0:T(8,128)(2,1)S(1)} %copy-done.5, ...), custom_call_target="tpu_custom_call" | custom-call | flops 1 | bytes 1 | tf_op jit(solution)/shard_map/open_norm/pallas_call | solution.py:1093
  12.2 1.2 open_scan.1
  13.5 17.2 %all_to_all.20.refs_1_ = f32[32,16,128]{2,1,0:T(8,128)S(1)} all-to-all(f32[32,16,128]{2,1,0:T(8,128)S(1)} %get-tuple-element.156), channel_id=1, replica_groups=mesh['dir'=2,'seq'=16] {'seq','dir'}, dimensions={0} | all-to-all | bytes 524288 | tf_op jit(solution)/shard_map/all_to_all | solution.py:1131
  30.7 7.7 %mid.1 = (f32[8,128]{1,0:T(8,128)S(1)}, bf16[512,768]{1,0:T(8,128)(2,1)S(1)}, bf16[512,768]{1,0:T(8,128)(2,1)S(1)}, f32[512,512]{1,0:T(8,128)S(1)}, f32[512,512]...) custom-call(f32[8,128]{1,0:T(8,128)S(1)} %get-tuple-element.155.refs, ...), custom_call_target="tpu_custom_call" | custom-call | flops 1 | bytes 1 | tf_op jit(solution)/shard_map/mid/pallas_call | solution.py:1093
  38.4 12.8 %all_to_all.21.refs_1_ = f32[32,16,128]{2,1,0:T(8,128)S(1)} all-to-all(f32[32,16,128]{2,1,0:T(8,128)S(1)} %get-tuple-element.165), channel_id=1, replica_groups=mesh['dir'=2,'seq'=16] {'seq','dir'}, dimensions={0} | all-to-all | bytes 524288 | tf_op jit(solution)/shard_map/all_to_all | solution.py:1131
  51.2 9.5 %turn.1 = (f32[8,128]{1,0:T(8,128)S(1)}, bf16[512,768]{1,0:T(8,128)(2,1)S(1)}, bf16[512,768]{1,0:T(8,128)(2,1)S(1)}, f32[512,512]{1,0:T(8,128)S(1)}, f32[512,512...) custom-call(f32[8,128]{1,0:T(8,128)S(1)} %get-tuple-element.164.refs, ...), custom_call_target="tpu_custom_call" | custom-call | flops 1 | bytes 1 | tf_op jit(solution)/shard_map/turn/pallas_call | solution.py:1093
  60.7 0.7 collective-permute-start.4
  61.5 12.6 %all_to_all.22.refs_0_.refs_1_ = f32[32,16,128]{2,1,0:T(8,128)S(1)} all-to-all(f32[32,16,128]{2,1,0:T(8,128)S(1)} %get-tuple-element.172), channel_id=1, replica_groups=mesh['dir'=2,'seq'=16] {'seq','dir'}, dimensions={0} | all-to-all | bytes 524288 | tf_op jit(solution)/shard_map/all_to_all | solution.py:1131
  74.4 0.7 collective-permute-start.5
  75.4 1.6 collective-permute-start.7
  77.1 2.9 %scan_one.1 = (f32[8,128]{1,0:T(8,128)S(1)}, bf16[512,768]{1,0:T(8,128)(2,1)S(1)}, bf16[512,768]{1,0:T(8,128)(2,1)S(1)}, f32[8,384]{1,0:T(8,128)S(1)}, bf16[3072...) custom-call(f32[8,128]{1,0:T(8,128)S(1)} %get-tuple-element.180.refs_0_, ...), custom_call_target="tpu_custom_call" | custom-call | flops 1 | bytes 1 | tf_op jit(solution)/shard_map/scan_one/pallas_call | solution.py:1093
  80.0 1.5 collective-permute-start.9
  81.4 7.4 %back.1 = (f32[8,128]{1,0:T(8,128)S(1)}, f32[512,512]{1,0:T(8,128)S(1)}, f32[512,512]{1,0:T(8,128)S(1)}, f32[512,768]{1,0:T(8,128)S(1)}, f32[512,768]{1,0:T(8,12...) custom-call(f32[8,128]{1,0:T(8,128)S(1)} %get-tuple-element.188.refs, ...), custom_call_target="tpu_custom_call" | custom-call | flops 1 | bytes 1 | tf_op jit(solution)/shard_map/back/pallas_call | solution.py:1093
  89.0 12.7 %all_to_all.23.refs_0_.refs_1_ = f32[32,16,128]{2,1,0:T(8,128)S(1)} all-to-all(f32[32,16,128]{2,1,0:T(8,128)S(1)} %get-tuple-element.202), channel_id=1, replica_groups=mesh['dir'=2,'seq'=16] {'seq','dir'}, dimensions={0} | all-to-all | bytes 524288 | tf_op jit(solution)/shard_map/all_to_all | solution.py:1131
  101.9 0.7 collective-permute-start.10
  103.0 1.6 collective-permute-start.12
  104.6 2.9 %scan_zero.1 = (f32[8,128]{1,0:T(8,128)S(1)}, bf16[512,768]{1,0:T(8,128)(2,1)S(1)}, bf16[512,768]{1,0:T(8,128)(2,1)S(1)}, f32[8,384]{1,0:T(8,128)S(1)}, bf16[307...) custom-call(f32[8,128]{1,0:T(8,128)S(1)} %get-tuple-element.206.refs_0_, ...), custom_call_target="tpu_custom_call" | custom-call | flops 1 | bytes 1 | tf_op jit(solution)/shard_map/scan_zero/pallas_call | solution.py:1093
  107.6 1.5 collective-permute-start.17
  109.1 4.0 %collective-permute-done.11.refs_7_ = bf16[768,128]{1,0:T(8,128)(2,1)S(1)} collective-permute-done((bf16[768,128]{1,0:T(8,128)(2,1)S(1)}, bf16[768,128]{1,0:T(8,128)(2,1)S(1)}, u32[]{:S(2)}, u32[]{:S(2)}) %collective-permute-start.11) | collective-permute-done | bytes 196640 | tf_op jit(solution)/shard_map/ppermute | solution.py:1114
  113.6 3.7 %final_norm.1 = (f32[8,128]{1,0:T(8,128)S(1)}, f32[512,512]{1,0:T(8,128)S(1)}, f32[8,512]{1,0:T(8,128)S(1)}) custom-call(f32[8,128]{1,0:T(8,128)S(1)} %get-tuple-element.222.refs_0_, bf16[512,768]{1,0:T(8,128)(2,1)S(1)} %get-tuple-element.223.refs_1_, bf16[512,768]{1,0:T(8,128)(2,1)S(1)} %get-tuple-element.224.refs_2_, ...), custom_call_target="tpu_custom_call" | custom-call | flops 1 | bytes 1 | tf_op jit(solution)/shard_map/final_norm/pallas_call | solution.py:1093
  117.3 1.1 collective-permute-start.24
  118.8 0.9 collective-permute-start.19
  119.7 0.8 collective-permute-start.14
  120.4 3.8 %collective-permute-done.18.refs_5_ = bf16[448,128]{1,0:T(8,128)(2,1)S(1)} collective-permute-done((bf16[448,128]{1,0:T(8,128)(2,1)S(1)}, bf16[448,128]{1,0:T(8,128)(2,1)S(1)}, u32[]{:S(2)}, u32[]{:S(2)}) %collective-permute-start.18) | collective-permute-done | bytes 114720 | tf_op jit(solution)/shard_map/ppermute | solution.py:1114
  124.3 1.4 collective-permute-start.15
  125.7 0.8 collective-permute-done.19.refs_6_
  126.6 1.3 collective-permute-start.16
  127.9 0.8 late_cores.1
  128.7 4.6 %collective-permute-done.20.refs_7_ = bf16[448,128]{1,0:T(8,128)(2,1)S(1)} collective-permute-done((bf16[448,128]{1,0:T(8,128)(2,1)S(1)}, bf16[448,128]{1,0:T(8,128)(2,1)S(1)}, u32[]{:S(2)}, u32[]{:S(2)}) %collective-permute-start.20) | collective-permute-done | bytes 114720 | tf_op jit(solution)/shard_map/ppermute | solution.py:1114
  133.3 3.5 %collective-permute-done.15.refs_1_.refs_3_ = bf16[1024,128]{1,0:T(8,128)(2,1)S(1)} collective-permute-done((bf16[1024,128]{1,0:T(8,128)(2,1)S(1)}, bf16[1024,128]{1,0:T(8,128)(2,1)S(1)}, u32[]{:S(2)}, u32[]{:S(2)}) %collective-permute-start.15) | collective-permute-done | bytes 262176 | tf_op jit(solution)/shard_map/ppermute | solution.py:1114
  136.9 2.5 %collective-permute-start.23 = (bf16[448,128]{1,0:T(8,128)(2,1)S(1)}, bf16[448,128]{1,0:T(8,128)(2,1)S(1)}, u32[]{:S(2)}, u32[]{:S(2)}) collective-permute-start(bf16[448,128]{1,0:T(8,128)(2,1)S(1)} %get-tuple-element.244.refs_1_), channel_id=1, source_target_pairs={{0,12},{1,13},{2,14},{3,15},{4,8},{5,9},{6,10},{7,11},{8,4},{9,5},... | collective-permute-start | bytes 344072 | tf_op jit(solution)/shard_map/ppermute | solution.py:1114
  139.5 3.1 %collective-permute-start.21 = (bf16[448,128]{1,0:T(8,128)(2,1)S(1)}, bf16[448,128]{1,0:T(8,128)(2,1)S(1)}, u32[]{:S(2)}, u32[]{:S(2)}) collective-permute-start(bf16[448,128]{1,0:T(8,128)(2,1)S(1)} %get-tuple-element.244.refs_1_), channel_id=1, source_target_pairs={{0,4},{1,5},{2,6},{3,7},{4,0},{5,1},{6,2},{7,3},{8,12},{9,13},{10,... | collective-permute-start | bytes 344072 | tf_op jit(solution)/shard_map/ppermute | solution.py:1114
  142.6 1.8 collective-permute-start.26
  144.3 4.8 %collective-permute-done.22.refs_3_ = bf16[448,128]{1,0:T(8,128)(2,1)S(1)} collective-permute-done((bf16[448,128]{1,0:T(8,128)(2,1)S(1)}, bf16[448,128]{1,0:T(8,128)(2,1)S(1)}, u32[]{:S(2)}, u32[]{:S(2)}) %collective-permute-start.22) | collective-permute-done | bytes 114720 | tf_op jit(solution)/shard_map/ppermute | solution.py:1114
  149.1 1.7 collective-permute-start.27
  150.8 1.5 join_out.1
  152.3 0.7 collective-permute-start.33
  153.1 1.5 collective-permute-start.32
  155.0 1.5 join_grad.1
  156.5 0.9 second_plane.1
  157.4 2.6 %collective-permute-start.29 = (bf16[608,128]{1,0:T(8,128)(2,1)S(1)}, bf16[608,128]{1,0:T(8,128)(2,1)S(1)}, u32[]{:S(2)}, u32[]{:S(2)}) collective-permute-start(bf16[608,128]{1,0:T(8,128)(2,1)S(1)} %get-tuple-element.257), channel_id=1, source_target_pairs={{0,8},{1,9},{2,10},{3,11},{4,12},{5,13},{6,14},{7,15},{8,0},{9,1},... | collective-permute-start | bytes 466952 | tf_op jit(solution)/shard_map/ppermute | solution.py:1114
  160.1 3.2 %collective-permute-done.28.refs_2_ = bf16[608,128]{1,0:T(8,128)(2,1)S(1)} collective-permute-done((bf16[608,128]{1,0:T(8,128)(2,1)S(1)}, bf16[608,128]{1,0:T(8,128)(2,1)S(1)}, u32[]{:S(2)}, u32[]{:S(2)}) %collective-permute-start.28) | collective-permute-done | bytes 155680 | tf_op jit(solution)/shard_map/ppermute | solution.py:1114
  163.3 2.1 collective-permute-start.30
  165.4 3.7 %collective-permute-done.30.refs_4_ = bf16[608,128]{1,0:T(8,128)(2,1)S(1)} collective-permute-done((bf16[608,128]{1,0:T(8,128)(2,1)S(1)}, bf16[608,128]{1,0:T(8,128)(2,1)S(1)}, u32[]{:S(2)}, u32[]{:S(2)}) %collective-permute-start.30) | collective-permute-done | bytes 155680 | tf_op jit(solution)/shard_map/ppermute | solution.py:1114
  169.2 2.2 collective-permute-start.37
  171.4 1.4 collective-permute-start.35
  172.8 4.5 %collective-permute-done.32.refs_3_ = bf16[1792,128]{1,0:T(8,128)(2,1)S(1)} collective-permute-done((bf16[1792,128]{1,0:T(8,128)(2,1)S(1)}, bf16[1792,128]{1,0:T(8,128)(2,1)S(1)}, u32[]{:S(2)}, u32[]{:S(2)}) %collective-permute-start.32) | collective-permute-done | bytes 458784 | tf_op jit(solution)/shard_map/ppermute | solution.py:1114
  177.4 9.0 %collective-permute-start.34 = (f32[80,128]{1,0:T(8,128)S(1)}, f32[80,128]{1,0:T(8,128)S(1)}, u32[]{:S(2)}, u32[]{:S(2)}) collective-permute-start(f32[80,128]{1,0:T(8,128)S(1)} %get-tuple-element.263.refs_1_), channel_id=1, source_target_pairs={{0,16},{16,0},{1,17},{17,1},{2,18},{18,2},{3,19},{19,3},{4,20},{20... | collective-permute-start | bytes 122888 | tf_op jit(solution)/shard_map/ppermute | solution.py:1109
  186.5 2.0 unpack_one.1
  188.5 0.6 small_out.1
  189.2 3.4 %collective-permute-start.40 = (bf16[1792,128]{1,0:T(8,128)(2,1)S(1)}, bf16[1792,128]{1,0:T(8,128)(2,1)S(1)}, u32[]{:S(2)}, u32[]{:S(2)}) collective-permute-start(bf16[1792,128]{1,0:T(8,128)(2,1)S(1)} %get-tuple-element.269.refs_1_), channel_id=1, source_target_pairs={{0,3},{1,2},{2,1},{3,0},{4,7},{5,6},{6,5},{7,4},{8,11},{9,10},{10,... | collective-permute-start | bytes 1376264 | tf_op jit(solution)/shard_map/ppermute | solution.py:1114
  192.6 5.0 %collective-permute-start.39 = (bf16[1792,128]{1,0:T(8,128)(2,1)S(1)}, bf16[1792,128]{1,0:T(8,128)(2,1)S(1)}, u32[]{:S(2)}, u32[]{:S(2)}) collective-permute-start(bf16[1792,128]{1,0:T(8,128)(2,1)S(1)} %get-tuple-element.269.refs_1_), channel_id=1, source_target_pairs={{0,2},{1,3},{2,0},{3,1},{4,6},{5,7},{6,4},{7,5},{8,10},{9,11},{10,... | collective-permute-start | bytes 1376264 | tf_op jit(solution)/shard_map/ppermute | solution.py:1114
  197.6 2.4 %collective-permute-start.41 = (bf16[1024,128]{1,0:T(8,128)(2,1)S(1)}, bf16[1024,128]{1,0:T(8,128)(2,1)S(1)}, u32[]{:S(2)}, u32[]{:S(2)}) collective-permute-start(bf16[1024,128]{1,0:T(8,128)(2,1)S(1)} %get-tuple-element.279.refs_1_), channel_id=1, source_target_pairs={{0,16},{16,0},{1,17},{17,1},{2,18},{18,2},{3,19},{19,3},{4,20},{20... | collective-permute-start | bytes 786440 | tf_op jit(solution)/shard_map/ppermute | solution.py:1109
  200.5 15.8 %collective-permute-done.39.refs_3_ = bf16[1792,128]{1,0:T(8,128)(2,1)S(1)} collective-permute-done((bf16[1792,128]{1,0:T(8,128)(2,1)S(1)}, bf16[1792,128]{1,0:T(8,128)(2,1)S(1)}, u32[]{:S(2)}, u32[]{:S(2)}) %collective-permute-start.39) | collective-permute-done | bytes 458784 | tf_op jit(solution)/shard_map/ppermute | solution.py:1114
  216.3 1.6 collective-permute-start.42
  219.1 2.0 unpack_zero.1
  221.2 1.6 unpack_gate.1
  (84 shorter events, 6.1 us)
Async XLA Ops:
  0.6 11.5 %collective-permute-start = (bf16[2,1,768,512]{3,2,1,0:T(8,128)(2,1)}, bf16[2,1,768,512]{3,2,1,0:T(8,128)(2,1)S(1)}, u32[]{:S(2)}, u32[]{:S(2)}) collective-permute-start(bf16[2,1,768,512]{3,2,1,0:T(8,128)(2,1)} %refs_11_.1), channel_id=1, source_target_pairs={{0,16},{16,0},{1,17},{17,1},{2,18},{18,2},{3,19},{19,3},{4,20},{20... | collective-permute-start | bytes 4718600 | tf_op jit(solution)/shard_map/ppermute | solution.py:1109
  0.8 11.4 %collective-permute-start.1 = (bf16[2,1,512,768]{3,2,1,0:T(8,128)(2,1)}, bf16[2,1,512,768]{3,2,1,0:T(8,128)(2,1)S(1)}, u32[]{:S(2)}, u32[]{:S(2)}) collective-permute-start(bf16[2,1,512,768]{3,2,1,0:T(8,128)(2,1)} %refs_3_.3), channel_id=1, source_target_pairs={{0,16},{16,0},{1,17},{17,1},{2,18},{18,2},{3,19},{19,3},{4,20},{20... | collective-permute-start | bytes 4718600 | tf_op jit(solution)/shard_map/ppermute | solution.py:1109
  1.2 10.9 %collective-permute-start.3 = (f32[2,1,2,384]{3,2,1,0:T(2,128)}, f32[2,1,2,384]{3,2,1,0:T(2,128)S(1)}, u32[]{:S(2)}, u32[]{:S(2)}) collective-permute-start(f32[2,1,2,384]{3,2,1,0:T(2,128)} %refs_5_.1), channel_id=1, source_target_pairs={{0,16},{16,0},{1,17},{17,1},{2,18},{18,2},{3,19},{19,3},{4,20},{20... | collective-permute-start | bytes 18440 | tf_op jit(solution)/shard_map/ppermute | solution.py:1109
  1.3 10.8 %collective-permute-start.2 = (f32[2,1,384]{2,1,0:T(1,128)}, f32[2,1,384]{2,1,0:T(1,128)S(1)}, u32[]{:S(2)}, u32[]{:S(2)}) collective-permute-start(f32[2,1,384]{2,1,0:T(1,128)} %refs_4_.1), channel_id=1, source_target_pairs={{0,16},{16,0},{1,17},{17,1},{2,18},{18,2},{3,19},{19,3},{4,20},{20... | collective-permute-start | bytes 9224 | tf_op jit(solution)/shard_map/ppermute | solution.py:1109
  1.7 1.4 copy-start
  3.1 1.2 copy-start.5
  4.4 0.7 copy-start.6
  5.1 0.7 copy-start.8
  5.7 0.7 copy-start.12
  6.4 0.7 copy-start.13
  7.1 0.7 copy-start.14
  12.2 18.5 %copy-start.1 = (bf16[2,1,512,768]{3,2,1,0:T(8,128)(2,1)S(1)}, bf16[2,1,512,768]{3,2,1,0:T(8,128)(2,1)}, u32[]{:S(2)}) copy-start(bf16[2,1,512,768]{3,2,1,0:T(8,128)(2,1)} %refs_3_.3) | copy-start | bytes 4718596
  12.2 18.5 %copy-start.2 = (bf16[2,1,768,512]{3,2,1,0:T(8,128)(2,1)S(1)}, bf16[2,1,768,512]{3,2,1,0:T(8,128)(2,1)}, u32[]{:S(2)}) copy-start(bf16[2,1,768,512]{3,2,1,0:T(8,128)(2,1)} %refs_11_.1) | copy-start | bytes 4718596
  12.2 18.5 %copy-start.3 = (bf16[2,512,512]{2,1,0:T(8,128)(2,1)S(1)}, bf16[2,512,512]{2,1,0:T(8,128)(2,1)}, u32[]{:S(2)}) copy-start(bf16[2,512,512]{2,1,0:T(8,128)(2,1)} %refs_20_.5) | copy-start | bytes 3145732
  12.2 18.5 %copy-start.7 = (f32[2,512]{1,0:T(2,128)S(1)}, f32[2,512]{1,0:T(2,128)}, u32[]{:S(2)}) copy-start(f32[2,512]{1,0:T(2,128)} %refs_9_.3) | copy-start | bytes 12292
  12.2 18.5 %copy-start.9 = (f32[2,512]{1,0:T(2,128)S(1)}, f32[2,512]{1,0:T(2,128)}, u32[]{:S(2)}) copy-start(f32[2,512]{1,0:T(2,128)} %refs_18_.5) | copy-start | bytes 12292
  12.2 18.5 %copy-start.10 = (f32[2,512]{1,0:T(2,128)S(1)}, f32[2,512]{1,0:T(2,128)}, u32[]{:S(2)}) copy-start(f32[2,512]{1,0:T(2,128)} %refs_10_.1) | copy-start | bytes 12292
  12.2 18.5 %copy-start.11 = (f32[2,512]{1,0:T(2,128)S(1)}, f32[2,512]{1,0:T(2,128)}, u32[]{:S(2)}) copy-start(f32[2,512]{1,0:T(2,128)} %refs_20_.4) | copy-start | bytes 12292
  30.7 20.5 %copy-start.4 = (f32[1024,512]{1,0:T(8,128)S(1)}, f32[1024,512]{1,0:T(8,128)}, u32[]{:S(2)}) copy-start(f32[1024,512]{1,0:T(8,128)} %refs_21_.3) | copy-start | bytes 6291460
  60.7 13.4 %collective-permute-start.4 = (bf16[4096,128]{1,0:T(8,128)(2,1)S(1)}, bf16[4096,128]{1,0:T(8,128)(2,1)S(1)}, u32[]{:S(2)}, u32[]{:S(2)}) collective-permute-start(bf16[4096,128]{1,0:T(8,128)(2,1)S(1)} %get-tuple-element.175), channel_id=1, source_target_pairs={{0,16},{16,0},{1,17},{17,1},{2,18},{18,2},{3,19},{19,3},{4,20},{20... | collective-permute-start | bytes 3145736 | tf_op jit(solution)/shard_map/ppermute | solution.py:1109
  61.4 27.5 %collective-permute-start.8 = (f32[512,512]{1,0:T(8,128)S(1)}, f32[512,512]{1,0:T(8,128)S(1)}, u32[]{:S(2)}, u32[]{:S(2)}) collective-permute-start(f32[512,512]{1,0:T(8,128)S(1)} %get-tuple-element.179.refs_1_), channel_id=1, source_target_pairs={{0,16},{16,0},{1,17},{17,1},{2,18},{18,2},{3,19},{19,3},{4,20},{20... | collective-permute-start | bytes 3145736 | tf_op jit(solution)/shard_map/ppermute | solution.py:1109
  74.4 14.6 %collective-permute-start.5 = (bf16[1024,128]{1,0:T(8,128)(2,1)S(1)}, bf16[1024,128]{1,0:T(8,128)(2,1)S(1)}, u32[]{:S(2)}, u32[]{:S(2)}) collective-permute-start(bf16[1024,128]{1,0:T(8,128)(2,1)S(1)} %get-tuple-element.176), channel_id=1, source_target_pairs={{0,1},{1,0},{2,3},{3,2},{4,5},{5,4},{6,7},{7,6},{8,9},{9,8},{10,11... | collective-permute-start | bytes 786440 | tf_op jit(solution)/shard_map/ppermute | solution.py:1114
  75.1 13.9 %collective-permute-start.6 = (bf16[1024,128]{1,0:T(8,128)(2,1)S(1)}, bf16[1024,128]{1,0:T(8,128)(2,1)S(1)}, u32[]{:S(2)}, u32[]{:S(2)}) collective-permute-start(bf16[1024,128]{1,0:T(8,128)(2,1)S(1)} %get-tuple-element.177), channel_id=1, source_target_pairs={{0,2},{1,3},{2,0},{3,1},{4,6},{5,7},{6,4},{7,5},{8,10},{9,11},{10,... | collective-permute-start | bytes 786440 | tf_op jit(solution)/shard_map/ppermute | solution.py:1114
  75.4 13.6 %collective-permute-start.7 = (bf16[1024,128]{1,0:T(8,128)(2,1)S(1)}, bf16[1024,128]{1,0:T(8,128)(2,1)S(1)}, u32[]{:S(2)}, u32[]{:S(2)}) collective-permute-start(bf16[1024,128]{1,0:T(8,128)(2,1)S(1)} %get-tuple-element.178), channel_id=1, source_target_pairs={{0,3},{1,2},{2,1},{3,0},{4,7},{5,6},{6,5},{7,4},{8,11},{9,10},{10,... | collective-permute-start | bytes 786440 | tf_op jit(solution)/shard_map/ppermute | solution.py:1114
  80.0 21.8 %collective-permute-start.9 = (bf16[3072,128]{1,0:T(8,128)(2,1)S(1)}, bf16[3072,128]{1,0:T(8,128)(2,1)S(1)}, u32[]{:S(2)}, u32[]{:S(2)}) collective-permute-start(bf16[3072,128]{1,0:T(8,128)(2,1)S(1)} %get-tuple-element.205), channel_id=1, source_target_pairs={{0,16},{16,0},{1,17},{17,1},{2,18},{18,2},{3,19},{19,3},{4,20},{20... | collective-permute-start | bytes 2359304 | tf_op jit(solution)/shard_map/ppermute | solution.py:1109
  88.9 24.2 %collective-permute-start.13 = (bf16[4096,128]{1,0:T(8,128)(2,1)S(1)}, bf16[4096,128]{1,0:T(8,128)(2,1)S(1)}, u32[]{:S(2)}, u32[]{:S(2)}) collective-permute-start(bf16[4096,128]{1,0:T(8,128)(2,1)S(1)} %get-tuple-element.218), channel_id=1, source_target_pairs={{0,16},{16,0},{1,17},{17,1},{2,18},{18,2},{3,19},{19,3},{4,20},{20... | collective-permute-start | bytes 3145736 | tf_op jit(solution)/shard_map/ppermute | solution.py:1109
  101.9 7.2 %collective-permute-start.10 = (bf16[768,128]{1,0:T(8,128)(2,1)S(1)}, bf16[768,128]{1,0:T(8,128)(2,1)S(1)}, u32[]{:S(2)}, u32[]{:S(2)}) collective-permute-start(bf16[768,128]{1,0:T(8,128)(2,1)S(1)} %get-tuple-element.214), channel_id=1, source_target_pairs={{0,1},{1,0},{2,3},{3,2},{4,5},{5,4},{6,7},{7,6},{8,9},{9,8},{10,11... | collective-permute-start | bytes 589832 | tf_op jit(solution)/shard_map/ppermute | solution.py:1114
  102.6 10.5 %collective-permute-start.11 = (bf16[768,128]{1,0:T(8,128)(2,1)S(1)}, bf16[768,128]{1,0:T(8,128)(2,1)S(1)}, u32[]{:S(2)}, u32[]{:S(2)}) collective-permute-start(bf16[768,128]{1,0:T(8,128)(2,1)S(1)} %get-tuple-element.215), channel_id=1, source_target_pairs={{0,2},{1,3},{2,0},{3,1},{4,6},{5,7},{6,4},{7,5},{8,10},{9,11},{10,... | collective-permute-start | bytes 589832 | tf_op jit(solution)/shard_map/ppermute | solution.py:1114
  103.0 10.1 %collective-permute-start.12 = (bf16[768,128]{1,0:T(8,128)(2,1)S(1)}, bf16[768,128]{1,0:T(8,128)(2,1)S(1)}, u32[]{:S(2)}, u32[]{:S(2)}) collective-permute-start(bf16[768,128]{1,0:T(8,128)(2,1)S(1)} %get-tuple-element.216), channel_id=1, source_target_pairs={{0,3},{1,2},{2,1},{3,0},{4,7},{5,6},{6,5},{7,4},{8,11},{9,10},{10,... | collective-permute-start | bytes 589832 | tf_op jit(solution)/shard_map/ppermute | solution.py:1114
  107.6 20.3 %collective-permute-start.17 = (bf16[3072,128]{1,0:T(8,128)(2,1)S(1)}, bf16[3072,128]{1,0:T(8,128)(2,1)S(1)}, u32[]{:S(2)}, u32[]{:S(2)}) collective-permute-start(bf16[3072,128]{1,0:T(8,128)(2,1)S(1)} %get-tuple-element.230), channel_id=1, source_target_pairs={{0,16},{16,0},{1,17},{17,1},{2,18},{18,2},{3,19},{19,3},{4,20},{20... | collective-permute-start | bytes 2359304 | tf_op jit(solution)/shard_map/ppermute | solution.py:1109
  117.3 37.2 %collective-permute-start.24 = (f32[512,512]{1,0:T(8,128)S(1)}, f32[512,512]{1,0:T(8,128)S(1)}, u32[]{:S(2)}, u32[]{:S(2)}) collective-permute-start(f32[512,512]{1,0:T(8,128)S(1)} %get-tuple-element.246.refs_1_), channel_id=1, source_target_pairs={{0,16},{16,0},{1,17},{17,1},{2,18},{18,2},{3,19},{19,3},{4,20},{20... | collective-permute-start | bytes 3145736 | tf_op jit(solution)/shard_map/ppermute | solution.py:1109
  118.4 5.9 %collective-permute-start.18 = (bf16[448,128]{1,0:T(8,128)(2,1)S(1)}, bf16[448,128]{1,0:T(8,128)(2,1)S(1)}, u32[]{:S(2)}, u32[]{:S(2)}) collective-permute-start(bf16[448,128]{1,0:T(8,128)(2,1)S(1)} %get-tuple-element.238), channel_id=1, source_target_pairs={{0,4},{1,5},{2,6},{3,7},{4,0},{5,1},{6,2},{7,3},{8,12},{9,13},{10,... | collective-permute-start | bytes 344072 | tf_op jit(solution)/shard_map/ppermute | solution.py:1114
  118.8 7.7 %collective-permute-start.19 = (bf16[448,128]{1,0:T(8,128)(2,1)S(1)}, bf16[448,128]{1,0:T(8,128)(2,1)S(1)}, u32[]{:S(2)}, u32[]{:S(2)}) collective-permute-start(bf16[448,128]{1,0:T(8,128)(2,1)S(1)} %get-tuple-element.239), channel_id=1, source_target_pairs={{0,8},{1,9},{2,10},{3,11},{4,12},{5,13},{6,14},{7,15},{8,0},{9,1},... | collective-permute-start | bytes 344072 | tf_op jit(solution)/shard_map/ppermute | solution.py:1114
  119.7 13.6 %collective-permute-start.14 = (bf16[1024,128]{1,0:T(8,128)(2,1)S(1)}, bf16[1024,128]{1,0:T(8,128)(2,1)S(1)}, u32[]{:S(2)}, u32[]{:S(2)}) collective-permute-start(bf16[1024,128]{1,0:T(8,128)(2,1)S(1)} %get-tuple-element.219), channel_id=1, source_target_pairs={{0,1},{1,0},{2,3},{3,2},{4,5},{5,4},{6,7},{7,6},{8,9},{9,8},{10,11... | collective-permute-start | bytes 786440 | tf_op jit(solution)/shard_map/ppermute | solution.py:1114
  124.3 12.6 %collective-permute-start.15 = (bf16[1024,128]{1,0:T(8,128)(2,1)S(1)}, bf16[1024,128]{1,0:T(8,128)(2,1)S(1)}, u32[]{:S(2)}, u32[]{:S(2)}) collective-permute-start(bf16[1024,128]{1,0:T(8,128)(2,1)S(1)} %get-tuple-element.220), channel_id=1, source_target_pairs={{0,2},{1,3},{2,0},{3,1},{4,6},{5,7},{6,4},{7,5},{8,10},{9,11},{10,... | collective-permute-start | bytes 786440 | tf_op jit(solution)/shard_map/ppermute | solution.py:1114
  126.6 10.3 %collective-permute-start.16 = (bf16[1024,128]{1,0:T(8,128)(2,1)S(1)}, bf16[1024,128]{1,0:T(8,128)(2,1)S(1)}, u32[]{:S(2)}, u32[]{:S(2)}) collective-permute-start(bf16[1024,128]{1,0:T(8,128)(2,1)S(1)} %get-tuple-element.221), channel_id=1, source_target_pairs={{0,3},{1,2},{2,1},{3,0},{4,7},{5,6},{6,5},{7,4},{8,11},{9,10},{10,... | collective-permute-start | bytes 786440 | tf_op jit(solution)/shard_map/ppermute | solution.py:1114
  127.9 5.4 %collective-permute-start.20 = (bf16[448,128]{1,0:T(8,128)(2,1)S(1)}, bf16[448,128]{1,0:T(8,128)(2,1)S(1)}, u32[]{:S(2)}, u32[]{:S(2)}) collective-permute-start(bf16[448,128]{1,0:T(8,128)(2,1)S(1)} %get-tuple-element.240), channel_id=1, source_target_pairs={{0,12},{1,13},{2,14},{3,15},{4,8},{5,9},{6,10},{7,11},{8,4},{9,5},... | collective-permute-start | bytes 344072 | tf_op jit(solution)/shard_map/ppermute | solution.py:1114
  136.9 5.6 %collective-permute-start.23 = (bf16[448,128]{1,0:T(8,128)(2,1)S(1)}, bf16[448,128]{1,0:T(8,128)(2,1)S(1)}, u32[]{:S(2)}, u32[]{:S(2)}) collective-permute-start(bf16[448,128]{1,0:T(8,128)(2,1)S(1)} %get-tuple-element.244.refs_1_), channel_id=1, source_target_pairs={{0,12},{1,13},{2,14},{3,15},{4,8},{5,9},{6,10},{7,11},{8,4},{9,5},... | collective-permute-start | bytes 344072 | tf_op jit(solution)/shard_map/ppermute | solution.py:1114
  139.5 9.6 %collective-permute-start.22 = (bf16[448,128]{1,0:T(8,128)(2,1)S(1)}, bf16[448,128]{1,0:T(8,128)(2,1)S(1)}, u32[]{:S(2)}, u32[]{:S(2)}) collective-permute-start(bf16[448,128]{1,0:T(8,128)(2,1)S(1)} %get-tuple-element.244.refs_1_), channel_id=1, source_target_pairs={{0,8},{1,9},{2,10},{3,11},{4,12},{5,13},{6,14},{7,15},{8,0},{9,1},... | collective-permute-start | bytes 344072 | tf_op jit(solution)/shard_map/ppermute | solution.py:1114
  139.5 13.6 %collective-permute-start.25 = (bf16[928,128]{1,0:T(8,128)(2,1)S(1)}, bf16[928,128]{1,0:T(8,128)(2,1)S(1)}, u32[]{:S(2)}, u32[]{:S(2)}) collective-permute-start(bf16[928,128]{1,0:T(8,128)(2,1)S(1)} %get-tuple-element.251), channel_id=1, source_target_pairs={{0,1},{1,0},{2,3},{3,2},{4,5},{5,4},{6,7},{7,6},{8,9},{9,8},{10,11... | collective-permute-start | bytes 712712 | tf_op jit(solution)/shard_map/ppermute | solution.py:1114
  139.5 12.8 %collective-permute-start.21 = (bf16[448,128]{1,0:T(8,128)(2,1)S(1)}, bf16[448,128]{1,0:T(8,128)(2,1)S(1)}, u32[]{:S(2)}, u32[]{:S(2)}) collective-permute-start(bf16[448,128]{1,0:T(8,128)(2,1)S(1)} %get-tuple-element.244.refs_1_), channel_id=1, source_target_pairs={{0,4},{1,5},{2,6},{3,7},{4,0},{5,1},{6,2},{7,3},{8,12},{9,13},{10,... | collective-permute-start | bytes 344072 | tf_op jit(solution)/shard_map/ppermute | solution.py:1114
  142.6 13.9 %collective-permute-start.26 = (bf16[928,128]{1,0:T(8,128)(2,1)S(1)}, bf16[928,128]{1,0:T(8,128)(2,1)S(1)}, u32[]{:S(2)}, u32[]{:S(2)}) collective-permute-start(bf16[928,128]{1,0:T(8,128)(2,1)S(1)} %get-tuple-element.252), channel_id=1, source_target_pairs={{0,2},{1,3},{2,0},{3,1},{4,6},{5,7},{6,4},{7,5},{8,10},{9,11},{10,... | collective-permute-start | bytes 712712 | tf_op jit(solution)/shard_map/ppermute | solution.py:1114
  149.1 7.4 %collective-permute-start.27 = (bf16[928,128]{1,0:T(8,128)(2,1)S(1)}, bf16[928,128]{1,0:T(8,128)(2,1)S(1)}, u32[]{:S(2)}, u32[]{:S(2)}) collective-permute-start(bf16[928,128]{1,0:T(8,128)(2,1)S(1)} %get-tuple-element.253), channel_id=1, source_target_pairs={{0,3},{1,2},{2,1},{3,0},{4,7},{5,6},{6,5},{7,4},{8,11},{9,10},{10,... | collective-permute-start | bytes 712712 | tf_op jit(solution)/shard_map/ppermute | solution.py:1114
  152.3 19.1 %collective-permute-start.33 = (bf16[1792,128]{1,0:T(8,128)(2,1)S(1)}, bf16[1792,128]{1,0:T(8,128)(2,1)S(1)}, u32[]{:S(2)}, u32[]{:S(2)}) collective-permute-start(bf16[1792,128]{1,0:T(8,128)(2,1)S(1)} %get-tuple-element.260.refs_1_), channel_id=1, source_target_pairs={{0,3},{1,2},{2,1},{3,0},{4,7},{5,6},{6,5},{7,4},{8,11},{9,10},{10,... | collective-permute-start | bytes 1376264 | tf_op jit(solution)/shard_map/ppermute | solution.py:1114
  153.1 24.3 %collective-permute-start.32 = (bf16[1792,128]{1,0:T(8,128)(2,1)S(1)}, bf16[1792,128]{1,0:T(8,128)(2,1)S(1)}, u32[]{:S(2)}, u32[]{:S(2)}) collective-permute-start(bf16[1792,128]{1,0:T(8,128)(2,1)S(1)} %get-tuple-element.260.refs_1_), channel_id=1, source_target_pairs={{0,2},{1,3},{2,0},{3,1},{4,6},{5,7},{6,4},{7,5},{8,10},{9,11},{10,... | collective-permute-start | bytes 1376264 | tf_op jit(solution)/shard_map/ppermute | solution.py:1114
  154.6 31.8 %collective-permute-start.31 = (bf16[1792,128]{1,0:T(8,128)(2,1)S(1)}, bf16[1792,128]{1,0:T(8,128)(2,1)S(1)}, u32[]{:S(2)}, u32[]{:S(2)}) collective-permute-start(bf16[1792,128]{1,0:T(8,128)(2,1)S(1)} %get-tuple-element.260.refs_1_), channel_id=1, source_target_pairs={{0,1},{1,0},{2,3},{3,2},{4,5},{5,4},{6,7},{7,6},{8,9},{9,8},{10,11... | collective-permute-start | bytes 1376264 | tf_op jit(solution)/shard_map/ppermute | solution.py:1114
  157.4 5.8 %collective-permute-start.28 = (bf16[608,128]{1,0:T(8,128)(2,1)S(1)}, bf16[608,128]{1,0:T(8,128)(2,1)S(1)}, u32[]{:S(2)}, u32[]{:S(2)}) collective-permute-start(bf16[608,128]{1,0:T(8,128)(2,1)S(1)} %get-tuple-element.256), channel_id=1, source_target_pairs={{0,4},{1,5},{2,6},{3,7},{4,0},{5,1},{6,2},{7,3},{8,12},{9,13},{10,... | collective-permute-start | bytes 466952 | tf_op jit(solution)/shard_map/ppermute | solution.py:1114
  157.4 8.0 %collective-permute-start.29 = (bf16[608,128]{1,0:T(8,128)(2,1)S(1)}, bf16[608,128]{1,0:T(8,128)(2,1)S(1)}, u32[]{:S(2)}, u32[]{:S(2)}) collective-permute-start(bf16[608,128]{1,0:T(8,128)(2,1)S(1)} %get-tuple-element.257), channel_id=1, source_target_pairs={{0,8},{1,9},{2,10},{3,11},{4,12},{5,13},{6,14},{7,15},{8,0},{9,1},... | collective-permute-start | bytes 466952 | tf_op jit(solution)/shard_map/ppermute | solution.py:1114
  163.3 5.9 %collective-permute-start.30 = (bf16[608,128]{1,0:T(8,128)(2,1)S(1)}, bf16[608,128]{1,0:T(8,128)(2,1)S(1)}, u32[]{:S(2)}, u32[]{:S(2)}) collective-permute-start(bf16[608,128]{1,0:T(8,128)(2,1)S(1)} %get-tuple-element.258), channel_id=1, source_target_pairs={{0,12},{1,13},{2,14},{3,15},{4,8},{5,9},{6,10},{7,11},{8,4},{9,5},... | collective-permute-start | bytes 466952 | tf_op jit(solution)/shard_map/ppermute | solution.py:1114
  169.2 19.9 %collective-permute-start.37 = (bf16[448,128]{1,0:T(8,128)(2,1)S(1)}, bf16[448,128]{1,0:T(8,128)(2,1)S(1)}, u32[]{:S(2)}, u32[]{:S(2)}) collective-permute-start(bf16[448,128]{1,0:T(8,128)(2,1)S(1)} %get-tuple-element.267.refs_1_), channel_id=1, source_target_pairs={{0,12},{1,13},{2,14},{3,15},{4,8},{5,9},{6,10},{7,11},{8,4},{9,5},... | collective-permute-start | bytes 344072 | tf_op jit(solution)/shard_map/ppermute | solution.py:1114
  171.4 17.7 %collective-permute-start.36 = (bf16[448,128]{1,0:T(8,128)(2,1)S(1)}, bf16[448,128]{1,0:T(8,128)(2,1)S(1)}, u32[]{:S(2)}, u32[]{:S(2)}) collective-permute-start(bf16[448,128]{1,0:T(8,128)(2,1)S(1)} %get-tuple-element.267.refs_1_), channel_id=1, source_target_pairs={{0,8},{1,9},{2,10},{3,11},{4,12},{5,13},{6,14},{7,15},{8,0},{9,1},... | collective-permute-start | bytes 344072 | tf_op jit(solution)/shard_map/ppermute | solution.py:1114
  171.4 17.7 %collective-permute-start.35 = (bf16[448,128]{1,0:T(8,128)(2,1)S(1)}, bf16[448,128]{1,0:T(8,128)(2,1)S(1)}, u32[]{:S(2)}, u32[]{:S(2)}) collective-permute-start(bf16[448,128]{1,0:T(8,128)(2,1)S(1)} %get-tuple-element.267.refs_1_), channel_id=1, source_target_pairs={{0,4},{1,5},{2,6},{3,7},{4,0},{5,1},{6,2},{7,3},{8,12},{9,13},{10,... | collective-permute-start | bytes 344072 | tf_op jit(solution)/shard_map/ppermute | solution.py:1114
  177.4 11.1 %collective-permute-start.34 = (f32[80,128]{1,0:T(8,128)S(1)}, f32[80,128]{1,0:T(8,128)S(1)}, u32[]{:S(2)}, u32[]{:S(2)}) collective-permute-start(f32[80,128]{1,0:T(8,128)S(1)} %get-tuple-element.263.refs_1_), channel_id=1, source_target_pairs={{0,16},{16,0},{1,17},{17,1},{2,18},{18,2},{3,19},{19,3},{4,20},{20... | collective-permute-start | bytes 122888 | tf_op jit(solution)/shard_map/ppermute | solution.py:1109
  189.2 11.2 %collective-permute-start.40 = (bf16[1792,128]{1,0:T(8,128)(2,1)S(1)}, bf16[1792,128]{1,0:T(8,128)(2,1)S(1)}, u32[]{:S(2)}, u32[]{:S(2)}) collective-permute-start(bf16[1792,128]{1,0:T(8,128)(2,1)S(1)} %get-tuple-element.269.refs_1_), channel_id=1, source_target_pairs={{0,3},{1,2},{2,1},{3,0},{4,7},{5,6},{6,5},{7,4},{8,11},{9,10},{10,... | collective-permute-start | bytes 1376264 | tf_op jit(solution)/shard_map/ppermute | solution.py:1114
  192.6 23.6 %collective-permute-start.39 = (bf16[1792,128]{1,0:T(8,128)(2,1)S(1)}, bf16[1792,128]{1,0:T(8,128)(2,1)S(1)}, u32[]{:S(2)}, u32[]{:S(2)}) collective-permute-start(bf16[1792,128]{1,0:T(8,128)(2,1)S(1)} %get-tuple-element.269.refs_1_), channel_id=1, source_target_pairs={{0,2},{1,3},{2,0},{3,1},{4,6},{5,7},{6,4},{7,5},{8,10},{9,11},{10,... | collective-permute-start | bytes 1376264 | tf_op jit(solution)/shard_map/ppermute | solution.py:1114
  197.6 18.6 %collective-permute-start.38 = (bf16[1792,128]{1,0:T(8,128)(2,1)S(1)}, bf16[1792,128]{1,0:T(8,128)(2,1)S(1)}, u32[]{:S(2)}, u32[]{:S(2)}) collective-permute-start(bf16[1792,128]{1,0:T(8,128)(2,1)S(1)} %get-tuple-element.269.refs_1_), channel_id=1, source_target_pairs={{0,1},{1,0},{2,3},{3,2},{4,5},{5,4},{6,7},{7,6},{8,9},{9,8},{10,11... | collective-permute-start | bytes 1376264 | tf_op jit(solution)/shard_map/ppermute | solution.py:1114
  197.6 23.5 %collective-permute-start.41 = (bf16[1024,128]{1,0:T(8,128)(2,1)S(1)}, bf16[1024,128]{1,0:T(8,128)(2,1)S(1)}, u32[]{:S(2)}, u32[]{:S(2)}) collective-permute-start(bf16[1024,128]{1,0:T(8,128)(2,1)S(1)} %get-tuple-element.279.refs_1_), channel_id=1, source_target_pairs={{0,16},{16,0},{1,17},{17,1},{2,18},{18,2},{3,19},{19,3},{4,20},{20... | collective-permute-start | bytes 786440 | tf_op jit(solution)/shard_map/ppermute | solution.py:1109
  216.3 4.8 %collective-permute-start.42 = (bf16[1024,128]{1,0:T(8,128)(2,1)S(1)}, bf16[1024,128]{1,0:T(8,128)(2,1)S(1)}, u32[]{:S(2)}, u32[]{:S(2)}) collective-permute-start(bf16[1024,128]{1,0:T(8,128)(2,1)S(1)} %get-tuple-element.280.refs_3_), channel_id=1, source_target_pairs={{0,16},{16,0},{1,17},{17,1},{2,18},{18,2},{3,19},{19,3},{4,20},{20... | collective-permute-start | bytes 786440 | tf_op jit(solution)/shard_map/ppermute | solution.py:1109

commit v3 on v2

--- a/solution.py
+++ b/solution.py
@@ -19,8 +19,8 @@
 
 
 LANES = 128
-ELEMENT_ROWS = 32
-UNROLL = 4
+ELEMENT_ROWS = 512
+UNROLL = 8
 RELAY = 50
 
 
@@ -260,36 +260,77 @@
         table[layer, base + i : base + i + 1, :] = row
 
 
-def open_kernel(
+def open_kernel(row_devices, tokens_from, x_out, normed_out, inv_out, tokens, natural, sems):
+    copy = pltpu.make_async_copy(
+        tokens_from.at[part_rows(lax.axis_index("dir"), tokens.shape[0])], tokens, sems.at[0]
+    )
+    copy.start()
+    copy.wait()
+    rows = x_out.shape[0]
+    span = rows // 8
+    fill_columns(natural, tokens[...].astype(f32))
+
+    def element(start, carry):
+        x = tile_order(natural, start // 8, ELEMENT_ROWS // 8, span)
+        normed, inv_scale = standardise(x)
+        block = pl.ds(start, ELEMENT_ROWS)
+        x_out[block, :] = x
+        normed_out[block, :] = normed
+        inv_out[block, :] = jnp.broadcast_to(inv_scale, (ELEMENT_ROWS, LANES))
+        return carry
+
+    over_blocks(rows, element)
+
+
+def open_second_kernel(
     row_devices,
-    tokens,
+    normed,
     segments,
     gain,
     bias,
     rate,
     turn,
+    rate_oth,
+    turn_oth,
     in_own,
-    x_out,
-    normed_out,
-    inv_out,
-    mixed_out,
-    drive_out,
+    in_oth,
+    mixed_low,
+    drive_own,
+    drive_oth,
     keep_own,
     keep_oth,
     whole_out,
+    ends_own,
+    ends_oth,
+    payload,
     table,
+    tiles,
     ids,
-    natural,
     rows8,
 ):
     core, _ = core_place(row_devices)
-    rows = x_out.shape[0]
+    rows = normed.shape[0]
     span = rows // 8
-    base = pl.multiple_of(core * rows, rows)
-    fill_columns(natural, tokens[pl.ds(base, rows), :].astype(f32))
+
+    def element(start, carry):
+        block = pl.ds(start, ELEMENT_ROWS)
+        mixed_low[block, :] = (normed[block, :] * gain[0:1, :] + bias[0:1, :]).astype(bf16)
+        return carry
+
+    over_blocks(rows, element)
     table[...] = jnp.zeros_like(table)
+    tiles[...] = jnp.zeros_like(tiles)
+    thirds = table.shape[2] // LANES
     for layer in range(table.shape[0]):
         table_rows(table, layer, 0, rate, turn)
+        table_rows(table, layer, 8, rate_oth, turn_oth)
+        for side in range(2):
+            for part in range(2):
+                for i in range(thirds):
+                    at = 8 * side + part * thirds + i
+                    tiles[layer, at : at + 1, :] = table[
+                        layer, 8 * side + part : 8 * side + part + 1, i * LANES : (i + 1) * LANES
+                    ]
 
     number = segments[...].astype(f32)
     count = number.shape[0]
@@ -325,63 +366,15 @@
     ids[...] = jnp.zeros_like(ids)
     ids[0:1, :] = jnp.broadcast_to(first_row[:, 0:1], (1, LANES))
     ids[1:2, :] = jnp.broadcast_to(last_row[:, LANES - 1 : LANES], (1, LANES))
-
-    def element(start, carry):
-        x = tile_order(natural, start // 8, ELEMENT_ROWS // 8, span)
-        normed, inv_scale = standardise(x)
-        block = pl.ds(start, ELEMENT_ROWS)
-        x_out[block, :] = x
-        normed_out[block, :] = normed
-        inv_out[block, :] = jnp.broadcast_to(inv_scale, (ELEMENT_ROWS, LANES))
-        mixed_out[block, :] = (normed * gain[0:1, :] + bias[0:1, :]).astype(bf16)
-        return carry
-
-    over_blocks(rows, element)
-    scale = table[0, 2:3, :]
-    drive_out[...] = dot(mixed_out[...], in_own[0, 0]) * jnp.concatenate([scale, scale], 1)
-
-
-def open_second_kernel(
-    row_devices,
-    mixed_low,
-    in_oth,
-    rate,
-    turn,
-    table_in,
-    drive_own,
-    keep_own,
-    keep_oth,
-    whole,
-    ids,
-    drive_oth,
-    ends_own,
-    ends_oth,
-    payload,
-    table,
-    tiles,
-):
-    core, _ = core_place(row_devices)
-    table[...] = table_in[...]
-    tiles[...] = jnp.zeros_like(tiles)
-    thirds = table.shape[2] // LANES
-    for layer in range(table.shape[0]):
-        table_rows(table, layer, 8, rate, turn)
-        for side in range(2):
-            for part in range(2):
-                for i in range(thirds):
-                    at = 8 * side + part * thirds + i
-                    tiles[layer, at : at + 1, :] = table[
-                        layer, 8 * side + part : 8 * side + part + 1, i * LANES : (i + 1) * LANES
-                    ]
-    scale = table[0, 10:11, :]
-    drive_oth[...] = dot(mixed_low[...], in_oth[0, 0]) * jnp.concatenate([scale, scale], 1)
-    rows = drive_own.shape[0]
+    for side, (matrix, drive) in enumerate(((in_own, drive_own), (in_oth, drive_oth))):
+        scale = table[0, 8 * side + 2 : 8 * side + 3, :]
+        drive[...] = dot(mixed_low[...], matrix[0, 0]) * jnp.concatenate([scale, scale], 1)
     lanes = make_lanes(table, tiles, 0, False, rows)
     first_pass(
         core == 0,
         (drive_own, drive_oth),
         (keep_own, keep_oth),
-        (whole.at[0], whole.at[1]),
+        (whole_out.at[0], whole_out.at[1]),
         lanes,
         ids,
         (ends_own, ends_oth),
@@ -595,7 +588,6 @@
     phi_rows,
     sig_rows,
     natural,
-    natural_out,
     states_own,
     states_oth,
     act_low,
@@ -631,13 +623,11 @@
         block = pl.ds(start, ELEMENT_ROWS)
         sig = jax.nn.sigmoid(wide[block, :] + glu_bias[1:2, :])
         sig_rows[block, :] = sig
-        result = x_in[block, :] + combined[block, :] * phi_rows[block, :] * sig
-        store_token_order(natural_out, start // 8, result, span)
+        block_out[block, :] = x_in[block, :] + combined[block, :] * phi_rows[block, :] * sig
         grad_out[block, :] = tile_order(natural, start // 8, ELEMENT_ROWS // 8, span)
         return carry
 
     over_blocks(rows, element_two)
-    join_columns(block_out, natural_out)
     sums[...] = jnp.zeros_like(sums)
     backward_half(
         1, info, grad_out, combined, phi_rows, sig_rows, normed, gain, bias, skip, glu, out_own, out_oth, masks,
@@ -814,18 +804,20 @@
 
 
 def final_kernel(
-    low_own, low_oth, in_own, in_oth, grad_in, combined_grad, normed, inv_scale, gain, skip, out, sums, wide, natural
+    low_own, low_oth, in_own, in_oth, grad_in, combined_grad, normed, inv_scale, gain, skip, block_out, out, sums, wide, natural, natural_out
 ):
     rows = grad_in.shape[0]
     sums[...] = jnp.zeros_like(sums)
 
     def finish(start, value):
         store_token_order(natural, start // 8, value, rows // 8)
+        store_token_order(natural_out, start // 8, block_out[pl.ds(start, ELEMENT_ROWS), :], rows // 8)
 
     norm_backward(
         0, low_own, low_oth, in_own, in_oth, grad_in, combined_grad, normed, inv_scale, gain, skip, sums, wide, finish
     )
-    join_columns(out, natural)
+    join_columns(out.at[0], natural_out)
+    join_columns(out.at[1], natural)
 
 
 def store_columns(out, first, values):
@@ -913,18 +905,13 @@
     payload[...] = payload_in[...]
 
 
-def first_plane_kernel(*refs):
-    early, inner, (mine, got), outs = refs[:4], refs[4:8], refs[8:10], refs[10:]
-    sum_parts([(early[0].shape[0], early), (inner[0].shape[0], inner)], outs[:4], 2)
-    sum_parts([(mine.shape[0], [mine, got])], outs[4:], 0)
-
-
-def late_cores_kernel(small_rows, mine, got, sums_turn, sums_back, sums_last, decay_late, decay_early, *outs):
-    pack = outs[:4]
-    small = outs[4]
-    small_pack(sums_turn, sums_back, sums_last, decay_late, decay_early, small)
-    sum_parts([(mine.shape[0], [mine, got])], pack, 0)
-    encode_small(small[...], pack, mine.shape[0] // 4)
+def first_plane_kernel(small_rows, *refs):
+    early, inner, (outer, got_outer, late, got_late), small_sums = refs[:4], refs[4:8], refs[8:12], refs[12:17]
+    first, second, small = refs[17:21], refs[21:25], refs[25]
+    sum_parts([(early[0].shape[0], early), (inner[0].shape[0], inner)], first, 2)
+    sum_parts([(outer.shape[0], [outer, got_outer]), (late.shape[0], [late, got_late])], second, 0)
+    small_pack(*small_sums, small)
+    encode_small(small[...], second, (outer.shape[0] + late.shape[0]) // 4)
 
 
 def planes_kernel(*refs):
@@ -941,12 +928,16 @@
     gather_parts(sizes, refs[:-1], 2, outs)
 
 
-def second_plane_kernel(small_rows, *refs):
-    outer, late, outs, small = refs[:4], refs[4:8], refs[8:12], refs[12]
-    late_rows = late[0].shape[0] - 2 * small_rows
-    sum_parts([(outer[0].shape[0], outer), (late_rows, late)], outs, 2)
-    small[...] = decode_small(late, late_rows, small_rows)
-    encode_small(small[...], outs, (outer[0].shape[0] + late_rows) // 4)
+def second_plane_kernel(small_rows, outer_rows, *refs):
+    sources, outs, small = refs[:4], refs[4:8], refs[8]
+    late_end = sources[0].shape[0] - 2 * small_rows
+    groups = [
+        (outer_rows, [source.at[0:outer_rows] for source in sources]),
+        (late_end - outer_rows, [source.at[outer_rows:late_end] for source in sources]),
+    ]
+    sum_parts(groups, outs, 2)
+    small[...] = decode_small(sources, late_end, small_rows)
+    encode_small(small[...], outs, late_end // 4)
 
 
 def second_planes_kernel(small_rows, *refs):
@@ -956,11 +947,12 @@
     small[...] = decode_small(sources, rows, small_rows)
 
 
-def join_kernel(mine, theirs, out):
+def join_kernel(mine, theirs, *outs):
     core = lax.axis_index("dir")
-    rows = mine.shape[0]
-    out[pl.ds(pl.multiple_of(core * rows, rows), rows), :] = mine[...]
-    out[pl.ds(pl.multiple_of((1 - core) * rows, rows), rows), :] = theirs[...]
+    rows = mine.shape[1]
+    for i, out in enumerate(outs):
+        out[part_rows(core, rows), :] = mine[i]
+        out[part_rows(1 - core, rows), :] = theirs[i]
 
 
 def matrix_columns(source, first, out):
@@ -1068,7 +1060,7 @@
         self.tile = None
 
     def run(self, kernel, outs, operands, scratch=(), flops=0, name=None, spare=8, after=(), free_outs=0, alias=None,
-            semaphores=0, cost=0):
+            semaphores=0, cost=0, far=False):
         whole = pl.BlockSpec(memory_space=pltpu.VMEM)
         free = pl.BlockSpec(memory_space=pl.ANY)
         waits = list(after) + ([] if self.tile is None else [self.tile])
@@ -1083,7 +1075,7 @@
         shapes = [jax.ShapeDtypeStruct((8, LANES), f32)]
         shapes += [jax.ShapeDtypeStruct(shape, dtype) for shape, dtype in outs]
         held = sum(jnp.dtype(dtype).itemsize * functools.reduce(lambda a, b: a * b, shape) for shape, dtype in scratch)
-        specs = [free] * skipped + [whole] * inputs
+        specs = [free] * skipped + [pl.BlockSpec(memory_space=pltpu.HBM) if far else whole] * inputs
         aliases = {}
         if alias is not None:
             for operand, out in alias.items():
@@ -1190,19 +1182,24 @@
     gate = 2.0 * rows * width * width
     scan = 1e9
 
-    x0, normed0, inv0, mixed0, drive_own0, keep_own, keep_oth, whole, table, ids = order.run(
+    x0, normed0, inv0 = order.run(
         here(open_kernel, row_devices),
-        [full, full, narrow, full_low, wide, narrow, narrow, ((2, 8, LANES), f32), table_shape, tile],
-        [tokens, segments, norm_gain, norm_bias, rate_params, turn_params, in_own],
-        [columns, tile],
-        flops=one + scan,
+        [full, full, narrow],
+        [tokens],
+        [full_low, columns],
+        far=True,
+        semaphores=1,
         name="open_norm",
-    )
-    drive_oth0, ends_own, ends_oth, payload, table, tiles = order.run(
+        cost=10,
+    )
+    (
+        mixed0, drive_own0, drive_oth0, keep_own, keep_oth, whole, ends_own, ends_oth, payload, table, tiles, ids,
+    ) = order.run(
         here(open_second_kernel, row_devices),
-        [wide, ends, ends, payload_shape, table_shape, ((layers, 16, LANES), f32)],
-        [mixed0, in_oth, rate_oth, turn_oth, table, drive_own0, keep_own, keep_oth, whole, ids],
-        flops=one + scan,
+        [full_low, wide, wide, narrow, narrow, ((2, 8, LANES), f32), ends, ends, payload_shape, table_shape,
+         ((layers, 16, LANES), f32), tile],
+        [normed0, segments, norm_gain, norm_bias, rate_params, turn_params, rate_oth, turn_oth, in_own, in_oth],
+        [tile],
         name="open_scan",
         after=[out_oth],
     )
@@ -1222,19 +1219,18 @@
     )
     gathered = exchanged(payload, row_devices)
     (
-        low_own1, low_oth1, half_out, grad1, combined_grad1, grad_own1, grad_oth1, ends_own, ends_oth, payload,
+        low_own1, low_oth1, out1, grad1, combined_grad1, grad_own1, grad_oth1, ends_own, ends_oth, payload,
         sums_turn, mine, theirs,
     ) = order.run(
         here(turn_kernel, row_devices),
         [wide_low, wide_low, full, full, full, wide, wide, ends, ends, payload_shape, sums_shape, outer_pack, outer_pack],
         [gathered, ends_own, ends_oth, drive_own1, drive_oth1, keep_own, keep_oth, whole, table, tiles,
          ids, out_own, out_oth, x1, normed1, norm_gain, norm_bias, skip_weight, glu_weight, glu_bias, cotangent],
-        [places, tile, full, full, full, full, columns, columns, wide, wide, full_low, full_low, full_low],
+        [places, tile, full, full, full, full, columns, wide, wide, full_low, full_low, full_low],
         flops=4 * one + 2 * gate + 4 * scan,
         name="turn",
     )
     got = swap(theirs)
-    got_half = swap(half_out)
     gathered = exchanged(payload, row_devices)
     early = order.run(
         early_cores_kernel, [((outer_size // 4, LANES), bf16)] * 4, [mine, got], name="early_cores", after=[gathered]
@@ -1261,10 +1257,10 @@
         name="back",
     )
     got_outer = swap(theirs_outer)
-    (payload,) = order.run(relay_kernel, [payload_shape], [payload], name="relay", after=early[1:] + [got_half], cost=RELAY)
+    (payload,) = order.run(relay_kernel, [payload_shape], [payload], name="relay", after=early[1:], cost=RELAY)
     gathered = exchanged(payload, row_devices)
     inner = order.run(
-        early_cores_kernel, [((in_size // 4, LANES), bf16)] * 4, [mine, got], name="inner_cores", after=[gathered]
+        early_cores_kernel, [((in_size // 4, LANES), bf16)] * 4, [mine, got], name="inner_cores", after=[gathered, got_outer]
     )
     inner = sent(inner, 0)
     in_low_own0, in_low_oth0, decay_sums0, mine, theirs = order.run(
@@ -1277,43 +1273,40 @@
     )
     got = swap(theirs)
     quarter = (outer_size + in_size) // 4
+    halves, sums_last = order.run(
+        final_kernel,
+        [((2, rows, width), f32), sums_shape],
+        [in_low_own0, in_low_oth0, in_own, in_oth, grad0, combined_grad0, normed0, inv0, norm_gain, skip_weight, out1],
+        [full, columns, columns],
+        name="final_norm",
+    )
+    quarter = (outer_size + in_size) // 4
+    small_rows = -(-(4 * layers * (width // LANES) + 6 * layers * (states // LANES)) // 16) * 16
+    small_shape = ((small_rows, LANES), f32)
     parts = order.run(
-        first_plane_kernel,
-        [((quarter // 4, LANES), bf16)] * 4 + [((outer_size // 4, LANES), bf16)] * 4,
-        early + inner + [mine_outer, got_outer],
+        here(first_plane_kernel, small_rows),
+        [((quarter // 4, LANES), bf16)] * 4 + [((quarter + 2 * small_rows, LANES), bf16)] * 4 + [small_shape],
+        early + inner + [mine_outer, got_outer, mine, got, sums_turn, sums_back, sums_last, decay_sums0, decay_sums1],
         name="first_plane",
+        cost=RELAY,
     )
     first = sent(parts[:4], 2)
-    outer = sent(parts[4:], 0)
-    half_grad, sums_last = order.run(
-        final_kernel,
-        [full, sums_shape],
-        [in_low_own0, in_low_oth0, in_own, in_oth, grad0, combined_grad0, normed0, inv0, norm_gain, skip_weight],
-        [full, columns],
-        name="final_norm",
-    )
-    small_rows = -(-(4 * layers * (width // LANES) + 6 * layers * (states // LANES)) // 16) * 16
-    *late, _ = order.run(
-        here(late_cores_kernel, small_rows),
-        [((in_size // 4 + 2 * small_rows, LANES), bf16)] * 4 + [((small_rows, LANES), f32)],
-        [mine, got, sums_turn, sums_back, sums_last, decay_sums0, decay_sums1],
-        name="late_cores",
-    )
-    late = sent(late, 0)
-    (share,) = order.run(planes_kernel, [((quarter // 4, LANES), bf16)], first, name="first_planes", after=outer[1:])
+    second = sent(parts[4:8], 0)
+    whole_rows = ((chip_rows, width), f32)
+    block_output, tokens_grad = order.run(
+        join_kernel, [whole_rows, whole_rows], [halves, swap(halves)], name="join"
+    )
+    (share,) = order.run(planes_kernel, [((quarter // 4, LANES), bf16)], first, name="first_planes")
     first = shared(beyond(share), 2)
-    whole_rows = ((chip_rows, width), f32)
-    (block_output,) = order.run(join_kernel, [whole_rows], [half_out, got_half], name="join_out")
     sizes = (outer_size // 16, in_size // 16)
     (full_quarter,) = order.run(
         here(gather_kernel, sizes), [((quarter, LANES), bf16)], first, name="first_gather"
     )
     first = shared(full_quarter, 0)
-    (tokens_grad,) = order.run(join_kernel, [whole_rows], [half_grad, swap(half_grad)], name="join_grad")
     *second, _ = order.run(
-        here(second_plane_kernel, small_rows),
+        here(second_plane_kernel, small_rows, outer_size // 4),
         [((quarter // 4 + 2 * small_rows, LANES), bf16)] * 4 + [((small_rows, LANES), f32)],
-        outer + late,
+        second,
         name="second_plane",
     )
     second = sent(second, 2)

time: 223 us -> 196 us (0.88)
  starting transfers between devices: 57.9 us -> 43.5 us
  Pallas kernels: 52 us -> 39.7 us
  local copies, waits for them, and re-layouts: 7.3 us -> 2.47 us
  waiting for transfers between devices: 49.3 us -> 54 us
    pallas_call x26 -> x24, Pallas kernels: 52 us -> 39.7 us  [run(): pl.pallas_call(body, out_shape=shapes, in_specs=specs, out_specs=[whole]...]
    ppermute x30 -> x27, starting transfers between devices: 38.8 us -> 31.5 us  [across(): return lax.ppermute(value, 'seq', [(i, i ^ bits) for i in range(count)])]
    ppermute x13 -> x12, starting transfers between devices: 19.1 us -> 12 us  [swap(): return lax.ppermute(value, 'dir', [(0, 1), (1, 0)])]
    unnamed x31 -> x25, local copies, waits for them, and re-layouts: 6.7 us -> 1.86 us
    ppermute x13 -> x12, waiting for transfers between devices: 0.03 us -> 2.67 us  [swap(): return lax.ppermute(value, 'dir', [(0, 1), (1, 0)])]
    ppermute x30 -> x27, waiting for transfers between devices: 49.3 us -> 51.4 us  [across(): return lax.ppermute(value, 'seq', [(i, i ^ bits) for i in range(count)])]
  transfers between devices with their start and end apart: 43 -> 39, of which waited for: 11 -> 14; matrix products, arithmetic and copies ran while one was open for 1% -> 1% of each run, Pallas kernels for 14% -> 11%
where the time goes in v3:
time: 196 us
  blocking collectives  55.4 us (28%)
  waiting for transfers between devices  54 us (28%)
  starting transfers between devices  43.5 us (22%)
  Pallas kernels  39.7 us (20%)
  local copies, waits for them, and re-layouts  2.47 us (1%)
    all_to_all x4, blocking collectives, exchanged(): lax.all_to_all(payload, ('seq', 'dir'), 0, 0, tiled=True, axis_index_grou...  55.4 us
    ppermute x27, waiting for transfers between devices, across(): return lax.ppermute(value, 'seq', [(i, i ^ bits) for i in range(count)])  51.4 us
    pallas_call x24, Pallas kernels, run(): pl.pallas_call(body, out_shape=shapes, in_specs=specs, out_specs=[whole]...  39.7 us
    ppermute x27, starting transfers between devices, across(): return lax.ppermute(value, 'seq', [(i, i ^ bits) for i in range(count)])  31.5 us
    ppermute x12, starting transfers between devices, swap(): return lax.ppermute(value, 'dir', [(0, 1), (1, 0)])  12 us
  transfers between devices with their start and end apart: 39, of which 14 were waited for; matrix products, arithmetic and copies ran while one was open for 1% of the time, Pallas kernels for 11%

profile of v3, /device:TPU:1, one launch (start us, length us, event | category | flops | bytes accessed | tf_op | source)
XLA Modules:
  0.0 196.1 jit_solution(436821774351215593)
XLA Ops:
  0.8 0.5 collective-permute-start.3
  1.4 0.4 collective-permute-start.2
  1.8 1.2 copy-done.11
  3.0 1.0 open_norm.1
  4.0 2.6 %collective-permute-done.1.refs_8_ = f32[2,1,384]{2,1,0:T(1,128)S(1)} collective-permute-done((f32[2,1,384]{2,1,0:T(1,128)}, f32[2,1,384]{2,1,0:T(1,128)S(1)}, u32[]{:S(2)}, u32[]{:S(2)}) %collective-permute-start.1) | collective-permute-done | bytes 3104 | tf_op jit(solution)/shard_map/ppermute | solution.py:1101
  6.8 1.8 open_scan.1
  8.5 17.2 %all_to_all.20.refs_1_ = f32[32,16,128]{2,1,0:T(8,128)S(1)} all-to-all(f32[32,16,128]{2,1,0:T(8,128)S(1)} %get-tuple-element.143), channel_id=1, replica_groups=mesh['dir'=2,'seq'=16] {'seq','dir'}, dimensions={0} | all-to-all | bytes 524288 | tf_op jit(solution)/shard_map/all_to_all | solution.py:1123
  25.7 4.3 %mid.1 = (f32[8,128]{1,0:T(8,128)S(1)}, bf16[512,768]{1,0:T(8,128)(2,1)S(1)}, bf16[512,768]{1,0:T(8,128)(2,1)S(1)}, f32[512,512]{1,0:T(8,128)S(1)}, f32[512,512]...) custom-call(f32[8,128]{1,0:T(8,128)S(1)} %get-tuple-element.142.refs, ...), custom_call_target="tpu_custom_call" | custom-call | flops 1 | bytes 1 | tf_op jit(solution)/shard_map/mid/pallas_call | solution.py:1085
  30.0 12.8 %all_to_all.21.refs_1_ = f32[32,16,128]{2,1,0:T(8,128)S(1)} all-to-all(f32[32,16,128]{2,1,0:T(8,128)S(1)} %get-tuple-element.156), channel_id=1, replica_groups=mesh['dir'=2,'seq'=16] {'seq','dir'}, dimensions={0} | all-to-all | bytes 524288 | tf_op jit(solution)/shard_map/all_to_all | solution.py:1123
  42.9 6.6 %turn.1 = (f32[8,128]{1,0:T(8,128)S(1)}, bf16[512,768]{1,0:T(8,128)(2,1)S(1)}, bf16[512,768]{1,0:T(8,128)(2,1)S(1)}, f32[512,512]{1,0:T(8,128)S(1)}, f32[512,512...) custom-call(f32[8,128]{1,0:T(8,128)S(1)} %get-tuple-element.155.refs, ...), custom_call_target="tpu_custom_call" | custom-call | flops 1 | bytes 1 | tf_op jit(solution)/shard_map/turn/pallas_call | solution.py:1085
  49.4 0.7 collective-permute-start.4
  50.1 12.3 %all_to_all.22.refs_0_.refs_1_ = f32[32,16,128]{2,1,0:T(8,128)S(1)} all-to-all(f32[32,16,128]{2,1,0:T(8,128)S(1)} %get-tuple-element.163), channel_id=1, replica_groups=mesh['dir'=2,'seq'=16] {'seq','dir'}, dimensions={0} | all-to-all | bytes 524288 | tf_op jit(solution)/shard_map/all_to_all | solution.py:1123
  62.4 0.3 early_cores.1
  62.7 0.7 collective-permute-start.5
  63.4 0.4 collective-permute-start.6
  63.8 1.6 collective-permute-start.7
  65.4 2.8 %scan_one.1 = (f32[8,128]{1,0:T(8,128)S(1)}, bf16[512,768]{1,0:T(8,128)(2,1)S(1)}, bf16[512,768]{1,0:T(8,128)(2,1)S(1)}, f32[8,384]{1,0:T(8,128)S(1)}, bf16[3072...) custom-call(f32[8,128]{1,0:T(8,128)S(1)} %get-tuple-element.170.refs_0_, ...), custom_call_target="tpu_custom_call" | custom-call | flops 1 | bytes 1 | tf_op jit(solution)/shard_map/scan_one/pallas_call | solution.py:1085
  68.3 1.5 collective-permute-start.9
  69.8 5.0 %back.1 = (f32[8,128]{1,0:T(8,128)S(1)}, f32[512,512]{1,0:T(8,128)S(1)}, f32[512,512]{1,0:T(8,128)S(1)}, f32[512,768]{1,0:T(8,128)S(1)}, f32[512,768]{1,0:T(8,12...) custom-call(f32[8,128]{1,0:T(8,128)S(1)} %get-tuple-element.178.refs, ...), custom_call_target="tpu_custom_call" | custom-call | flops 1 | bytes 1 | tf_op jit(solution)/shard_map/back/pallas_call | solution.py:1085
  74.9 1.8 collective-permute-done.6.refs_1_.refs_3_
  76.7 13.1 %all_to_all.23.refs_0_.refs_1_ = f32[32,16,128]{2,1,0:T(8,128)S(1)} all-to-all(f32[32,16,128]{2,1,0:T(8,128)S(1)} %get-tuple-element.192), channel_id=1, replica_groups=mesh['dir'=2,'seq'=16] {'seq','dir'}, dimensions={0} | all-to-all | bytes 524288 | tf_op jit(solution)/shard_map/all_to_all | solution.py:1123
  90.0 2.9 %scan_zero.1 = (f32[8,128]{1,0:T(8,128)S(1)}, bf16[512,768]{1,0:T(8,128)(2,1)S(1)}, bf16[512,768]{1,0:T(8,128)(2,1)S(1)}, f32[8,384]{1,0:T(8,128)S(1)}, bf16[307...) custom-call(f32[8,128]{1,0:T(8,128)S(1)} %get-tuple-element.197.refs_0_, ...), custom_call_target="tpu_custom_call" | custom-call | flops 1 | bytes 1 | tf_op jit(solution)/shard_map/scan_zero/pallas_call | solution.py:1085
  93.0 0.7 collective-permute-start.13
  93.7 1.1 collective-permute-start.11
  94.8 1.5 collective-permute-start.12
  96.3 3.4 %final_norm.1 = (f32[8,128]{1,0:T(8,128)S(1)}, f32[2,512,512]{2,1,0:T(8,128)S(1)}, f32[8,512]{1,0:T(8,128)S(1)}) custom-call(f32[8,128]{1,0:T(8,128)S(1)} %get-tuple-element.203.refs_0_, bf16[512,768]{1,0:T(8,128)(2,1)S(1)} %get-tuple-element.204.refs_1_, bf16[512,768]{1,0:T(8,128)(2,1)S(1)} %get-tuple-element.205.refs_2_, ...), custom_call_target="tpu_custom_call" | custom-call | flops 1 | bytes 1 | tf_op jit(solution)/shard_map/final_norm/pallas_call | solution.py:1085
  99.7 1.0 collective-permute-start.14
  100.7 4.0 %collective-permute-done.12.refs_8_ = bf16[768,128]{1,0:T(8,128)(2,1)S(1)} collective-permute-done((bf16[768,128]{1,0:T(8,128)(2,1)S(1)}, bf16[768,128]{1,0:T(8,128)(2,1)S(1)}, u32[]{:S(2)}, u32[]{:S(2)}) %collective-permute-start.12) | collective-permute-done | bytes 196640 | tf_op jit(solution)/shard_map/ppermute | solution.py:1106
  104.7 1.5 first_plane.1
  106.2 0.4 collective-permute-start.15
  106.5 1.1 collective-permute-start.21
  107.7 1.5 collective-permute-start.23
  109.2 0.6 collective-permute-done.15.refs_2_
  109.8 0.2 collective-permute-start.16
  110.1 2.3 %collective-permute-start.17 = (bf16[448,128]{1,0:T(8,128)(2,1)S(1)}, bf16[448,128]{1,0:T(8,128)(2,1)S(1)}, u32[]{:S(2)}, u32[]{:S(2)}) collective-permute-start(bf16[448,128]{1,0:T(8,128)(2,1)S(1)} %get-tuple-element.232), channel_id=1, source_target_pairs={{0,12},{1,13},{2,14},{3,15},{4,8},{5,9},{6,10},{7,11},{8,4},{9,5},... | collective-permute-start | bytes 344072 | tf_op jit(solution)/shard_map/ppermute | solution.py:1106
  112.4 2.3 %join.1 = (f32[8,128]{1,0:T(8,128)S(1)}, f32[1024,512]{1,0:T(8,128)}, f32[1024,512]{1,0:T(8,128)}) custom-call(f32[8,128]{1,0:T(8,128)S(1)} %get-tuple-element.224.refs_0_, f32[2,512,512]{2,1,0:T(8,128)S(1)} %get-tuple-element.225.refs_1_, f32[2,512,512]{2,1,0:T(8,128)S(1)} %collective-permute-done.14.refs_2_), custom_call_target="tpu_custom_call" | custom-call | flops 1 | bytes 1 | tf_op jit(solution)/shard_map/join/pallas_call | solution.py:1085
  114.7 5.8 %collective-permute-done.16.refs_3_ = bf16[448,128]{1,0:T(8,128)(2,1)S(1)} collective-permute-done((bf16[448,128]{1,0:T(8,128)(2,1)S(1)}, bf16[448,128]{1,0:T(8,128)(2,1)S(1)}, u32[]{:S(2)}, u32[]{:S(2)}) %collective-permute-start.16) | collective-permute-done | bytes 114720 | tf_op jit(solution)/shard_map/ppermute | solution.py:1106
  120.6 3.9 %collective-permute-start.19 = (bf16[448,128]{1,0:T(8,128)(2,1)S(1)}, bf16[448,128]{1,0:T(8,128)(2,1)S(1)}, u32[]{:S(2)}, u32[]{:S(2)}) collective-permute-start(bf16[448,128]{1,0:T(8,128)(2,1)S(1)} %get-tuple-element.234.refs_1_), channel_id=1, source_target_pairs={{0,8},{1,9},{2,10},{3,11},{4,12},{5,13},{6,14},{7,15},{8,0},{9,1},... | collective-permute-start | bytes 344072 | tf_op jit(solution)/shard_map/ppermute | solution.py:1106
  124.6 1.6 collective-permute-done.20.refs_4_
  126.1 6.4 %collective-permute-start.18 = (bf16[448,128]{1,0:T(8,128)(2,1)S(1)}, bf16[448,128]{1,0:T(8,128)(2,1)S(1)}, u32[]{:S(2)}, u32[]{:S(2)}) collective-permute-start(bf16[448,128]{1,0:T(8,128)(2,1)S(1)} %get-tuple-element.234.refs_1_), channel_id=1, source_target_pairs={{0,4},{1,5},{2,6},{3,7},{4,0},{5,1},{6,2},{7,3},{8,12},{9,13},{10,... | collective-permute-start | bytes 344072 | tf_op jit(solution)/shard_map/ppermute | solution.py:1106
  132.6 2.2 %collective-permute-done.19.refs_3_ = bf16[448,128]{1,0:T(8,128)(2,1)S(1)} collective-permute-done((bf16[448,128]{1,0:T(8,128)(2,1)S(1)}, bf16[448,128]{1,0:T(8,128)(2,1)S(1)}, u32[]{:S(2)}, u32[]{:S(2)}) %collective-permute-start.19) | collective-permute-done | bytes 114720 | tf_op jit(solution)/shard_map/ppermute | solution.py:1106
  134.7 2.6 %collective-permute-done.18.refs_2_ = bf16[448,128]{1,0:T(8,128)(2,1)S(1)} collective-permute-done((bf16[448,128]{1,0:T(8,128)(2,1)S(1)}, bf16[448,128]{1,0:T(8,128)(2,1)S(1)}, u32[]{:S(2)}, u32[]{:S(2)}) %collective-permute-start.18) | collective-permute-done | bytes 114720 | tf_op jit(solution)/shard_map/ppermute | solution.py:1106
  137.5 1.3 collective-permute-start.28
  138.8 1.3 collective-permute-start.27
  140.1 0.9 second_plane.1
  141.0 7.2 %collective-permute-done.24.refs_2_ = bf16[608,128]{1,0:T(8,128)(2,1)S(1)} collective-permute-done((bf16[608,128]{1,0:T(8,128)(2,1)S(1)}, bf16[608,128]{1,0:T(8,128)(2,1)S(1)}, u32[]{:S(2)}, u32[]{:S(2)}) %collective-permute-start.24) | collective-permute-done | bytes 155680 | tf_op jit(solution)/shard_map/ppermute | solution.py:1106
  148.2 6.0 %collective-permute-done.26.refs_4_ = bf16[608,128]{1,0:T(8,128)(2,1)S(1)} collective-permute-done((bf16[608,128]{1,0:T(8,128)(2,1)S(1)}, bf16[608,128]{1,0:T(8,128)(2,1)S(1)}, u32[]{:S(2)}, u32[]{:S(2)}) %collective-permute-start.26) | collective-permute-done | bytes 155680 | tf_op jit(solution)/shard_map/ppermute | solution.py:1106
  154.4 4.4 %collective-permute-start.32 = (bf16[448,128]{1,0:T(8,128)(2,1)S(1)}, bf16[448,128]{1,0:T(8,128)(2,1)S(1)}, u32[]{:S(2)}, u32[]{:S(2)}) collective-permute-start(bf16[448,128]{1,0:T(8,128)(2,1)S(1)} %get-tuple-element.253.refs_1_), channel_id=1, source_target_pairs={{0,8},{1,9},{2,10},{3,11},{4,12},{5,13},{6,14},{7,15},{8,0},{9,1},... | collective-permute-start | bytes 344072 | tf_op jit(solution)/shard_map/ppermute | solution.py:1106
  158.8 0.2 collective-permute-done.28.refs_3_
  159.0 2.9 %collective-permute-start.30 = (f32[80,128]{1,0:T(8,128)S(1)}, f32[80,128]{1,0:T(8,128)S(1)}, u32[]{:S(2)}, u32[]{:S(2)}) collective-permute-start(f32[80,128]{1,0:T(8,128)S(1)} %get-tuple-element.249.refs_1_), channel_id=1, source_target_pairs={{0,16},{16,0},{1,17},{17,1},{2,18},{18,2},{3,19},{19,3},{4,20},{20... | collective-permute-start | bytes 122888 | tf_op jit(solution)/shard_map/ppermute | solution.py:1101
  162.0 2.0 %unpack_one.1 = (f32[8,128]{1,0:T(8,128)S(1)}, f32[2,1,768,512]{3,2,1,0:T(8,128)}, f32[2,1,512,768]{3,2,1,0:T(8,128)}) custom-call(f32[8,128]{1,0:T(8,128)S(1)} %get-tuple-element.247.refs_0_, bf16[1792,128]{1,0:T(8,128)(2,1)S(1)} %get-tuple-element.246.refs_1_, bf16[1792,128]{1,0:T(8,128)(2,1)S(1)} %collective-permute-done.27.refs_2_, ...), custom_call_target="tpu_custom_call" | custom-call | flops 1 | bytes 1 | tf_op jit(solution)/shard_map/unpack_one/pallas_call | solution.py:1085
  164.0 0.6 small_out.1
  164.7 2.1 %collective-permute-done.32.refs_3_ = bf16[448,128]{1,0:T(8,128)(2,1)S(1)} collective-permute-done((bf16[448,128]{1,0:T(8,128)(2,1)S(1)}, bf16[448,128]{1,0:T(8,128)(2,1)S(1)}, u32[]{:S(2)}, u32[]{:S(2)}) %collective-permute-start.32) | collective-permute-done | bytes 114720 | tf_op jit(solution)/shard_map/ppermute | solution.py:1106
  166.8 0.7 collective-permute-start.36
  167.5 1.8 collective-permute-start.35
  169.3 0.5 collective-permute-start.34
  169.8 2.9 %collective-permute-start.37 = (bf16[1024,128]{1,0:T(8,128)(2,1)S(1)}, bf16[1024,128]{1,0:T(8,128)(2,1)S(1)}, u32[]{:S(2)}, u32[]{:S(2)}) collective-permute-start(bf16[1024,128]{1,0:T(8,128)(2,1)S(1)} %get-tuple-element.265.refs_1_), channel_id=1, source_target_pairs={{0,16},{16,0},{1,17},{17,1},{2,18},{18,2},{3,19},{19,3},{4,20},{20... | collective-permute-start | bytes 786440 | tf_op jit(solution)/shard_map/ppermute | solution.py:1101
  172.7 4.8 %collective-permute-done.36.refs_4_ = bf16[1792,128]{1,0:T(8,128)(2,1)S(1)} collective-permute-done((bf16[1792,128]{1,0:T(8,128)(2,1)S(1)}, bf16[1792,128]{1,0:T(8,128)(2,1)S(1)}, u32[]{:S(2)}, u32[]{:S(2)}) %collective-permute-start.36) | collective-permute-done | bytes 458784 | tf_op jit(solution)/shard_map/ppermute | solution.py:1106
  177.5 12.5 %collective-permute-done.35.refs_3_ = bf16[1792,128]{1,0:T(8,128)(2,1)S(1)} collective-permute-done((bf16[1792,128]{1,0:T(8,128)(2,1)S(1)}, bf16[1792,128]{1,0:T(8,128)(2,1)S(1)}, u32[]{:S(2)}, u32[]{:S(2)}) %collective-permute-start.35) | collective-permute-done | bytes 458784 | tf_op jit(solution)/shard_map/ppermute | solution.py:1106
  190.1 1.1 collective-permute-start.38
  191.3 0.6 copy.25
  191.9 0.6 reshape.33
  192.5 2.0 %unpack_zero.1 = (f32[8,128]{1,0:T(8,128)S(1)}, f32[2,1,768,512]{3,2,1,0:T(8,128)}, f32[2,1,512,768]{3,2,1,0:T(8,128)}) custom-call(f32[8,128]{1,0:T(8,128)S(1)} %get-tuple-element.256.refs_0_, bf16[1792,128]{1,0:T(8,128)(2,1)S(1)} %get-tuple-element.255.refs_1_, ...), custom_call_target="tpu_custom_call", output_to_operand_aliasing={{1}: (5, {}), {2}: (6, {})} | custom-call | flops 1 | bytes 1 | tf_op jit(solution)/shard_map/unpack_zero/pallas_call | solution.py:1085
  194.5 1.6 unpack_gate.1
  (68 shorter events, 1.4 us)
Async XLA Ops:
  0.6 6.0 %copy-start = (bf16[2,1,512,768]{3,2,1,0:T(8,128)(2,1)S(1)}, bf16[2,1,512,768]{3,2,1,0:T(8,128)(2,1)}, u32[]{:S(2)}) copy-start(bf16[2,1,512,768]{3,2,1,0:T(8,128)(2,1)} %refs_3_.1) | copy-start | bytes 4718596
  0.7 6.0 %copy-start.10 = (f32[2,1,384]{2,1,0:T(1,128)S(1)}, f32[2,1,384]{2,1,0:T(1,128)}, u32[]{:S(2)}) copy-start(f32[2,1,384]{2,1,0:T(1,128)} %refs_6_.1) | copy-start | bytes 9220
  0.7 6.0 %copy-start.8 = (f32[2,1,2,384]{3,2,1,0:T(2,128)S(1)}, f32[2,1,2,384]{3,2,1,0:T(2,128)}, u32[]{:S(2)}) copy-start(f32[2,1,2,384]{3,2,1,0:T(2,128)} %refs_7_.1) | copy-start | bytes 18436
  0.7 6.0 %copy-start.4 = (f32[2,512]{1,0:T(2,128)S(1)}, f32[2,512]{1,0:T(2,128)}, u32[]{:S(2)}) copy-start(f32[2,512]{1,0:T(2,128)} %refs_9_.3) | copy-start | bytes 12292
  0.7 6.0 %copy-start.6 = (f32[2,512]{1,0:T(2,128)S(1)}, f32[2,512]{1,0:T(2,128)}, u32[]{:S(2)}) copy-start(f32[2,512]{1,0:T(2,128)} %refs_18_.5) | copy-start | bytes 12292
  0.7 6.0 %copy-start.9 = (s32[1024]{0:T(1024)S(1)}, s32[1024]{0:T(1024)}, u32[]{:S(2)}) copy-start(s32[1024]{0:T(1024)} %param.13) | copy-start | bytes 12292
  0.7 6.0 %collective-permute-start = (bf16[2,1,768,512]{3,2,1,0:T(8,128)(2,1)}, bf16[2,1,768,512]{3,2,1,0:T(8,128)(2,1)S(1)}, u32[]{:S(2)}, u32[]{:S(2)}) collective-permute-start(bf16[2,1,768,512]{3,2,1,0:T(8,128)(2,1)} %refs_11_.1), channel_id=1, source_target_pairs={{0,16},{16,0},{1,17},{17,1},{2,18},{18,2},{3,19},{19,3},{4,20},{20... | collective-permute-start | bytes 4718600 | tf_op jit(solution)/shard_map/ppermute | solution.py:1101
  0.8 5.8 %collective-permute-start.3 = (bf16[2,1,512,768]{3,2,1,0:T(8,128)(2,1)}, bf16[2,1,512,768]{3,2,1,0:T(8,128)(2,1)S(1)}, u32[]{:S(2)}, u32[]{:S(2)}) collective-permute-start(bf16[2,1,512,768]{3,2,1,0:T(8,128)(2,1)} %refs_3_.1), channel_id=1, source_target_pairs={{0,16},{16,0},{1,17},{17,1},{2,18},{18,2},{3,19},{19,3},{4,20},{20... | collective-permute-start | bytes 4718600 | tf_op jit(solution)/shard_map/ppermute | solution.py:1101
  1.3 5.4 %collective-permute-start.1 = (f32[2,1,384]{2,1,0:T(1,128)}, f32[2,1,384]{2,1,0:T(1,128)S(1)}, u32[]{:S(2)}, u32[]{:S(2)}) collective-permute-start(f32[2,1,384]{2,1,0:T(1,128)} %refs_6_.1), channel_id=1, source_target_pairs={{0,16},{16,0},{1,17},{17,1},{2,18},{18,2},{3,19},{19,3},{4,20},{20... | collective-permute-start | bytes 9224 | tf_op jit(solution)/shard_map/ppermute | solution.py:1101
  1.4 5.3 %collective-permute-start.2 = (f32[2,1,2,384]{3,2,1,0:T(2,128)}, f32[2,1,2,384]{3,2,1,0:T(2,128)S(1)}, u32[]{:S(2)}, u32[]{:S(2)}) collective-permute-start(f32[2,1,2,384]{3,2,1,0:T(2,128)} %refs_7_.1), channel_id=1, source_target_pairs={{0,16},{16,0},{1,17},{17,1},{2,18},{18,2},{3,19},{19,3},{4,20},{20... | collective-permute-start | bytes 18440 | tf_op jit(solution)/shard_map/ppermute | solution.py:1101
  1.8 1.2 copy-start.11
  6.7 19.0 %copy-start.1 = (bf16[2,1,768,512]{3,2,1,0:T(8,128)(2,1)S(1)}, bf16[2,1,768,512]{3,2,1,0:T(8,128)(2,1)}, u32[]{:S(2)}) copy-start(bf16[2,1,768,512]{3,2,1,0:T(8,128)(2,1)} %refs_11_.1) | copy-start | bytes 4718596
  6.7 19.0 %copy-start.2 = (bf16[2,512,512]{2,1,0:T(8,128)(2,1)S(1)}, bf16[2,512,512]{2,1,0:T(8,128)(2,1)}, u32[]{:S(2)}) copy-start(bf16[2,512,512]{2,1,0:T(8,128)(2,1)} %refs_20_.5) | copy-start | bytes 3145732
  6.7 19.0 %copy-start.5 = (f32[2,512]{1,0:T(2,128)S(1)}, f32[2,512]{1,0:T(2,128)}, u32[]{:S(2)}) copy-start(f32[2,512]{1,0:T(2,128)} %refs_10_.3) | copy-start | bytes 12292
  6.8 19.0 %copy-start.7 = (f32[2,512]{1,0:T(2,128)S(1)}, f32[2,512]{1,0:T(2,128)}, u32[]{:S(2)}) copy-start(f32[2,512]{1,0:T(2,128)} %refs_20_.4) | copy-start | bytes 12292
  25.7 17.2 %copy-start.3 = (f32[1024,512]{1,0:T(8,128)S(1)}, f32[1024,512]{1,0:T(8,128)}, u32[]{:S(2)}) copy-start(f32[1024,512]{1,0:T(8,128)} %refs_21_.3) | copy-start | bytes 6291460
  49.4 13.0 %collective-permute-start.4 = (bf16[4096,128]{1,0:T(8,128)(2,1)S(1)}, bf16[4096,128]{1,0:T(8,128)(2,1)S(1)}, u32[]{:S(2)}, u32[]{:S(2)}) collective-permute-start(bf16[4096,128]{1,0:T(8,128)(2,1)S(1)} %get-tuple-element.166), channel_id=1, source_target_pairs={{0,16},{16,0},{1,17},{17,1},{2,18},{18,2},{3,19},{19,3},{4,20},{20... | collective-permute-start | bytes 3145736 | tf_op jit(solution)/shard_map/ppermute | solution.py:1101
  62.7 12.2 %collective-permute-start.5 = (bf16[1024,128]{1,0:T(8,128)(2,1)S(1)}, bf16[1024,128]{1,0:T(8,128)(2,1)S(1)}, u32[]{:S(2)}, u32[]{:S(2)}) collective-permute-start(bf16[1024,128]{1,0:T(8,128)(2,1)S(1)} %get-tuple-element.167), channel_id=1, source_target_pairs={{0,1},{1,0},{2,3},{3,2},{4,5},{5,4},{6,7},{7,6},{8,9},{9,8},{10,11... | collective-permute-start | bytes 786440 | tf_op jit(solution)/shard_map/ppermute | solution.py:1106
  63.4 13.3 %collective-permute-start.6 = (bf16[1024,128]{1,0:T(8,128)(2,1)S(1)}, bf16[1024,128]{1,0:T(8,128)(2,1)S(1)}, u32[]{:S(2)}, u32[]{:S(2)}) collective-permute-start(bf16[1024,128]{1,0:T(8,128)(2,1)S(1)} %get-tuple-element.168), channel_id=1, source_target_pairs={{0,2},{1,3},{2,0},{3,1},{4,6},{5,7},{6,4},{7,5},{8,10},{9,11},{10,... | collective-permute-start | bytes 786440 | tf_op jit(solution)/shard_map/ppermute | solution.py:1106
  63.8 12.9 %collective-permute-start.7 = (bf16[1024,128]{1,0:T(8,128)(2,1)S(1)}, bf16[1024,128]{1,0:T(8,128)(2,1)S(1)}, u32[]{:S(2)}, u32[]{:S(2)}) collective-permute-start(bf16[1024,128]{1,0:T(8,128)(2,1)S(1)} %get-tuple-element.169), channel_id=1, source_target_pairs={{0,3},{1,2},{2,1},{3,0},{4,7},{5,6},{6,5},{7,4},{8,11},{9,10},{10,... | collective-permute-start | bytes 786440 | tf_op jit(solution)/shard_map/ppermute | solution.py:1106
  68.3 21.6 %collective-permute-start.9 = (bf16[3072,128]{1,0:T(8,128)(2,1)S(1)}, bf16[3072,128]{1,0:T(8,128)(2,1)S(1)}, u32[]{:S(2)}, u32[]{:S(2)}) collective-permute-start(bf16[3072,128]{1,0:T(8,128)(2,1)S(1)} %get-tuple-element.196), channel_id=1, source_target_pairs={{0,16},{16,0},{1,17},{17,1},{2,18},{18,2},{3,19},{19,3},{4,20},{20... | collective-permute-start | bytes 2359304 | tf_op jit(solution)/shard_map/ppermute | solution.py:1101
  74.8 15.0 %collective-permute-start.8 = (bf16[4096,128]{1,0:T(8,128)(2,1)S(1)}, bf16[4096,128]{1,0:T(8,128)(2,1)S(1)}, u32[]{:S(2)}, u32[]{:S(2)}) collective-permute-start(bf16[4096,128]{1,0:T(8,128)(2,1)S(1)} %get-tuple-element.193), channel_id=1, source_target_pairs={{0,16},{16,0},{1,17},{17,1},{2,18},{18,2},{3,19},{19,3},{4,20},{20... | collective-permute-start | bytes 3145736 | tf_op jit(solution)/shard_map/ppermute | solution.py:1101
  93.0 11.7 %collective-permute-start.13 = (bf16[3072,128]{1,0:T(8,128)(2,1)S(1)}, bf16[3072,128]{1,0:T(8,128)(2,1)S(1)}, u32[]{:S(2)}, u32[]{:S(2)}) collective-permute-start(bf16[3072,128]{1,0:T(8,128)(2,1)S(1)} %get-tuple-element.218), channel_id=1, source_target_pairs={{0,16},{16,0},{1,17},{17,1},{2,18},{18,2},{3,19},{19,3},{4,20},{20... | collective-permute-start | bytes 2359304 | tf_op jit(solution)/shard_map/ppermute | solution.py:1101
  93.6 7.1 %collective-permute-start.10 = (bf16[768,128]{1,0:T(8,128)(2,1)S(1)}, bf16[768,128]{1,0:T(8,128)(2,1)S(1)}, u32[]{:S(2)}, u32[]{:S(2)}) collective-permute-start(bf16[768,128]{1,0:T(8,128)(2,1)S(1)} %get-tuple-element.213), channel_id=1, source_target_pairs={{0,1},{1,0},{2,3},{3,2},{4,5},{5,4},{6,7},{7,6},{8,9},{9,8},{10,11... | collective-permute-start | bytes 589832 | tf_op jit(solution)/shard_map/ppermute | solution.py:1106
  93.7 6.9 %collective-permute-start.11 = (bf16[768,128]{1,0:T(8,128)(2,1)S(1)}, bf16[768,128]{1,0:T(8,128)(2,1)S(1)}, u32[]{:S(2)}, u32[]{:S(2)}) collective-permute-start(bf16[768,128]{1,0:T(8,128)(2,1)S(1)} %get-tuple-element.214), channel_id=1, source_target_pairs={{0,2},{1,3},{2,0},{3,1},{4,6},{5,7},{6,4},{7,5},{8,10},{9,11},{10,... | collective-permute-start | bytes 589832 | tf_op jit(solution)/shard_map/ppermute | solution.py:1106
  94.8 9.8 %collective-permute-start.12 = (bf16[768,128]{1,0:T(8,128)(2,1)S(1)}, bf16[768,128]{1,0:T(8,128)(2,1)S(1)}, u32[]{:S(2)}, u32[]{:S(2)}) collective-permute-start(bf16[768,128]{1,0:T(8,128)(2,1)S(1)} %get-tuple-element.215), channel_id=1, source_target_pairs={{0,3},{1,2},{2,1},{3,0},{4,7},{5,6},{6,5},{7,4},{8,11},{9,10},{10,... | collective-permute-start | bytes 589832 | tf_op jit(solution)/shard_map/ppermute | solution.py:1106
  99.7 10.3 %collective-permute-start.14 = (f32[2,512,512]{2,1,0:T(8,128)S(1)}, f32[2,512,512]{2,1,0:T(8,128)S(1)}, u32[]{:S(2)}, u32[]{:S(2)}) collective-permute-start(f32[2,512,512]{2,1,0:T(8,128)S(1)} %get-tuple-element.225.refs_1_), channel_id=1, source_target_pairs={{0,16},{16,0},{1,17},{17,1},{2,18},{18,2},{3,19},{19,3},{4,20},{20... | collective-permute-start | bytes 6291464 | tf_op jit(solution)/shard_map/ppermute | solution.py:1101
  106.2 3.6 %collective-permute-start.15 = (bf16[448,128]{1,0:T(8,128)(2,1)S(1)}, bf16[448,128]{1,0:T(8,128)(2,1)S(1)}, u32[]{:S(2)}, u32[]{:S(2)}) collective-permute-start(bf16[448,128]{1,0:T(8,128)(2,1)S(1)} %get-tuple-element.230), channel_id=1, source_target_pairs={{0,4},{1,5},{2,6},{3,7},{4,0},{5,1},{6,2},{7,3},{8,12},{9,13},{10,... | collective-permute-start | bytes 344072 | tf_op jit(solution)/shard_map/ppermute | solution.py:1106
  106.5 32.2 %collective-permute-start.21 = (bf16[1952,128]{1,0:T(8,128)(2,1)S(1)}, bf16[1952,128]{1,0:T(8,128)(2,1)S(1)}, u32[]{:S(2)}, u32[]{:S(2)}) collective-permute-start(bf16[1952,128]{1,0:T(8,128)(2,1)S(1)} %get-tuple-element.237), channel_id=1, source_target_pairs={{0,1},{1,0},{2,3},{3,2},{4,5},{5,4},{6,7},{7,6},{8,9},{9,8},{10,11... | collective-permute-start | bytes 1499144 | tf_op jit(solution)/shard_map/ppermute | solution.py:1106
  107.6 32.5 %collective-permute-start.22 = (bf16[1952,128]{1,0:T(8,128)(2,1)S(1)}, bf16[1952,128]{1,0:T(8,128)(2,1)S(1)}, u32[]{:S(2)}, u32[]{:S(2)}) collective-permute-start(bf16[1952,128]{1,0:T(8,128)(2,1)S(1)} %get-tuple-element.238), channel_id=1, source_target_pairs={{0,2},{1,3},{2,0},{3,1},{4,6},{5,7},{6,4},{7,5},{8,10},{9,11},{10,... | collective-permute-start | bytes 1499144 | tf_op jit(solution)/shard_map/ppermute | solution.py:1106
  107.7 32.4 %collective-permute-start.23 = (bf16[1952,128]{1,0:T(8,128)(2,1)S(1)}, bf16[1952,128]{1,0:T(8,128)(2,1)S(1)}, u32[]{:S(2)}, u32[]{:S(2)}) collective-permute-start(bf16[1952,128]{1,0:T(8,128)(2,1)S(1)} %get-tuple-element.239), channel_id=1, source_target_pairs={{0,3},{1,2},{2,1},{3,0},{4,7},{5,6},{6,5},{7,4},{8,11},{9,10},{10,... | collective-permute-start | bytes 1499144 | tf_op jit(solution)/shard_map/ppermute | solution.py:1106
  109.8 10.7 %collective-permute-start.16 = (bf16[448,128]{1,0:T(8,128)(2,1)S(1)}, bf16[448,128]{1,0:T(8,128)(2,1)S(1)}, u32[]{:S(2)}, u32[]{:S(2)}) collective-permute-start(bf16[448,128]{1,0:T(8,128)(2,1)S(1)} %get-tuple-element.231), channel_id=1, source_target_pairs={{0,8},{1,9},{2,10},{3,11},{4,12},{5,13},{6,14},{7,15},{8,0},{9,1},... | collective-permute-start | bytes 344072 | tf_op jit(solution)/shard_map/ppermute | solution.py:1106
  110.1 10.4 %collective-permute-start.17 = (bf16[448,128]{1,0:T(8,128)(2,1)S(1)}, bf16[448,128]{1,0:T(8,128)(2,1)S(1)}, u32[]{:S(2)}, u32[]{:S(2)}) collective-permute-start(bf16[448,128]{1,0:T(8,128)(2,1)S(1)} %get-tuple-element.232), channel_id=1, source_target_pairs={{0,12},{1,13},{2,14},{3,15},{4,8},{5,9},{6,10},{7,11},{8,4},{9,5},... | collective-permute-start | bytes 344072 | tf_op jit(solution)/shard_map/ppermute | solution.py:1106
  120.6 5.6 %collective-permute-start.20 = (bf16[448,128]{1,0:T(8,128)(2,1)S(1)}, bf16[448,128]{1,0:T(8,128)(2,1)S(1)}, u32[]{:S(2)}, u32[]{:S(2)}) collective-permute-start(bf16[448,128]{1,0:T(8,128)(2,1)S(1)} %get-tuple-element.234.refs_1_), channel_id=1, source_target_pairs={{0,12},{1,13},{2,14},{3,15},{4,8},{5,9},{6,10},{7,11},{8,4},{9,5},... | collective-permute-start | bytes 344072 | tf_op jit(solution)/shard_map/ppermute | solution.py:1106
  120.6 14.1 %collective-permute-start.19 = (bf16[448,128]{1,0:T(8,128)(2,1)S(1)}, bf16[448,128]{1,0:T(8,128)(2,1)S(1)}, u32[]{:S(2)}, u32[]{:S(2)}) collective-permute-start(bf16[448,128]{1,0:T(8,128)(2,1)S(1)} %get-tuple-element.234.refs_1_), channel_id=1, source_target_pairs={{0,8},{1,9},{2,10},{3,11},{4,12},{5,13},{6,14},{7,15},{8,0},{9,1},... | collective-permute-start | bytes 344072 | tf_op jit(solution)/shard_map/ppermute | solution.py:1106
  126.1 11.2 %collective-permute-start.18 = (bf16[448,128]{1,0:T(8,128)(2,1)S(1)}, bf16[448,128]{1,0:T(8,128)(2,1)S(1)}, u32[]{:S(2)}, u32[]{:S(2)}) collective-permute-start(bf16[448,128]{1,0:T(8,128)(2,1)S(1)} %get-tuple-element.234.refs_1_), channel_id=1, source_target_pairs={{0,4},{1,5},{2,6},{3,7},{4,0},{5,1},{6,2},{7,3},{8,12},{9,13},{10,... | collective-permute-start | bytes 344072 | tf_op jit(solution)/shard_map/ppermute | solution.py:1106
  137.4 21.4 %collective-permute-start.29 = (bf16[1792,128]{1,0:T(8,128)(2,1)S(1)}, bf16[1792,128]{1,0:T(8,128)(2,1)S(1)}, u32[]{:S(2)}, u32[]{:S(2)}) collective-permute-start(bf16[1792,128]{1,0:T(8,128)(2,1)S(1)} %get-tuple-element.246.refs_1_), channel_id=1, source_target_pairs={{0,3},{1,2},{2,1},{3,0},{4,7},{5,6},{6,5},{7,4},{8,11},{9,10},{10,... | collective-permute-start | bytes 1376264 | tf_op jit(solution)/shard_map/ppermute | solution.py:1106
  137.5 21.5 %collective-permute-start.28 = (bf16[1792,128]{1,0:T(8,128)(2,1)S(1)}, bf16[1792,128]{1,0:T(8,128)(2,1)S(1)}, u32[]{:S(2)}, u32[]{:S(2)}) collective-permute-start(bf16[1792,128]{1,0:T(8,128)(2,1)S(1)} %get-tuple-element.246.refs_1_), channel_id=1, source_target_pairs={{0,2},{1,3},{2,0},{3,1},{4,6},{5,7},{6,4},{7,5},{8,10},{9,11},{10,... | collective-permute-start | bytes 1376264 | tf_op jit(solution)/shard_map/ppermute | solution.py:1106
  138.8 23.1 %collective-permute-start.27 = (bf16[1792,128]{1,0:T(8,128)(2,1)S(1)}, bf16[1792,128]{1,0:T(8,128)(2,1)S(1)}, u32[]{:S(2)}, u32[]{:S(2)}) collective-permute-start(bf16[1792,128]{1,0:T(8,128)(2,1)S(1)} %get-tuple-element.246.refs_1_), channel_id=1, source_target_pairs={{0,1},{1,0},{2,3},{3,2},{4,5},{5,4},{6,7},{7,6},{8,9},{9,8},{10,11... | collective-permute-start | bytes 1376264 | tf_op jit(solution)/shard_map/ppermute | solution.py:1106
  141.0 7.2 %collective-permute-start.24 = (bf16[608,128]{1,0:T(8,128)(2,1)S(1)}, bf16[608,128]{1,0:T(8,128)(2,1)S(1)}, u32[]{:S(2)}, u32[]{:S(2)}) collective-permute-start(bf16[608,128]{1,0:T(8,128)(2,1)S(1)} %get-tuple-element.242), channel_id=1, source_target_pairs={{0,4},{1,5},{2,6},{3,7},{4,0},{5,1},{6,2},{7,3},{8,12},{9,13},{10,... | collective-permute-start | bytes 466952 | tf_op jit(solution)/shard_map/ppermute | solution.py:1106
  141.0 7.2 %collective-permute-start.25 = (bf16[608,128]{1,0:T(8,128)(2,1)S(1)}, bf16[608,128]{1,0:T(8,128)(2,1)S(1)}, u32[]{:S(2)}, u32[]{:S(2)}) collective-permute-start(bf16[608,128]{1,0:T(8,128)(2,1)S(1)} %get-tuple-element.243), channel_id=1, source_target_pairs={{0,8},{1,9},{2,10},{3,11},{4,12},{5,13},{6,14},{7,15},{8,0},{9,1},... | collective-permute-start | bytes 466952 | tf_op jit(solution)/shard_map/ppermute | solution.py:1106
  148.2 6.0 %collective-permute-start.26 = (bf16[608,128]{1,0:T(8,128)(2,1)S(1)}, bf16[608,128]{1,0:T(8,128)(2,1)S(1)}, u32[]{:S(2)}, u32[]{:S(2)}) collective-permute-start(bf16[608,128]{1,0:T(8,128)(2,1)S(1)} %get-tuple-element.244), channel_id=1, source_target_pairs={{0,12},{1,13},{2,14},{3,15},{4,8},{5,9},{6,10},{7,11},{8,4},{9,5},... | collective-permute-start | bytes 466952 | tf_op jit(solution)/shard_map/ppermute | solution.py:1106
  154.3 10.4 %collective-permute-start.33 = (bf16[448,128]{1,0:T(8,128)(2,1)S(1)}, bf16[448,128]{1,0:T(8,128)(2,1)S(1)}, u32[]{:S(2)}, u32[]{:S(2)}) collective-permute-start(bf16[448,128]{1,0:T(8,128)(2,1)S(1)} %get-tuple-element.253.refs_1_), channel_id=1, source_target_pairs={{0,12},{1,13},{2,14},{3,15},{4,8},{5,9},{6,10},{7,11},{8,4},{9,5},... | collective-permute-start | bytes 344072 | tf_op jit(solution)/shard_map/ppermute | solution.py:1106
  154.4 12.4 %collective-permute-start.32 = (bf16[448,128]{1,0:T(8,128)(2,1)S(1)}, bf16[448,128]{1,0:T(8,128)(2,1)S(1)}, u32[]{:S(2)}, u32[]{:S(2)}) collective-permute-start(bf16[448,128]{1,0:T(8,128)(2,1)S(1)} %get-tuple-element.253.refs_1_), channel_id=1, source_target_pairs={{0,8},{1,9},{2,10},{3,11},{4,12},{5,13},{6,14},{7,15},{8,0},{9,1},... | collective-permute-start | bytes 344072 | tf_op jit(solution)/shard_map/ppermute | solution.py:1106
  158.8 8.0 %collective-permute-start.31 = (bf16[448,128]{1,0:T(8,128)(2,1)S(1)}, bf16[448,128]{1,0:T(8,128)(2,1)S(1)}, u32[]{:S(2)}, u32[]{:S(2)}) collective-permute-start(bf16[448,128]{1,0:T(8,128)(2,1)S(1)} %get-tuple-element.253.refs_1_), channel_id=1, source_target_pairs={{0,4},{1,5},{2,6},{3,7},{4,0},{5,1},{6,2},{7,3},{8,12},{9,13},{10,... | collective-permute-start | bytes 344072 | tf_op jit(solution)/shard_map/ppermute | solution.py:1106
  159.0 5.0 %collective-permute-start.30 = (f32[80,128]{1,0:T(8,128)S(1)}, f32[80,128]{1,0:T(8,128)S(1)}, u32[]{:S(2)}, u32[]{:S(2)}) collective-permute-start(f32[80,128]{1,0:T(8,128)S(1)} %get-tuple-element.249.refs_1_), channel_id=1, source_target_pairs={{0,16},{16,0},{1,17},{17,1},{2,18},{18,2},{3,19},{19,3},{4,20},{20... | collective-permute-start | bytes 122888 | tf_op jit(solution)/shard_map/ppermute | solution.py:1101
  166.8 10.7 %collective-permute-start.36 = (bf16[1792,128]{1,0:T(8,128)(2,1)S(1)}, bf16[1792,128]{1,0:T(8,128)(2,1)S(1)}, u32[]{:S(2)}, u32[]{:S(2)}) collective-permute-start(bf16[1792,128]{1,0:T(8,128)(2,1)S(1)} %get-tuple-element.255.refs_1_), channel_id=1, source_target_pairs={{0,3},{1,2},{2,1},{3,0},{4,7},{5,6},{6,5},{7,4},{8,11},{9,10},{10,... | collective-permute-start | bytes 1376264 | tf_op jit(solution)/shard_map/ppermute | solution.py:1106
  167.5 22.6 %collective-permute-start.35 = (bf16[1792,128]{1,0:T(8,128)(2,1)S(1)}, bf16[1792,128]{1,0:T(8,128)(2,1)S(1)}, u32[]{:S(2)}, u32[]{:S(2)}) collective-permute-start(bf16[1792,128]{1,0:T(8,128)(2,1)S(1)} %get-tuple-element.255.refs_1_), channel_id=1, source_target_pairs={{0,2},{1,3},{2,0},{3,1},{4,6},{5,7},{6,4},{7,5},{8,10},{9,11},{10,... | collective-permute-start | bytes 1376264 | tf_op jit(solution)/shard_map/ppermute | solution.py:1106
  169.3 20.7 %collective-permute-start.34 = (bf16[1792,128]{1,0:T(8,128)(2,1)S(1)}, bf16[1792,128]{1,0:T(8,128)(2,1)S(1)}, u32[]{:S(2)}, u32[]{:S(2)}) collective-permute-start(bf16[1792,128]{1,0:T(8,128)(2,1)S(1)} %get-tuple-element.255.refs_1_), channel_id=1, source_target_pairs={{0,1},{1,0},{2,3},{3,2},{4,5},{5,4},{6,7},{7,6},{8,9},{9,8},{10,11... | collective-permute-start | bytes 1376264 | tf_op jit(solution)/shard_map/ppermute | solution.py:1106
  169.8 24.7 %collective-permute-start.37 = (bf16[1024,128]{1,0:T(8,128)(2,1)S(1)}, bf16[1024,128]{1,0:T(8,128)(2,1)S(1)}, u32[]{:S(2)}, u32[]{:S(2)}) collective-permute-start(bf16[1024,128]{1,0:T(8,128)(2,1)S(1)} %get-tuple-element.265.refs_1_), channel_id=1, source_target_pairs={{0,16},{16,0},{1,17},{17,1},{2,18},{18,2},{3,19},{19,3},{4,20},{20... | collective-permute-start | bytes 786440 | tf_op jit(solution)/shard_map/ppermute | solution.py:1101
  190.1 4.3 %collective-permute-start.38 = (bf16[1024,128]{1,0:T(8,128)(2,1)S(1)}, bf16[1024,128]{1,0:T(8,128)(2,1)S(1)}, u32[]{:S(2)}, u32[]{:S(2)}) collective-permute-start(bf16[1024,128]{1,0:T(8,128)(2,1)S(1)} %get-tuple-element.266.refs_3_), channel_id=1, source_target_pairs={{0,16},{16,0},{1,17},{17,1},{2,18},{18,2},{3,19},{19,3},{4,20},{20... | collective-permute-start | bytes 786440 | tf_op jit(solution)/shard_map/ppermute | solution.py:1101

commit v4 on v3

--- a/solution.py
+++ b/solution.py
@@ -21,7 +21,7 @@
 LANES = 128
 ELEMENT_ROWS = 512
 UNROLL = 8
-RELAY = 50
+CORES_COST = 0
 
 
 def core_place(row_devices):
@@ -135,28 +135,27 @@
     return re, im
 
 
-def first_pass(running_up, drives, masks, wholes, lanes, ids_ref, ends, payload):
+def first_pass(running_up, place, drives, masks, wholes, lanes, ids_ref, ends, payload):
     states = lanes.states
     thirds = states // LANES
     nothing = jnp.zeros((8, states), f32)
     zero = (nothing, nothing)
     values, _ = sweep(running_up, drives, masks, lanes, (zero, zero))
-    one = jnp.zeros((16, LANES), f32)
-    payload[0] = one
+    tiles = []
     for side in range(2):
         ends[side][:, :states] = values[side][0]
         ends[side][:, states:] = values[side][1]
         upward = running_up if side == 0 else jnp.logical_not(running_up)
         start = jnp.zeros((1, states), f32)
         re, im = run_chain(upward, lanes, side, ends[side], wholes[side], (start, start), None)
-        base = jnp.where(upward, 0, 8)
         for i in range(thirds):
-            payload[0, pl.ds(base + i, 1), :] = re[:, LANES * i : LANES * (i + 1)]
-            payload[0, pl.ds(base + thirds + i, 1), :] = im[:, LANES * i : LANES * (i + 1)]
-        payload[0, 8 * side + 6 : 8 * side + 8, :] = ids_ref[0:2, :]
-    one = payload[0]
-    for i in range(1, payload.shape[0]):
-        payload[i] = one
+            payload[side, i : i + 1, :] = re[:, LANES * i : LANES * (i + 1)]
+            payload[side, thirds + i : thirds + i + 1, :] = im[:, LANES * i : LANES * (i + 1)]
+        payload[side, 6:8, :] = ids_ref[0:2, :]
+    first, second = payload[0], payload[1]
+    for i in range(payload.shape[0]):
+        to_later = jnp.logical_xor(running_up, i < place)
+        payload[i] = jnp.where(to_later, first, second)
 
 
 def entering(upward, place, lanes, side, gathered, ids_ref, small):
@@ -167,15 +166,14 @@
     block_re, block_im = lanes.block[side]
     re = jnp.zeros((thirds, LANES), f32)
     im = jnp.zeros((thirds, LANES), f32)
-    base = jnp.where(upward, 0, 8)
     key = jnp.where(upward, ids_ref[0:1, :], ids_ref[1:2, :])
     for distance in range(min(count - 1, LONGEST_RUN // rows), 0, -1):
         source = jnp.where(upward, place - distance, place + distance)
         inside = jnp.logical_and(source >= 0, source < count)
         source = jnp.clip(source, 0, count - 1)
-        sent_re = gathered[source, pl.ds(base, thirds), :]
-        sent_im = gathered[source, pl.ds(base + thirds, thirds), :]
-        sent_key = gathered[source, pl.ds(jnp.where(upward, base + 7, base + 6), 1), :]
+        sent_re = gathered[source, 0:thirds, :]
+        sent_im = gathered[source, thirds : 2 * thirds, :]
+        sent_key = gathered[source, pl.ds(jnp.where(upward, 7, 6), 1), :]
         joined = jnp.where(jnp.logical_and(sent_key == key, inside), 1.0, 0.0)
         re, im = (
             joined * sent_re + block_re * re - block_im * im,
@@ -308,7 +306,7 @@
     ids,
     rows8,
 ):
-    core, _ = core_place(row_devices)
+    core, place = core_place(row_devices)
     rows = normed.shape[0]
     span = rows // 8
 
@@ -372,6 +370,7 @@
     lanes = make_lanes(table, tiles, 0, False, rows)
     first_pass(
         core == 0,
+        core_place(row_devices)[1],
         (drive_own, drive_oth),
         (keep_own, keep_oth),
         (whole_out.at[0], whole_out.at[1]),
@@ -488,6 +487,7 @@
     lanes = make_lanes(rows_ref, tiles_ref, 1, False, rows)
     first_pass(
         info[0] == 0,
+        info[1],
         (next_own, next_oth),
         masks,
         (whole.at[0], whole.at[1]),
@@ -535,6 +535,7 @@
     lanes = make_lanes(rows_ref, tiles_ref, layer, True, rows)
     first_pass(
         info[0] == 1,
+        info[1],
         (grad_own, grad_oth),
         (masks[1], masks[0]),
         (whole.at[1], whole.at[0]),
@@ -804,20 +805,21 @@
 
 
 def final_kernel(
-    low_own, low_oth, in_own, in_oth, grad_in, combined_grad, normed, inv_scale, gain, skip, block_out, out, sums, wide, natural, natural_out
+    low_own, low_oth, in_own, in_oth, grad_in, combined_grad, normed, inv_scale, gain, skip, block_out, halves, sums, wide,
+    *columns,
 ):
     rows = grad_in.shape[0]
     sums[...] = jnp.zeros_like(sums)
 
     def finish(start, value):
-        store_token_order(natural, start // 8, value, rows // 8)
-        store_token_order(natural_out, start // 8, block_out[pl.ds(start, ELEMENT_ROWS), :], rows // 8)
+        store_token_order(columns[1], start // 8, value, rows // 8)
 
     norm_backward(
         0, low_own, low_oth, in_own, in_oth, grad_in, combined_grad, normed, inv_scale, gain, skip, sums, wide, finish
     )
-    join_columns(out.at[0], natural_out)
-    join_columns(out.at[1], natural)
+    store_token_order(columns[0], 0, block_out[...], rows // 8)
+    for i in range(2):
+        join_columns(halves.at[i], columns[i])
 
 
 def store_columns(out, first, values):
@@ -879,72 +881,102 @@
             first += rows
 
 
-def encode_small(value, outs, first):
-    high = value.astype(bf16)
-    low = (value - high.astype(f32)).astype(bf16)
-    rows = value.shape[0]
-    for out in outs:
-        out[first : first + rows, :] = high
-        out[first + rows : first + 2 * rows, :] = low
-
-
-def decode_small(sources, first, rows):
-    return paired(
-        [
-            source[first : first + rows, :].astype(f32) + source[first + rows : first + 2 * rows, :].astype(f32)
-            for source in sources
-        ]
-    )
-
-
-def early_cores_kernel(mine, got, *outs):
-    sum_parts([(mine.shape[0], [mine, got])], outs, 0)
-
-
 def relay_kernel(payload_in, payload):
     payload[...] = payload_in[...]
 
 
-def first_plane_kernel(small_rows, *refs):
-    early, inner, (outer, got_outer, late, got_late), small_sums = refs[:4], refs[4:8], refs[8:12], refs[12:17]
-    first, second, small = refs[17:21], refs[21:25], refs[25]
-    sum_parts([(early[0].shape[0], early), (inner[0].shape[0], inner)], first, 2)
-    sum_parts([(outer.shape[0], [outer, got_outer]), (late.shape[0], [late, got_late])], second, 0)
-    small_pack(*small_sums, small)
-    encode_small(small[...], second, (outer.shape[0] + late.shape[0]) // 4)
+def add_rows(out, at, sources, start, rows):
+    where = pl.ds(pl.multiple_of(start, rows), rows)
+    out[at : at + rows, :] = paired([source[where, :].astype(f32) for source in sources]).astype(out.dtype)
+
+
+def put_small(outs, first, value):
+    for out in outs:
+        out[first : first + value.shape[0], :] = value.astype(out.dtype)
+
+
+def half_groups(outer, inner, side):
+    return ((outer // 2, side * (outer // 2)), (inner // 2, side * (inner // 2)))
+
+
+def cores_kernel(outer_half, half, outer, got_outer, inner, got_inner, *refs):
+    small_sums, (a_keep, a_send, b_keep, b_send), small = refs[:-5], refs[-5:-1], refs[-1]
+    outer_rows, inner_rows = 2 * outer_half, 2 * (half - outer_half)
+    mine = slot(0, 4)
+    for side, out, parts in ((0, a_keep, (0, 2)), (0, a_send, (1, 3)), (1, b_keep, (0, 1)), (1, b_send, (2, 3))):
+        (rows_one, at_one), (rows_two, at_two) = half_groups(outer_rows, inner_rows, side)
+        for place, k in enumerate(parts):
+            which = jnp.bitwise_xor(mine, k)
+            add_rows(out, place * half, [outer, got_outer], which * outer_rows + at_one, rows_one)
+            add_rows(out, place * half + rows_one, [inner, got_inner], which * inner_rows + at_two, rows_two)
+    if small_sums:
+        small_pack(*small_sums, small)
+        put_small((a_keep, a_send), 2 * half, small[...])
+
+
+def half_kernel(half, a_own, a_got, b_own, b_got, a_keep, a_send, b_keep, b_send):
+    for own, got, outs in ((a_own, a_got, (a_keep, a_send)), (b_own, b_got, (b_keep, b_send))):
+        for i, out in enumerate(outs):
+            add_rows(out, 0, [own, got], i * half, half)
+    if a_own.shape[0] > 2 * half:
+        put_small((a_keep, a_send), half, a_own[2 * half :, :].astype(f32) + a_got[2 * half :, :].astype(f32))
+
+
+def plane_kernel(half, outer_half, a_own, a_got, b_own, b_got, *outs):
+    groups = []
+    for own, got in ((a_own, a_got), (b_own, b_got)):
+        groups.append((outer_half, [own.at[0:outer_half], got.at[0:outer_half]]))
+        groups.append((half - outer_half, [own.at[outer_half:half], got.at[outer_half:half]]))
+    sum_parts(groups, outs, 2)
+    if a_own.shape[0] > half:
+        put_small(outs, half // 2, a_own[half:, :].astype(f32) + a_got[half:, :].astype(f32))
 
 
 def planes_kernel(*refs):
     refs[-1][...] = paired([source[...].astype(f32) for source in refs[:-1]]).astype(bf16)
 
 
-def gather_kernel(sizes, *refs):
-    out = refs[-1]
-    outs = []
-    first = 0
-    for rows in sizes:
-        outs.append(out.at[first : first + 4 * rows])
-        first += 4 * rows
-    gather_parts(sizes, refs[:-1], 2, outs)
-
-
-def second_plane_kernel(small_rows, outer_rows, *refs):
-    sources, outs, small = refs[:4], refs[4:8], refs[8]
-    late_end = sources[0].shape[0] - 2 * small_rows
-    groups = [
-        (outer_rows, [source.at[0:outer_rows] for source in sources]),
-        (late_end - outer_rows, [source.at[outer_rows:late_end] for source in sources]),
-    ]
-    sum_parts(groups, outs, 2)
-    small[...] = decode_small(sources, late_end, small_rows)
-    encode_small(small[...], outs, late_end // 4)
-
-
-def second_planes_kernel(small_rows, *refs):
+def second_planes_kernel(*refs):
     sources, out, small = refs[:-2], refs[-2], refs[-1]
     rows = out.shape[0]
     out[...] = paired([source[0:rows, :].astype(f32) for source in sources]).astype(bf16)
-    small[...] = decode_small(sources, rows, small_rows)
+    small[...] = paired([source[rows:, :].astype(f32) for source in sources])
+
+
+def gather_kernel(outer_half, *refs):
+    sources, outs = refs[:4], refs[4:]
+    half = outs[0].shape[0]
+    sizes, places = [], []
+    for out in outs:
+        sizes += [outer_half // 4, (half - outer_half) // 4]
+        places += [out.at[0:outer_half], out.at[outer_half:half]]
+    gather_parts(sizes, sources, 2, places)
+
+
+def pair_kernel(a_own, a_got, b_own, b_got, a_out, b_out):
+    half = a_own.shape[0]
+    for own, got, out in ((a_own, a_got, a_out), (b_own, b_got, b_out)):
+        out[0:half, :] = own[...]
+        out[half : 2 * half, :] = got[...]
+
+
+def last_pair_kernel(a_own, a_got, b_own, b_got, through, through_out, a_out, b_out):
+    pair_kernel(a_own, a_got, b_own, b_got, a_out, b_out)
+
+
+def assemble(outer_half, a_own, a_got, b_own, b_got, outer, inner):
+    half = a_own.shape[0] // 2
+    mine = slot(0, 4)
+    for side, sources in ((0, (a_own, a_got, a_own, a_got)), (1, (b_own, b_own, b_got, b_got))):
+        second = (0, 0, 1, 1) if side == 0 else (0, 1, 0, 1)
+        for k, source in enumerate(sources):
+            which = jnp.bitwise_xor(mine, k)
+            first = second[k] * half
+            rows = outer_half
+            outer[part_rows(2 * which + side, rows), :] = source[first : first + rows, :]
+            if inner is not None:
+                rows = half - outer_half
+                inner[part_rows(2 * which + side, rows), :] = source[first + outer_half : first + half, :]
 
 
 def join_kernel(mine, theirs, *outs):
@@ -961,13 +993,13 @@
         out[:, i * LANES : (i + 1) * LANES] = source[first + i * rows : first + (i + 1) * rows, :].astype(f32)
 
 
-def gate_part_kernel(quarter_rows, first, *refs):
+def gate_part_kernel(outer_half, first, *refs):
     sources, out, whole = refs[:-2], refs[-2], refs[-1]
-    gather_parts((quarter_rows,), sources, 0, (whole,))
+    assemble(outer_half, *sources, whole, None)
     out[...] = whole[first : first + out.shape[0], :]
 
 
-def unpack_kernel(layer, olds, sizes, *refs):
+def unpack_kernel(layer, olds, outer_half, *refs):
     refs = list(refs)
     take = lambda n: [refs.pop(0) for _ in range(n)]
     sources = take(4)
@@ -976,7 +1008,7 @@
     buffers = take(2)
     whole = take(2)
     (sems,) = refs
-    gather_parts(sizes, sources, 0, whole)
+    assemble(outer_half, *sources, *whole)
     copies = []
     for i in range(2):
         matrix_columns(whole[i], 0, buffers[i])
@@ -986,15 +1018,18 @@
         copy.wait()
 
 
-def gate_kernel(mine_early, theirs_early, mine_middle, theirs_middle, out):
+def gate_kernel(layer, *refs):
+    mine, theirs, (out, buffer, sems) = refs[0], refs[1], refs[-3:]
     core = lax.axis_index("dir")
-    half = out.shape[1] // 2
-    width = out.shape[2]
-    for layer, mine, theirs in ((1, mine_early, theirs_early), (0, mine_middle, theirs_middle)):
-        for source, which in ((mine, core), (theirs, 1 - core)):
-            rows = pl.ds(pl.multiple_of(which * half, half), half)
-            for i in range(width // LANES):
-                out[layer, rows, i * LANES : (i + 1) * LANES] = source[i * half : (i + 1) * half, :].astype(f32)
+    half = buffer.shape[0] // 2
+    width = buffer.shape[1]
+    for source, which in ((mine, core), (theirs, 1 - core)):
+        rows = part_rows(which, half)
+        for i in range(width // LANES):
+            buffer[rows, i * LANES : (i + 1) * LANES] = source[i * half : (i + 1) * half, :].astype(f32)
+    copy = pltpu.make_async_copy(buffer, out.at[layer], sems.at[0])
+    copy.start()
+    copy.wait()
 
 
 def small_pack(sums_turn, sums_back, sums_last, decay_late, decay_early, out):
@@ -1050,9 +1085,9 @@
             grad_damping = grad_scale * square / scale - (grad_re * re + grad_im * im)
             grad_rotation = grad_im * re - grad_re * im
             log_rate = grad_damping * damping
-            rate[layer : layer + 1, lanes] = log_rate
-            turn[2 * layer : 2 * layer + 1, lanes] = grad_rotation * step_size
-            turn[2 * layer + 1 : 2 * layer + 2, lanes] = log_rate + grad_rotation * rotation
+            rate[layer, 0:1, lanes] = log_rate
+            turn[layer, 0, 0:1, lanes] = grad_rotation * step_size
+            turn[layer, 0, 1:2, lanes] = log_rate + grad_rotation * rotation
 
 
 class Order:
@@ -1165,7 +1200,7 @@
     wide = ((rows, 2 * states), f32)
     wide_low = ((rows, 2 * states), bf16)
     ends = ((8, 2 * states), f32)
-    payload_shape = ((2 * row_devices, 16, LANES), f32)
+    payload_shape = ((2 * row_devices, 8, LANES), f32)
     narrow = ((rows, LANES), f32)
     tile = ((8, LANES), f32)
     sums_shape = ((8, width), f32)
@@ -1230,12 +1265,8 @@
         flops=4 * one + 2 * gate + 4 * scan,
         name="turn",
     )
-    got = swap(theirs)
+    first_outer = [mine, swap(theirs)]
     gathered = exchanged(payload, row_devices)
-    early = order.run(
-        early_cores_kernel, [((outer_size // 4, LANES), bf16)] * 4, [mine, got], name="early_cores", after=[gathered]
-    )
-    early = sent(early, 0)
     in_low_own1, in_low_oth1, decay_sums1, mine, theirs = order.run(
         here(scan_kernel, 1, row_devices),
         [wide_low, wide_low, decay_shape, inner_pack, inner_pack],
@@ -1243,8 +1274,9 @@
          ids, low_own1, low_oth1, drive_own1, drive_oth1, mixed1],
         [places, tile, wide, wide],
         name="scan_one",
-    )
-    got = swap(theirs)
+        after=[first_outer[1]],
+    )
+    first_inner = [mine, swap(theirs)]
     (
         grad0, combined_grad0, grad_own0, grad_oth0, ends_own, ends_oth, payload, sums_back, mine_outer, theirs_outer,
     ) = order.run(
@@ -1256,13 +1288,51 @@
         [full, full_low, full_low],
         name="back",
     )
-    got_outer = swap(theirs_outer)
-    (payload,) = order.run(relay_kernel, [payload_shape], [payload], name="relay", after=early[1:], cost=RELAY)
+    second_outer = [mine_outer, swap(theirs_outer)]
+    outer_half = outer_size // 8
+    half = outer_half + in_size // 8
+    share_rows = half // 2
+    small_rows = -(-(4 * layers * (width // LANES) + 6 * layers * (states // LANES)) // 16) * 16
+    small_shape = ((small_rows, LANES), f32)
+
+    def low(count):
+        return ((count, LANES), bf16)
+
+    def from_cores(packs, extra, sums, name, after=()):
+        a_keep, a_send, b_keep, b_send, _ = order.run(
+            here(cores_kernel, outer_half, half),
+            [low(2 * half + extra)] * 2 + [low(2 * half)] * 2 + [small_shape],
+            packs + sums,
+            name=name,
+            after=after,
+            cost=CORES_COST,
+        )
+        return [a_keep, across(a_send, 1), b_keep, across(b_send, 2)]
+
+    def from_first(parts, extra, name):
+        a_keep, a_send, b_keep, b_send = order.run(
+            here(half_kernel, half), [low(half + extra)] * 2 + [low(half)] * 2, parts, name=name
+        )
+        return [a_keep, across(a_send, 2), b_keep, across(b_send, 1)]
+
+    def from_second(parts, extra, name):
+        return sent(
+            order.run(here(plane_kernel, half, outer_half), [low(share_rows + extra)] * 4, parts, name=name), 2
+        )
+
+    def gathered_half(parts, name, after=()):
+        a_half, b_half = order.run(
+            here(gather_kernel, outer_half), [low(half)] * 2, parts, name=name, after=after
+        )
+        return a_half, across(a_half, 2), b_half, across(b_half, 1)
+
+    def gathered_whole(halves, name):
+        a_pair, b_pair = order.run(pair_kernel, [low(2 * half)] * 2, list(halves), name=name)
+        return [a_pair, across(a_pair, 1), b_pair, across(b_pair, 2)]
+
+    first = from_cores(first_outer + first_inner, 0, [], "first_cores")
+    (payload,) = order.run(relay_kernel, [payload_shape], [payload], name="relay", cost=50)
     gathered = exchanged(payload, row_devices)
-    inner = order.run(
-        early_cores_kernel, [((in_size // 4, LANES), bf16)] * 4, [mine, got], name="inner_cores", after=[gathered, got_outer]
-    )
-    inner = sent(inner, 0)
     in_low_own0, in_low_oth0, decay_sums0, mine, theirs = order.run(
         here(scan_kernel, 0, row_devices),
         [wide_low, wide_low, decay_shape, inner_pack, inner_pack],
@@ -1270,9 +1340,10 @@
          ids, low_own0, low_oth0, drive_own0, drive_oth0, mixed0],
         [places, tile, wide, wide],
         name="scan_zero",
-    )
-    got = swap(theirs)
-    quarter = (outer_size + in_size) // 4
+        after=[first[1], first[3], second_outer[1]],
+    )
+    second_inner = [mine, swap(theirs)]
+    first = from_first(first, 0, "first_half")
     halves, sums_last = order.run(
         final_kernel,
         [((2, rows, width), f32), sums_shape],
@@ -1280,55 +1351,38 @@
         [full, columns, columns],
         name="final_norm",
     )
-    quarter = (outer_size + in_size) // 4
-    small_rows = -(-(4 * layers * (width // LANES) + 6 * layers * (states // LANES)) // 16) * 16
-    small_shape = ((small_rows, LANES), f32)
-    parts = order.run(
-        here(first_plane_kernel, small_rows),
-        [((quarter // 4, LANES), bf16)] * 4 + [((quarter + 2 * small_rows, LANES), bf16)] * 4 + [small_shape],
-        early + inner + [mine_outer, got_outer, mine, got, sums_turn, sums_back, sums_last, decay_sums0, decay_sums1],
-        name="first_plane",
-        cost=RELAY,
-    )
-    first = sent(parts[:4], 2)
-    second = sent(parts[4:8], 0)
-    whole_rows = ((chip_rows, width), f32)
-    block_output, tokens_grad = order.run(
-        join_kernel, [whole_rows, whole_rows], [halves, swap(halves)], name="join"
-    )
-    (share,) = order.run(planes_kernel, [((quarter // 4, LANES), bf16)], first, name="first_planes")
+    first = from_second(first, 0, "first_plane")
+    second = from_cores(
+        second_outer + second_inner, small_rows, [sums_turn, sums_back, sums_last, decay_sums0, decay_sums1],
+        "second_cores",
+    )
+    (share,) = order.run(planes_kernel, [low(share_rows)], first, name="first_planes")
     first = shared(beyond(share), 2)
-    sizes = (outer_size // 16, in_size // 16)
-    (full_quarter,) = order.run(
-        here(gather_kernel, sizes), [((quarter, LANES), bf16)], first, name="first_gather"
-    )
-    first = shared(full_quarter, 0)
-    *second, _ = order.run(
-        here(second_plane_kernel, small_rows, outer_size // 4),
-        [((quarter // 4 + 2 * small_rows, LANES), bf16)] * 4 + [((small_rows, LANES), f32)],
-        second,
-        name="second_plane",
-    )
-    second = sent(second, 2)
-    share, small = order.run(
-        here(second_planes_kernel, small_rows), [((quarter // 4, LANES), bf16), ((small_rows, LANES), f32)], second,
-        name="second_planes",
-    )
+    second = from_first(second, small_rows, "second_half")
+    second = from_second(second, small_rows, "second_plane")
+    first = gathered_half(first, "first_gather")
+    share, small = order.run(second_planes_kernel, [low(share_rows), small_shape], second, name="second_planes")
     second = shared(beyond(share), 2)
+    first = gathered_whole(first, "first_pair")
     small = beyond(small)
     got_small = swap(small)
     in_shape, out_shape = input_matrix.shape, output_matrix.shape
 
     def gate_part(quarters, name):
         (value,) = order.run(
-            here(gate_part_kernel, outer_size // 4, out_size), [((glu_size, LANES), bf16)], quarters,
-            [((outer_size, LANES), bf16)], name=name,
+            here(gate_part_kernel, outer_half, out_size), [low(glu_size)], quarters, [outer_pack], name=name
         )
         return value
 
+    def gate_out(layer, mine, theirs, old, name):
+        return order.run(
+            here(gate_kernel, layer), [(glu_weight.shape, f32)], [mine, theirs] + old, [((width, width), f32)],
+            name=name, free_outs=1, alias={2: 0} if old else None, semaphores=1,
+        )
+
     def unpack(quarters, layer, old, name):
         return order.run(
-            here(unpack_kernel, layer, len(old), (outer_size // 4, in_size // 4)),
+            here(unpack_kernel, layer, len(old), outer_half),
             [(out_shape, f32), (in_shape, f32)],
             quarters + old,
             [(out_shape[2:], f32), (in_shape[2:], f32), outer_pack, inner_pack],
@@ -1338,26 +1392,31 @@
             semaphores=2,
         )
 
+    second = gathered_half(second, "second_gather", [first[1], first[3]])
+    halves, a_pair, b_pair = order.run(
+        last_pair_kernel, [((2, rows, width), f32), low(2 * half), low(2 * half)], list(second) + [halves],
+        name="second_pair", free_outs=1, alias={4: 0},
+    )
+    second = [a_pair, across(a_pair, 1), b_pair, across(b_pair, 2)]
     gate_one = gate_part(first, "gate_one")
     got_one = swap(gate_one)
     results = unpack(first, 1, [], "unpack_one")
     gain_grad, bias_grad, rate_grad, turn_grad, skip_grad, gate_grad = order.run(
         small_out_kernel,
-        [((layers, width), f32), ((layers, width), f32), ((layers, states), f32), ((2 * layers, states), f32),
+        [((layers, width), f32), ((layers, width), f32), (rate_params.shape, f32), (turn_params.shape, f32),
          ((layers, width), f32), ((layers, width), f32)],
         [small, got_small, table],
         name="small_out",
     )
-    (full_quarter,) = order.run(
-        here(gather_kernel, sizes), [((quarter, LANES), bf16)], second, name="second_gather"
-    )
-    second = shared(full_quarter, 0)
+    whole_rows = ((chip_rows, width), f32)
+    block_output, tokens_grad = order.run(
+        join_kernel, [whole_rows, whole_rows], [halves, swap(halves)], name="join"
+    )
+    glu_all = gate_out(1, gate_one, got_one, [], "gate_out_one")
     gate_zero = gate_part(second, "gate_zero")
     got_zero = swap(gate_zero)
     out_all, in_all = unpack(second, 0, list(results), "unpack_zero")
-    (glu_all,) = order.run(
-        gate_kernel, [(glu_weight.shape, f32)], [gate_one, got_one, gate_zero, got_zero], name="unpack_gate"
-    )
+    (glu_all,) = gate_out(0, gate_zero, got_zero, list(glu_all), "gate_out_zero")
     return (
         block_output,
         tokens_grad,
@@ -1365,8 +1424,8 @@
         bias_grad,
         in_all,
         out_all,
-        rate_grad.reshape(rate_params.shape),
-        turn_grad.reshape(turn_params.shape),
+        rate_grad,
+        turn_grad,
         skip_grad,
         glu_all,
         gate_grad,

time: 196 us -> 171 us (0.87)
  waiting for transfers between devices: 54 us -> 40.1 us
  blocking collectives: 55.4 us -> 48.2 us
  starting transfers between devices: 43.5 us -> 39.5 us
    ppermute x27 -> x28, waiting for transfers between devices: 51.4 us -> 37.4 us  [across(): return lax.ppermute(value, 'seq', [(i, i ^ bits) for i in range(count)])]
    all_to_all x4, blocking collectives: 55.4 us -> 48.2 us  [exchanged(): lax.all_to_all(payload, ('seq', 'dir'), 0, 0, tiled=True, axis_index_grou...]
    ppermute x27 -> x28, starting transfers between devices: 31.5 us -> 28.2 us  [across(): return lax.ppermute(value, 'seq', [(i, i ^ bits) for i in range(count)])]
    pallas_call x24 -> x29, Pallas kernels: 39.7 us -> 41 us  [run(): pl.pallas_call(body, out_shape=shapes, in_specs=specs, out_specs=[whole]...]
  transfers between devices with their start and end apart: 39 -> 40, of which waited for: 14 -> 17; matrix products, arithmetic and copies ran while one was open for 1% -> 0% of each run, Pallas kernels for 11% -> 11%
where the time goes in v4:
time: 171 us
  blocking collectives  48.2 us (28%)
  Pallas kernels  41 us (24%)
  waiting for transfers between devices  40.1 us (23%)
  starting transfers between devices  39.5 us (23%)
    all_to_all x4, blocking collectives, exchanged(): lax.all_to_all(payload, ('seq', 'dir'), 0, 0, tiled=True, axis_index_grou...  48.2 us
    pallas_call x29, Pallas kernels, run(): pl.pallas_call(body, out_shape=shapes, in_specs=specs, out_specs=[whole]...  41 us
    ppermute x28, waiting for transfers between devices, across(): return lax.ppermute(value, 'seq', [(i, i ^ bits) for i in range(count)])  37.4 us
    ppermute x28, starting transfers between devices, across(): return lax.ppermute(value, 'seq', [(i, i ^ bits) for i in range(count)])  28.2 us
    ppermute x12, starting transfers between devices, swap(): return lax.ppermute(value, 'dir', [(0, 1), (1, 0)])  11.3 us
  transfers between devices with their start and end apart: 40, of which 17 were waited for; matrix products, arithmetic and copies ran while one was open for 0% of the time, Pallas kernels for 11%

profile of v4, /device:TPU:1, one launch (start us, length us, event | category | flops | bytes accessed | tf_op | source)
XLA Modules:
  0.0 171.2 jit_solution(2740958153924478091)
XLA Ops:
  0.8 0.5 collective-permute-start.3
  1.4 0.4 collective-permute-start.2
  1.8 1.2 copy-done.11
  3.0 1.0 open_norm.1
  4.0 2.6 %collective-permute-done.1.refs_8_ = f32[2,1,384]{2,1,0:T(1,128)S(1)} collective-permute-done((f32[2,1,384]{2,1,0:T(1,128)}, f32[2,1,384]{2,1,0:T(1,128)S(1)}, u32[]{:S(2)}, u32[]{:S(2)}) %collective-permute-start.1) | collective-permute-done | bytes 3104 | tf_op jit(solution)/shard_map/ppermute | solution.py:1136
  6.8 1.8 %open_scan.1 = (f32[8,128]{1,0:T(8,128)S(1)}, bf16[512,512]{1,0:T(8,128)(2,1)S(1)}, f32[512,768]{1,0:T(8,128)S(1)}, f32[512,768]{1,0:T(8,128)S(1)}, f32[512,128]...) custom-call(bf16[2,1,768,512]{3,2,1,0:T(8,128)(2,1)S(1)} %collective, ...), custom_call_target="tpu_custom_call" | custom-call | flops 1 | bytes 1 | tf_op jit(solution)/shard_map/open_scan/pallas_call | solution.py:1120
  8.6 15.1 %all_to_all.20.refs_1_ = f32[32,8,128]{2,1,0:T(8,128)S(1)} all-to-all(f32[32,8,128]{2,1,0:T(8,128)S(1)} %get-tuple-element.160), channel_id=1, replica_groups=mesh['dir'=2,'seq'=16] {'seq','dir'}, dimensions={0} | all-to-all | bytes 262144 | tf_op jit(solution)/shard_map/all_to_all | solution.py:1158
  23.7 4.3 %mid.1 = (f32[8,128]{1,0:T(8,128)S(1)}, bf16[512,768]{1,0:T(8,128)(2,1)S(1)}, bf16[512,768]{1,0:T(8,128)(2,1)S(1)}, f32[512,512]{1,0:T(8,128)S(1)}, f32[512,512]...) custom-call(f32[8,128]{1,0:T(8,128)S(1)} %get-tuple-element.159.refs, ...), custom_call_target="tpu_custom_call" | custom-call | flops 1 | bytes 1 | tf_op jit(solution)/shard_map/mid/pallas_call | solution.py:1120
  28.1 10.0 %all_to_all.21.refs_1_ = f32[32,8,128]{2,1,0:T(8,128)S(1)} all-to-all(f32[32,8,128]{2,1,0:T(8,128)S(1)} %get-tuple-element.173), channel_id=1, replica_groups=mesh['dir'=2,'seq'=16] {'seq','dir'}, dimensions={0} | all-to-all | bytes 262144 | tf_op jit(solution)/shard_map/all_to_all | solution.py:1158
  38.1 6.5 %turn.1 = (f32[8,128]{1,0:T(8,128)S(1)}, bf16[512,768]{1,0:T(8,128)(2,1)S(1)}, bf16[512,768]{1,0:T(8,128)(2,1)S(1)}, f32[512,512]{1,0:T(8,128)S(1)}, f32[512,512...) custom-call(f32[8,128]{1,0:T(8,128)S(1)} %get-tuple-element.172.refs, ...), custom_call_target="tpu_custom_call" | custom-call | flops 1 | bytes 1 | tf_op jit(solution)/shard_map/turn/pallas_call | solution.py:1120
  44.9 9.8 %all_to_all.22.refs_2_ = f32[32,8,128]{2,1,0:T(8,128)S(1)} all-to-all(f32[32,8,128]{2,1,0:T(8,128)S(1)} %get-tuple-element.182), channel_id=1, replica_groups=mesh['dir'=2,'seq'=16] {'seq','dir'}, dimensions={0} | all-to-all | bytes 262144 | tf_op jit(solution)/shard_map/all_to_all | solution.py:1158
  54.8 2.8 %scan_one.1 = (f32[8,128]{1,0:T(8,128)S(1)}, bf16[512,768]{1,0:T(8,128)(2,1)S(1)}, bf16[512,768]{1,0:T(8,128)(2,1)S(1)}, f32[8,384]{1,0:T(8,128)S(1)}, bf16[3072...) custom-call(bf16[4096,128]{1,0:T(8,128)(2,1)S(1)} %collective-permute-done.4.refs_0_.refs_2_, ...), custom_call_target="tpu_custom_call" | custom-call | flops 1 | bytes 1 | tf_op jit(solution)/shard_map/scan_one/pallas_call | solution.py:1120
  57.9 5.1 %back.1 = (f32[8,128]{1,0:T(8,128)S(1)}, f32[512,512]{1,0:T(8,128)S(1)}, f32[512,512]{1,0:T(8,128)S(1)}, f32[512,768]{1,0:T(8,128)S(1)}, f32[512,768]{1,0:T(8,12...) custom-call(f32[8,128]{1,0:T(8,128)S(1)} %get-tuple-element.190.refs, ...), custom_call_target="tpu_custom_call" | custom-call | flops 1 | bytes 1 | tf_op jit(solution)/shard_map/back/pallas_call | solution.py:1120
  63.4 1.0 first_cores.1
  64.4 0.6 collective-permute-start.7
  65.1 13.2 %all_to_all.23.refs_4_ = f32[32,8,128]{2,1,0:T(8,128)S(1)} all-to-all(f32[32,8,128]{2,1,0:T(8,128)S(1)} %get-tuple-element.212), channel_id=1, replica_groups=mesh['dir'=2,'seq'=16] {'seq','dir'}, dimensions={0} | all-to-all | bytes 262144 | tf_op jit(solution)/shard_map/all_to_all | solution.py:1158
  78.3 2.9 %scan_zero.1 = (f32[8,128]{1,0:T(8,128)S(1)}, bf16[512,768]{1,0:T(8,128)(2,1)S(1)}, bf16[512,768]{1,0:T(8,128)(2,1)S(1)}, f32[8,384]{1,0:T(8,128)S(1)}, bf16[307...) custom-call(bf16[1792,128]{1,0:T(8,128)(2,1)S(1)} %collective-permute-done.6.refs_0_.refs_2_, ...), custom_call_target="tpu_custom_call" | custom-call | flops 1 | bytes 1 | tf_op jit(solution)/shard_map/scan_zero/pallas_call | solution.py:1120
  81.2 0.5 collective-permute-start.11
  81.9 1.1 collective-permute-start.9
  83.0 0.5 collective-permute-start.10
  83.6 3.4 %final_norm.1 = (f32[8,128]{1,0:T(8,128)S(1)}, f32[2,512,512]{2,1,0:T(8,128)S(1)}, f32[8,512]{1,0:T(8,128)S(1)}) custom-call(f32[8,128]{1,0:T(8,128)S(1)} %get-tuple-element.221.refs_0_, bf16[512,768]{1,0:T(8,128)(2,1)S(1)} %get-tuple-element.222.refs_1_, bf16[512,768]{1,0:T(8,128)(2,1)S(1)} %get-tuple-element.223.refs_2_, ...), custom_call_target="tpu_custom_call" | custom-call | flops 1 | bytes 1 | tf_op jit(solution)/shard_map/final_norm/pallas_call | solution.py:1120
  87.0 2.2 %collective-permute-done.9.refs_2_ = bf16[896,128]{1,0:T(8,128)(2,1)S(1)} collective-permute-done((bf16[896,128]{1,0:T(8,128)(2,1)S(1)}, bf16[896,128]{1,0:T(8,128)(2,1)S(1)}, u32[]{:S(2)}, u32[]{:S(2)}) %collective-permute-start.9) | collective-permute-done | bytes 229408 | tf_op jit(solution)/shard_map/ppermute | solution.py:1141
  89.2 0.6 collective-permute-done.10.refs_4_
  89.9 1.1 second_cores.1
  91.0 0.8 collective-permute-start.15
  91.8 1.1 collective-permute-start.16
  93.2 0.9 collective-permute-start.13
  94.1 2.4 %collective-permute-start.14 = (bf16[448,128]{1,0:T(8,128)(2,1)S(1)}, bf16[448,128]{1,0:T(8,128)(2,1)S(1)}, u32[]{:S(2)}, u32[]{:S(2)}) collective-permute-start(bf16[448,128]{1,0:T(8,128)(2,1)S(1)} %get-tuple-element.246), channel_id=1, source_target_pairs={{0,12},{1,13},{2,14},{3,15},{4,8},{5,9},{6,10},{7,11},{8,4},{9,5},... | collective-permute-start | bytes 344072 | tf_op jit(solution)/shard_map/ppermute | solution.py:1141
  96.5 1.5 collective-permute-done.12.refs_2_
  98.1 4.1 %collective-permute-done.14.refs_4_ = bf16[448,128]{1,0:T(8,128)(2,1)S(1)} collective-permute-done((bf16[448,128]{1,0:T(8,128)(2,1)S(1)}, bf16[448,128]{1,0:T(8,128)(2,1)S(1)}, u32[]{:S(2)}, u32[]{:S(2)}) %collective-permute-start.14) | collective-permute-done | bytes 114720 | tf_op jit(solution)/shard_map/ppermute | solution.py:1141
  102.8 1.1 collective-permute-start.17
  103.9 0.7 collective-permute-start.18
  104.6 0.9 collective-permute-start.21
  105.5 2.3 %collective-permute-start.20 = (bf16[448,128]{1,0:T(8,128)(2,1)S(1)}, bf16[448,128]{1,0:T(8,128)(2,1)S(1)}, u32[]{:S(2)}, u32[]{:S(2)}) collective-permute-start(bf16[448,128]{1,0:T(8,128)(2,1)S(1)} %get-tuple-element.258.refs_1_), channel_id=1, source_target_pairs={{0,8},{1,9},{2,10},{3,11},{4,12},{5,13},{6,14},{7,15},{8,0},{9,1},... | collective-permute-start | bytes 344072 | tf_op jit(solution)/shard_map/ppermute | solution.py:1141
  107.7 0.4 collective-permute-start.19
  108.1 0.6 collective-permute-done.18.refs_4_
  108.9 1.3 collective-permute-done.21.refs_4_
  110.1 7.9 %collective-permute-done.20.refs_3_ = bf16[448,128]{1,0:T(8,128)(2,1)S(1)} collective-permute-done((bf16[448,128]{1,0:T(8,128)(2,1)S(1)}, bf16[448,128]{1,0:T(8,128)(2,1)S(1)}, u32[]{:S(2)}, u32[]{:S(2)}) %collective-permute-start.20) | collective-permute-done | bytes 114720 | tf_op jit(solution)/shard_map/ppermute | solution.py:1141
  118.1 0.5 collective-permute-start.25
  118.6 0.4 collective-permute-start.26
  119.0 0.4 collective-permute-start.23
  119.5 3.1 %collective-permute-start.24 = (bf16[528,128]{1,0:T(8,128)(2,1)S(1)}, bf16[528,128]{1,0:T(8,128)(2,1)S(1)}, u32[]{:S(2)}, u32[]{:S(2)}) collective-permute-start(bf16[528,128]{1,0:T(8,128)(2,1)S(1)} %get-tuple-element.263), channel_id=1, source_target_pairs={{0,12},{1,13},{2,14},{3,15},{4,8},{5,9},{6,10},{7,11},{8,4},{9,5},... | collective-permute-start | bytes 405512 | tf_op jit(solution)/shard_map/ppermute | solution.py:1141
  122.6 2.2 %collective-permute-done.22.refs_2_ = bf16[528,128]{1,0:T(8,128)(2,1)S(1)} collective-permute-done((bf16[528,128]{1,0:T(8,128)(2,1)S(1)}, bf16[528,128]{1,0:T(8,128)(2,1)S(1)}, u32[]{:S(2)}, u32[]{:S(2)}) %collective-permute-start.22) | collective-permute-done | bytes 135200 | tf_op jit(solution)/shard_map/ppermute | solution.py:1141
  124.8 3.9 %collective-permute-done.24.refs_4_ = bf16[528,128]{1,0:T(8,128)(2,1)S(1)} collective-permute-done((bf16[528,128]{1,0:T(8,128)(2,1)S(1)}, bf16[528,128]{1,0:T(8,128)(2,1)S(1)}, u32[]{:S(2)}, u32[]{:S(2)}) %collective-permute-start.24) | collective-permute-done | bytes 135200 | tf_op jit(solution)/shard_map/ppermute | solution.py:1141
  128.9 0.4 collective-permute-start.27
  129.3 1.4 collective-permute-start.28
  130.7 1.7 collective-permute-start.31
  132.3 3.8 %collective-permute-start.30 = (bf16[448,128]{1,0:T(8,128)(2,1)S(1)}, bf16[448,128]{1,0:T(8,128)(2,1)S(1)}, u32[]{:S(2)}, u32[]{:S(2)}) collective-permute-start(bf16[448,128]{1,0:T(8,128)(2,1)S(1)} %get-tuple-element.270.refs_3_), channel_id=1, source_target_pairs={{0,8},{1,9},{2,10},{3,11},{4,12},{5,13},{6,14},{7,15},{8,0},{9,1},... | collective-permute-start | bytes 344072 | tf_op jit(solution)/shard_map/ppermute | solution.py:1141
  136.1 4.7 %collective-permute-done.30.refs_5_ = bf16[448,128]{1,0:T(8,128)(2,1)S(1)} collective-permute-done((bf16[448,128]{1,0:T(8,128)(2,1)S(1)}, bf16[448,128]{1,0:T(8,128)(2,1)S(1)}, u32[]{:S(2)}, u32[]{:S(2)}) %collective-permute-start.30) | collective-permute-done | bytes 114720 | tf_op jit(solution)/shard_map/ppermute | solution.py:1141
  140.8 0.5 collective-permute-start.32
  141.7 4.2 %collective-permute-done.32.refs_2_ = bf16[896,128]{1,0:T(8,128)(2,1)S(1)} collective-permute-done((bf16[896,128]{1,0:T(8,128)(2,1)S(1)}, bf16[896,128]{1,0:T(8,128)(2,1)S(1)}, u32[]{:S(2)}, u32[]{:S(2)}) %collective-permute-start.32) | collective-permute-done | bytes 229408 | tf_op jit(solution)/shard_map/ppermute | solution.py:1141
  146.3 7.0 %collective-permute-start.35 = (f32[2,512,512]{2,1,0:T(8,128)S(1)}, f32[2,512,512]{2,1,0:T(8,128)S(1)}, u32[]{:S(2)}, u32[]{:S(2)}) collective-permute-start(f32[2,512,512]{2,1,0:T(8,128)S(1)} %get-tuple-element.280.refs_1_), channel_id=1, source_target_pairs={{0,16},{16,0},{1,17},{17,1},{2,18},{18,2},{3,19},{19,3},{4,20},{20... | collective-permute-start | bytes 6291464 | tf_op jit(solution)/shard_map/ppermute | solution.py:1136
  153.2 0.7 collective-permute-start.37
  154.0 1.7 collective-permute-start.38
  155.7 0.7 collective-permute-start.36
  156.5 2.0 %unpack_one.1 = (f32[8,128]{1,0:T(8,128)S(1)}, f32[2,1,768,512]{3,2,1,0:T(8,128)}, f32[2,1,512,768]{3,2,1,0:T(8,128)}) custom-call(f32[8,128]{1,0:T(8,128)S(1)} %get-tuple-element.276.refs_0_, bf16[1792,128]{1,0:T(8,128)(2,1)S(1)} %get-tuple-element.267.refs_1_, bf16[1792,128]{1,0:T(8,128)(2,1)S(1)} %collective-permute-done.27.refs_0_.refs_2_, ...), custom_call_target="tpu_custom_call" | custom-call | flops 1 | bytes 1 | tf_op jit(solution)/shard_map/unpack_one/pallas_call | solution.py:1120
  158.5 0.6 small_out.1
  159.2 2.3 %join.1 = (f32[8,128]{1,0:T(8,128)S(1)}, f32[1024,512]{1,0:T(8,128)}, f32[1024,512]{1,0:T(8,128)}) custom-call(f32[8,128]{1,0:T(8,128)S(1)} %get-tuple-element.279.refs_0_, f32[2,512,512]{2,1,0:T(8,128)S(1)} %get-tuple-element.280.refs_1_, f32[2,512,512]{2,1,0:T(8,128)S(1)} %collective-permute-done.35.refs_2_), custom_call_target="tpu_custom_call" | custom-call | flops 1 | bytes 1 | tf_op jit(solution)/shard_map/join/pallas_call | solution.py:1120
  161.5 1.1 gate_out_one.1
  162.6 2.7 %collective-permute-done.37.refs_2_ = bf16[1792,128]{1,0:T(8,128)(2,1)S(1)} collective-permute-done((bf16[1792,128]{1,0:T(8,128)(2,1)S(1)}, bf16[1792,128]{1,0:T(8,128)(2,1)S(1)}, u32[]{:S(2)}, u32[]{:S(2)}) %collective-permute-start.37) | collective-permute-done | bytes 458784 | tf_op jit(solution)/shard_map/ppermute | solution.py:1141
  165.3 0.8 collective-permute-done.38.refs_4_
  166.3 1.0 collective-permute-start.39
  167.3 2.0 %unpack_zero.1 = (f32[8,128]{1,0:T(8,128)S(1)}, f32[2,1,768,512]{3,2,1,0:T(8,128)}, f32[2,1,512,768]{3,2,1,0:T(8,128)}) custom-call(f32[8,128]{1,0:T(8,128)S(1)} %get-tuple-element.290.refs_0_, bf16[1792,128]{1,0:T(8,128)(2,1)S(1)} %get-tuple-element.288.refs_1_, ...), custom_call_target="tpu_custom_call", output_to_operand_aliasing={{1}: (5, {}), {2}: (6, {})} | custom-call | flops 1 | bytes 1 | tf_op jit(solution)/shard_map/unpack_zero/pallas_call | solution.py:1120
  169.3 1.7 gate_out_zero.1
  (73 shorter events, 3.9 us)
Async XLA Ops:
  0.6 6.0 %copy-start = (bf16[2,1,512,768]{3,2,1,0:T(8,128)(2,1)S(1)}, bf16[2,1,512,768]{3,2,1,0:T(8,128)(2,1)}, u32[]{:S(2)}) copy-start(bf16[2,1,512,768]{3,2,1,0:T(8,128)(2,1)} %refs_3_.1) | copy-start | bytes 4718596
  0.7 6.0 %copy-start.10 = (f32[2,1,384]{2,1,0:T(1,128)S(1)}, f32[2,1,384]{2,1,0:T(1,128)}, u32[]{:S(2)}) copy-start(f32[2,1,384]{2,1,0:T(1,128)} %refs_6_.1) | copy-start | bytes 9220
  0.7 6.0 %copy-start.8 = (f32[2,1,2,384]{3,2,1,0:T(2,128)S(1)}, f32[2,1,2,384]{3,2,1,0:T(2,128)}, u32[]{:S(2)}) copy-start(f32[2,1,2,384]{3,2,1,0:T(2,128)} %refs_7_.1) | copy-start | bytes 18436
  0.7 6.0 %copy-start.4 = (f32[2,512]{1,0:T(2,128)S(1)}, f32[2,512]{1,0:T(2,128)}, u32[]{:S(2)}) copy-start(f32[2,512]{1,0:T(2,128)} %refs_9_.3) | copy-start | bytes 12292
  0.7 6.0 %copy-start.6 = (f32[2,512]{1,0:T(2,128)S(1)}, f32[2,512]{1,0:T(2,128)}, u32[]{:S(2)}) copy-start(f32[2,512]{1,0:T(2,128)} %refs_18_.5) | copy-start | bytes 12292
  0.7 6.0 %copy-start.9 = (s32[1024]{0:T(1024)S(1)}, s32[1024]{0:T(1024)}, u32[]{:S(2)}) copy-start(s32[1024]{0:T(1024)} %param.13) | copy-start | bytes 12292
  0.7 6.0 %collective-permute-start = (bf16[2,1,768,512]{3,2,1,0:T(8,128)(2,1)}, bf16[2,1,768,512]{3,2,1,0:T(8,128)(2,1)S(1)}, u32[]{:S(2)}, u32[]{:S(2)}) collective-permute-start(bf16[2,1,768,512]{3,2,1,0:T(8,128)(2,1)} %refs_11_.1), channel_id=1, source_target_pairs={{0,16},{16,0},{1,17},{17,1},{2,18},{18,2},{3,19},{19,3},{4,20},{20... | collective-permute-start | bytes 4718600 | tf_op jit(solution)/shard_map/ppermute | solution.py:1136
  0.8 5.8 %collective-permute-start.3 = (bf16[2,1,512,768]{3,2,1,0:T(8,128)(2,1)}, bf16[2,1,512,768]{3,2,1,0:T(8,128)(2,1)S(1)}, u32[]{:S(2)}, u32[]{:S(2)}) collective-permute-start(bf16[2,1,512,768]{3,2,1,0:T(8,128)(2,1)} %refs_3_.1), channel_id=1, source_target_pairs={{0,16},{16,0},{1,17},{17,1},{2,18},{18,2},{3,19},{19,3},{4,20},{20... | collective-permute-start | bytes 4718600 | tf_op jit(solution)/shard_map/ppermute | solution.py:1136
  1.3 5.4 %collective-permute-start.1 = (f32[2,1,384]{2,1,0:T(1,128)}, f32[2,1,384]{2,1,0:T(1,128)S(1)}, u32[]{:S(2)}, u32[]{:S(2)}) collective-permute-start(f32[2,1,384]{2,1,0:T(1,128)} %refs_6_.1), channel_id=1, source_target_pairs={{0,16},{16,0},{1,17},{17,1},{2,18},{18,2},{3,19},{19,3},{4,20},{20... | collective-permute-start | bytes 9224 | tf_op jit(solution)/shard_map/ppermute | solution.py:1136
  1.4 5.3 %collective-permute-start.2 = (f32[2,1,2,384]{3,2,1,0:T(2,128)}, f32[2,1,2,384]{3,2,1,0:T(2,128)S(1)}, u32[]{:S(2)}, u32[]{:S(2)}) collective-permute-start(f32[2,1,2,384]{3,2,1,0:T(2,128)} %refs_7_.1), channel_id=1, source_target_pairs={{0,16},{16,0},{1,17},{17,1},{2,18},{18,2},{3,19},{19,3},{4,20},{20... | collective-permute-start | bytes 18440 | tf_op jit(solution)/shard_map/ppermute | solution.py:1136
  1.8 1.2 copy-start.11
  6.7 17.0 %copy-start.1 = (bf16[2,1,768,512]{3,2,1,0:T(8,128)(2,1)S(1)}, bf16[2,1,768,512]{3,2,1,0:T(8,128)(2,1)}, u32[]{:S(2)}) copy-start(bf16[2,1,768,512]{3,2,1,0:T(8,128)(2,1)} %refs_11_.1) | copy-start | bytes 4718596
  6.7 17.0 %copy-start.2 = (bf16[2,512,512]{2,1,0:T(8,128)(2,1)S(1)}, bf16[2,512,512]{2,1,0:T(8,128)(2,1)}, u32[]{:S(2)}) copy-start(bf16[2,512,512]{2,1,0:T(8,128)(2,1)} %refs_20_.5) | copy-start | bytes 3145732
  6.7 16.9 %copy-start.5 = (f32[2,512]{1,0:T(2,128)S(1)}, f32[2,512]{1,0:T(2,128)}, u32[]{:S(2)}) copy-start(f32[2,512]{1,0:T(2,128)} %refs_10_.3) | copy-start | bytes 12292
  6.8 16.9 %copy-start.7 = (f32[2,512]{1,0:T(2,128)S(1)}, f32[2,512]{1,0:T(2,128)}, u32[]{:S(2)}) copy-start(f32[2,512]{1,0:T(2,128)} %refs_20_.4) | copy-start | bytes 12292
  23.7 14.4 %copy-start.3 = (f32[1024,512]{1,0:T(8,128)S(1)}, f32[1024,512]{1,0:T(8,128)}, u32[]{:S(2)}) copy-start(f32[1024,512]{1,0:T(8,128)} %refs_21_.3) | copy-start | bytes 6291460
  44.6 10.2 %collective-permute-start.4 = (bf16[4096,128]{1,0:T(8,128)(2,1)S(1)}, bf16[4096,128]{1,0:T(8,128)(2,1)S(1)}, u32[]{:S(2)}, u32[]{:S(2)}) collective-permute-start(bf16[4096,128]{1,0:T(8,128)(2,1)S(1)} %get-tuple-element.180), channel_id=1, source_target_pairs={{0,16},{16,0},{1,17},{17,1},{2,18},{18,2},{3,19},{19,3},{4,20},{20... | collective-permute-start | bytes 3145736 | tf_op jit(solution)/shard_map/ppermute | solution.py:1136
  57.6 5.8 %collective-permute-start.5 = (bf16[3072,128]{1,0:T(8,128)(2,1)S(1)}, bf16[3072,128]{1,0:T(8,128)(2,1)S(1)}, u32[]{:S(2)}, u32[]{:S(2)}) collective-permute-start(bf16[3072,128]{1,0:T(8,128)(2,1)S(1)} %get-tuple-element.205), channel_id=1, source_target_pairs={{0,16},{16,0},{1,17},{17,1},{2,18},{18,2},{3,19},{19,3},{4,20},{20... | collective-permute-start | bytes 2359304 | tf_op jit(solution)/shard_map/ppermute | solution.py:1136
  63.1 15.2 %collective-permute-start.8 = (bf16[4096,128]{1,0:T(8,128)(2,1)S(1)}, bf16[4096,128]{1,0:T(8,128)(2,1)S(1)}, u32[]{:S(2)}, u32[]{:S(2)}) collective-permute-start(bf16[4096,128]{1,0:T(8,128)(2,1)S(1)} %get-tuple-element.208), channel_id=1, source_target_pairs={{0,16},{16,0},{1,17},{17,1},{2,18},{18,2},{3,19},{19,3},{4,20},{20... | collective-permute-start | bytes 3145736 | tf_op jit(solution)/shard_map/ppermute | solution.py:1136
  64.3 13.9 %collective-permute-start.6 = (bf16[1792,128]{1,0:T(8,128)(2,1)S(1)}, bf16[1792,128]{1,0:T(8,128)(2,1)S(1)}, u32[]{:S(2)}, u32[]{:S(2)}) collective-permute-start(bf16[1792,128]{1,0:T(8,128)(2,1)S(1)} %get-tuple-element.206), channel_id=1, source_target_pairs={{0,1},{1,0},{2,3},{3,2},{4,5},{5,4},{6,7},{7,6},{8,9},{9,8},{10,11... | collective-permute-start | bytes 1376264 | tf_op jit(solution)/shard_map/ppermute | solution.py:1141
  64.4 13.9 %collective-permute-start.7 = (bf16[1792,128]{1,0:T(8,128)(2,1)S(1)}, bf16[1792,128]{1,0:T(8,128)(2,1)S(1)}, u32[]{:S(2)}, u32[]{:S(2)}) collective-permute-start(bf16[1792,128]{1,0:T(8,128)(2,1)S(1)} %get-tuple-element.207), channel_id=1, source_target_pairs={{0,2},{1,3},{2,0},{3,1},{4,6},{5,7},{6,4},{7,5},{8,10},{9,11},{10,... | collective-permute-start | bytes 1376264 | tf_op jit(solution)/shard_map/ppermute | solution.py:1141
  81.2 8.7 %collective-permute-start.11 = (bf16[3072,128]{1,0:T(8,128)(2,1)S(1)}, bf16[3072,128]{1,0:T(8,128)(2,1)S(1)}, u32[]{:S(2)}, u32[]{:S(2)}) collective-permute-start(bf16[3072,128]{1,0:T(8,128)(2,1)S(1)} %get-tuple-element.236), channel_id=1, source_target_pairs={{0,16},{16,0},{1,17},{17,1},{2,18},{18,2},{3,19},{19,3},{4,20},{20... | collective-permute-start | bytes 2359304 | tf_op jit(solution)/shard_map/ppermute | solution.py:1136
  81.9 7.3 %collective-permute-start.9 = (bf16[896,128]{1,0:T(8,128)(2,1)S(1)}, bf16[896,128]{1,0:T(8,128)(2,1)S(1)}, u32[]{:S(2)}, u32[]{:S(2)}) collective-permute-start(bf16[896,128]{1,0:T(8,128)(2,1)S(1)} %get-tuple-element.230), channel_id=1, source_target_pairs={{0,2},{1,3},{2,0},{3,1},{4,6},{5,7},{6,4},{7,5},{8,10},{9,11},{10,... | collective-permute-start | bytes 688136 | tf_op jit(solution)/shard_map/ppermute | solution.py:1141
  83.0 6.8 %collective-permute-start.10 = (bf16[896,128]{1,0:T(8,128)(2,1)S(1)}, bf16[896,128]{1,0:T(8,128)(2,1)S(1)}, u32[]{:S(2)}, u32[]{:S(2)}) collective-permute-start(bf16[896,128]{1,0:T(8,128)(2,1)S(1)} %get-tuple-element.232), channel_id=1, source_target_pairs={{0,1},{1,0},{2,3},{3,2},{4,5},{5,4},{6,7},{7,6},{8,9},{9,8},{10,11... | collective-permute-start | bytes 688136 | tf_op jit(solution)/shard_map/ppermute | solution.py:1141
  91.0 11.6 %collective-permute-start.15 = (bf16[1872,128]{1,0:T(8,128)(2,1)S(1)}, bf16[1872,128]{1,0:T(8,128)(2,1)S(1)}, u32[]{:S(2)}, u32[]{:S(2)}) collective-permute-start(bf16[1872,128]{1,0:T(8,128)(2,1)S(1)} %get-tuple-element.249), channel_id=1, source_target_pairs={{0,1},{1,0},{2,3},{3,2},{4,5},{5,4},{6,7},{7,6},{8,9},{9,8},{10,11... | collective-permute-start | bytes 1437704 | tf_op jit(solution)/shard_map/ppermute | solution.py:1141
  91.8 10.7 %collective-permute-start.16 = (bf16[1792,128]{1,0:T(8,128)(2,1)S(1)}, bf16[1792,128]{1,0:T(8,128)(2,1)S(1)}, u32[]{:S(2)}, u32[]{:S(2)}) collective-permute-start(bf16[1792,128]{1,0:T(8,128)(2,1)S(1)} %get-tuple-element.251), channel_id=1, source_target_pairs={{0,2},{1,3},{2,0},{3,1},{4,6},{5,7},{6,4},{7,5},{8,10},{9,11},{10,... | collective-permute-start | bytes 1376264 | tf_op jit(solution)/shard_map/ppermute | solution.py:1141
  93.0 5.0 %collective-permute-start.12 = (bf16[448,128]{1,0:T(8,128)(2,1)S(1)}, bf16[448,128]{1,0:T(8,128)(2,1)S(1)}, u32[]{:S(2)}, u32[]{:S(2)}) collective-permute-start(bf16[448,128]{1,0:T(8,128)(2,1)S(1)} %get-tuple-element.244), channel_id=1, source_target_pairs={{0,4},{1,5},{2,6},{3,7},{4,0},{5,1},{6,2},{7,3},{8,12},{9,13},{10,... | collective-permute-start | bytes 344072 | tf_op jit(solution)/shard_map/ppermute | solution.py:1141
  93.2 4.9 %collective-permute-start.13 = (bf16[448,128]{1,0:T(8,128)(2,1)S(1)}, bf16[448,128]{1,0:T(8,128)(2,1)S(1)}, u32[]{:S(2)}, u32[]{:S(2)}) collective-permute-start(bf16[448,128]{1,0:T(8,128)(2,1)S(1)} %get-tuple-element.245), channel_id=1, source_target_pairs={{0,8},{1,9},{2,10},{3,11},{4,12},{5,13},{6,14},{7,15},{8,0},{9,1},... | collective-permute-start | bytes 344072 | tf_op jit(solution)/shard_map/ppermute | solution.py:1141
  94.1 8.1 %collective-permute-start.14 = (bf16[448,128]{1,0:T(8,128)(2,1)S(1)}, bf16[448,128]{1,0:T(8,128)(2,1)S(1)}, u32[]{:S(2)}, u32[]{:S(2)}) collective-permute-start(bf16[448,128]{1,0:T(8,128)(2,1)S(1)} %get-tuple-element.246), channel_id=1, source_target_pairs={{0,12},{1,13},{2,14},{3,15},{4,8},{5,9},{6,10},{7,11},{8,4},{9,5},... | collective-permute-start | bytes 344072 | tf_op jit(solution)/shard_map/ppermute | solution.py:1141
  102.8 5.9 %collective-permute-start.17 = (bf16[976,128]{1,0:T(8,128)(2,1)S(1)}, bf16[976,128]{1,0:T(8,128)(2,1)S(1)}, u32[]{:S(2)}, u32[]{:S(2)}) collective-permute-start(bf16[976,128]{1,0:T(8,128)(2,1)S(1)} %get-tuple-element.254), channel_id=1, source_target_pairs={{0,2},{1,3},{2,0},{3,1},{4,6},{5,7},{6,4},{7,5},{8,10},{9,11},{10,... | collective-permute-start | bytes 749576 | tf_op jit(solution)/shard_map/ppermute | solution.py:1141
  103.9 4.9 %collective-permute-start.18 = (bf16[896,128]{1,0:T(8,128)(2,1)S(1)}, bf16[896,128]{1,0:T(8,128)(2,1)S(1)}, u32[]{:S(2)}, u32[]{:S(2)}) collective-permute-start(bf16[896,128]{1,0:T(8,128)(2,1)S(1)} %get-tuple-element.256), channel_id=1, source_target_pairs={{0,1},{1,0},{2,3},{3,2},{4,5},{5,4},{6,7},{7,6},{8,9},{9,8},{10,11... | collective-permute-start | bytes 688136 | tf_op jit(solution)/shard_map/ppermute | solution.py:1141
  104.6 5.5 %collective-permute-start.21 = (bf16[448,128]{1,0:T(8,128)(2,1)S(1)}, bf16[448,128]{1,0:T(8,128)(2,1)S(1)}, u32[]{:S(2)}, u32[]{:S(2)}) collective-permute-start(bf16[448,128]{1,0:T(8,128)(2,1)S(1)} %get-tuple-element.258.refs_1_), channel_id=1, source_target_pairs={{0,12},{1,13},{2,14},{3,15},{4,8},{5,9},{6,10},{7,11},{8,4},{9,5},... | collective-permute-start | bytes 344072 | tf_op jit(solution)/shard_map/ppermute | solution.py:1141
  105.5 12.6 %collective-permute-start.20 = (bf16[448,128]{1,0:T(8,128)(2,1)S(1)}, bf16[448,128]{1,0:T(8,128)(2,1)S(1)}, u32[]{:S(2)}, u32[]{:S(2)}) collective-permute-start(bf16[448,128]{1,0:T(8,128)(2,1)S(1)} %get-tuple-element.258.refs_1_), channel_id=1, source_target_pairs={{0,8},{1,9},{2,10},{3,11},{4,12},{5,13},{6,14},{7,15},{8,0},{9,1},... | collective-permute-start | bytes 344072 | tf_op jit(solution)/shard_map/ppermute | solution.py:1141
  107.7 10.3 %collective-permute-start.19 = (bf16[448,128]{1,0:T(8,128)(2,1)S(1)}, bf16[448,128]{1,0:T(8,128)(2,1)S(1)}, u32[]{:S(2)}, u32[]{:S(2)}) collective-permute-start(bf16[448,128]{1,0:T(8,128)(2,1)S(1)} %get-tuple-element.258.refs_1_), channel_id=1, source_target_pairs={{0,4},{1,5},{2,6},{3,7},{4,0},{5,1},{6,2},{7,3},{8,12},{9,13},{10,... | collective-permute-start | bytes 344072 | tf_op jit(solution)/shard_map/ppermute | solution.py:1141
  118.1 10.7 %collective-permute-start.25 = (bf16[896,128]{1,0:T(8,128)(2,1)S(1)}, bf16[896,128]{1,0:T(8,128)(2,1)S(1)}, u32[]{:S(2)}, u32[]{:S(2)}) collective-permute-start(bf16[896,128]{1,0:T(8,128)(2,1)S(1)} %get-tuple-element.265.refs_1_), channel_id=1, source_target_pairs={{0,2},{1,3},{2,0},{3,1},{4,6},{5,7},{6,4},{7,5},{8,10},{9,11},{10,... | collective-permute-start | bytes 688136 | tf_op jit(solution)/shard_map/ppermute | solution.py:1141
  118.6 10.2 %collective-permute-start.26 = (bf16[896,128]{1,0:T(8,128)(2,1)S(1)}, bf16[896,128]{1,0:T(8,128)(2,1)S(1)}, u32[]{:S(2)}, u32[]{:S(2)}) collective-permute-start(bf16[896,128]{1,0:T(8,128)(2,1)S(1)} %get-tuple-element.266.refs_3_), channel_id=1, source_target_pairs={{0,1},{1,0},{2,3},{3,2},{4,5},{5,4},{6,7},{7,6},{8,9},{9,8},{10,11... | collective-permute-start | bytes 688136 | tf_op jit(solution)/shard_map/ppermute | solution.py:1141
  119.0 5.8 %collective-permute-start.22 = (bf16[528,128]{1,0:T(8,128)(2,1)S(1)}, bf16[528,128]{1,0:T(8,128)(2,1)S(1)}, u32[]{:S(2)}, u32[]{:S(2)}) collective-permute-start(bf16[528,128]{1,0:T(8,128)(2,1)S(1)} %get-tuple-element.261), channel_id=1, source_target_pairs={{0,4},{1,5},{2,6},{3,7},{4,0},{5,1},{6,2},{7,3},{8,12},{9,13},{10,... | collective-permute-start | bytes 405512 | tf_op jit(solution)/shard_map/ppermute | solution.py:1141
  119.0 5.8 %collective-permute-start.23 = (bf16[528,128]{1,0:T(8,128)(2,1)S(1)}, bf16[528,128]{1,0:T(8,128)(2,1)S(1)}, u32[]{:S(2)}, u32[]{:S(2)}) collective-permute-start(bf16[528,128]{1,0:T(8,128)(2,1)S(1)} %get-tuple-element.262), channel_id=1, source_target_pairs={{0,8},{1,9},{2,10},{3,11},{4,12},{5,13},{6,14},{7,15},{8,0},{9,1},... | collective-permute-start | bytes 405512 | tf_op jit(solution)/shard_map/ppermute | solution.py:1141
  119.5 9.2 %collective-permute-start.24 = (bf16[528,128]{1,0:T(8,128)(2,1)S(1)}, bf16[528,128]{1,0:T(8,128)(2,1)S(1)}, u32[]{:S(2)}, u32[]{:S(2)}) collective-permute-start(bf16[528,128]{1,0:T(8,128)(2,1)S(1)} %get-tuple-element.263), channel_id=1, source_target_pairs={{0,12},{1,13},{2,14},{3,15},{4,8},{5,9},{6,10},{7,11},{8,4},{9,5},... | collective-permute-start | bytes 405512 | tf_op jit(solution)/shard_map/ppermute | solution.py:1141
  128.9 11.9 %collective-permute-start.27 = (bf16[1792,128]{1,0:T(8,128)(2,1)S(1)}, bf16[1792,128]{1,0:T(8,128)(2,1)S(1)}, u32[]{:S(2)}, u32[]{:S(2)}) collective-permute-start(bf16[1792,128]{1,0:T(8,128)(2,1)S(1)} %get-tuple-element.267.refs_1_), channel_id=1, source_target_pairs={{0,1},{1,0},{2,3},{3,2},{4,5},{5,4},{6,7},{7,6},{8,9},{9,8},{10,11... | collective-permute-start | bytes 1376264 | tf_op jit(solution)/shard_map/ppermute | solution.py:1141
  129.3 11.5 %collective-permute-start.28 = (bf16[1792,128]{1,0:T(8,128)(2,1)S(1)}, bf16[1792,128]{1,0:T(8,128)(2,1)S(1)}, u32[]{:S(2)}, u32[]{:S(2)}) collective-permute-start(bf16[1792,128]{1,0:T(8,128)(2,1)S(1)} %get-tuple-element.268.refs_3_), channel_id=1, source_target_pairs={{0,2},{1,3},{2,0},{3,1},{4,6},{5,7},{6,4},{7,5},{8,10},{9,11},{10,... | collective-permute-start | bytes 1376264 | tf_op jit(solution)/shard_map/ppermute | solution.py:1141
  130.7 5.4 %collective-permute-start.31 = (bf16[448,128]{1,0:T(8,128)(2,1)S(1)}, bf16[448,128]{1,0:T(8,128)(2,1)S(1)}, u32[]{:S(2)}, u32[]{:S(2)}) collective-permute-start(bf16[448,128]{1,0:T(8,128)(2,1)S(1)} %get-tuple-element.270.refs_3_), channel_id=1, source_target_pairs={{0,12},{1,13},{2,14},{3,15},{4,8},{5,9},{6,10},{7,11},{8,4},{9,5},... | collective-permute-start | bytes 344072 | tf_op jit(solution)/shard_map/ppermute | solution.py:1141
  132.3 8.4 %collective-permute-start.30 = (bf16[448,128]{1,0:T(8,128)(2,1)S(1)}, bf16[448,128]{1,0:T(8,128)(2,1)S(1)}, u32[]{:S(2)}, u32[]{:S(2)}) collective-permute-start(bf16[448,128]{1,0:T(8,128)(2,1)S(1)} %get-tuple-element.270.refs_3_), channel_id=1, source_target_pairs={{0,8},{1,9},{2,10},{3,11},{4,12},{5,13},{6,14},{7,15},{8,0},{9,1},... | collective-permute-start | bytes 344072 | tf_op jit(solution)/shard_map/ppermute | solution.py:1141
  136.1 4.7 %collective-permute-start.29 = (bf16[448,128]{1,0:T(8,128)(2,1)S(1)}, bf16[448,128]{1,0:T(8,128)(2,1)S(1)}, u32[]{:S(2)}, u32[]{:S(2)}) collective-permute-start(bf16[448,128]{1,0:T(8,128)(2,1)S(1)} %get-tuple-element.270.refs_3_), channel_id=1, source_target_pairs={{0,4},{1,5},{2,6},{3,7},{4,0},{5,1},{6,2},{7,3},{8,12},{9,13},{10,... | collective-permute-start | bytes 344072 | tf_op jit(solution)/shard_map/ppermute | solution.py:1141
  140.8 5.1 %collective-permute-start.32 = (bf16[896,128]{1,0:T(8,128)(2,1)S(1)}, bf16[896,128]{1,0:T(8,128)(2,1)S(1)}, u32[]{:S(2)}, u32[]{:S(2)}) collective-permute-start(bf16[896,128]{1,0:T(8,128)(2,1)S(1)} %get-tuple-element.272.refs_1_), channel_id=1, source_target_pairs={{0,2},{1,3},{2,0},{3,1},{4,6},{5,7},{6,4},{7,5},{8,10},{9,11},{10,... | collective-permute-start | bytes 688136 | tf_op jit(solution)/shard_map/ppermute | solution.py:1141
  141.3 4.9 %collective-permute-start.33 = (bf16[896,128]{1,0:T(8,128)(2,1)S(1)}, bf16[896,128]{1,0:T(8,128)(2,1)S(1)}, u32[]{:S(2)}, u32[]{:S(2)}) collective-permute-start(bf16[896,128]{1,0:T(8,128)(2,1)S(1)} %get-tuple-element.273.refs_3_), channel_id=1, source_target_pairs={{0,1},{1,0},{2,3},{3,2},{4,5},{5,4},{6,7},{7,6},{8,9},{9,8},{10,11... | collective-permute-start | bytes 688136 | tf_op jit(solution)/shard_map/ppermute | solution.py:1141
  146.3 12.9 %collective-permute-start.35 = (f32[2,512,512]{2,1,0:T(8,128)S(1)}, f32[2,512,512]{2,1,0:T(8,128)S(1)}, u32[]{:S(2)}, u32[]{:S(2)}) collective-permute-start(f32[2,512,512]{2,1,0:T(8,128)S(1)} %get-tuple-element.280.refs_1_), channel_id=1, source_target_pairs={{0,16},{16,0},{1,17},{17,1},{2,18},{18,2},{3,19},{19,3},{4,20},{20... | collective-permute-start | bytes 6291464 | tf_op jit(solution)/shard_map/ppermute | solution.py:1136
  153.2 12.1 %collective-permute-start.37 = (bf16[1792,128]{1,0:T(8,128)(2,1)S(1)}, bf16[1792,128]{1,0:T(8,128)(2,1)S(1)}, u32[]{:S(2)}, u32[]{:S(2)}) collective-permute-start(bf16[1792,128]{1,0:T(8,128)(2,1)S(1)} %get-tuple-element.288.refs_1_), channel_id=1, source_target_pairs={{0,1},{1,0},{2,3},{3,2},{4,5},{5,4},{6,7},{7,6},{8,9},{9,8},{10,11... | collective-permute-start | bytes 1376264 | tf_op jit(solution)/shard_map/ppermute | solution.py:1141
  154.0 12.2 %collective-permute-start.38 = (bf16[1792,128]{1,0:T(8,128)(2,1)S(1)}, bf16[1792,128]{1,0:T(8,128)(2,1)S(1)}, u32[]{:S(2)}, u32[]{:S(2)}) collective-permute-start(bf16[1792,128]{1,0:T(8,128)(2,1)S(1)} %get-tuple-element.289.refs_3_), channel_id=1, source_target_pairs={{0,2},{1,3},{2,0},{3,1},{4,6},{5,7},{6,4},{7,5},{8,10},{9,11},{10,... | collective-permute-start | bytes 1376264 | tf_op jit(solution)/shard_map/ppermute | solution.py:1141
  155.7 5.7 %collective-permute-start.36 = (bf16[1024,128]{1,0:T(8,128)(2,1)S(1)}, bf16[1024,128]{1,0:T(8,128)(2,1)S(1)}, u32[]{:S(2)}, u32[]{:S(2)}) collective-permute-start(bf16[1024,128]{1,0:T(8,128)(2,1)S(1)} %get-tuple-element.286.refs_1_), channel_id=1, source_target_pairs={{0,16},{16,0},{1,17},{17,1},{2,18},{18,2},{3,19},{19,3},{4,20},{20... | collective-permute-start | bytes 786440 | tf_op jit(solution)/shard_map/ppermute | solution.py:1136
  156.4 2.1 %collective-permute-start.34 = (f32[80,128]{1,0:T(8,128)S(1)}, f32[80,128]{1,0:T(8,128)S(1)}, u32[]{:S(2)}, u32[]{:S(2)}) collective-permute-start(f32[80,128]{1,0:T(8,128)S(1)} %get-tuple-element.278.refs_1_), channel_id=1, source_target_pairs={{0,16},{16,0},{1,17},{17,1},{2,18},{18,2},{3,19},{19,3},{4,20},{20... | collective-permute-start | bytes 122888 | tf_op jit(solution)/shard_map/ppermute | solution.py:1136
  166.3 3.0 %collective-permute-start.39 = (bf16[1024,128]{1,0:T(8,128)(2,1)S(1)}, bf16[1024,128]{1,0:T(8,128)(2,1)S(1)}, u32[]{:S(2)}, u32[]{:S(2)}) collective-permute-start(bf16[1024,128]{1,0:T(8,128)(2,1)S(1)} %get-tuple-element.299.refs_1_), channel_id=1, source_target_pairs={{0,16},{16,0},{1,17},{17,1},{2,18},{18,2},{3,19},{19,3},{4,20},{20... | collective-permute-start | bytes 786440 | tf_op jit(solution)/shard_map/ppermute | solution.py:1136

commit v5 on v4

--- a/solution.py
+++ b/solution.py
@@ -148,14 +148,11 @@
         upward = running_up if side == 0 else jnp.logical_not(running_up)
         start = jnp.zeros((1, states), f32)
         re, im = run_chain(upward, lanes, side, ends[side], wholes[side], (start, start), None)
-        for i in range(thirds):
-            payload[side, i : i + 1, :] = re[:, LANES * i : LANES * (i + 1)]
-            payload[side, thirds + i : thirds + i + 1, :] = im[:, LANES * i : LANES * (i + 1)]
-        payload[side, 6:8, :] = ids_ref[0:2, :]
-    first, second = payload[0], payload[1]
+        rows = [part[:, LANES * i : LANES * (i + 1)] for part in (re, im) for i in range(thirds)]
+        tiles.append(jnp.concatenate(rows + [ids_ref[0:2, :]], 0))
     for i in range(payload.shape[0]):
         to_later = jnp.logical_xor(running_up, i < place)
-        payload[i] = jnp.where(to_later, first, second)
+        payload[i] = jnp.where(to_later, tiles[0], tiles[1]).astype(payload.dtype)
 
 
 def entering(upward, place, lanes, side, gathered, ids_ref, small):
@@ -171,9 +168,9 @@
         source = jnp.where(upward, place - distance, place + distance)
         inside = jnp.logical_and(source >= 0, source < count)
         source = jnp.clip(source, 0, count - 1)
-        sent_re = gathered[source, 0:thirds, :]
-        sent_im = gathered[source, thirds : 2 * thirds, :]
-        sent_key = gathered[source, pl.ds(jnp.where(upward, 7, 6), 1), :]
+        sent = gathered[source].astype(f32)
+        sent_re, sent_im = sent[0:thirds], sent[thirds : 2 * thirds]
+        sent_key = jnp.where(upward, sent[7:8], sent[6:7])
         joined = jnp.where(jnp.logical_and(sent_key == key, inside), 1.0, 0.0)
         re, im = (
             joined * sent_re + block_re * re - block_im * im,
@@ -1200,7 +1197,7 @@
     wide = ((rows, 2 * states), f32)
     wide_low = ((rows, 2 * states), bf16)
     ends = ((8, 2 * states), f32)
-    payload_shape = ((2 * row_devices, 8, LANES), f32)
+    payload_shape = ((2 * row_devices, 8, LANES), bf16)
     narrow = ((rows, LANES), f32)
     tile = ((8, LANES), f32)
     sums_shape = ((8, width), f32)
@@ -1309,20 +1306,23 @@
         )
         return [a_keep, across(a_send, 1), b_keep, across(b_send, 2)]
 
-    def from_first(parts, extra, name):
+    def from_first(parts, extra, name, after=()):
         a_keep, a_send, b_keep, b_send = order.run(
-            here(half_kernel, half), [low(half + extra)] * 2 + [low(half)] * 2, parts, name=name
+            here(half_kernel, half), [low(half + extra)] * 2 + [low(half)] * 2, parts, name=name, after=after
         )
         return [a_keep, across(a_send, 2), b_keep, across(b_send, 1)]
 
-    def from_second(parts, extra, name):
+    def from_second(parts, extra, name, cost=0):
         return sent(
-            order.run(here(plane_kernel, half, outer_half), [low(share_rows + extra)] * 4, parts, name=name), 2
+            order.run(
+                here(plane_kernel, half, outer_half), [low(share_rows + extra)] * 4, parts, name=name, cost=cost
+            ),
+            2,
         )
 
-    def gathered_half(parts, name, after=()):
+    def gathered_half(parts, name, after=(), cost=0):
         a_half, b_half = order.run(
-            here(gather_kernel, outer_half), [low(half)] * 2, parts, name=name, after=after
+            here(gather_kernel, outer_half), [low(half)] * 2, parts, name=name, after=after, cost=cost
         )
         return a_half, across(a_half, 2), b_half, across(b_half, 1)
 
@@ -1333,6 +1333,7 @@
     first = from_cores(first_outer + first_inner, 0, [], "first_cores")
     (payload,) = order.run(relay_kernel, [payload_shape], [payload], name="relay", cost=50)
     gathered = exchanged(payload, row_devices)
+    first = from_first(first, 0, "first_half", [gathered])
     in_low_own0, in_low_oth0, decay_sums0, mine, theirs = order.run(
         here(scan_kernel, 0, row_devices),
         [wide_low, wide_low, decay_shape, inner_pack, inner_pack],
@@ -1340,10 +1341,9 @@
          ids, low_own0, low_oth0, drive_own0, drive_oth0, mixed0],
         [places, tile, wide, wide],
         name="scan_zero",
-        after=[first[1], first[3], second_outer[1]],
+        after=[second_outer[1]],
     )
     second_inner = [mine, swap(theirs)]
-    first = from_first(first, 0, "first_half")
     halves, sums_last = order.run(
         final_kernel,
         [((2, rows, width), f32), sums_shape],
@@ -1351,16 +1351,16 @@
         [full, columns, columns],
         name="final_norm",
     )
-    first = from_second(first, 0, "first_plane")
+    first = from_second(first, 0, "first_plane", 50)
     second = from_cores(
         second_outer + second_inner, small_rows, [sums_turn, sums_back, sums_last, decay_sums0, decay_sums1],
         "second_cores",
     )
-    (share,) = order.run(planes_kernel, [low(share_rows)], first, name="first_planes")
+    (share,) = order.run(planes_kernel, [low(share_rows)], first, name="first_planes", cost=50)
     first = shared(beyond(share), 2)
     second = from_first(second, small_rows, "second_half")
+    first = gathered_half(first, "first_gather", cost=50)
     second = from_second(second, small_rows, "second_plane")
-    first = gathered_half(first, "first_gather")
     share, small = order.run(second_planes_kernel, [low(share_rows), small_shape], second, name="second_planes")
     second = shared(beyond(share), 2)
     first = gathered_whole(first, "first_pair")
@@ -1392,10 +1392,10 @@
             semaphores=2,
         )
 
-    second = gathered_half(second, "second_gather", [first[1], first[3]])
+    second = gathered_half(second, "second_gather", cost=50)
     halves, a_pair, b_pair = order.run(
         last_pair_kernel, [((2, rows, width), f32), low(2 * half), low(2 * half)], list(second) + [halves],
-        name="second_pair", free_outs=1, alias={4: 0},
+        name="second_pair", free_outs=1, alias={4: 0}, after=[first[1], first[3]],
     )
     second = [a_pair, across(a_pair, 1), b_pair, across(b_pair, 2)]
     gate_one = gate_part(first, "gate_one")

time: 171 us -> 161 us (0.942)
  waiting for transfers between devices: 40.1 us -> 35.9 us
  blocking collectives: 48.2 us -> 44.8 us
  starting transfers between devices: 39.5 us -> 36.7 us
    ppermute x28, waiting for transfers between devices: 37.4 us -> 33.2 us  [across(): return lax.ppermute(value, 'seq', [(i, i ^ bits) for i in range(count)])]
    all_to_all x4, blocking collectives: 48.2 us -> 44.8 us  [exchanged(): lax.all_to_all(payload, ('seq', 'dir'), 0, 0, tiled=True, axis_index_grou...]
    ppermute x12, starting transfers between devices: 11.3 us -> 9.44 us  [swap(): return lax.ppermute(value, 'dir', [(0, 1), (1, 0)])]
  transfers between devices with their start and end apart: 40 -> 40, of which waited for: 17 -> 12; matrix products, arithmetic and copies ran while one was open for 0% -> 0% of each run, Pallas kernels for 11% -> 15%
where the time goes in v5:
time: 161 us
  blocking collectives  44.8 us (28%)
  Pallas kernels  41.1 us (26%)
  starting transfers between devices  36.7 us (23%)
  waiting for transfers between devices  35.9 us (22%)
    all_to_all x4, blocking collectives, exchanged(): lax.all_to_all(payload, ('seq', 'dir'), 0, 0, tiled=True, axis_index_grou...  44.8 us
    pallas_call x29, Pallas kernels, run(): pl.pallas_call(body, out_shape=shapes, in_specs=specs, out_specs=[whole]...  41.1 us
    ppermute x28, waiting for transfers between devices, across(): return lax.ppermute(value, 'seq', [(i, i ^ bits) for i in range(count)])  33.2 us
    ppermute x28, starting transfers between devices, across(): return lax.ppermute(value, 'seq', [(i, i ^ bits) for i in range(count)])  27.2 us
    ppermute x12, starting transfers between devices, swap(): return lax.ppermute(value, 'dir', [(0, 1), (1, 0)])  9.44 us
  transfers between devices with their start and end apart: 40, of which 12 were waited for; matrix products, arithmetic and copies ran while one was open for 0% of the time, Pallas kernels for 15%

profile of v5, /device:TPU:1, one launch (start us, length us, event | category | flops | bytes accessed | tf_op | source)
XLA Modules:
  0.0 161.0 jit_solution(2625734675098352897)
XLA Ops:
  0.8 0.5 collective-permute-start.3
  1.4 0.4 collective-permute-start.2
  1.8 1.2 copy-done.11
  3.0 1.0 open_norm.1
  4.0 2.6 %collective-permute-done.1.refs_8_ = f32[2,1,384]{2,1,0:T(1,128)S(1)} collective-permute-done((f32[2,1,384]{2,1,0:T(1,128)}, f32[2,1,384]{2,1,0:T(1,128)S(1)}, u32[]{:S(2)}, u32[]{:S(2)}) %collective-permute-start.1) | collective-permute-done | bytes 3104 | tf_op jit(solution)/shard_map/ppermute | solution.py:1133
  6.8 1.8 %open_scan.1 = (f32[8,128]{1,0:T(8,128)S(1)}, bf16[512,512]{1,0:T(8,128)(2,1)S(1)}, f32[512,768]{1,0:T(8,128)S(1)}, f32[512,768]{1,0:T(8,128)S(1)}, f32[512,128]...) custom-call(bf16[2,1,768,512]{3,2,1,0:T(8,128)(2,1)S(1)} %collective, ...), custom_call_target="tpu_custom_call" | custom-call | flops 1 | bytes 1 | tf_op jit(solution)/shard_map/open_scan/pallas_call | solution.py:1117
  8.6 14.2 %all_to_all.20.refs_1_ = bf16[32,8,128]{2,1,0:T(8,128)(2,1)S(1)} all-to-all(bf16[32,8,128]{2,1,0:T(8,128)(2,1)S(1)} %get-tuple-element.160), channel_id=1, replica_groups=mesh['dir'=2,'seq'=16] {'seq','dir'}, dimensions={0} | all-to-all | bytes 131072 | tf_op jit(solution)/shard_map/all_to_all | solution.py:1155
  22.8 4.3 %mid.1 = (f32[8,128]{1,0:T(8,128)S(1)}, bf16[512,768]{1,0:T(8,128)(2,1)S(1)}, bf16[512,768]{1,0:T(8,128)(2,1)S(1)}, f32[512,512]{1,0:T(8,128)S(1)}, f32[512,512]...) custom-call(f32[8,128]{1,0:T(8,128)S(1)} %get-tuple-element.159.refs, ...), custom_call_target="tpu_custom_call" | custom-call | flops 1 | bytes 1 | tf_op jit(solution)/shard_map/mid/pallas_call | solution.py:1117
  27.1 9.1 %all_to_all.21.refs_1_ = bf16[32,8,128]{2,1,0:T(8,128)(2,1)S(1)} all-to-all(bf16[32,8,128]{2,1,0:T(8,128)(2,1)S(1)} %get-tuple-element.173), channel_id=1, replica_groups=mesh['dir'=2,'seq'=16] {'seq','dir'}, dimensions={0} | all-to-all | bytes 131072 | tf_op jit(solution)/shard_map/all_to_all | solution.py:1155
  36.2 6.5 %turn.1 = (f32[8,128]{1,0:T(8,128)S(1)}, bf16[512,768]{1,0:T(8,128)(2,1)S(1)}, bf16[512,768]{1,0:T(8,128)(2,1)S(1)}, f32[512,512]{1,0:T(8,128)S(1)}, f32[512,512...) custom-call(f32[8,128]{1,0:T(8,128)S(1)} %get-tuple-element.172.refs, ...), custom_call_target="tpu_custom_call" | custom-call | flops 1 | bytes 1 | tf_op jit(solution)/shard_map/turn/pallas_call | solution.py:1117
  42.8 0.5 collective-permute-start.4
  43.2 8.8 %all_to_all.22.refs_2_ = bf16[32,8,128]{2,1,0:T(8,128)(2,1)S(1)} all-to-all(bf16[32,8,128]{2,1,0:T(8,128)(2,1)S(1)} %get-tuple-element.182), channel_id=1, replica_groups=mesh['dir'=2,'seq'=16] {'seq','dir'}, dimensions={0} | all-to-all | bytes 131072 | tf_op jit(solution)/shard_map/all_to_all | solution.py:1155
  52.0 2.9 %scan_one.1 = (f32[8,128]{1,0:T(8,128)S(1)}, bf16[512,768]{1,0:T(8,128)(2,1)S(1)}, bf16[512,768]{1,0:T(8,128)(2,1)S(1)}, f32[8,384]{1,0:T(8,128)S(1)}, bf16[3072...) custom-call(bf16[4096,128]{1,0:T(8,128)(2,1)S(1)} %collective-permute-done.4.refs_0_.refs_2_, ...), custom_call_target="tpu_custom_call" | custom-call | flops 1 | bytes 1 | tf_op jit(solution)/shard_map/scan_one/pallas_call | solution.py:1117
  54.9 0.5 collective-permute-start.6
  55.4 5.2 %back.1 = (f32[8,128]{1,0:T(8,128)S(1)}, f32[512,512]{1,0:T(8,128)S(1)}, f32[512,512]{1,0:T(8,128)S(1)}, f32[512,768]{1,0:T(8,128)S(1)}, f32[512,768]{1,0:T(8,12...) custom-call(f32[8,128]{1,0:T(8,128)S(1)} %get-tuple-element.190.refs, ...), custom_call_target="tpu_custom_call" | custom-call | flops 1 | bytes 1 | tf_op jit(solution)/shard_map/back/pallas_call | solution.py:1117
  60.5 0.2 collective-permute-start.5
  60.7 1.0 first_cores.1
  61.7 0.2 collective-permute-start.7
  61.8 0.5 collective-permute-start.8
  62.3 12.7 %all_to_all.23.refs_0_.refs_2_ = bf16[32,8,128]{2,1,0:T(8,128)(2,1)S(1)} all-to-all(bf16[32,8,128]{2,1,0:T(8,128)(2,1)S(1)} %get-tuple-element.209), channel_id=1, replica_groups=mesh['dir'=2,'seq'=16] {'seq','dir'}, dimensions={0} | all-to-all | bytes 131072 | tf_op jit(solution)/shard_map/all_to_all | solution.py:1155
  75.0 0.2 first_half.1
  75.3 1.1 collective-permute-start.9
  76.4 0.5 collective-permute-start.10
  76.9 3.0 %scan_zero.1 = (f32[8,128]{1,0:T(8,128)S(1)}, bf16[512,768]{1,0:T(8,128)(2,1)S(1)}, bf16[512,768]{1,0:T(8,128)(2,1)S(1)}, f32[8,384]{1,0:T(8,128)S(1)}, bf16[307...) custom-call(bf16[4096,128]{1,0:T(8,128)(2,1)S(1)} %collective-permute-done.5.refs_0_.refs_2_, ...), custom_call_target="tpu_custom_call" | custom-call | flops 1 | bytes 1 | tf_op jit(solution)/shard_map/scan_zero/pallas_call | solution.py:1117
  79.9 1.0 collective-permute-start.11
  80.9 3.4 %final_norm.1 = (f32[8,128]{1,0:T(8,128)S(1)}, f32[2,512,512]{2,1,0:T(8,128)S(1)}, f32[8,512]{1,0:T(8,128)S(1)}) custom-call(f32[8,128]{1,0:T(8,128)S(1)} %get-tuple-element.221.refs_0_, bf16[512,768]{1,0:T(8,128)(2,1)S(1)} %get-tuple-element.222.refs_1_, bf16[512,768]{1,0:T(8,128)(2,1)S(1)} %get-tuple-element.223.refs_2_, ...), custom_call_target="tpu_custom_call" | custom-call | flops 1 | bytes 1 | tf_op jit(solution)/shard_map/final_norm/pallas_call | solution.py:1117
  84.5 0.4 collective-permute-start.12
  84.9 0.5 collective-permute-start.13
  85.4 2.7 %collective-permute-start.14 = (bf16[448,128]{1,0:T(8,128)(2,1)S(1)}, bf16[448,128]{1,0:T(8,128)(2,1)S(1)}, u32[]{:S(2)}, u32[]{:S(2)}) collective-permute-start(bf16[448,128]{1,0:T(8,128)(2,1)S(1)} %get-tuple-element.246), channel_id=1, source_target_pairs={{0,12},{1,13},{2,14},{3,15},{4,8},{5,9},{6,10},{7,11},{8,4},{9,5},... | collective-permute-start | bytes 344072 | tf_op jit(solution)/shard_map/ppermute | solution.py:1138
  88.1 1.1 second_cores.1
  89.2 1.2 collective-permute-start.16
  90.5 0.2 collective-permute-start.15
  90.6 4.5 %collective-permute-done.13.refs_3_ = bf16[448,128]{1,0:T(8,128)(2,1)S(1)} collective-permute-done((bf16[448,128]{1,0:T(8,128)(2,1)S(1)}, bf16[448,128]{1,0:T(8,128)(2,1)S(1)}, u32[]{:S(2)}, u32[]{:S(2)}) %collective-permute-start.13) | collective-permute-done | bytes 114720 | tf_op jit(solution)/shard_map/ppermute | solution.py:1138
  95.2 1.3 collective-permute-start.19
  96.6 2.7 %collective-permute-start.18 = (bf16[448,128]{1,0:T(8,128)(2,1)S(1)}, bf16[448,128]{1,0:T(8,128)(2,1)S(1)}, u32[]{:S(2)}, u32[]{:S(2)}) collective-permute-start(bf16[448,128]{1,0:T(8,128)(2,1)S(1)} %get-tuple-element.253.refs_1_), channel_id=1, source_target_pairs={{0,8},{1,9},{2,10},{3,11},{4,12},{5,13},{6,14},{7,15},{8,0},{9,1},... | collective-permute-start | bytes 344072 | tf_op jit(solution)/shard_map/ppermute | solution.py:1138
  99.2 1.2 collective-permute-done.16.refs_4_
  100.4 1.4 collective-permute-done.15.refs_2_
  101.8 0.2 second_half.1
  102.1 1.1 collective-permute-start.20
  103.2 5.6 %collective-permute-done.18.refs_3_ = bf16[448,128]{1,0:T(8,128)(2,1)S(1)} collective-permute-done((bf16[448,128]{1,0:T(8,128)(2,1)S(1)}, bf16[448,128]{1,0:T(8,128)(2,1)S(1)}, u32[]{:S(2)}, u32[]{:S(2)}) %collective-permute-start.18) | collective-permute-done | bytes 114720 | tf_op jit(solution)/shard_map/ppermute | solution.py:1138
  109.1 1.3 collective-permute-start.23
  110.4 2.2 %collective-permute-start.24 = (bf16[528,128]{1,0:T(8,128)(2,1)S(1)}, bf16[528,128]{1,0:T(8,128)(2,1)S(1)}, u32[]{:S(2)}, u32[]{:S(2)}) collective-permute-start(bf16[528,128]{1,0:T(8,128)(2,1)S(1)} %get-tuple-element.263), channel_id=1, source_target_pairs={{0,12},{1,13},{2,14},{3,15},{4,8},{5,9},{6,10},{7,11},{8,4},{9,5},... | collective-permute-start | bytes 405512 | tf_op jit(solution)/shard_map/ppermute | solution.py:1138
  112.6 1.1 collective-permute-start.25
  113.8 1.1 collective-permute-done.22.refs_2_
  114.8 3.9 %collective-permute-done.24.refs_4_ = bf16[528,128]{1,0:T(8,128)(2,1)S(1)} collective-permute-done((bf16[528,128]{1,0:T(8,128)(2,1)S(1)}, bf16[528,128]{1,0:T(8,128)(2,1)S(1)}, u32[]{:S(2)}, u32[]{:S(2)}) %collective-permute-start.24) | collective-permute-done | bytes 135200 | tf_op jit(solution)/shard_map/ppermute | solution.py:1138
  118.8 1.1 collective-permute-start.31
  119.9 4.0 %collective-permute-start.30 = (bf16[448,128]{1,0:T(8,128)(2,1)S(1)}, bf16[448,128]{1,0:T(8,128)(2,1)S(1)}, u32[]{:S(2)}, u32[]{:S(2)}) collective-permute-start(bf16[448,128]{1,0:T(8,128)(2,1)S(1)} %get-tuple-element.270.refs_1_), channel_id=1, source_target_pairs={{0,8},{1,9},{2,10},{3,11},{4,12},{5,13},{6,14},{7,15},{8,0},{9,1},... | collective-permute-start | bytes 344072 | tf_op jit(solution)/shard_map/ppermute | solution.py:1138
  124.0 0.6 collective-permute-start.27
  124.6 0.8 collective-permute-start.28
  125.4 5.2 %collective-permute-done.30.refs_3_ = bf16[448,128]{1,0:T(8,128)(2,1)S(1)} collective-permute-done((bf16[448,128]{1,0:T(8,128)(2,1)S(1)}, bf16[448,128]{1,0:T(8,128)(2,1)S(1)}, u32[]{:S(2)}, u32[]{:S(2)}) %collective-permute-start.30) | collective-permute-done | bytes 114720 | tf_op jit(solution)/shard_map/ppermute | solution.py:1138
  130.7 2.2 %collective-permute-start.32 = (bf16[896,128]{1,0:T(8,128)(2,1)S(1)}, bf16[896,128]{1,0:T(8,128)(2,1)S(1)}, u32[]{:S(2)}, u32[]{:S(2)}) collective-permute-start(bf16[896,128]{1,0:T(8,128)(2,1)S(1)} %get-tuple-element.272.refs_3_), channel_id=1, source_target_pairs={{0,2},{1,3},{2,0},{3,1},{4,6},{5,7},{6,4},{7,5},{8,10},{9,11},{10,... | collective-permute-start | bytes 688136 | tf_op jit(solution)/shard_map/ppermute | solution.py:1138
  132.9 6.2 %collective-permute-done.32.refs_4_ = bf16[896,128]{1,0:T(8,128)(2,1)S(1)} collective-permute-done((bf16[896,128]{1,0:T(8,128)(2,1)S(1)}, bf16[896,128]{1,0:T(8,128)(2,1)S(1)}, u32[]{:S(2)}, u32[]{:S(2)}) %collective-permute-start.32) | collective-permute-done | bytes 229408 | tf_op jit(solution)/shard_map/ppermute | solution.py:1138
  139.3 4.2 %collective-permute-start.35 = (f32[2,512,512]{2,1,0:T(8,128)S(1)}, f32[2,512,512]{2,1,0:T(8,128)S(1)}, u32[]{:S(2)}, u32[]{:S(2)}) collective-permute-start(f32[2,512,512]{2,1,0:T(8,128)S(1)} %get-tuple-element.280.refs_1_), channel_id=1, source_target_pairs={{0,16},{16,0},{1,17},{17,1},{2,18},{18,2},{3,19},{19,3},{4,20},{20... | collective-permute-start | bytes 6291464 | tf_op jit(solution)/shard_map/ppermute | solution.py:1133
  143.5 0.4 collective-permute-start.37
  143.9 0.9 collective-permute-start.38
  144.9 0.7 collective-permute-start.36
  145.7 2.0 %unpack_one.1 = (f32[8,128]{1,0:T(8,128)S(1)}, f32[2,1,768,512]{3,2,1,0:T(8,128)}, f32[2,1,512,768]{3,2,1,0:T(8,128)}) custom-call(f32[8,128]{1,0:T(8,128)S(1)} %get-tuple-element.276.refs_0_, bf16[1792,128]{1,0:T(8,128)(2,1)S(1)} %get-tuple-element.267.refs_1_, bf16[1792,128]{1,0:T(8,128)(2,1)S(1)} %collective-permute-done.27.refs_0_.refs_2_, ...), custom_call_target="tpu_custom_call" | custom-call | flops 1 | bytes 1 | tf_op jit(solution)/shard_map/unpack_one/pallas_call | solution.py:1117
  147.7 0.6 small_out.1
  148.4 2.3 %join.1 = (f32[8,128]{1,0:T(8,128)S(1)}, f32[1024,512]{1,0:T(8,128)}, f32[1024,512]{1,0:T(8,128)}) custom-call(f32[8,128]{1,0:T(8,128)S(1)} %get-tuple-element.279.refs_0_, f32[2,512,512]{2,1,0:T(8,128)S(1)} %get-tuple-element.280.refs_1_, f32[2,512,512]{2,1,0:T(8,128)S(1)} %collective-permute-done.35.refs_2_), custom_call_target="tpu_custom_call" | custom-call | flops 1 | bytes 1 | tf_op jit(solution)/shard_map/join/pallas_call | solution.py:1117
  150.7 1.1 gate_out_one.1
  151.8 3.8 %collective-permute-done.37.refs_2_ = bf16[1792,128]{1,0:T(8,128)(2,1)S(1)} collective-permute-done((bf16[1792,128]{1,0:T(8,128)(2,1)S(1)}, bf16[1792,128]{1,0:T(8,128)(2,1)S(1)}, u32[]{:S(2)}, u32[]{:S(2)}) %collective-permute-start.37) | collective-permute-done | bytes 458784 | tf_op jit(solution)/shard_map/ppermute | solution.py:1138
  155.8 1.2 collective-permute-start.39
  157.0 2.0 %unpack_zero.1 = (f32[8,128]{1,0:T(8,128)S(1)}, f32[2,1,768,512]{3,2,1,0:T(8,128)}, f32[2,1,512,768]{3,2,1,0:T(8,128)}) custom-call(f32[8,128]{1,0:T(8,128)S(1)} %get-tuple-element.290.refs_0_, bf16[1792,128]{1,0:T(8,128)(2,1)S(1)} %get-tuple-element.288.refs_1_, ...), custom_call_target="tpu_custom_call", output_to_operand_aliasing={{1}: (5, {}), {2}: (6, {})} | custom-call | flops 1 | bytes 1 | tf_op jit(solution)/shard_map/unpack_zero/pallas_call | solution.py:1117
  159.1 1.7 %gate_out_zero.1 = (f32[8,128]{1,0:T(8,128)}, f32[2,512,512]{2,1,0:T(8,128)}) custom-call(f32[8,128]{1,0:T(8,128)S(1)} %get-tuple-element.298.refs_0_, bf16[1024,128]{1,0:T(8,128)(2,1)S(1)} %get-tuple-element.299.refs_1_, bf16[1024,128]{1,0:T(8,128)(2,1)S(1)} %collective-permute-done.39.refs_2_, ...), custom_call_target="tpu_custom_call", output_to_operand_aliasing={{1}: (3, {})} | custom-call | flops 1 | bytes 1 | tf_op jit(solution)/shard_map/gate_out_zero/pallas_call | solution.py:1117
  (73 shorter events, 1.7 us)
Async XLA Ops:
  0.6 6.0 %copy-start = (bf16[2,1,512,768]{3,2,1,0:T(8,128)(2,1)S(1)}, bf16[2,1,512,768]{3,2,1,0:T(8,128)(2,1)}, u32[]{:S(2)}) copy-start(bf16[2,1,512,768]{3,2,1,0:T(8,128)(2,1)} %refs_3_.1) | copy-start | bytes 4718596
  0.7 6.0 %copy-start.10 = (f32[2,1,384]{2,1,0:T(1,128)S(1)}, f32[2,1,384]{2,1,0:T(1,128)}, u32[]{:S(2)}) copy-start(f32[2,1,384]{2,1,0:T(1,128)} %refs_6_.1) | copy-start | bytes 9220
  0.7 6.0 %copy-start.8 = (f32[2,1,2,384]{3,2,1,0:T(2,128)S(1)}, f32[2,1,2,384]{3,2,1,0:T(2,128)}, u32[]{:S(2)}) copy-start(f32[2,1,2,384]{3,2,1,0:T(2,128)} %refs_7_.1) | copy-start | bytes 18436
  0.7 6.0 %copy-start.4 = (f32[2,512]{1,0:T(2,128)S(1)}, f32[2,512]{1,0:T(2,128)}, u32[]{:S(2)}) copy-start(f32[2,512]{1,0:T(2,128)} %refs_9_.3) | copy-start | bytes 12292
  0.7 6.0 %copy-start.6 = (f32[2,512]{1,0:T(2,128)S(1)}, f32[2,512]{1,0:T(2,128)}, u32[]{:S(2)}) copy-start(f32[2,512]{1,0:T(2,128)} %refs_18_.5) | copy-start | bytes 12292
  0.7 6.0 %copy-start.9 = (s32[1024]{0:T(1024)S(1)}, s32[1024]{0:T(1024)}, u32[]{:S(2)}) copy-start(s32[1024]{0:T(1024)} %param.13) | copy-start | bytes 12292
  0.7 6.0 %collective-permute-start = (bf16[2,1,768,512]{3,2,1,0:T(8,128)(2,1)}, bf16[2,1,768,512]{3,2,1,0:T(8,128)(2,1)S(1)}, u32[]{:S(2)}, u32[]{:S(2)}) collective-permute-start(bf16[2,1,768,512]{3,2,1,0:T(8,128)(2,1)} %refs_11_.1), channel_id=1, source_target_pairs={{0,16},{16,0},{1,17},{17,1},{2,18},{18,2},{3,19},{19,3},{4,20},{20... | collective-permute-start | bytes 4718600 | tf_op jit(solution)/shard_map/ppermute | solution.py:1133
  0.8 5.8 %collective-permute-start.3 = (bf16[2,1,512,768]{3,2,1,0:T(8,128)(2,1)}, bf16[2,1,512,768]{3,2,1,0:T(8,128)(2,1)S(1)}, u32[]{:S(2)}, u32[]{:S(2)}) collective-permute-start(bf16[2,1,512,768]{3,2,1,0:T(8,128)(2,1)} %refs_3_.1), channel_id=1, source_target_pairs={{0,16},{16,0},{1,17},{17,1},{2,18},{18,2},{3,19},{19,3},{4,20},{20... | collective-permute-start | bytes 4718600 | tf_op jit(solution)/shard_map/ppermute | solution.py:1133
  1.3 5.4 %collective-permute-start.1 = (f32[2,1,384]{2,1,0:T(1,128)}, f32[2,1,384]{2,1,0:T(1,128)S(1)}, u32[]{:S(2)}, u32[]{:S(2)}) collective-permute-start(f32[2,1,384]{2,1,0:T(1,128)} %refs_6_.1), channel_id=1, source_target_pairs={{0,16},{16,0},{1,17},{17,1},{2,18},{18,2},{3,19},{19,3},{4,20},{20... | collective-permute-start | bytes 9224 | tf_op jit(solution)/shard_map/ppermute | solution.py:1133
  1.4 5.3 %collective-permute-start.2 = (f32[2,1,2,384]{3,2,1,0:T(2,128)}, f32[2,1,2,384]{3,2,1,0:T(2,128)S(1)}, u32[]{:S(2)}, u32[]{:S(2)}) collective-permute-start(f32[2,1,2,384]{3,2,1,0:T(2,128)} %refs_7_.1), channel_id=1, source_target_pairs={{0,16},{16,0},{1,17},{17,1},{2,18},{18,2},{3,19},{19,3},{4,20},{20... | collective-permute-start | bytes 18440 | tf_op jit(solution)/shard_map/ppermute | solution.py:1133
  1.8 1.2 copy-start.11
  6.7 16.0 %copy-start.1 = (bf16[2,1,768,512]{3,2,1,0:T(8,128)(2,1)S(1)}, bf16[2,1,768,512]{3,2,1,0:T(8,128)(2,1)}, u32[]{:S(2)}) copy-start(bf16[2,1,768,512]{3,2,1,0:T(8,128)(2,1)} %refs_11_.1) | copy-start | bytes 4718596
  6.7 16.0 %copy-start.2 = (bf16[2,512,512]{2,1,0:T(8,128)(2,1)S(1)}, bf16[2,512,512]{2,1,0:T(8,128)(2,1)}, u32[]{:S(2)}) copy-start(bf16[2,512,512]{2,1,0:T(8,128)(2,1)} %refs_20_.5) | copy-start | bytes 3145732
  6.7 16.0 %copy-start.5 = (f32[2,512]{1,0:T(2,128)S(1)}, f32[2,512]{1,0:T(2,128)}, u32[]{:S(2)}) copy-start(f32[2,512]{1,0:T(2,128)} %refs_10_.3) | copy-start | bytes 12292
  6.8 16.0 %copy-start.7 = (f32[2,512]{1,0:T(2,128)S(1)}, f32[2,512]{1,0:T(2,128)}, u32[]{:S(2)}) copy-start(f32[2,512]{1,0:T(2,128)} %refs_20_.4) | copy-start | bytes 12292
  22.8 13.5 %copy-start.3 = (f32[1024,512]{1,0:T(8,128)S(1)}, f32[1024,512]{1,0:T(8,128)}, u32[]{:S(2)}) copy-start(f32[1024,512]{1,0:T(8,128)} %refs_21_.3) | copy-start | bytes 6291460
  42.8 9.3 %collective-permute-start.4 = (bf16[4096,128]{1,0:T(8,128)(2,1)S(1)}, bf16[4096,128]{1,0:T(8,128)(2,1)S(1)}, u32[]{:S(2)}, u32[]{:S(2)}) collective-permute-start(bf16[4096,128]{1,0:T(8,128)(2,1)S(1)} %get-tuple-element.180), channel_id=1, source_target_pairs={{0,16},{16,0},{1,17},{17,1},{2,18},{18,2},{3,19},{19,3},{4,20},{20... | collective-permute-start | bytes 3145736 | tf_op jit(solution)/shard_map/ppermute | solution.py:1133
  54.9 5.8 %collective-permute-start.6 = (bf16[3072,128]{1,0:T(8,128)(2,1)S(1)}, bf16[3072,128]{1,0:T(8,128)(2,1)S(1)}, u32[]{:S(2)}, u32[]{:S(2)}) collective-permute-start(bf16[3072,128]{1,0:T(8,128)(2,1)S(1)} %get-tuple-element.206), channel_id=1, source_target_pairs={{0,16},{16,0},{1,17},{17,1},{2,18},{18,2},{3,19},{19,3},{4,20},{20... | collective-permute-start | bytes 2359304 | tf_op jit(solution)/shard_map/ppermute | solution.py:1133
  60.5 16.4 %collective-permute-start.5 = (bf16[4096,128]{1,0:T(8,128)(2,1)S(1)}, bf16[4096,128]{1,0:T(8,128)(2,1)S(1)}, u32[]{:S(2)}, u32[]{:S(2)}) collective-permute-start(bf16[4096,128]{1,0:T(8,128)(2,1)S(1)} %get-tuple-element.202), channel_id=1, source_target_pairs={{0,16},{16,0},{1,17},{17,1},{2,18},{18,2},{3,19},{19,3},{4,20},{20... | collective-permute-start | bytes 3145736 | tf_op jit(solution)/shard_map/ppermute | solution.py:1133
  61.7 13.4 %collective-permute-start.7 = (bf16[1792,128]{1,0:T(8,128)(2,1)S(1)}, bf16[1792,128]{1,0:T(8,128)(2,1)S(1)}, u32[]{:S(2)}, u32[]{:S(2)}) collective-permute-start(bf16[1792,128]{1,0:T(8,128)(2,1)S(1)} %get-tuple-element.212), channel_id=1, source_target_pairs={{0,1},{1,0},{2,3},{3,2},{4,5},{5,4},{6,7},{7,6},{8,9},{9,8},{10,11... | collective-permute-start | bytes 1376264 | tf_op jit(solution)/shard_map/ppermute | solution.py:1138
  61.8 13.2 %collective-permute-start.8 = (bf16[1792,128]{1,0:T(8,128)(2,1)S(1)}, bf16[1792,128]{1,0:T(8,128)(2,1)S(1)}, u32[]{:S(2)}, u32[]{:S(2)}) collective-permute-start(bf16[1792,128]{1,0:T(8,128)(2,1)S(1)} %get-tuple-element.214), channel_id=1, source_target_pairs={{0,2},{1,3},{2,0},{3,1},{4,6},{5,7},{6,4},{7,5},{8,10},{9,11},{10,... | collective-permute-start | bytes 1376264 | tf_op jit(solution)/shard_map/ppermute | solution.py:1138
  75.3 9.1 %collective-permute-start.9 = (bf16[896,128]{1,0:T(8,128)(2,1)S(1)}, bf16[896,128]{1,0:T(8,128)(2,1)S(1)}, u32[]{:S(2)}, u32[]{:S(2)}) collective-permute-start(bf16[896,128]{1,0:T(8,128)(2,1)S(1)} %get-tuple-element.230), channel_id=1, source_target_pairs={{0,2},{1,3},{2,0},{3,1},{4,6},{5,7},{6,4},{7,5},{8,10},{9,11},{10,... | collective-permute-start | bytes 688136 | tf_op jit(solution)/shard_map/ppermute | solution.py:1138
  76.4 8.0 %collective-permute-start.10 = (bf16[896,128]{1,0:T(8,128)(2,1)S(1)}, bf16[896,128]{1,0:T(8,128)(2,1)S(1)}, u32[]{:S(2)}, u32[]{:S(2)}) collective-permute-start(bf16[896,128]{1,0:T(8,128)(2,1)S(1)} %get-tuple-element.232), channel_id=1, source_target_pairs={{0,1},{1,0},{2,3},{3,2},{4,5},{5,4},{6,7},{7,6},{8,9},{9,8},{10,11... | collective-permute-start | bytes 688136 | tf_op jit(solution)/shard_map/ppermute | solution.py:1138
  79.9 8.2 %collective-permute-start.11 = (bf16[3072,128]{1,0:T(8,128)(2,1)S(1)}, bf16[3072,128]{1,0:T(8,128)(2,1)S(1)}, u32[]{:S(2)}, u32[]{:S(2)}) collective-permute-start(bf16[3072,128]{1,0:T(8,128)(2,1)S(1)} %get-tuple-element.236), channel_id=1, source_target_pairs={{0,16},{16,0},{1,17},{17,1},{2,18},{18,2},{3,19},{19,3},{4,20},{20... | collective-permute-start | bytes 2359304 | tf_op jit(solution)/shard_map/ppermute | solution.py:1133
  84.5 6.1 %collective-permute-start.12 = (bf16[448,128]{1,0:T(8,128)(2,1)S(1)}, bf16[448,128]{1,0:T(8,128)(2,1)S(1)}, u32[]{:S(2)}, u32[]{:S(2)}) collective-permute-start(bf16[448,128]{1,0:T(8,128)(2,1)S(1)} %get-tuple-element.244), channel_id=1, source_target_pairs={{0,4},{1,5},{2,6},{3,7},{4,0},{5,1},{6,2},{7,3},{8,12},{9,13},{10,... | collective-permute-start | bytes 344072 | tf_op jit(solution)/shard_map/ppermute | solution.py:1138
  84.9 10.3 %collective-permute-start.13 = (bf16[448,128]{1,0:T(8,128)(2,1)S(1)}, bf16[448,128]{1,0:T(8,128)(2,1)S(1)}, u32[]{:S(2)}, u32[]{:S(2)}) collective-permute-start(bf16[448,128]{1,0:T(8,128)(2,1)S(1)} %get-tuple-element.245), channel_id=1, source_target_pairs={{0,8},{1,9},{2,10},{3,11},{4,12},{5,13},{6,14},{7,15},{8,0},{9,1},... | collective-permute-start | bytes 344072 | tf_op jit(solution)/shard_map/ppermute | solution.py:1138
  85.4 9.8 %collective-permute-start.14 = (bf16[448,128]{1,0:T(8,128)(2,1)S(1)}, bf16[448,128]{1,0:T(8,128)(2,1)S(1)}, u32[]{:S(2)}, u32[]{:S(2)}) collective-permute-start(bf16[448,128]{1,0:T(8,128)(2,1)S(1)} %get-tuple-element.246), channel_id=1, source_target_pairs={{0,12},{1,13},{2,14},{3,15},{4,8},{5,9},{6,10},{7,11},{8,4},{9,5},... | collective-permute-start | bytes 344072 | tf_op jit(solution)/shard_map/ppermute | solution.py:1138
  89.2 11.2 %collective-permute-start.16 = (bf16[1792,128]{1,0:T(8,128)(2,1)S(1)}, bf16[1792,128]{1,0:T(8,128)(2,1)S(1)}, u32[]{:S(2)}, u32[]{:S(2)}) collective-permute-start(bf16[1792,128]{1,0:T(8,128)(2,1)S(1)} %get-tuple-element.251), channel_id=1, source_target_pairs={{0,2},{1,3},{2,0},{3,1},{4,6},{5,7},{6,4},{7,5},{8,10},{9,11},{10,... | collective-permute-start | bytes 1376264 | tf_op jit(solution)/shard_map/ppermute | solution.py:1138
  90.5 11.3 %collective-permute-start.15 = (bf16[1872,128]{1,0:T(8,128)(2,1)S(1)}, bf16[1872,128]{1,0:T(8,128)(2,1)S(1)}, u32[]{:S(2)}, u32[]{:S(2)}) collective-permute-start(bf16[1872,128]{1,0:T(8,128)(2,1)S(1)} %get-tuple-element.249), channel_id=1, source_target_pairs={{0,1},{1,0},{2,3},{3,2},{4,5},{5,4},{6,7},{7,6},{8,9},{9,8},{10,11... | collective-permute-start | bytes 1437704 | tf_op jit(solution)/shard_map/ppermute | solution.py:1138
  95.2 8.0 %collective-permute-start.19 = (bf16[448,128]{1,0:T(8,128)(2,1)S(1)}, bf16[448,128]{1,0:T(8,128)(2,1)S(1)}, u32[]{:S(2)}, u32[]{:S(2)}) collective-permute-start(bf16[448,128]{1,0:T(8,128)(2,1)S(1)} %get-tuple-element.253.refs_1_), channel_id=1, source_target_pairs={{0,12},{1,13},{2,14},{3,15},{4,8},{5,9},{6,10},{7,11},{8,4},{9,5},... | collective-permute-start | bytes 344072 | tf_op jit(solution)/shard_map/ppermute | solution.py:1138
  96.6 12.2 %collective-permute-start.18 = (bf16[448,128]{1,0:T(8,128)(2,1)S(1)}, bf16[448,128]{1,0:T(8,128)(2,1)S(1)}, u32[]{:S(2)}, u32[]{:S(2)}) collective-permute-start(bf16[448,128]{1,0:T(8,128)(2,1)S(1)} %get-tuple-element.253.refs_1_), channel_id=1, source_target_pairs={{0,8},{1,9},{2,10},{3,11},{4,12},{5,13},{6,14},{7,15},{8,0},{9,1},... | collective-permute-start | bytes 344072 | tf_op jit(solution)/shard_map/ppermute | solution.py:1138
  99.2 9.6 %collective-permute-start.17 = (bf16[448,128]{1,0:T(8,128)(2,1)S(1)}, bf16[448,128]{1,0:T(8,128)(2,1)S(1)}, u32[]{:S(2)}, u32[]{:S(2)}) collective-permute-start(bf16[448,128]{1,0:T(8,128)(2,1)S(1)} %get-tuple-element.253.refs_1_), channel_id=1, source_target_pairs={{0,4},{1,5},{2,6},{3,7},{4,0},{5,1},{6,2},{7,3},{8,12},{9,13},{10,... | collective-permute-start | bytes 344072 | tf_op jit(solution)/shard_map/ppermute | solution.py:1138
  102.0 6.8 %collective-permute-start.21 = (bf16[896,128]{1,0:T(8,128)(2,1)S(1)}, bf16[896,128]{1,0:T(8,128)(2,1)S(1)}, u32[]{:S(2)}, u32[]{:S(2)}) collective-permute-start(bf16[896,128]{1,0:T(8,128)(2,1)S(1)} %get-tuple-element.258), channel_id=1, source_target_pairs={{0,1},{1,0},{2,3},{3,2},{4,5},{5,4},{6,7},{7,6},{8,9},{9,8},{10,11... | collective-permute-start | bytes 688136 | tf_op jit(solution)/shard_map/ppermute | solution.py:1138
  102.1 6.8 %collective-permute-start.20 = (bf16[976,128]{1,0:T(8,128)(2,1)S(1)}, bf16[976,128]{1,0:T(8,128)(2,1)S(1)}, u32[]{:S(2)}, u32[]{:S(2)}) collective-permute-start(bf16[976,128]{1,0:T(8,128)(2,1)S(1)} %get-tuple-element.256), channel_id=1, source_target_pairs={{0,2},{1,3},{2,0},{3,1},{4,6},{5,7},{6,4},{7,5},{8,10},{9,11},{10,... | collective-permute-start | bytes 749576 | tf_op jit(solution)/shard_map/ppermute | solution.py:1138
  109.0 5.8 %collective-permute-start.22 = (bf16[528,128]{1,0:T(8,128)(2,1)S(1)}, bf16[528,128]{1,0:T(8,128)(2,1)S(1)}, u32[]{:S(2)}, u32[]{:S(2)}) collective-permute-start(bf16[528,128]{1,0:T(8,128)(2,1)S(1)} %get-tuple-element.261), channel_id=1, source_target_pairs={{0,4},{1,5},{2,6},{3,7},{4,0},{5,1},{6,2},{7,3},{8,12},{9,13},{10,... | collective-permute-start | bytes 405512 | tf_op jit(solution)/shard_map/ppermute | solution.py:1138
  109.1 5.8 %collective-permute-start.23 = (bf16[528,128]{1,0:T(8,128)(2,1)S(1)}, bf16[528,128]{1,0:T(8,128)(2,1)S(1)}, u32[]{:S(2)}, u32[]{:S(2)}) collective-permute-start(bf16[528,128]{1,0:T(8,128)(2,1)S(1)} %get-tuple-element.262), channel_id=1, source_target_pairs={{0,8},{1,9},{2,10},{3,11},{4,12},{5,13},{6,14},{7,15},{8,0},{9,1},... | collective-permute-start | bytes 405512 | tf_op jit(solution)/shard_map/ppermute | solution.py:1138
  110.4 8.4 %collective-permute-start.24 = (bf16[528,128]{1,0:T(8,128)(2,1)S(1)}, bf16[528,128]{1,0:T(8,128)(2,1)S(1)}, u32[]{:S(2)}, u32[]{:S(2)}) collective-permute-start(bf16[528,128]{1,0:T(8,128)(2,1)S(1)} %get-tuple-element.263), channel_id=1, source_target_pairs={{0,12},{1,13},{2,14},{3,15},{4,8},{5,9},{6,10},{7,11},{8,4},{9,5},... | collective-permute-start | bytes 405512 | tf_op jit(solution)/shard_map/ppermute | solution.py:1138
  112.6 11.4 %collective-permute-start.25 = (bf16[896,128]{1,0:T(8,128)(2,1)S(1)}, bf16[896,128]{1,0:T(8,128)(2,1)S(1)}, u32[]{:S(2)}, u32[]{:S(2)}) collective-permute-start(bf16[896,128]{1,0:T(8,128)(2,1)S(1)} %get-tuple-element.265.refs_1_), channel_id=1, source_target_pairs={{0,2},{1,3},{2,0},{3,1},{4,6},{5,7},{6,4},{7,5},{8,10},{9,11},{10,... | collective-permute-start | bytes 688136 | tf_op jit(solution)/shard_map/ppermute | solution.py:1138
  113.7 10.2 %collective-permute-start.26 = (bf16[896,128]{1,0:T(8,128)(2,1)S(1)}, bf16[896,128]{1,0:T(8,128)(2,1)S(1)}, u32[]{:S(2)}, u32[]{:S(2)}) collective-permute-start(bf16[896,128]{1,0:T(8,128)(2,1)S(1)} %get-tuple-element.266.refs_3_), channel_id=1, source_target_pairs={{0,1},{1,0},{2,3},{3,2},{4,5},{5,4},{6,7},{7,6},{8,9},{9,8},{10,11... | collective-permute-start | bytes 688136 | tf_op jit(solution)/shard_map/ppermute | solution.py:1138
  118.8 6.6 %collective-permute-start.31 = (bf16[448,128]{1,0:T(8,128)(2,1)S(1)}, bf16[448,128]{1,0:T(8,128)(2,1)S(1)}, u32[]{:S(2)}, u32[]{:S(2)}) collective-permute-start(bf16[448,128]{1,0:T(8,128)(2,1)S(1)} %get-tuple-element.270.refs_1_), channel_id=1, source_target_pairs={{0,12},{1,13},{2,14},{3,15},{4,8},{5,9},{6,10},{7,11},{8,4},{9,5},... | collective-permute-start | bytes 344072 | tf_op jit(solution)/shard_map/ppermute | solution.py:1138
  119.9 10.7 %collective-permute-start.30 = (bf16[448,128]{1,0:T(8,128)(2,1)S(1)}, bf16[448,128]{1,0:T(8,128)(2,1)S(1)}, u32[]{:S(2)}, u32[]{:S(2)}) collective-permute-start(bf16[448,128]{1,0:T(8,128)(2,1)S(1)} %get-tuple-element.270.refs_1_), channel_id=1, source_target_pairs={{0,8},{1,9},{2,10},{3,11},{4,12},{5,13},{6,14},{7,15},{8,0},{9,1},... | collective-permute-start | bytes 344072 | tf_op jit(solution)/shard_map/ppermute | solution.py:1138
  123.9 6.7 %collective-permute-start.29 = (bf16[448,128]{1,0:T(8,128)(2,1)S(1)}, bf16[448,128]{1,0:T(8,128)(2,1)S(1)}, u32[]{:S(2)}, u32[]{:S(2)}) collective-permute-start(bf16[448,128]{1,0:T(8,128)(2,1)S(1)} %get-tuple-element.270.refs_1_), channel_id=1, source_target_pairs={{0,4},{1,5},{2,6},{3,7},{4,0},{5,1},{6,2},{7,3},{8,12},{9,13},{10,... | collective-permute-start | bytes 344072 | tf_op jit(solution)/shard_map/ppermute | solution.py:1138
  124.0 15.2 %collective-permute-start.27 = (bf16[1792,128]{1,0:T(8,128)(2,1)S(1)}, bf16[1792,128]{1,0:T(8,128)(2,1)S(1)}, u32[]{:S(2)}, u32[]{:S(2)}) collective-permute-start(bf16[1792,128]{1,0:T(8,128)(2,1)S(1)} %get-tuple-element.267.refs_1_), channel_id=1, source_target_pairs={{0,1},{1,0},{2,3},{3,2},{4,5},{5,4},{6,7},{7,6},{8,9},{9,8},{10,11... | collective-permute-start | bytes 1376264 | tf_op jit(solution)/shard_map/ppermute | solution.py:1138
  124.6 14.6 %collective-permute-start.28 = (bf16[1792,128]{1,0:T(8,128)(2,1)S(1)}, bf16[1792,128]{1,0:T(8,128)(2,1)S(1)}, u32[]{:S(2)}, u32[]{:S(2)}) collective-permute-start(bf16[1792,128]{1,0:T(8,128)(2,1)S(1)} %get-tuple-element.268.refs_3_), channel_id=1, source_target_pairs={{0,2},{1,3},{2,0},{3,1},{4,6},{5,7},{6,4},{7,5},{8,10},{9,11},{10,... | collective-permute-start | bytes 1376264 | tf_op jit(solution)/shard_map/ppermute | solution.py:1138
  130.7 8.4 %collective-permute-start.32 = (bf16[896,128]{1,0:T(8,128)(2,1)S(1)}, bf16[896,128]{1,0:T(8,128)(2,1)S(1)}, u32[]{:S(2)}, u32[]{:S(2)}) collective-permute-start(bf16[896,128]{1,0:T(8,128)(2,1)S(1)} %get-tuple-element.272.refs_3_), channel_id=1, source_target_pairs={{0,2},{1,3},{2,0},{3,1},{4,6},{5,7},{6,4},{7,5},{8,10},{9,11},{10,... | collective-permute-start | bytes 688136 | tf_op jit(solution)/shard_map/ppermute | solution.py:1138
  132.9 6.3 %collective-permute-start.33 = (bf16[896,128]{1,0:T(8,128)(2,1)S(1)}, bf16[896,128]{1,0:T(8,128)(2,1)S(1)}, u32[]{:S(2)}, u32[]{:S(2)}) collective-permute-start(bf16[896,128]{1,0:T(8,128)(2,1)S(1)} %get-tuple-element.273.refs_5_), channel_id=1, source_target_pairs={{0,1},{1,0},{2,3},{3,2},{4,5},{5,4},{6,7},{7,6},{8,9},{9,8},{10,11... | collective-permute-start | bytes 688136 | tf_op jit(solution)/shard_map/ppermute | solution.py:1138
  139.3 9.1 %collective-permute-start.35 = (f32[2,512,512]{2,1,0:T(8,128)S(1)}, f32[2,512,512]{2,1,0:T(8,128)S(1)}, u32[]{:S(2)}, u32[]{:S(2)}) collective-permute-start(f32[2,512,512]{2,1,0:T(8,128)S(1)} %get-tuple-element.280.refs_1_), channel_id=1, source_target_pairs={{0,16},{16,0},{1,17},{17,1},{2,18},{18,2},{3,19},{19,3},{4,20},{20... | collective-permute-start | bytes 6291464 | tf_op jit(solution)/shard_map/ppermute | solution.py:1133
  143.5 12.1 %collective-permute-start.37 = (bf16[1792,128]{1,0:T(8,128)(2,1)S(1)}, bf16[1792,128]{1,0:T(8,128)(2,1)S(1)}, u32[]{:S(2)}, u32[]{:S(2)}) collective-permute-start(bf16[1792,128]{1,0:T(8,128)(2,1)S(1)} %get-tuple-element.288.refs_1_), channel_id=1, source_target_pairs={{0,1},{1,0},{2,3},{3,2},{4,5},{5,4},{6,7},{7,6},{8,9},{9,8},{10,11... | collective-permute-start | bytes 1376264 | tf_op jit(solution)/shard_map/ppermute | solution.py:1138
  143.9 11.8 %collective-permute-start.38 = (bf16[1792,128]{1,0:T(8,128)(2,1)S(1)}, bf16[1792,128]{1,0:T(8,128)(2,1)S(1)}, u32[]{:S(2)}, u32[]{:S(2)}) collective-permute-start(bf16[1792,128]{1,0:T(8,128)(2,1)S(1)} %get-tuple-element.289.refs_3_), channel_id=1, source_target_pairs={{0,2},{1,3},{2,0},{3,1},{4,6},{5,7},{6,4},{7,5},{8,10},{9,11},{10,... | collective-permute-start | bytes 1376264 | tf_op jit(solution)/shard_map/ppermute | solution.py:1138
  144.9 5.8 %collective-permute-start.36 = (bf16[1024,128]{1,0:T(8,128)(2,1)S(1)}, bf16[1024,128]{1,0:T(8,128)(2,1)S(1)}, u32[]{:S(2)}, u32[]{:S(2)}) collective-permute-start(bf16[1024,128]{1,0:T(8,128)(2,1)S(1)} %get-tuple-element.286.refs_1_), channel_id=1, source_target_pairs={{0,16},{16,0},{1,17},{17,1},{2,18},{18,2},{3,19},{19,3},{4,20},{20... | collective-permute-start | bytes 786440 | tf_op jit(solution)/shard_map/ppermute | solution.py:1133
  145.6 2.1 %collective-permute-start.34 = (f32[80,128]{1,0:T(8,128)S(1)}, f32[80,128]{1,0:T(8,128)S(1)}, u32[]{:S(2)}, u32[]{:S(2)}) collective-permute-start(f32[80,128]{1,0:T(8,128)S(1)} %get-tuple-element.278.refs_1_), channel_id=1, source_target_pairs={{0,16},{16,0},{1,17},{17,1},{2,18},{18,2},{3,19},{19,3},{4,20},{20... | collective-permute-start | bytes 122888 | tf_op jit(solution)/shard_map/ppermute | solution.py:1133
  155.8 3.3 %collective-permute-start.39 = (bf16[1024,128]{1,0:T(8,128)(2,1)S(1)}, bf16[1024,128]{1,0:T(8,128)(2,1)S(1)}, u32[]{:S(2)}, u32[]{:S(2)}) collective-permute-start(bf16[1024,128]{1,0:T(8,128)(2,1)S(1)} %get-tuple-element.299.refs_1_), channel_id=1, source_target_pairs={{0,16},{16,0},{1,17},{17,1},{2,18},{18,2},{3,19},{19,3},{4,20},{20... | collective-permute-start | bytes 786440 | tf_op jit(solution)/shard_map/ppermute | solution.py:1133

commit v6 on v5

--- a/solution.py
+++ b/solution.py
@@ -114,7 +114,7 @@
                 sums = visit(side, rows, re, im, sums)
         return tuple(new), sums
 
-    return lax.fori_loop(0, span, step, (init, totals), unroll=UNROLL)
+    return lax.fori_loop(0, span, step, (init, totals), unroll=UNROLL if totals else span)
 
 
 def run_chain(first_up, lanes, side, ends, whole, start, places):
@@ -277,56 +277,18 @@
     over_blocks(rows, element)
 
 
-def open_second_kernel(
-    row_devices,
-    normed,
-    segments,
-    gain,
-    bias,
-    rate,
-    turn,
-    rate_oth,
-    turn_oth,
-    in_own,
-    in_oth,
-    mixed_low,
-    drive_own,
-    drive_oth,
-    keep_own,
-    keep_oth,
-    whole_out,
-    ends_own,
-    ends_oth,
-    payload,
-    table,
-    tiles,
-    ids,
-    rows8,
+def open_masks_kernel(
+    row_devices, segments, rate, turn, cotangent_from, table, keep_own, keep_oth, whole_out, ids, grad_out, rows8, natural,
+    part, sems,
 ):
-    core, place = core_place(row_devices)
-    rows = normed.shape[0]
+    core, _ = core_place(row_devices)
+    rows = grad_out.shape[0]
     span = rows // 8
-
-    def element(start, carry):
-        block = pl.ds(start, ELEMENT_ROWS)
-        mixed_low[block, :] = (normed[block, :] * gain[0:1, :] + bias[0:1, :]).astype(bf16)
-        return carry
-
-    over_blocks(rows, element)
+    copy = pltpu.make_async_copy(cotangent_from.at[part_rows(core, rows)], part, sems.at[0])
+    copy.start()
     table[...] = jnp.zeros_like(table)
-    tiles[...] = jnp.zeros_like(tiles)
-    thirds = table.shape[2] // LANES
     for layer in range(table.shape[0]):
         table_rows(table, layer, 0, rate, turn)
-        table_rows(table, layer, 8, rate_oth, turn_oth)
-        for side in range(2):
-            for part in range(2):
-                for i in range(thirds):
-                    at = 8 * side + part * thirds + i
-                    tiles[layer, at : at + 1, :] = table[
-                        layer, 8 * side + part : 8 * side + part + 1, i * LANES : (i + 1) * LANES
-                    ]
-
     number = segments[...].astype(f32)
     count = number.shape[0]
     lane = lax.broadcasted_iota(jnp.int32, number.shape, 1)
@@ -361,6 +323,57 @@
     ids[...] = jnp.zeros_like(ids)
     ids[0:1, :] = jnp.broadcast_to(first_row[:, 0:1], (1, LANES))
     ids[1:2, :] = jnp.broadcast_to(last_row[:, LANES - 1 : LANES], (1, LANES))
+    copy.wait()
+    fill_columns(natural, part[...])
+    grad_out[...] = tile_order(natural, 0, span, span)
+
+
+def open_second_kernel(
+    row_devices,
+    normed,
+    gain,
+    bias,
+    table_in,
+    keep_own,
+    keep_oth,
+    whole,
+    ids,
+    rate_oth,
+    turn_oth,
+    in_own,
+    in_oth,
+    mixed_low,
+    drive_own,
+    drive_oth,
+    ends_own,
+    ends_oth,
+    payload,
+    table,
+    tiles,
+):
+    core, place = core_place(row_devices)
+    rows = normed.shape[0]
+    span = rows // 8
+
+    def element(start, carry):
+        block = pl.ds(start, ELEMENT_ROWS)
+        mixed_low[block, :] = (normed[block, :] * gain[0:1, :] + bias[0:1, :]).astype(bf16)
+        return carry
+
+    over_blocks(rows, element)
+    table[...] = table_in[...]
+    tiles[...] = jnp.zeros_like(tiles)
+    thirds = table.shape[2] // LANES
+    for layer in range(table.shape[0]):
+        table_rows(table, layer, 8, rate_oth, turn_oth)
+        for side in range(2):
+            for part in range(2):
+                for i in range(thirds):
+                    at = 8 * side + part * thirds + i
+                    tiles[layer, at : at + 1, :] = table[
+                        layer, 8 * side + part : 8 * side + part + 1, i * LANES : (i + 1) * LANES
+                    ]
+
     for side, (matrix, drive) in enumerate(((in_own, drive_own), (in_oth, drive_oth))):
         scale = table[0, 8 * side + 2 : 8 * side + 3, :]
         drive[...] = dot(mixed_low[...], matrix[0, 0]) * jnp.concatenate([scale, scale], 1)
@@ -370,7 +383,7 @@
         core_place(row_devices)[1],
         (drive_own, drive_oth),
         (keep_own, keep_oth),
-        (whole_out.at[0], whole_out.at[1]),
+        (whole.at[0], whole.at[1]),
         lanes,
         ids,
         (ends_own, ends_oth),
@@ -565,11 +578,10 @@
     skip,
     glu,
     glu_bias,
-    cotangent,
+    grad_in,
     low_own,
     low_oth,
     block_out,
-    grad_out,
     combined_grad,
     grad_own,
     grad_oth,
@@ -585,7 +597,6 @@
     combined,
     phi_rows,
     sig_rows,
-    natural,
     states_own,
     states_oth,
     act_low,
@@ -614,21 +625,18 @@
 
     over_blocks(rows, element)
     wide[...] = dot(act_low[...], glu[1])
-    base = pl.multiple_of(info[0] * rows, rows)
-    fill_columns(natural, cotangent[pl.ds(base, rows), :])
 
     def element_two(start, carry):
         block = pl.ds(start, ELEMENT_ROWS)
         sig = jax.nn.sigmoid(wide[block, :] + glu_bias[1:2, :])
         sig_rows[block, :] = sig
         block_out[block, :] = x_in[block, :] + combined[block, :] * phi_rows[block, :] * sig
-        grad_out[block, :] = tile_order(natural, start // 8, ELEMENT_ROWS // 8, span)
         return carry
 
     over_blocks(rows, element_two)
     sums[...] = jnp.zeros_like(sums)
     backward_half(
-        1, info, grad_out, combined, phi_rows, sig_rows, normed, gain, bias, skip, glu, out_own, out_oth, masks,
+        1, info, grad_in, combined, phi_rows, sig_rows, normed, gain, bias, skip, glu, out_own, out_oth, masks,
         whole, rows_ref, tiles_ref, ids, gate_low, combined_grad, combined_low, grad_own, grad_oth,
         (next_ends_own, next_ends_oth), payload, sums, wide,
     )
@@ -802,21 +810,23 @@
 
 
 def final_kernel(
-    low_own, low_oth, in_own, in_oth, grad_in, combined_grad, normed, inv_scale, gain, skip, block_out, halves, sums, wide,
-    *columns,
+    low_own, low_oth, in_own, in_oth, grad_in, combined_grad, normed, inv_scale, gain, skip, out, sums, wide
 ):
-    rows = grad_in.shape[0]
     sums[...] = jnp.zeros_like(sums)
 
     def finish(start, value):
-        store_token_order(columns[1], start // 8, value, rows // 8)
+        out[pl.ds(start, ELEMENT_ROWS), :] = value
 
     norm_backward(
         0, low_own, low_oth, in_own, in_oth, grad_in, combined_grad, normed, inv_scale, gain, skip, sums, wide, finish
     )
-    store_token_order(columns[0], 0, block_out[...], rows // 8)
-    for i in range(2):
-        join_columns(halves.at[i], columns[i])
+
+
+def token_order_kernel(block_out, tokens_grad, halves, *columns):
+    rows = block_out.shape[0]
+    for source, part, out in ((block_out, columns[0], halves.at[0]), (tokens_grad, columns[1], halves.at[1])):
+        store_token_order(part, 0, source[...], rows // 8)
+        join_columns(out, part)
 
 
 def store_columns(out, first, values):
@@ -1092,7 +1102,7 @@
         self.tile = None
 
     def run(self, kernel, outs, operands, scratch=(), flops=0, name=None, spare=8, after=(), free_outs=0, alias=None,
-            semaphores=0, cost=0, far=False):
+            semaphores=0, cost=0, far=False, far_last=False):
         whole = pl.BlockSpec(memory_space=pltpu.VMEM)
         free = pl.BlockSpec(memory_space=pl.ANY)
         waits = list(after) + ([] if self.tile is None else [self.tile])
@@ -1108,6 +1118,8 @@
         shapes += [jax.ShapeDtypeStruct(shape, dtype) for shape, dtype in outs]
         held = sum(jnp.dtype(dtype).itemsize * functools.reduce(lambda a, b: a * b, shape) for shape, dtype in scratch)
         specs = [free] * skipped + [pl.BlockSpec(memory_space=pltpu.HBM) if far else whole] * inputs
+        if far_last:
+            specs[-1] = pl.BlockSpec(memory_space=pltpu.HBM)
         aliases = {}
         if alias is not None:
             for operand, out in alias.items():
@@ -1224,14 +1236,19 @@
         name="open_norm",
         cost=10,
     )
-    (
-        mixed0, drive_own0, drive_oth0, keep_own, keep_oth, whole, ends_own, ends_oth, payload, table, tiles, ids,
-    ) = order.run(
+    table, keep_own, keep_oth, whole, ids, grad1 = order.run(
+        here(open_masks_kernel, row_devices),
+        [table_shape, narrow, narrow, ((2, 8, LANES), f32), tile, full],
+        [segments, rate_params, turn_params, cotangent],
+        [tile, columns, full],
+        far_last=True,
+        semaphores=1,
+        name="open_masks",
+    )
+    mixed0, drive_own0, drive_oth0, ends_own, ends_oth, payload, table, tiles = order.run(
         here(open_second_kernel, row_devices),
-        [full_low, wide, wide, narrow, narrow, ((2, 8, LANES), f32), ends, ends, payload_shape, table_shape,
-         ((layers, 16, LANES), f32), tile],
-        [normed0, segments, norm_gain, norm_bias, rate_params, turn_params, rate_oth, turn_oth, in_own, in_oth],
-        [tile],
+        [full_low, wide, wide, ends, ends, payload_shape, table_shape, ((layers, 16, LANES), f32)],
+        [normed0, norm_gain, norm_bias, table, keep_own, keep_oth, whole, ids, rate_oth, turn_oth, in_own, in_oth],
         name="open_scan",
         after=[out_oth],
     )
@@ -1251,14 +1268,14 @@
     )
     gathered = exchanged(payload, row_devices)
     (
-        low_own1, low_oth1, out1, grad1, combined_grad1, grad_own1, grad_oth1, ends_own, ends_oth, payload,
+        low_own1, low_oth1, out1, combined_grad1, grad_own1, grad_oth1, ends_own, ends_oth, payload,
         sums_turn, mine, theirs,
     ) = order.run(
         here(turn_kernel, row_devices),
-        [wide_low, wide_low, full, full, full, wide, wide, ends, ends, payload_shape, sums_shape, outer_pack, outer_pack],
+        [wide_low, wide_low, full, full, wide, wide, ends, ends, payload_shape, sums_shape, outer_pack, outer_pack],
         [gathered, ends_own, ends_oth, drive_own1, drive_oth1, keep_own, keep_oth, whole, table, tiles,
-         ids, out_own, out_oth, x1, normed1, norm_gain, norm_bias, skip_weight, glu_weight, glu_bias, cotangent],
-        [places, tile, full, full, full, full, columns, wide, wide, full_low, full_low, full_low],
+         ids, out_own, out_oth, x1, normed1, norm_gain, norm_bias, skip_weight, glu_weight, glu_bias, grad1],
+        [places, tile, full, full, full, full, wide, wide, full_low, full_low, full_low],
         flops=4 * one + 2 * gate + 4 * scan,
         name="turn",
     )
@@ -1344,17 +1361,20 @@
         after=[second_outer[1]],
     )
     second_inner = [mine, swap(theirs)]
-    halves, sums_last = order.run(
+    grad_x, sums_last = order.run(
         final_kernel,
-        [((2, rows, width), f32), sums_shape],
-        [in_low_own0, in_low_oth0, in_own, in_oth, grad0, combined_grad0, normed0, inv0, norm_gain, skip_weight, out1],
-        [full, columns, columns],
+        [full, sums_shape],
+        [in_low_own0, in_low_oth0, in_own, in_oth, grad0, combined_grad0, normed0, inv0, norm_gain, skip_weight],
+        [full],
         name="final_norm",
     )
     first = from_second(first, 0, "first_plane", 50)
     second = from_cores(
         second_outer + second_inner, small_rows, [sums_turn, sums_back, sums_last, decay_sums0, decay_sums1],
         "second_cores",
+    )
+    (halves,) = order.run(
+        token_order_kernel, [((2, rows, width), f32)], [out1, grad_x], [columns, columns], name="token_order"
     )
     (share,) = order.run(planes_kernel, [low(share_rows)], first, name="first_planes", cost=50)
     first = shared(beyond(share), 2)

time: 161 us -> 157 us (0.975)
  starting transfers between devices: 36.7 us -> 33.9 us
    ppermute x12, starting transfers between devices: 9.44 us -> 7.69 us  [swap(): return lax.ppermute(value, 'dir', [(0, 1), (1, 0)])]
    pallas_call x29 -> x31, Pallas kernels: 41.1 us -> 40.1 us  [run(): pl.pallas_call(body, out_shape=shapes, in_specs=specs, out_specs=[whole]...]
  transfers between devices with their start and end apart: 40 -> 40, of which waited for: 12 -> 14; matrix products, arithmetic and copies ran while one was open for 0% -> 0% of each run, Pallas kernels for 15% -> 15%
where the time goes in v6:
time: 157 us
  blocking collectives  44.8 us (29%)
  Pallas kernels  40.1 us (26%)
  waiting for transfers between devices  35.6 us (23%)
  starting transfers between devices  33.9 us (22%)
    all_to_all x4, blocking collectives, exchanged(): lax.all_to_all(payload, ('seq', 'dir'), 0, 0, tiled=True, axis_index_grou...  44.8 us
    pallas_call x31, Pallas kernels, run(): pl.pallas_call(body, out_shape=shapes, in_specs=specs, out_specs=[whole]...  40.1 us
    ppermute x28, waiting for transfers between devices, across(): return lax.ppermute(value, 'seq', [(i, i ^ bits) for i in range(count)])  34 us
    ppermute x28, starting transfers between devices, across(): return lax.ppermute(value, 'seq', [(i, i ^ bits) for i in range(count)])  26.2 us
    ppermute x12, starting transfers between devices, swap(): return lax.ppermute(value, 'dir', [(0, 1), (1, 0)])  7.69 us
  transfers between devices with their start and end apart: 40, of which 14 were waited for; matrix products, arithmetic and copies ran while one was open for 0% of the time, Pallas kernels for 15%

profile of v6, /device:TPU:1, one launch (start us, length us, event | category | flops | bytes accessed | tf_op | source)
XLA Modules:
  0.0 156.9 jit_solution(15028614128072516251)
XLA Ops:
  0.8 0.5 collective-permute-start.3
  1.3 0.4 collective-permute-start.2
  1.8 1.2 copy-done.11
  3.0 1.0 open_norm.1
  4.1 1.1 open_masks.1
  5.1 1.5 collective-permute-done.1.refs_10_
  6.7 1.5 open_scan.1
  8.2 14.2 %all_to_all.20.refs_1_ = bf16[32,8,128]{2,1,0:T(8,128)(2,1)S(1)} all-to-all(bf16[32,8,128]{2,1,0:T(8,128)(2,1)S(1)} %get-tuple-element.170), channel_id=1, replica_groups=mesh['dir'=2,'seq'=16] {'seq','dir'}, dimensions={0} | all-to-all | bytes 131072 | tf_op jit(solution)/shard_map/all_to_all | solution.py:1167
  22.4 4.3 %mid.1 = (f32[8,128]{1,0:T(8,128)S(1)}, bf16[512,768]{1,0:T(8,128)(2,1)S(1)}, bf16[512,768]{1,0:T(8,128)(2,1)S(1)}, f32[512,512]{1,0:T(8,128)S(1)}, f32[512,512]...) custom-call(f32[8,128]{1,0:T(8,128)S(1)} %get-tuple-element.169.refs, ...), custom_call_target="tpu_custom_call" | custom-call | flops 1 | bytes 1 | tf_op jit(solution)/shard_map/mid/pallas_call | solution.py:1129
  26.7 9.1 %all_to_all.21.refs_1_ = bf16[32,8,128]{2,1,0:T(8,128)(2,1)S(1)} all-to-all(bf16[32,8,128]{2,1,0:T(8,128)(2,1)S(1)} %get-tuple-element.179), channel_id=1, replica_groups=mesh['dir'=2,'seq'=16] {'seq','dir'}, dimensions={0} | all-to-all | bytes 131072 | tf_op jit(solution)/shard_map/all_to_all | solution.py:1167
  35.8 5.4 %turn.1 = (f32[8,128]{1,0:T(8,128)S(1)}, bf16[512,768]{1,0:T(8,128)(2,1)S(1)}, bf16[512,768]{1,0:T(8,128)(2,1)S(1)}, f32[512,512]{1,0:T(8,128)S(1)}, f32[512,512...) custom-call(f32[8,128]{1,0:T(8,128)S(1)} %get-tuple-element.178.refs, ...), custom_call_target="tpu_custom_call" | custom-call | flops 1 | bytes 1 | tf_op jit(solution)/shard_map/turn/pallas_call | solution.py:1129
  41.2 0.5 collective-permute-start.4
  41.7 8.8 %all_to_all.22.refs_2_ = bf16[32,8,128]{2,1,0:T(8,128)(2,1)S(1)} all-to-all(bf16[32,8,128]{2,1,0:T(8,128)(2,1)S(1)} %get-tuple-element.189), channel_id=1, replica_groups=mesh['dir'=2,'seq'=16] {'seq','dir'}, dimensions={0} | all-to-all | bytes 131072 | tf_op jit(solution)/shard_map/all_to_all | solution.py:1167
  50.5 2.8 %scan_one.1 = (f32[8,128]{1,0:T(8,128)S(1)}, bf16[512,768]{1,0:T(8,128)(2,1)S(1)}, bf16[512,768]{1,0:T(8,128)(2,1)S(1)}, f32[8,384]{1,0:T(8,128)S(1)}, bf16[3072...) custom-call(bf16[4096,128]{1,0:T(8,128)(2,1)S(1)} %collective-permute-done.4.refs_0_.refs_2_, ...), custom_call_target="tpu_custom_call" | custom-call | flops 1 | bytes 1 | tf_op jit(solution)/shard_map/scan_one/pallas_call | solution.py:1129
  53.3 0.5 collective-permute-start.6
  53.8 4.5 %back.1 = (f32[8,128]{1,0:T(8,128)S(1)}, f32[512,512]{1,0:T(8,128)S(1)}, f32[512,512]{1,0:T(8,128)S(1)}, f32[512,768]{1,0:T(8,128)S(1)}, f32[512,768]{1,0:T(8,12...) custom-call(f32[8,128]{1,0:T(8,128)S(1)} %get-tuple-element.197.refs, ...), custom_call_target="tpu_custom_call" | custom-call | flops 1 | bytes 1 | tf_op jit(solution)/shard_map/back/pallas_call | solution.py:1129
  58.4 1.0 first_cores.1
  59.6 0.5 collective-permute-start.8
  60.1 12.7 %all_to_all.23.refs_0_.refs_2_ = bf16[32,8,128]{2,1,0:T(8,128)(2,1)S(1)} all-to-all(bf16[32,8,128]{2,1,0:T(8,128)(2,1)S(1)} %get-tuple-element.215), channel_id=1, replica_groups=mesh['dir'=2,'seq'=16] {'seq','dir'}, dimensions={0} | all-to-all | bytes 131072 | tf_op jit(solution)/shard_map/all_to_all | solution.py:1167
  73.0 1.1 collective-permute-start.9
  74.1 0.5 collective-permute-start.10
  74.7 2.9 %scan_zero.1 = (f32[8,128]{1,0:T(8,128)S(1)}, bf16[512,768]{1,0:T(8,128)(2,1)S(1)}, bf16[512,768]{1,0:T(8,128)(2,1)S(1)}, f32[8,384]{1,0:T(8,128)S(1)}, bf16[307...) custom-call(bf16[4096,128]{1,0:T(8,128)(2,1)S(1)} %collective-permute-done.5.refs_0_.refs_2_, ...), custom_call_target="tpu_custom_call" | custom-call | flops 1 | bytes 1 | tf_op jit(solution)/shard_map/scan_zero/pallas_call | solution.py:1129
  77.5 1.0 collective-permute-start.11
  78.5 1.4 final_norm.1
  79.9 0.7 collective-permute-done.10.refs_4_
  80.7 0.3 collective-permute-start.12
  81.0 0.5 collective-permute-start.13
  81.5 2.8 %collective-permute-start.14 = (bf16[448,128]{1,0:T(8,128)(2,1)S(1)}, bf16[448,128]{1,0:T(8,128)(2,1)S(1)}, u32[]{:S(2)}, u32[]{:S(2)}) collective-permute-start(bf16[448,128]{1,0:T(8,128)(2,1)S(1)} %get-tuple-element.254), channel_id=1, source_target_pairs={{0,12},{1,13},{2,14},{3,15},{4,8},{5,9},{6,10},{7,11},{8,4},{9,5},... | collective-permute-start | bytes 344072 | tf_op jit(solution)/shard_map/ppermute | solution.py:1150
  84.3 1.1 second_cores.1
  85.4 0.6 collective-permute-start.16
  86.1 1.1 collective-permute-start.15
  87.1 2.3 %token_order.1 = (f32[8,128]{1,0:T(8,128)S(1)}, f32[2,512,512]{2,1,0:T(8,128)S(1)}) custom-call(f32[8,128]{1,0:T(8,128)S(1)} %get-tuple-element.247.refs_0_, f32[512,512]{1,0:T(8,128)S(1)} %get-tuple-element.248.refs_1_, f32[512,512]{1,0:T(8,128)S(1)} %get-tuple-element.249.refs_2_), custom_call_target="tpu_custom_call" | custom-call | flops 1 | bytes 1 | tf_op jit(solution)/shard_map/token_order/pallas_call | solution.py:1129
  89.4 1.1 collective-permute-done.14.refs_4_
  90.6 0.7 collective-permute-start.19
  91.3 3.1 %collective-permute-start.18 = (bf16[448,128]{1,0:T(8,128)(2,1)S(1)}, bf16[448,128]{1,0:T(8,128)(2,1)S(1)}, u32[]{:S(2)}, u32[]{:S(2)}) collective-permute-start(bf16[448,128]{1,0:T(8,128)(2,1)S(1)} %get-tuple-element.261.refs_1_), channel_id=1, source_target_pairs={{0,8},{1,9},{2,10},{3,11},{4,12},{5,13},{6,14},{7,15},{8,0},{9,1},... | collective-permute-start | bytes 344072 | tf_op jit(solution)/shard_map/ppermute | solution.py:1150
  94.4 0.7 collective-permute-done.16.refs_4_
  95.1 1.0 collective-permute-done.15.refs_2_
  96.1 0.2 second_half.1
  96.3 0.9 collective-permute-start.21
  97.2 0.4 collective-permute-start.20
  97.6 6.3 %collective-permute-done.18.refs_3_ = bf16[448,128]{1,0:T(8,128)(2,1)S(1)} collective-permute-done((bf16[448,128]{1,0:T(8,128)(2,1)S(1)}, bf16[448,128]{1,0:T(8,128)(2,1)S(1)}, u32[]{:S(2)}, u32[]{:S(2)}) %collective-permute-start.18) | collective-permute-done | bytes 114720 | tf_op jit(solution)/shard_map/ppermute | solution.py:1150
  104.2 0.2 collective-permute-start.23
  104.4 3.3 %collective-permute-start.24 = (bf16[528,128]{1,0:T(8,128)(2,1)S(1)}, bf16[528,128]{1,0:T(8,128)(2,1)S(1)}, u32[]{:S(2)}, u32[]{:S(2)}) collective-permute-start(bf16[528,128]{1,0:T(8,128)(2,1)S(1)} %get-tuple-element.271), channel_id=1, source_target_pairs={{0,12},{1,13},{2,14},{3,15},{4,8},{5,9},{6,10},{7,11},{8,4},{9,5},... | collective-permute-start | bytes 405512 | tf_op jit(solution)/shard_map/ppermute | solution.py:1150
  107.7 0.6 collective-permute-start.25
  108.4 0.3 collective-permute-start.26
  108.6 0.5 collective-permute-done.22.refs_2_
  109.2 1.9 %collective-permute-done.23.refs_3_ = bf16[528,128]{1,0:T(8,128)(2,1)S(1)} collective-permute-done((bf16[528,128]{1,0:T(8,128)(2,1)S(1)}, bf16[528,128]{1,0:T(8,128)(2,1)S(1)}, u32[]{:S(2)}, u32[]{:S(2)}) %collective-permute-start.23) | collective-permute-done | bytes 135200 | tf_op jit(solution)/shard_map/ppermute | solution.py:1150
  111.1 1.8 %collective-permute-done.24.refs_4_ = bf16[528,128]{1,0:T(8,128)(2,1)S(1)} collective-permute-done((bf16[528,128]{1,0:T(8,128)(2,1)S(1)}, bf16[528,128]{1,0:T(8,128)(2,1)S(1)}, u32[]{:S(2)}, u32[]{:S(2)}) %collective-permute-start.24) | collective-permute-done | bytes 135200 | tf_op jit(solution)/shard_map/ppermute | solution.py:1150
  113.0 1.9 %collective-permute-start.31 = (bf16[448,128]{1,0:T(8,128)(2,1)S(1)}, bf16[448,128]{1,0:T(8,128)(2,1)S(1)}, u32[]{:S(2)}, u32[]{:S(2)}) collective-permute-start(bf16[448,128]{1,0:T(8,128)(2,1)S(1)} %get-tuple-element.278.refs_1_), channel_id=1, source_target_pairs={{0,12},{1,13},{2,14},{3,15},{4,8},{5,9},{6,10},{7,11},{8,4},{9,5},... | collective-permute-start | bytes 344072 | tf_op jit(solution)/shard_map/ppermute | solution.py:1150
  114.8 5.4 %collective-permute-start.30 = (bf16[448,128]{1,0:T(8,128)(2,1)S(1)}, bf16[448,128]{1,0:T(8,128)(2,1)S(1)}, u32[]{:S(2)}, u32[]{:S(2)}) collective-permute-start(bf16[448,128]{1,0:T(8,128)(2,1)S(1)} %get-tuple-element.278.refs_1_), channel_id=1, source_target_pairs={{0,8},{1,9},{2,10},{3,11},{4,12},{5,13},{6,14},{7,15},{8,0},{9,1},... | collective-permute-start | bytes 344072 | tf_op jit(solution)/shard_map/ppermute | solution.py:1150
  120.5 7.5 %collective-permute-done.30.refs_3_ = bf16[448,128]{1,0:T(8,128)(2,1)S(1)} collective-permute-done((bf16[448,128]{1,0:T(8,128)(2,1)S(1)}, bf16[448,128]{1,0:T(8,128)(2,1)S(1)}, u32[]{:S(2)}, u32[]{:S(2)}) %collective-permute-start.30) | collective-permute-done | bytes 114720 | tf_op jit(solution)/shard_map/ppermute | solution.py:1150
  128.3 7.6 %collective-permute-done.32.refs_4_ = bf16[896,128]{1,0:T(8,128)(2,1)S(1)} collective-permute-done((bf16[896,128]{1,0:T(8,128)(2,1)S(1)}, bf16[896,128]{1,0:T(8,128)(2,1)S(1)}, u32[]{:S(2)}, u32[]{:S(2)}) %collective-permute-start.32) | collective-permute-done | bytes 229408 | tf_op jit(solution)/shard_map/ppermute | solution.py:1150
  136.0 2.5 %collective-permute-start.35 = (f32[2,512,512]{2,1,0:T(8,128)S(1)}, f32[2,512,512]{2,1,0:T(8,128)S(1)}, u32[]{:S(2)}, u32[]{:S(2)}) collective-permute-start(f32[2,512,512]{2,1,0:T(8,128)S(1)} %get-tuple-element.288.refs_1_), channel_id=1, source_target_pairs={{0,16},{16,0},{1,17},{17,1},{2,18},{18,2},{3,19},{19,3},{4,20},{20... | collective-permute-start | bytes 6291464 | tf_op jit(solution)/shard_map/ppermute | solution.py:1145
  138.5 1.4 collective-permute-start.37
  140.0 0.7 collective-permute-start.36
  140.8 2.0 %unpack_one.1 = (f32[8,128]{1,0:T(8,128)S(1)}, f32[2,1,768,512]{3,2,1,0:T(8,128)}, f32[2,1,512,768]{3,2,1,0:T(8,128)}) custom-call(f32[8,128]{1,0:T(8,128)S(1)} %get-tuple-element.284.refs_0_, bf16[1792,128]{1,0:T(8,128)(2,1)S(1)} %get-tuple-element.275.refs_1_, bf16[1792,128]{1,0:T(8,128)(2,1)S(1)} %collective-permute-done.27.refs_0_.refs_2_, ...), custom_call_target="tpu_custom_call" | custom-call | flops 1 | bytes 1 | tf_op jit(solution)/shard_map/unpack_one/pallas_call | solution.py:1129
  142.8 0.6 small_out.1
  143.4 2.3 %join.1 = (f32[8,128]{1,0:T(8,128)S(1)}, f32[1024,512]{1,0:T(8,128)}, f32[1024,512]{1,0:T(8,128)}) custom-call(f32[8,128]{1,0:T(8,128)S(1)} %get-tuple-element.287.refs_0_, f32[2,512,512]{2,1,0:T(8,128)S(1)} %get-tuple-element.288.refs_1_, f32[2,512,512]{2,1,0:T(8,128)S(1)} %collective-permute-done.35.refs_2_), custom_call_target="tpu_custom_call" | custom-call | flops 1 | bytes 1 | tf_op jit(solution)/shard_map/join/pallas_call | solution.py:1129
  145.7 1.1 gate_out_one.1
  146.9 3.7 %collective-permute-done.37.refs_2_ = bf16[1792,128]{1,0:T(8,128)(2,1)S(1)} collective-permute-done((bf16[1792,128]{1,0:T(8,128)(2,1)S(1)}, bf16[1792,128]{1,0:T(8,128)(2,1)S(1)}, u32[]{:S(2)}, u32[]{:S(2)}) %collective-permute-start.37) | collective-permute-done | bytes 458784 | tf_op jit(solution)/shard_map/ppermute | solution.py:1150
  150.6 1.1 collective-permute-done.38.refs_4_
  151.8 1.2 collective-permute-start.39
  153.0 2.0 %unpack_zero.1 = (f32[8,128]{1,0:T(8,128)S(1)}, f32[2,1,768,512]{3,2,1,0:T(8,128)}, f32[2,1,512,768]{3,2,1,0:T(8,128)}) custom-call(f32[8,128]{1,0:T(8,128)S(1)} %get-tuple-element.298.refs_0_, bf16[1792,128]{1,0:T(8,128)(2,1)S(1)} %get-tuple-element.296.refs_1_, ...), custom_call_target="tpu_custom_call", output_to_operand_aliasing={{1}: (5, {}), {2}: (6, {})} | custom-call | flops 1 | bytes 1 | tf_op jit(solution)/shard_map/unpack_zero/pallas_call | solution.py:1129
  155.0 1.7 %gate_out_zero.1 = (f32[8,128]{1,0:T(8,128)}, f32[2,512,512]{2,1,0:T(8,128)}) custom-call(f32[8,128]{1,0:T(8,128)S(1)} %get-tuple-element.306.refs_0_, bf16[1024,128]{1,0:T(8,128)(2,1)S(1)} %get-tuple-element.307.refs_1_, bf16[1024,128]{1,0:T(8,128)(2,1)S(1)} %collective-permute-done.39.refs_2_, ...), custom_call_target="tpu_custom_call", output_to_operand_aliasing={{1}: (3, {})} | custom-call | flops 1 | bytes 1 | tf_op jit(solution)/shard_map/gate_out_zero/pallas_call | solution.py:1129
  (75 shorter events, 2.2 us)
Async XLA Ops:
  0.6 3.4 %copy-start.10 = (f32[2,1,384]{2,1,0:T(1,128)S(1)}, f32[2,1,384]{2,1,0:T(1,128)}, u32[]{:S(2)}) copy-start(f32[2,1,384]{2,1,0:T(1,128)} %refs_2_.1) | copy-start | bytes 9220
  0.7 3.4 %copy-start.8 = (f32[2,1,2,384]{3,2,1,0:T(2,128)S(1)}, f32[2,1,2,384]{3,2,1,0:T(2,128)}, u32[]{:S(2)}) copy-start(f32[2,1,2,384]{3,2,1,0:T(2,128)} %refs_3_.3) | copy-start | bytes 18436
  0.7 3.4 %copy-start.3 = (f32[1024,512]{1,0:T(8,128)S(1)}, f32[1024,512]{1,0:T(8,128)}, u32[]{:S(2)}) copy-start(f32[1024,512]{1,0:T(8,128)} %refs_4_.2) | copy-start | bytes 6291460
  0.7 3.4 %copy-start.9 = (s32[1024]{0:T(1024)S(1)}, s32[1024]{0:T(1024)}, u32[]{:S(2)}) copy-start(s32[1024]{0:T(1024)} %param.13) | copy-start | bytes 12292
  0.7 6.0 %collective-permute-start = (bf16[2,1,768,512]{3,2,1,0:T(8,128)(2,1)}, bf16[2,1,768,512]{3,2,1,0:T(8,128)(2,1)S(1)}, u32[]{:S(2)}, u32[]{:S(2)}) collective-permute-start(bf16[2,1,768,512]{3,2,1,0:T(8,128)(2,1)} %refs_11_.1), channel_id=1, source_target_pairs={{0,16},{16,0},{1,17},{17,1},{2,18},{18,2},{3,19},{19,3},{4,20},{20... | collective-permute-start | bytes 4718600 | tf_op jit(solution)/shard_map/ppermute | solution.py:1145
  0.8 5.8 %collective-permute-start.3 = (bf16[2,1,512,768]{3,2,1,0:T(8,128)(2,1)}, bf16[2,1,512,768]{3,2,1,0:T(8,128)(2,1)S(1)}, u32[]{:S(2)}, u32[]{:S(2)}) collective-permute-start(bf16[2,1,512,768]{3,2,1,0:T(8,128)(2,1)} %refs_3_.5), channel_id=1, source_target_pairs={{0,16},{16,0},{1,17},{17,1},{2,18},{18,2},{3,19},{19,3},{4,20},{20... | collective-permute-start | bytes 4718600 | tf_op jit(solution)/shard_map/ppermute | solution.py:1145
  1.3 5.4 %collective-permute-start.1 = (f32[2,1,384]{2,1,0:T(1,128)}, f32[2,1,384]{2,1,0:T(1,128)S(1)}, u32[]{:S(2)}, u32[]{:S(2)}) collective-permute-start(f32[2,1,384]{2,1,0:T(1,128)} %refs_2_.1), channel_id=1, source_target_pairs={{0,16},{16,0},{1,17},{17,1},{2,18},{18,2},{3,19},{19,3},{4,20},{20... | collective-permute-start | bytes 9224 | tf_op jit(solution)/shard_map/ppermute | solution.py:1145
  1.3 5.3 %collective-permute-start.2 = (f32[2,1,2,384]{3,2,1,0:T(2,128)}, f32[2,1,2,384]{3,2,1,0:T(2,128)S(1)}, u32[]{:S(2)}, u32[]{:S(2)}) collective-permute-start(f32[2,1,2,384]{3,2,1,0:T(2,128)} %refs_3_.3), channel_id=1, source_target_pairs={{0,16},{16,0},{1,17},{17,1},{2,18},{18,2},{3,19},{19,3},{4,20},{20... | collective-permute-start | bytes 18440 | tf_op jit(solution)/shard_map/ppermute | solution.py:1145
  1.8 1.2 copy-start.11
  4.0 2.6 %copy-start = (bf16[2,1,512,768]{3,2,1,0:T(8,128)(2,1)S(1)}, bf16[2,1,512,768]{3,2,1,0:T(8,128)(2,1)}, u32[]{:S(2)}) copy-start(bf16[2,1,512,768]{3,2,1,0:T(8,128)(2,1)} %refs_3_.5) | copy-start | bytes 4718596
  4.0 2.6 %copy-start.4 = (f32[2,512]{1,0:T(2,128)S(1)}, f32[2,512]{1,0:T(2,128)}, u32[]{:S(2)}) copy-start(f32[2,512]{1,0:T(2,128)} %refs_9_.3) | copy-start | bytes 12292
  4.0 2.6 %copy-start.6 = (f32[2,512]{1,0:T(2,128)S(1)}, f32[2,512]{1,0:T(2,128)}, u32[]{:S(2)}) copy-start(f32[2,512]{1,0:T(2,128)} %refs_18_.5) | copy-start | bytes 12292
  6.7 15.7 %copy-start.1 = (bf16[2,1,768,512]{3,2,1,0:T(8,128)(2,1)S(1)}, bf16[2,1,768,512]{3,2,1,0:T(8,128)(2,1)}, u32[]{:S(2)}) copy-start(bf16[2,1,768,512]{3,2,1,0:T(8,128)(2,1)} %refs_11_.1) | copy-start | bytes 4718596
  6.7 15.7 %copy-start.2 = (bf16[2,512,512]{2,1,0:T(8,128)(2,1)S(1)}, bf16[2,512,512]{2,1,0:T(8,128)(2,1)}, u32[]{:S(2)}) copy-start(bf16[2,512,512]{2,1,0:T(8,128)(2,1)} %refs_20_.5) | copy-start | bytes 3145732
  6.7 15.7 %copy-start.5 = (f32[2,512]{1,0:T(2,128)S(1)}, f32[2,512]{1,0:T(2,128)}, u32[]{:S(2)}) copy-start(f32[2,512]{1,0:T(2,128)} %refs_10_.1) | copy-start | bytes 12292
  6.7 15.7 %copy-start.7 = (f32[2,512]{1,0:T(2,128)S(1)}, f32[2,512]{1,0:T(2,128)}, u32[]{:S(2)}) copy-start(f32[2,512]{1,0:T(2,128)} %refs_20_.4) | copy-start | bytes 12292
  41.2 9.3 %collective-permute-start.4 = (bf16[4096,128]{1,0:T(8,128)(2,1)S(1)}, bf16[4096,128]{1,0:T(8,128)(2,1)S(1)}, u32[]{:S(2)}, u32[]{:S(2)}) collective-permute-start(bf16[4096,128]{1,0:T(8,128)(2,1)S(1)} %get-tuple-element.187), channel_id=1, source_target_pairs={{0,16},{16,0},{1,17},{17,1},{2,18},{18,2},{3,19},{19,3},{4,20},{20... | collective-permute-start | bytes 3145736 | tf_op jit(solution)/shard_map/ppermute | solution.py:1145
  53.3 5.1 %collective-permute-start.6 = (bf16[3072,128]{1,0:T(8,128)(2,1)S(1)}, bf16[3072,128]{1,0:T(8,128)(2,1)S(1)}, u32[]{:S(2)}, u32[]{:S(2)}) collective-permute-start(bf16[3072,128]{1,0:T(8,128)(2,1)S(1)} %get-tuple-element.212), channel_id=1, source_target_pairs={{0,16},{16,0},{1,17},{17,1},{2,18},{18,2},{3,19},{19,3},{4,20},{20... | collective-permute-start | bytes 2359304 | tf_op jit(solution)/shard_map/ppermute | solution.py:1145
  58.2 16.4 %collective-permute-start.5 = (bf16[4096,128]{1,0:T(8,128)(2,1)S(1)}, bf16[4096,128]{1,0:T(8,128)(2,1)S(1)}, u32[]{:S(2)}, u32[]{:S(2)}) collective-permute-start(bf16[4096,128]{1,0:T(8,128)(2,1)S(1)} %get-tuple-element.208), channel_id=1, source_target_pairs={{0,16},{16,0},{1,17},{17,1},{2,18},{18,2},{3,19},{19,3},{4,20},{20... | collective-permute-start | bytes 3145736 | tf_op jit(solution)/shard_map/ppermute | solution.py:1145
  59.5 13.3 %collective-permute-start.7 = (bf16[1792,128]{1,0:T(8,128)(2,1)S(1)}, bf16[1792,128]{1,0:T(8,128)(2,1)S(1)}, u32[]{:S(2)}, u32[]{:S(2)}) collective-permute-start(bf16[1792,128]{1,0:T(8,128)(2,1)S(1)} %get-tuple-element.218), channel_id=1, source_target_pairs={{0,1},{1,0},{2,3},{3,2},{4,5},{5,4},{6,7},{7,6},{8,9},{9,8},{10,11... | collective-permute-start | bytes 1376264 | tf_op jit(solution)/shard_map/ppermute | solution.py:1150
  59.6 13.2 %collective-permute-start.8 = (bf16[1792,128]{1,0:T(8,128)(2,1)S(1)}, bf16[1792,128]{1,0:T(8,128)(2,1)S(1)}, u32[]{:S(2)}, u32[]{:S(2)}) collective-permute-start(bf16[1792,128]{1,0:T(8,128)(2,1)S(1)} %get-tuple-element.220), channel_id=1, source_target_pairs={{0,2},{1,3},{2,0},{3,1},{4,6},{5,7},{6,4},{7,5},{8,10},{9,11},{10,... | collective-permute-start | bytes 1376264 | tf_op jit(solution)/shard_map/ppermute | solution.py:1150
  73.0 6.9 %collective-permute-start.9 = (bf16[896,128]{1,0:T(8,128)(2,1)S(1)}, bf16[896,128]{1,0:T(8,128)(2,1)S(1)}, u32[]{:S(2)}, u32[]{:S(2)}) collective-permute-start(bf16[896,128]{1,0:T(8,128)(2,1)S(1)} %get-tuple-element.235), channel_id=1, source_target_pairs={{0,2},{1,3},{2,0},{3,1},{4,6},{5,7},{6,4},{7,5},{8,10},{9,11},{10,... | collective-permute-start | bytes 688136 | tf_op jit(solution)/shard_map/ppermute | solution.py:1150
  74.1 6.5 %collective-permute-start.10 = (bf16[896,128]{1,0:T(8,128)(2,1)S(1)}, bf16[896,128]{1,0:T(8,128)(2,1)S(1)}, u32[]{:S(2)}, u32[]{:S(2)}) collective-permute-start(bf16[896,128]{1,0:T(8,128)(2,1)S(1)} %get-tuple-element.237), channel_id=1, source_target_pairs={{0,1},{1,0},{2,3},{3,2},{4,5},{5,4},{6,7},{7,6},{8,9},{9,8},{10,11... | collective-permute-start | bytes 688136 | tf_op jit(solution)/shard_map/ppermute | solution.py:1150
  77.5 6.8 %collective-permute-start.11 = (bf16[3072,128]{1,0:T(8,128)(2,1)S(1)}, bf16[3072,128]{1,0:T(8,128)(2,1)S(1)}, u32[]{:S(2)}, u32[]{:S(2)}) collective-permute-start(bf16[3072,128]{1,0:T(8,128)(2,1)S(1)} %get-tuple-element.241), channel_id=1, source_target_pairs={{0,16},{16,0},{1,17},{17,1},{2,18},{18,2},{3,19},{19,3},{4,20},{20... | collective-permute-start | bytes 2359304 | tf_op jit(solution)/shard_map/ppermute | solution.py:1145
  80.7 8.7 %collective-permute-start.12 = (bf16[448,128]{1,0:T(8,128)(2,1)S(1)}, bf16[448,128]{1,0:T(8,128)(2,1)S(1)}, u32[]{:S(2)}, u32[]{:S(2)}) collective-permute-start(bf16[448,128]{1,0:T(8,128)(2,1)S(1)} %get-tuple-element.252), channel_id=1, source_target_pairs={{0,4},{1,5},{2,6},{3,7},{4,0},{5,1},{6,2},{7,3},{8,12},{9,13},{10,... | collective-permute-start | bytes 344072 | tf_op jit(solution)/shard_map/ppermute | solution.py:1150
  81.0 8.4 %collective-permute-start.13 = (bf16[448,128]{1,0:T(8,128)(2,1)S(1)}, bf16[448,128]{1,0:T(8,128)(2,1)S(1)}, u32[]{:S(2)}, u32[]{:S(2)}) collective-permute-start(bf16[448,128]{1,0:T(8,128)(2,1)S(1)} %get-tuple-element.253), channel_id=1, source_target_pairs={{0,8},{1,9},{2,10},{3,11},{4,12},{5,13},{6,14},{7,15},{8,0},{9,1},... | collective-permute-start | bytes 344072 | tf_op jit(solution)/shard_map/ppermute | solution.py:1150
  81.5 9.0 %collective-permute-start.14 = (bf16[448,128]{1,0:T(8,128)(2,1)S(1)}, bf16[448,128]{1,0:T(8,128)(2,1)S(1)}, u32[]{:S(2)}, u32[]{:S(2)}) collective-permute-start(bf16[448,128]{1,0:T(8,128)(2,1)S(1)} %get-tuple-element.254), channel_id=1, source_target_pairs={{0,12},{1,13},{2,14},{3,15},{4,8},{5,9},{6,10},{7,11},{8,4},{9,5},... | collective-permute-start | bytes 344072 | tf_op jit(solution)/shard_map/ppermute | solution.py:1150
  85.4 9.6 %collective-permute-start.16 = (bf16[1792,128]{1,0:T(8,128)(2,1)S(1)}, bf16[1792,128]{1,0:T(8,128)(2,1)S(1)}, u32[]{:S(2)}, u32[]{:S(2)}) collective-permute-start(bf16[1792,128]{1,0:T(8,128)(2,1)S(1)} %get-tuple-element.259), channel_id=1, source_target_pairs={{0,2},{1,3},{2,0},{3,1},{4,6},{5,7},{6,4},{7,5},{8,10},{9,11},{10,... | collective-permute-start | bytes 1376264 | tf_op jit(solution)/shard_map/ppermute | solution.py:1150
  86.1 10.0 %collective-permute-start.15 = (bf16[1872,128]{1,0:T(8,128)(2,1)S(1)}, bf16[1872,128]{1,0:T(8,128)(2,1)S(1)}, u32[]{:S(2)}, u32[]{:S(2)}) collective-permute-start(bf16[1872,128]{1,0:T(8,128)(2,1)S(1)} %get-tuple-element.257), channel_id=1, source_target_pairs={{0,1},{1,0},{2,3},{3,2},{4,5},{5,4},{6,7},{7,6},{8,9},{9,8},{10,11... | collective-permute-start | bytes 1437704 | tf_op jit(solution)/shard_map/ppermute | solution.py:1150
  90.6 7.0 %collective-permute-start.19 = (bf16[448,128]{1,0:T(8,128)(2,1)S(1)}, bf16[448,128]{1,0:T(8,128)(2,1)S(1)}, u32[]{:S(2)}, u32[]{:S(2)}) collective-permute-start(bf16[448,128]{1,0:T(8,128)(2,1)S(1)} %get-tuple-element.261.refs_1_), channel_id=1, source_target_pairs={{0,12},{1,13},{2,14},{3,15},{4,8},{5,9},{6,10},{7,11},{8,4},{9,5},... | collective-permute-start | bytes 344072 | tf_op jit(solution)/shard_map/ppermute | solution.py:1150
  91.3 12.6 %collective-permute-start.18 = (bf16[448,128]{1,0:T(8,128)(2,1)S(1)}, bf16[448,128]{1,0:T(8,128)(2,1)S(1)}, u32[]{:S(2)}, u32[]{:S(2)}) collective-permute-start(bf16[448,128]{1,0:T(8,128)(2,1)S(1)} %get-tuple-element.261.refs_1_), channel_id=1, source_target_pairs={{0,8},{1,9},{2,10},{3,11},{4,12},{5,13},{6,14},{7,15},{8,0},{9,1},... | collective-permute-start | bytes 344072 | tf_op jit(solution)/shard_map/ppermute | solution.py:1150
  94.4 9.5 %collective-permute-start.17 = (bf16[448,128]{1,0:T(8,128)(2,1)S(1)}, bf16[448,128]{1,0:T(8,128)(2,1)S(1)}, u32[]{:S(2)}, u32[]{:S(2)}) collective-permute-start(bf16[448,128]{1,0:T(8,128)(2,1)S(1)} %get-tuple-element.261.refs_1_), channel_id=1, source_target_pairs={{0,4},{1,5},{2,6},{3,7},{4,0},{5,1},{6,2},{7,3},{8,12},{9,13},{10,... | collective-permute-start | bytes 344072 | tf_op jit(solution)/shard_map/ppermute | solution.py:1150
  96.3 7.7 %collective-permute-start.21 = (bf16[896,128]{1,0:T(8,128)(2,1)S(1)}, bf16[896,128]{1,0:T(8,128)(2,1)S(1)}, u32[]{:S(2)}, u32[]{:S(2)}) collective-permute-start(bf16[896,128]{1,0:T(8,128)(2,1)S(1)} %get-tuple-element.266), channel_id=1, source_target_pairs={{0,1},{1,0},{2,3},{3,2},{4,5},{5,4},{6,7},{7,6},{8,9},{9,8},{10,11... | collective-permute-start | bytes 688136 | tf_op jit(solution)/shard_map/ppermute | solution.py:1150
  97.2 6.8 %collective-permute-start.20 = (bf16[976,128]{1,0:T(8,128)(2,1)S(1)}, bf16[976,128]{1,0:T(8,128)(2,1)S(1)}, u32[]{:S(2)}, u32[]{:S(2)}) collective-permute-start(bf16[976,128]{1,0:T(8,128)(2,1)S(1)} %get-tuple-element.264), channel_id=1, source_target_pairs={{0,2},{1,3},{2,0},{3,1},{4,6},{5,7},{6,4},{7,5},{8,10},{9,11},{10,... | collective-permute-start | bytes 749576 | tf_op jit(solution)/shard_map/ppermute | solution.py:1150
  104.1 5.1 %collective-permute-start.22 = (bf16[528,128]{1,0:T(8,128)(2,1)S(1)}, bf16[528,128]{1,0:T(8,128)(2,1)S(1)}, u32[]{:S(2)}, u32[]{:S(2)}) collective-permute-start(bf16[528,128]{1,0:T(8,128)(2,1)S(1)} %get-tuple-element.269), channel_id=1, source_target_pairs={{0,4},{1,5},{2,6},{3,7},{4,0},{5,1},{6,2},{7,3},{8,12},{9,13},{10,... | collective-permute-start | bytes 405512 | tf_op jit(solution)/shard_map/ppermute | solution.py:1150
  104.2 6.9 %collective-permute-start.23 = (bf16[528,128]{1,0:T(8,128)(2,1)S(1)}, bf16[528,128]{1,0:T(8,128)(2,1)S(1)}, u32[]{:S(2)}, u32[]{:S(2)}) collective-permute-start(bf16[528,128]{1,0:T(8,128)(2,1)S(1)} %get-tuple-element.270), channel_id=1, source_target_pairs={{0,8},{1,9},{2,10},{3,11},{4,12},{5,13},{6,14},{7,15},{8,0},{9,1},... | collective-permute-start | bytes 405512 | tf_op jit(solution)/shard_map/ppermute | solution.py:1150
  104.4 8.5 %collective-permute-start.24 = (bf16[528,128]{1,0:T(8,128)(2,1)S(1)}, bf16[528,128]{1,0:T(8,128)(2,1)S(1)}, u32[]{:S(2)}, u32[]{:S(2)}) collective-permute-start(bf16[528,128]{1,0:T(8,128)(2,1)S(1)} %get-tuple-element.271), channel_id=1, source_target_pairs={{0,12},{1,13},{2,14},{3,15},{4,8},{5,9},{6,10},{7,11},{8,4},{9,5},... | collective-permute-start | bytes 405512 | tf_op jit(solution)/shard_map/ppermute | solution.py:1150
  107.7 12.6 %collective-permute-start.25 = (bf16[896,128]{1,0:T(8,128)(2,1)S(1)}, bf16[896,128]{1,0:T(8,128)(2,1)S(1)}, u32[]{:S(2)}, u32[]{:S(2)}) collective-permute-start(bf16[896,128]{1,0:T(8,128)(2,1)S(1)} %get-tuple-element.273.refs_1_), channel_id=1, source_target_pairs={{0,2},{1,3},{2,0},{3,1},{4,6},{5,7},{6,4},{7,5},{8,10},{9,11},{10,... | collective-permute-start | bytes 688136 | tf_op jit(solution)/shard_map/ppermute | solution.py:1150
  108.4 11.9 %collective-permute-start.26 = (bf16[896,128]{1,0:T(8,128)(2,1)S(1)}, bf16[896,128]{1,0:T(8,128)(2,1)S(1)}, u32[]{:S(2)}, u32[]{:S(2)}) collective-permute-start(bf16[896,128]{1,0:T(8,128)(2,1)S(1)} %get-tuple-element.274.refs_3_), channel_id=1, source_target_pairs={{0,1},{1,0},{2,3},{3,2},{4,5},{5,4},{6,7},{7,6},{8,9},{9,8},{10,11... | collective-permute-start | bytes 688136 | tf_op jit(solution)/shard_map/ppermute | solution.py:1150
  113.0 7.6 %collective-permute-start.31 = (bf16[448,128]{1,0:T(8,128)(2,1)S(1)}, bf16[448,128]{1,0:T(8,128)(2,1)S(1)}, u32[]{:S(2)}, u32[]{:S(2)}) collective-permute-start(bf16[448,128]{1,0:T(8,128)(2,1)S(1)} %get-tuple-element.278.refs_1_), channel_id=1, source_target_pairs={{0,12},{1,13},{2,14},{3,15},{4,8},{5,9},{6,10},{7,11},{8,4},{9,5},... | collective-permute-start | bytes 344072 | tf_op jit(solution)/shard_map/ppermute | solution.py:1150
  114.8 13.2 %collective-permute-start.30 = (bf16[448,128]{1,0:T(8,128)(2,1)S(1)}, bf16[448,128]{1,0:T(8,128)(2,1)S(1)}, u32[]{:S(2)}, u32[]{:S(2)}) collective-permute-start(bf16[448,128]{1,0:T(8,128)(2,1)S(1)} %get-tuple-element.278.refs_1_), channel_id=1, source_target_pairs={{0,8},{1,9},{2,10},{3,11},{4,12},{5,13},{6,14},{7,15},{8,0},{9,1},... | collective-permute-start | bytes 344072 | tf_op jit(solution)/shard_map/ppermute | solution.py:1150
  120.3 7.8 %collective-permute-start.29 = (bf16[448,128]{1,0:T(8,128)(2,1)S(1)}, bf16[448,128]{1,0:T(8,128)(2,1)S(1)}, u32[]{:S(2)}, u32[]{:S(2)}) collective-permute-start(bf16[448,128]{1,0:T(8,128)(2,1)S(1)} %get-tuple-element.278.refs_1_), channel_id=1, source_target_pairs={{0,4},{1,5},{2,6},{3,7},{4,0},{5,1},{6,2},{7,3},{8,12},{9,13},{10,... | collective-permute-start | bytes 344072 | tf_op jit(solution)/shard_map/ppermute | solution.py:1150
  120.3 15.6 %collective-permute-start.27 = (bf16[1792,128]{1,0:T(8,128)(2,1)S(1)}, bf16[1792,128]{1,0:T(8,128)(2,1)S(1)}, u32[]{:S(2)}, u32[]{:S(2)}) collective-permute-start(bf16[1792,128]{1,0:T(8,128)(2,1)S(1)} %get-tuple-element.275.refs_1_), channel_id=1, source_target_pairs={{0,1},{1,0},{2,3},{3,2},{4,5},{5,4},{6,7},{7,6},{8,9},{9,8},{10,11... | collective-permute-start | bytes 1376264 | tf_op jit(solution)/shard_map/ppermute | solution.py:1150
  120.4 15.5 %collective-permute-start.28 = (bf16[1792,128]{1,0:T(8,128)(2,1)S(1)}, bf16[1792,128]{1,0:T(8,128)(2,1)S(1)}, u32[]{:S(2)}, u32[]{:S(2)}) collective-permute-start(bf16[1792,128]{1,0:T(8,128)(2,1)S(1)} %get-tuple-element.276.refs_3_), channel_id=1, source_target_pairs={{0,2},{1,3},{2,0},{3,1},{4,6},{5,7},{6,4},{7,5},{8,10},{9,11},{10,... | collective-permute-start | bytes 1376264 | tf_op jit(solution)/shard_map/ppermute | solution.py:1150
  128.1 7.8 %collective-permute-start.32 = (bf16[896,128]{1,0:T(8,128)(2,1)S(1)}, bf16[896,128]{1,0:T(8,128)(2,1)S(1)}, u32[]{:S(2)}, u32[]{:S(2)}) collective-permute-start(bf16[896,128]{1,0:T(8,128)(2,1)S(1)} %get-tuple-element.280.refs_3_), channel_id=1, source_target_pairs={{0,2},{1,3},{2,0},{3,1},{4,6},{5,7},{6,4},{7,5},{8,10},{9,11},{10,... | collective-permute-start | bytes 688136 | tf_op jit(solution)/shard_map/ppermute | solution.py:1150
  128.2 7.8 %collective-permute-start.33 = (bf16[896,128]{1,0:T(8,128)(2,1)S(1)}, bf16[896,128]{1,0:T(8,128)(2,1)S(1)}, u32[]{:S(2)}, u32[]{:S(2)}) collective-permute-start(bf16[896,128]{1,0:T(8,128)(2,1)S(1)} %get-tuple-element.281.refs_5_), channel_id=1, source_target_pairs={{0,1},{1,0},{2,3},{3,2},{4,5},{5,4},{6,7},{7,6},{8,9},{9,8},{10,11... | collective-permute-start | bytes 688136 | tf_op jit(solution)/shard_map/ppermute | solution.py:1150
  136.0 7.4 %collective-permute-start.35 = (f32[2,512,512]{2,1,0:T(8,128)S(1)}, f32[2,512,512]{2,1,0:T(8,128)S(1)}, u32[]{:S(2)}, u32[]{:S(2)}) collective-permute-start(f32[2,512,512]{2,1,0:T(8,128)S(1)} %get-tuple-element.288.refs_1_), channel_id=1, source_target_pairs={{0,16},{16,0},{1,17},{17,1},{2,18},{18,2},{3,19},{19,3},{4,20},{20... | collective-permute-start | bytes 6291464 | tf_op jit(solution)/shard_map/ppermute | solution.py:1145
  138.5 12.1 %collective-permute-start.37 = (bf16[1792,128]{1,0:T(8,128)(2,1)S(1)}, bf16[1792,128]{1,0:T(8,128)(2,1)S(1)}, u32[]{:S(2)}, u32[]{:S(2)}) collective-permute-start(bf16[1792,128]{1,0:T(8,128)(2,1)S(1)} %get-tuple-element.296.refs_1_), channel_id=1, source_target_pairs={{0,1},{1,0},{2,3},{3,2},{4,5},{5,4},{6,7},{7,6},{8,9},{9,8},{10,11... | collective-permute-start | bytes 1376264 | tf_op jit(solution)/shard_map/ppermute | solution.py:1150
  139.9 11.8 %collective-permute-start.38 = (bf16[1792,128]{1,0:T(8,128)(2,1)S(1)}, bf16[1792,128]{1,0:T(8,128)(2,1)S(1)}, u32[]{:S(2)}, u32[]{:S(2)}) collective-permute-start(bf16[1792,128]{1,0:T(8,128)(2,1)S(1)} %get-tuple-element.297.refs_3_), channel_id=1, source_target_pairs={{0,2},{1,3},{2,0},{3,1},{4,6},{5,7},{6,4},{7,5},{8,10},{9,11},{10,... | collective-permute-start | bytes 1376264 | tf_op jit(solution)/shard_map/ppermute | solution.py:1150
  140.0 5.7 %collective-permute-start.36 = (bf16[1024,128]{1,0:T(8,128)(2,1)S(1)}, bf16[1024,128]{1,0:T(8,128)(2,1)S(1)}, u32[]{:S(2)}, u32[]{:S(2)}) collective-permute-start(bf16[1024,128]{1,0:T(8,128)(2,1)S(1)} %get-tuple-element.294.refs_1_), channel_id=1, source_target_pairs={{0,16},{16,0},{1,17},{17,1},{2,18},{18,2},{3,19},{19,3},{4,20},{20... | collective-permute-start | bytes 786440 | tf_op jit(solution)/shard_map/ppermute | solution.py:1145
  140.7 2.1 %collective-permute-start.34 = (f32[80,128]{1,0:T(8,128)S(1)}, f32[80,128]{1,0:T(8,128)S(1)}, u32[]{:S(2)}, u32[]{:S(2)}) collective-permute-start(f32[80,128]{1,0:T(8,128)S(1)} %get-tuple-element.286.refs_1_), channel_id=1, source_target_pairs={{0,16},{16,0},{1,17},{17,1},{2,18},{18,2},{3,19},{19,3},{4,20},{20... | collective-permute-start | bytes 122888 | tf_op jit(solution)/shard_map/ppermute | solution.py:1145
  151.8 3.3 %collective-permute-start.39 = (bf16[1024,128]{1,0:T(8,128)(2,1)S(1)}, bf16[1024,128]{1,0:T(8,128)(2,1)S(1)}, u32[]{:S(2)}, u32[]{:S(2)}) collective-permute-start(bf16[1024,128]{1,0:T(8,128)(2,1)S(1)} %get-tuple-element.307.refs_1_), channel_id=1, source_target_pairs={{0,16},{16,0},{1,17},{17,1},{2,18},{18,2},{3,19},{19,3},{4,20},{20... | collective-permute-start | bytes 786440 | tf_op jit(solution)/shard_map/ppermute | solution.py:1145

commit v7 on v6

--- a/solution.py
+++ b/solution.py
@@ -20,7 +20,7 @@
 
 LANES = 128
 ELEMENT_ROWS = 512
-UNROLL = 8
+UNROLL = 16
 CORES_COST = 0
 
 
@@ -90,31 +90,40 @@
     states = lanes.states
     span = drives[0].shape[0] // 8
 
-    def step(i, carry):
-        values, sums = carry
-        up = pl.multiple_of(i * 8, 8)
-        down = pl.multiple_of((span - 1 - i) * 8, 8)
-        places = (jnp.where(first_forward, up, down), jnp.where(first_forward, down, up))
-        new = []
+    def one_side(side, i, values, sums):
+        upward = first_forward if side == 0 else jnp.logical_not(first_forward)
+        rows = pl.ds(pl.multiple_of(jnp.where(upward, i, span - 1 - i) * 8, 8), 8)
+        keep = masks[side][rows, :]
+        keep = jnp.concatenate([keep] * (states // LANES), 1)
+        step_re, step_im = lanes.step[side]
+        step_re, step_im = step_re * keep, step_im * keep
+        re, im = values
+        drive_re = drives[side][rows, :states]
+        drive_im = drives[side][rows, states:]
+        re, im = (
+            step_re * re - step_im * im + drive_re,
+            step_re * im + step_im * re + drive_im,
+        )
+        if visit is not None:
+            sums = visit(side, rows, re, im, sums)
+        return (re, im), sums
+
+    if totals:
+        values, sums = [], []
         for side in range(2):
-            rows = pl.ds(pl.multiple_of(places[side], 8), 8)
-            keep = masks[side][rows, :]
-            keep = jnp.concatenate([keep] * (states // LANES), 1)
-            step_re, step_im = lanes.step[side]
-            step_re, step_im = step_re * keep, step_im * keep
-            re, im = values[side]
-            drive_re = drives[side][rows, :states]
-            drive_im = drives[side][rows, states:]
-            re, im = (
-                step_re * re - step_im * im + drive_re,
-                step_re * im + step_im * re + drive_im,
-            )
-            new.append((re, im))
-            if visit is not None:
-                sums = visit(side, rows, re, im, sums)
-        return tuple(new), sums
-
-    return lax.fori_loop(0, span, step, (init, totals), unroll=UNROLL if totals else span)
+
+            def step(i, carry, side=side):
+                return one_side(side, i, *carry)
+
+            value, total = lax.fori_loop(0, span, step, (init[side], totals[side]), unroll=UNROLL)
+            values.append(value)
+            sums.append(total)
+        return tuple(values), tuple(sums)
+
+    def step(i, values):
+        return tuple(one_side(side, i, values[side], ())[0] for side in range(2))
+
+    return lax.fori_loop(0, span, step, init, unroll=span), ()
 
 
 def run_chain(first_up, lanes, side, ends, whole, start, places):
@@ -665,13 +674,11 @@
         moved_im = adjoints[side][where, width:] - drive_im
         adjoints[side][where, :width] = re
         adjoints[side][where, width:] = im
-        mine = sums[side]
-        mine = (
-            mine[0] + (re * moved_re + im * moved_im),
-            mine[1] + (im * moved_re - re * moved_im),
-            mine[2] + (re * drive_re + im * drive_im),
+        return (
+            sums[0] + (re * moved_re + im * moved_im),
+            sums[1] + (im * moved_re - re * moved_im),
+            sums[2] + (re * drive_re + im * drive_im),
         )
-        return (mine, sums[1]) if side == 0 else (sums[0], mine)
 
     _, sums = sweep(
         running_up, grads, (masks[1], masks[0]), lanes, init, visit, ((zero, zero, zero), (zero, zero, zero))

time: 157 us -> 157 us (level)
  no operation moved by 1% of the time
where the time goes in v7:
time: 157 us
  blocking collectives  44.8 us (29%)
  Pallas kernels  39.9 us (25%)
  waiting for transfers between devices  35.6 us (23%)
  starting transfers between devices  33.9 us (22%)
    all_to_all x4, blocking collectives, exchanged(): lax.all_to_all(payload, ('seq', 'dir'), 0, 0, tiled=True, axis_index_grou...  44.8 us
    pallas_call x31, Pallas kernels, run(): pl.pallas_call(body, out_shape=shapes, in_specs=specs, out_specs=[whole]...  39.9 us
    ppermute x28, waiting for transfers between devices, across(): return lax.ppermute(value, 'seq', [(i, i ^ bits) for i in range(count)])  34.1 us
    ppermute x28, starting transfers between devices, across(): return lax.ppermute(value, 'seq', [(i, i ^ bits) for i in range(count)])  26.2 us
    ppermute x12, starting transfers between devices, swap(): return lax.ppermute(value, 'dir', [(0, 1), (1, 0)])  7.66 us
  transfers between devices with their start and end apart: 40, of which 14 were waited for; matrix products, arithmetic and copies ran while one was open for 0% of the time, Pallas kernels for 15%

profile of v7, /device:TPU:1, one launch (start us, length us, event | category | flops | bytes accessed | tf_op | source)
XLA Modules:
  0.0 156.8 jit_solution(14990452653978906549)
XLA Ops:
  0.8 0.5 collective-permute-start.3
  1.3 0.4 collective-permute-start.2
  1.8 1.2 copy-done.11
  3.0 1.0 open_norm.1
  4.1 1.1 open_masks.1
  5.1 1.5 collective-permute-done.1.refs_10_
  6.7 1.5 open_scan.1
  8.2 14.2 %all_to_all.20.refs_1_ = bf16[32,8,128]{2,1,0:T(8,128)(2,1)S(1)} all-to-all(bf16[32,8,128]{2,1,0:T(8,128)(2,1)S(1)} %get-tuple-element.170), channel_id=1, replica_groups=mesh['dir'=2,'seq'=16] {'seq','dir'}, dimensions={0} | all-to-all | bytes 131072 | tf_op jit(solution)/shard_map/all_to_all | solution.py:1174
  22.4 4.3 %mid.1 = (f32[8,128]{1,0:T(8,128)S(1)}, bf16[512,768]{1,0:T(8,128)(2,1)S(1)}, bf16[512,768]{1,0:T(8,128)(2,1)S(1)}, f32[512,512]{1,0:T(8,128)S(1)}, f32[512,512]...) custom-call(f32[8,128]{1,0:T(8,128)S(1)} %get-tuple-element.169.refs, ...), custom_call_target="tpu_custom_call" | custom-call | flops 1 | bytes 1 | tf_op jit(solution)/shard_map/mid/pallas_call | solution.py:1136
  26.7 9.1 %all_to_all.21.refs_1_ = bf16[32,8,128]{2,1,0:T(8,128)(2,1)S(1)} all-to-all(bf16[32,8,128]{2,1,0:T(8,128)(2,1)S(1)} %get-tuple-element.179), channel_id=1, replica_groups=mesh['dir'=2,'seq'=16] {'seq','dir'}, dimensions={0} | all-to-all | bytes 131072 | tf_op jit(solution)/shard_map/all_to_all | solution.py:1174
  35.8 5.4 %turn.1 = (f32[8,128]{1,0:T(8,128)S(1)}, bf16[512,768]{1,0:T(8,128)(2,1)S(1)}, bf16[512,768]{1,0:T(8,128)(2,1)S(1)}, f32[512,512]{1,0:T(8,128)S(1)}, f32[512,512...) custom-call(f32[8,128]{1,0:T(8,128)S(1)} %get-tuple-element.178.refs, ...), custom_call_target="tpu_custom_call" | custom-call | flops 1 | bytes 1 | tf_op jit(solution)/shard_map/turn/pallas_call | solution.py:1136
  41.2 0.4 collective-permute-start.4
  41.6 8.8 %all_to_all.22.refs_2_ = bf16[32,8,128]{2,1,0:T(8,128)(2,1)S(1)} all-to-all(bf16[32,8,128]{2,1,0:T(8,128)(2,1)S(1)} %get-tuple-element.189), channel_id=1, replica_groups=mesh['dir'=2,'seq'=16] {'seq','dir'}, dimensions={0} | all-to-all | bytes 131072 | tf_op jit(solution)/shard_map/all_to_all | solution.py:1174
  50.5 2.7 %scan_one.1 = (f32[8,128]{1,0:T(8,128)S(1)}, bf16[512,768]{1,0:T(8,128)(2,1)S(1)}, bf16[512,768]{1,0:T(8,128)(2,1)S(1)}, f32[8,384]{1,0:T(8,128)S(1)}, bf16[3072...) custom-call(bf16[4096,128]{1,0:T(8,128)(2,1)S(1)} %collective-permute-done.4.refs_0_.refs_2_, ...), custom_call_target="tpu_custom_call" | custom-call | flops 1 | bytes 1 | tf_op jit(solution)/shard_map/scan_one/pallas_call | solution.py:1136
  53.2 0.5 collective-permute-start.6
  53.7 4.5 %back.1 = (f32[8,128]{1,0:T(8,128)S(1)}, f32[512,512]{1,0:T(8,128)S(1)}, f32[512,512]{1,0:T(8,128)S(1)}, f32[512,768]{1,0:T(8,128)S(1)}, f32[512,768]{1,0:T(8,12...) custom-call(f32[8,128]{1,0:T(8,128)S(1)} %get-tuple-element.197.refs, ...), custom_call_target="tpu_custom_call" | custom-call | flops 1 | bytes 1 | tf_op jit(solution)/shard_map/back/pallas_call | solution.py:1136
  58.3 1.0 first_cores.1
  59.5 0.5 collective-permute-start.8
  60.0 12.7 %all_to_all.23.refs_0_.refs_2_ = bf16[32,8,128]{2,1,0:T(8,128)(2,1)S(1)} all-to-all(bf16[32,8,128]{2,1,0:T(8,128)(2,1)S(1)} %get-tuple-element.215), channel_id=1, replica_groups=mesh['dir'=2,'seq'=16] {'seq','dir'}, dimensions={0} | all-to-all | bytes 131072 | tf_op jit(solution)/shard_map/all_to_all | solution.py:1174
  72.7 0.2 first_half.1
  72.9 1.1 collective-permute-start.9
  74.0 0.6 collective-permute-start.10
  74.6 2.8 %scan_zero.1 = (f32[8,128]{1,0:T(8,128)S(1)}, bf16[512,768]{1,0:T(8,128)(2,1)S(1)}, bf16[512,768]{1,0:T(8,128)(2,1)S(1)}, f32[8,384]{1,0:T(8,128)S(1)}, bf16[307...) custom-call(bf16[4096,128]{1,0:T(8,128)(2,1)S(1)} %collective-permute-done.5.refs_0_.refs_2_, ...), custom_call_target="tpu_custom_call" | custom-call | flops 1 | bytes 1 | tf_op jit(solution)/shard_map/scan_zero/pallas_call | solution.py:1136
  77.4 1.0 collective-permute-start.11
  78.4 1.4 final_norm.1
  79.8 0.7 collective-permute-done.10.refs_4_
  80.6 0.3 collective-permute-start.12
  80.9 0.5 collective-permute-start.13
  81.4 2.8 %collective-permute-start.14 = (bf16[448,128]{1,0:T(8,128)(2,1)S(1)}, bf16[448,128]{1,0:T(8,128)(2,1)S(1)}, u32[]{:S(2)}, u32[]{:S(2)}) collective-permute-start(bf16[448,128]{1,0:T(8,128)(2,1)S(1)} %get-tuple-element.254), channel_id=1, source_target_pairs={{0,12},{1,13},{2,14},{3,15},{4,8},{5,9},{6,10},{7,11},{8,4},{9,5},... | collective-permute-start | bytes 344072 | tf_op jit(solution)/shard_map/ppermute | solution.py:1157
  84.2 1.1 second_cores.1
  85.3 0.6 collective-permute-start.16
  85.9 1.1 collective-permute-start.15
  87.0 2.3 %token_order.1 = (f32[8,128]{1,0:T(8,128)S(1)}, f32[2,512,512]{2,1,0:T(8,128)S(1)}) custom-call(f32[8,128]{1,0:T(8,128)S(1)} %get-tuple-element.247.refs_0_, f32[512,512]{1,0:T(8,128)S(1)} %get-tuple-element.248.refs_1_, f32[512,512]{1,0:T(8,128)S(1)} %get-tuple-element.249.refs_2_), custom_call_target="tpu_custom_call" | custom-call | flops 1 | bytes 1 | tf_op jit(solution)/shard_map/token_order/pallas_call | solution.py:1136
  89.3 1.1 collective-permute-done.14.refs_4_
  90.5 0.7 collective-permute-start.19
  91.1 3.1 %collective-permute-start.18 = (bf16[448,128]{1,0:T(8,128)(2,1)S(1)}, bf16[448,128]{1,0:T(8,128)(2,1)S(1)}, u32[]{:S(2)}, u32[]{:S(2)}) collective-permute-start(bf16[448,128]{1,0:T(8,128)(2,1)S(1)} %get-tuple-element.261.refs_1_), channel_id=1, source_target_pairs={{0,8},{1,9},{2,10},{3,11},{4,12},{5,13},{6,14},{7,15},{8,0},{9,1},... | collective-permute-start | bytes 344072 | tf_op jit(solution)/shard_map/ppermute | solution.py:1157
  94.3 0.7 collective-permute-done.16.refs_4_
  94.9 0.8 collective-permute-done.15.refs_2_
  95.8 0.2 second_half.1
  96.0 1.1 collective-permute-start.21
  97.1 0.4 collective-permute-start.20
  97.4 6.3 %collective-permute-done.18.refs_3_ = bf16[448,128]{1,0:T(8,128)(2,1)S(1)} collective-permute-done((bf16[448,128]{1,0:T(8,128)(2,1)S(1)}, bf16[448,128]{1,0:T(8,128)(2,1)S(1)}, u32[]{:S(2)}, u32[]{:S(2)}) %collective-permute-start.18) | collective-permute-done | bytes 114720 | tf_op jit(solution)/shard_map/ppermute | solution.py:1157
  104.0 0.3 collective-permute-start.23
  104.3 3.2 %collective-permute-start.24 = (bf16[528,128]{1,0:T(8,128)(2,1)S(1)}, bf16[528,128]{1,0:T(8,128)(2,1)S(1)}, u32[]{:S(2)}, u32[]{:S(2)}) collective-permute-start(bf16[528,128]{1,0:T(8,128)(2,1)S(1)} %get-tuple-element.271), channel_id=1, source_target_pairs={{0,12},{1,13},{2,14},{3,15},{4,8},{5,9},{6,10},{7,11},{8,4},{9,5},... | collective-permute-start | bytes 405512 | tf_op jit(solution)/shard_map/ppermute | solution.py:1157
  107.6 0.6 collective-permute-start.25
  108.3 0.8 collective-permute-done.22.refs_2_
  109.0 1.9 %collective-permute-done.23.refs_3_ = bf16[528,128]{1,0:T(8,128)(2,1)S(1)} collective-permute-done((bf16[528,128]{1,0:T(8,128)(2,1)S(1)}, bf16[528,128]{1,0:T(8,128)(2,1)S(1)}, u32[]{:S(2)}, u32[]{:S(2)}) %collective-permute-start.23) | collective-permute-done | bytes 135200 | tf_op jit(solution)/shard_map/ppermute | solution.py:1157
  111.0 1.7 %collective-permute-done.24.refs_4_ = bf16[528,128]{1,0:T(8,128)(2,1)S(1)} collective-permute-done((bf16[528,128]{1,0:T(8,128)(2,1)S(1)}, bf16[528,128]{1,0:T(8,128)(2,1)S(1)}, u32[]{:S(2)}, u32[]{:S(2)}) %collective-permute-start.24) | collective-permute-done | bytes 135200 | tf_op jit(solution)/shard_map/ppermute | solution.py:1157
  112.8 1.9 %collective-permute-start.31 = (bf16[448,128]{1,0:T(8,128)(2,1)S(1)}, bf16[448,128]{1,0:T(8,128)(2,1)S(1)}, u32[]{:S(2)}, u32[]{:S(2)}) collective-permute-start(bf16[448,128]{1,0:T(8,128)(2,1)S(1)} %get-tuple-element.278.refs_1_), channel_id=1, source_target_pairs={{0,12},{1,13},{2,14},{3,15},{4,8},{5,9},{6,10},{7,11},{8,4},{9,5},... | collective-permute-start | bytes 344072 | tf_op jit(solution)/shard_map/ppermute | solution.py:1157
  114.6 5.5 %collective-permute-start.30 = (bf16[448,128]{1,0:T(8,128)(2,1)S(1)}, bf16[448,128]{1,0:T(8,128)(2,1)S(1)}, u32[]{:S(2)}, u32[]{:S(2)}) collective-permute-start(bf16[448,128]{1,0:T(8,128)(2,1)S(1)} %get-tuple-element.278.refs_1_), channel_id=1, source_target_pairs={{0,8},{1,9},{2,10},{3,11},{4,12},{5,13},{6,14},{7,15},{8,0},{9,1},... | collective-permute-start | bytes 344072 | tf_op jit(solution)/shard_map/ppermute | solution.py:1157
  120.4 7.6 %collective-permute-done.30.refs_3_ = bf16[448,128]{1,0:T(8,128)(2,1)S(1)} collective-permute-done((bf16[448,128]{1,0:T(8,128)(2,1)S(1)}, bf16[448,128]{1,0:T(8,128)(2,1)S(1)}, u32[]{:S(2)}, u32[]{:S(2)}) %collective-permute-start.30) | collective-permute-done | bytes 114720 | tf_op jit(solution)/shard_map/ppermute | solution.py:1157
  128.1 7.6 %collective-permute-done.32.refs_4_ = bf16[896,128]{1,0:T(8,128)(2,1)S(1)} collective-permute-done((bf16[896,128]{1,0:T(8,128)(2,1)S(1)}, bf16[896,128]{1,0:T(8,128)(2,1)S(1)}, u32[]{:S(2)}, u32[]{:S(2)}) %collective-permute-start.32) | collective-permute-done | bytes 229408 | tf_op jit(solution)/shard_map/ppermute | solution.py:1157
  135.9 2.5 %collective-permute-start.35 = (f32[2,512,512]{2,1,0:T(8,128)S(1)}, f32[2,512,512]{2,1,0:T(8,128)S(1)}, u32[]{:S(2)}, u32[]{:S(2)}) collective-permute-start(f32[2,512,512]{2,1,0:T(8,128)S(1)} %get-tuple-element.288.refs_1_), channel_id=1, source_target_pairs={{0,16},{16,0},{1,17},{17,1},{2,18},{18,2},{3,19},{19,3},{4,20},{20... | collective-permute-start | bytes 6291464 | tf_op jit(solution)/shard_map/ppermute | solution.py:1152
  138.4 1.4 collective-permute-start.37
  139.9 0.7 collective-permute-start.36
  140.6 2.0 %unpack_one.1 = (f32[8,128]{1,0:T(8,128)S(1)}, f32[2,1,768,512]{3,2,1,0:T(8,128)}, f32[2,1,512,768]{3,2,1,0:T(8,128)}) custom-call(f32[8,128]{1,0:T(8,128)S(1)} %get-tuple-element.284.refs_0_, bf16[1792,128]{1,0:T(8,128)(2,1)S(1)} %get-tuple-element.275.refs_1_, bf16[1792,128]{1,0:T(8,128)(2,1)S(1)} %collective-permute-done.27.refs_0_.refs_2_, ...), custom_call_target="tpu_custom_call" | custom-call | flops 1 | bytes 1 | tf_op jit(solution)/shard_map/unpack_one/pallas_call | solution.py:1136
  142.7 0.6 small_out.1
  143.3 2.3 %join.1 = (f32[8,128]{1,0:T(8,128)S(1)}, f32[1024,512]{1,0:T(8,128)}, f32[1024,512]{1,0:T(8,128)}) custom-call(f32[8,128]{1,0:T(8,128)S(1)} %get-tuple-element.287.refs_0_, f32[2,512,512]{2,1,0:T(8,128)S(1)} %get-tuple-element.288.refs_1_, f32[2,512,512]{2,1,0:T(8,128)S(1)} %collective-permute-done.35.refs_2_), custom_call_target="tpu_custom_call" | custom-call | flops 1 | bytes 1 | tf_op jit(solution)/shard_map/join/pallas_call | solution.py:1136
  145.6 1.1 gate_out_one.1
  146.7 3.7 %collective-permute-done.37.refs_2_ = bf16[1792,128]{1,0:T(8,128)(2,1)S(1)} collective-permute-done((bf16[1792,128]{1,0:T(8,128)(2,1)S(1)}, bf16[1792,128]{1,0:T(8,128)(2,1)S(1)}, u32[]{:S(2)}, u32[]{:S(2)}) %collective-permute-start.37) | collective-permute-done | bytes 458784 | tf_op jit(solution)/shard_map/ppermute | solution.py:1157
  150.5 1.1 collective-permute-done.38.refs_4_
  151.6 1.2 collective-permute-start.39
  152.9 2.0 %unpack_zero.1 = (f32[8,128]{1,0:T(8,128)S(1)}, f32[2,1,768,512]{3,2,1,0:T(8,128)}, f32[2,1,512,768]{3,2,1,0:T(8,128)}) custom-call(f32[8,128]{1,0:T(8,128)S(1)} %get-tuple-element.298.refs_0_, bf16[1792,128]{1,0:T(8,128)(2,1)S(1)} %get-tuple-element.296.refs_1_, ...), custom_call_target="tpu_custom_call", output_to_operand_aliasing={{1}: (5, {}), {2}: (6, {})} | custom-call | flops 1 | bytes 1 | tf_op jit(solution)/shard_map/unpack_zero/pallas_call | solution.py:1136
  154.9 1.7 %gate_out_zero.1 = (f32[8,128]{1,0:T(8,128)}, f32[2,512,512]{2,1,0:T(8,128)}) custom-call(f32[8,128]{1,0:T(8,128)S(1)} %get-tuple-element.306.refs_0_, bf16[1024,128]{1,0:T(8,128)(2,1)S(1)} %get-tuple-element.307.refs_1_, bf16[1024,128]{1,0:T(8,128)(2,1)S(1)} %collective-permute-done.39.refs_2_, ...), custom_call_target="tpu_custom_call", output_to_operand_aliasing={{1}: (3, {})} | custom-call | flops 1 | bytes 1 | tf_op jit(solution)/shard_map/gate_out_zero/pallas_call | solution.py:1136
  (75 shorter events, 2.1 us)
Async XLA Ops:
  0.6 3.4 %copy-start.10 = (f32[2,1,384]{2,1,0:T(1,128)S(1)}, f32[2,1,384]{2,1,0:T(1,128)}, u32[]{:S(2)}) copy-start(f32[2,1,384]{2,1,0:T(1,128)} %refs_2_.1) | copy-start | bytes 9220
  0.7 3.4 %copy-start.8 = (f32[2,1,2,384]{3,2,1,0:T(2,128)S(1)}, f32[2,1,2,384]{3,2,1,0:T(2,128)}, u32[]{:S(2)}) copy-start(f32[2,1,2,384]{3,2,1,0:T(2,128)} %refs_3_.3) | copy-start | bytes 18436
  0.7 3.4 %copy-start.3 = (f32[1024,512]{1,0:T(8,128)S(1)}, f32[1024,512]{1,0:T(8,128)}, u32[]{:S(2)}) copy-start(f32[1024,512]{1,0:T(8,128)} %refs_4_.2) | copy-start | bytes 6291460
  0.7 3.4 %copy-start.9 = (s32[1024]{0:T(1024)S(1)}, s32[1024]{0:T(1024)}, u32[]{:S(2)}) copy-start(s32[1024]{0:T(1024)} %param.13) | copy-start | bytes 12292
  0.7 6.0 %collective-permute-start = (bf16[2,1,768,512]{3,2,1,0:T(8,128)(2,1)}, bf16[2,1,768,512]{3,2,1,0:T(8,128)(2,1)S(1)}, u32[]{:S(2)}, u32[]{:S(2)}) collective-permute-start(bf16[2,1,768,512]{3,2,1,0:T(8,128)(2,1)} %refs_11_.1), channel_id=1, source_target_pairs={{0,16},{16,0},{1,17},{17,1},{2,18},{18,2},{3,19},{19,3},{4,20},{20... | collective-permute-start | bytes 4718600 | tf_op jit(solution)/shard_map/ppermute | solution.py:1152
  0.8 5.8 %collective-permute-start.3 = (bf16[2,1,512,768]{3,2,1,0:T(8,128)(2,1)}, bf16[2,1,512,768]{3,2,1,0:T(8,128)(2,1)S(1)}, u32[]{:S(2)}, u32[]{:S(2)}) collective-permute-start(bf16[2,1,512,768]{3,2,1,0:T(8,128)(2,1)} %refs_3_.5), channel_id=1, source_target_pairs={{0,16},{16,0},{1,17},{17,1},{2,18},{18,2},{3,19},{19,3},{4,20},{20... | collective-permute-start | bytes 4718600 | tf_op jit(solution)/shard_map/ppermute | solution.py:1152
  1.3 5.4 %collective-permute-start.1 = (f32[2,1,384]{2,1,0:T(1,128)}, f32[2,1,384]{2,1,0:T(1,128)S(1)}, u32[]{:S(2)}, u32[]{:S(2)}) collective-permute-start(f32[2,1,384]{2,1,0:T(1,128)} %refs_2_.1), channel_id=1, source_target_pairs={{0,16},{16,0},{1,17},{17,1},{2,18},{18,2},{3,19},{19,3},{4,20},{20... | collective-permute-start | bytes 9224 | tf_op jit(solution)/shard_map/ppermute | solution.py:1152
  1.3 5.3 %collective-permute-start.2 = (f32[2,1,2,384]{3,2,1,0:T(2,128)}, f32[2,1,2,384]{3,2,1,0:T(2,128)S(1)}, u32[]{:S(2)}, u32[]{:S(2)}) collective-permute-start(f32[2,1,2,384]{3,2,1,0:T(2,128)} %refs_3_.3), channel_id=1, source_target_pairs={{0,16},{16,0},{1,17},{17,1},{2,18},{18,2},{3,19},{19,3},{4,20},{20... | collective-permute-start | bytes 18440 | tf_op jit(solution)/shard_map/ppermute | solution.py:1152
  1.8 1.2 copy-start.11
  4.0 2.6 %copy-start = (bf16[2,1,512,768]{3,2,1,0:T(8,128)(2,1)S(1)}, bf16[2,1,512,768]{3,2,1,0:T(8,128)(2,1)}, u32[]{:S(2)}) copy-start(bf16[2,1,512,768]{3,2,1,0:T(8,128)(2,1)} %refs_3_.5) | copy-start | bytes 4718596
  4.0 2.6 %copy-start.4 = (f32[2,512]{1,0:T(2,128)S(1)}, f32[2,512]{1,0:T(2,128)}, u32[]{:S(2)}) copy-start(f32[2,512]{1,0:T(2,128)} %refs_9_.3) | copy-start | bytes 12292
  4.0 2.6 %copy-start.6 = (f32[2,512]{1,0:T(2,128)S(1)}, f32[2,512]{1,0:T(2,128)}, u32[]{:S(2)}) copy-start(f32[2,512]{1,0:T(2,128)} %refs_18_.5) | copy-start | bytes 12292
  6.7 15.7 %copy-start.1 = (bf16[2,1,768,512]{3,2,1,0:T(8,128)(2,1)S(1)}, bf16[2,1,768,512]{3,2,1,0:T(8,128)(2,1)}, u32[]{:S(2)}) copy-start(bf16[2,1,768,512]{3,2,1,0:T(8,128)(2,1)} %refs_11_.1) | copy-start | bytes 4718596
  6.7 15.7 %copy-start.2 = (bf16[2,512,512]{2,1,0:T(8,128)(2,1)S(1)}, bf16[2,512,512]{2,1,0:T(8,128)(2,1)}, u32[]{:S(2)}) copy-start(bf16[2,512,512]{2,1,0:T(8,128)(2,1)} %refs_20_.5) | copy-start | bytes 3145732
  6.7 15.7 %copy-start.5 = (f32[2,512]{1,0:T(2,128)S(1)}, f32[2,512]{1,0:T(2,128)}, u32[]{:S(2)}) copy-start(f32[2,512]{1,0:T(2,128)} %refs_10_.1) | copy-start | bytes 12292
  6.7 15.7 %copy-start.7 = (f32[2,512]{1,0:T(2,128)S(1)}, f32[2,512]{1,0:T(2,128)}, u32[]{:S(2)}) copy-start(f32[2,512]{1,0:T(2,128)} %refs_20_.4) | copy-start | bytes 12292
  41.2 9.3 %collective-permute-start.4 = (bf16[4096,128]{1,0:T(8,128)(2,1)S(1)}, bf16[4096,128]{1,0:T(8,128)(2,1)S(1)}, u32[]{:S(2)}, u32[]{:S(2)}) collective-permute-start(bf16[4096,128]{1,0:T(8,128)(2,1)S(1)} %get-tuple-element.187), channel_id=1, source_target_pairs={{0,16},{16,0},{1,17},{17,1},{2,18},{18,2},{3,19},{19,3},{4,20},{20... | collective-permute-start | bytes 3145736 | tf_op jit(solution)/shard_map/ppermute | solution.py:1152
  53.2 5.1 %collective-permute-start.6 = (bf16[3072,128]{1,0:T(8,128)(2,1)S(1)}, bf16[3072,128]{1,0:T(8,128)(2,1)S(1)}, u32[]{:S(2)}, u32[]{:S(2)}) collective-permute-start(bf16[3072,128]{1,0:T(8,128)(2,1)S(1)} %get-tuple-element.212), channel_id=1, source_target_pairs={{0,16},{16,0},{1,17},{17,1},{2,18},{18,2},{3,19},{19,3},{4,20},{20... | collective-permute-start | bytes 2359304 | tf_op jit(solution)/shard_map/ppermute | solution.py:1152
  58.1 16.4 %collective-permute-start.5 = (bf16[4096,128]{1,0:T(8,128)(2,1)S(1)}, bf16[4096,128]{1,0:T(8,128)(2,1)S(1)}, u32[]{:S(2)}, u32[]{:S(2)}) collective-permute-start(bf16[4096,128]{1,0:T(8,128)(2,1)S(1)} %get-tuple-element.208), channel_id=1, source_target_pairs={{0,16},{16,0},{1,17},{17,1},{2,18},{18,2},{3,19},{19,3},{4,20},{20... | collective-permute-start | bytes 3145736 | tf_op jit(solution)/shard_map/ppermute | solution.py:1152
  59.3 13.4 %collective-permute-start.7 = (bf16[1792,128]{1,0:T(8,128)(2,1)S(1)}, bf16[1792,128]{1,0:T(8,128)(2,1)S(1)}, u32[]{:S(2)}, u32[]{:S(2)}) collective-permute-start(bf16[1792,128]{1,0:T(8,128)(2,1)S(1)} %get-tuple-element.218), channel_id=1, source_target_pairs={{0,1},{1,0},{2,3},{3,2},{4,5},{5,4},{6,7},{7,6},{8,9},{9,8},{10,11... | collective-permute-start | bytes 1376264 | tf_op jit(solution)/shard_map/ppermute | solution.py:1157
  59.5 13.2 %collective-permute-start.8 = (bf16[1792,128]{1,0:T(8,128)(2,1)S(1)}, bf16[1792,128]{1,0:T(8,128)(2,1)S(1)}, u32[]{:S(2)}, u32[]{:S(2)}) collective-permute-start(bf16[1792,128]{1,0:T(8,128)(2,1)S(1)} %get-tuple-element.220), channel_id=1, source_target_pairs={{0,2},{1,3},{2,0},{3,1},{4,6},{5,7},{6,4},{7,5},{8,10},{9,11},{10,... | collective-permute-start | bytes 1376264 | tf_op jit(solution)/shard_map/ppermute | solution.py:1157
  72.9 6.8 %collective-permute-start.9 = (bf16[896,128]{1,0:T(8,128)(2,1)S(1)}, bf16[896,128]{1,0:T(8,128)(2,1)S(1)}, u32[]{:S(2)}, u32[]{:S(2)}) collective-permute-start(bf16[896,128]{1,0:T(8,128)(2,1)S(1)} %get-tuple-element.235), channel_id=1, source_target_pairs={{0,2},{1,3},{2,0},{3,1},{4,6},{5,7},{6,4},{7,5},{8,10},{9,11},{10,... | collective-permute-start | bytes 688136 | tf_op jit(solution)/shard_map/ppermute | solution.py:1157
  74.0 6.5 %collective-permute-start.10 = (bf16[896,128]{1,0:T(8,128)(2,1)S(1)}, bf16[896,128]{1,0:T(8,128)(2,1)S(1)}, u32[]{:S(2)}, u32[]{:S(2)}) collective-permute-start(bf16[896,128]{1,0:T(8,128)(2,1)S(1)} %get-tuple-element.237), channel_id=1, source_target_pairs={{0,1},{1,0},{2,3},{3,2},{4,5},{5,4},{6,7},{7,6},{8,9},{9,8},{10,11... | collective-permute-start | bytes 688136 | tf_op jit(solution)/shard_map/ppermute | solution.py:1157
  77.4 6.9 %collective-permute-start.11 = (bf16[3072,128]{1,0:T(8,128)(2,1)S(1)}, bf16[3072,128]{1,0:T(8,128)(2,1)S(1)}, u32[]{:S(2)}, u32[]{:S(2)}) collective-permute-start(bf16[3072,128]{1,0:T(8,128)(2,1)S(1)} %get-tuple-element.241), channel_id=1, source_target_pairs={{0,16},{16,0},{1,17},{17,1},{2,18},{18,2},{3,19},{19,3},{4,20},{20... | collective-permute-start | bytes 2359304 | tf_op jit(solution)/shard_map/ppermute | solution.py:1152
  80.6 8.7 %collective-permute-start.12 = (bf16[448,128]{1,0:T(8,128)(2,1)S(1)}, bf16[448,128]{1,0:T(8,128)(2,1)S(1)}, u32[]{:S(2)}, u32[]{:S(2)}) collective-permute-start(bf16[448,128]{1,0:T(8,128)(2,1)S(1)} %get-tuple-element.252), channel_id=1, source_target_pairs={{0,4},{1,5},{2,6},{3,7},{4,0},{5,1},{6,2},{7,3},{8,12},{9,13},{10,... | collective-permute-start | bytes 344072 | tf_op jit(solution)/shard_map/ppermute | solution.py:1157
  80.9 8.4 %collective-permute-start.13 = (bf16[448,128]{1,0:T(8,128)(2,1)S(1)}, bf16[448,128]{1,0:T(8,128)(2,1)S(1)}, u32[]{:S(2)}, u32[]{:S(2)}) collective-permute-start(bf16[448,128]{1,0:T(8,128)(2,1)S(1)} %get-tuple-element.253), channel_id=1, source_target_pairs={{0,8},{1,9},{2,10},{3,11},{4,12},{5,13},{6,14},{7,15},{8,0},{9,1},... | collective-permute-start | bytes 344072 | tf_op jit(solution)/shard_map/ppermute | solution.py:1157
  81.4 9.0 %collective-permute-start.14 = (bf16[448,128]{1,0:T(8,128)(2,1)S(1)}, bf16[448,128]{1,0:T(8,128)(2,1)S(1)}, u32[]{:S(2)}, u32[]{:S(2)}) collective-permute-start(bf16[448,128]{1,0:T(8,128)(2,1)S(1)} %get-tuple-element.254), channel_id=1, source_target_pairs={{0,12},{1,13},{2,14},{3,15},{4,8},{5,9},{6,10},{7,11},{8,4},{9,5},... | collective-permute-start | bytes 344072 | tf_op jit(solution)/shard_map/ppermute | solution.py:1157
  85.3 9.6 %collective-permute-start.16 = (bf16[1792,128]{1,0:T(8,128)(2,1)S(1)}, bf16[1792,128]{1,0:T(8,128)(2,1)S(1)}, u32[]{:S(2)}, u32[]{:S(2)}) collective-permute-start(bf16[1792,128]{1,0:T(8,128)(2,1)S(1)} %get-tuple-element.259), channel_id=1, source_target_pairs={{0,2},{1,3},{2,0},{3,1},{4,6},{5,7},{6,4},{7,5},{8,10},{9,11},{10,... | collective-permute-start | bytes 1376264 | tf_op jit(solution)/shard_map/ppermute | solution.py:1157
  85.9 9.9 %collective-permute-start.15 = (bf16[1872,128]{1,0:T(8,128)(2,1)S(1)}, bf16[1872,128]{1,0:T(8,128)(2,1)S(1)}, u32[]{:S(2)}, u32[]{:S(2)}) collective-permute-start(bf16[1872,128]{1,0:T(8,128)(2,1)S(1)} %get-tuple-element.257), channel_id=1, source_target_pairs={{0,1},{1,0},{2,3},{3,2},{4,5},{5,4},{6,7},{7,6},{8,9},{9,8},{10,11... | collective-permute-start | bytes 1437704 | tf_op jit(solution)/shard_map/ppermute | solution.py:1157
  90.5 7.0 %collective-permute-start.19 = (bf16[448,128]{1,0:T(8,128)(2,1)S(1)}, bf16[448,128]{1,0:T(8,128)(2,1)S(1)}, u32[]{:S(2)}, u32[]{:S(2)}) collective-permute-start(bf16[448,128]{1,0:T(8,128)(2,1)S(1)} %get-tuple-element.261.refs_1_), channel_id=1, source_target_pairs={{0,12},{1,13},{2,14},{3,15},{4,8},{5,9},{6,10},{7,11},{8,4},{9,5},... | collective-permute-start | bytes 344072 | tf_op jit(solution)/shard_map/ppermute | solution.py:1157
  91.1 12.6 %collective-permute-start.18 = (bf16[448,128]{1,0:T(8,128)(2,1)S(1)}, bf16[448,128]{1,0:T(8,128)(2,1)S(1)}, u32[]{:S(2)}, u32[]{:S(2)}) collective-permute-start(bf16[448,128]{1,0:T(8,128)(2,1)S(1)} %get-tuple-element.261.refs_1_), channel_id=1, source_target_pairs={{0,8},{1,9},{2,10},{3,11},{4,12},{5,13},{6,14},{7,15},{8,0},{9,1},... | collective-permute-start | bytes 344072 | tf_op jit(solution)/shard_map/ppermute | solution.py:1157
  94.3 9.5 %collective-permute-start.17 = (bf16[448,128]{1,0:T(8,128)(2,1)S(1)}, bf16[448,128]{1,0:T(8,128)(2,1)S(1)}, u32[]{:S(2)}, u32[]{:S(2)}) collective-permute-start(bf16[448,128]{1,0:T(8,128)(2,1)S(1)} %get-tuple-element.261.refs_1_), channel_id=1, source_target_pairs={{0,4},{1,5},{2,6},{3,7},{4,0},{5,1},{6,2},{7,3},{8,12},{9,13},{10,... | collective-permute-start | bytes 344072 | tf_op jit(solution)/shard_map/ppermute | solution.py:1157
  96.0 7.8 %collective-permute-start.21 = (bf16[896,128]{1,0:T(8,128)(2,1)S(1)}, bf16[896,128]{1,0:T(8,128)(2,1)S(1)}, u32[]{:S(2)}, u32[]{:S(2)}) collective-permute-start(bf16[896,128]{1,0:T(8,128)(2,1)S(1)} %get-tuple-element.266), channel_id=1, source_target_pairs={{0,1},{1,0},{2,3},{3,2},{4,5},{5,4},{6,7},{7,6},{8,9},{9,8},{10,11... | collective-permute-start | bytes 688136 | tf_op jit(solution)/shard_map/ppermute | solution.py:1157
  97.1 6.8 %collective-permute-start.20 = (bf16[976,128]{1,0:T(8,128)(2,1)S(1)}, bf16[976,128]{1,0:T(8,128)(2,1)S(1)}, u32[]{:S(2)}, u32[]{:S(2)}) collective-permute-start(bf16[976,128]{1,0:T(8,128)(2,1)S(1)} %get-tuple-element.264), channel_id=1, source_target_pairs={{0,2},{1,3},{2,0},{3,1},{4,6},{5,7},{6,4},{7,5},{8,10},{9,11},{10,... | collective-permute-start | bytes 749576 | tf_op jit(solution)/shard_map/ppermute | solution.py:1157
  104.0 5.1 %collective-permute-start.22 = (bf16[528,128]{1,0:T(8,128)(2,1)S(1)}, bf16[528,128]{1,0:T(8,128)(2,1)S(1)}, u32[]{:S(2)}, u32[]{:S(2)}) collective-permute-start(bf16[528,128]{1,0:T(8,128)(2,1)S(1)} %get-tuple-element.269), channel_id=1, source_target_pairs={{0,4},{1,5},{2,6},{3,7},{4,0},{5,1},{6,2},{7,3},{8,12},{9,13},{10,... | collective-permute-start | bytes 405512 | tf_op jit(solution)/shard_map/ppermute | solution.py:1157
  104.0 6.9 %collective-permute-start.23 = (bf16[528,128]{1,0:T(8,128)(2,1)S(1)}, bf16[528,128]{1,0:T(8,128)(2,1)S(1)}, u32[]{:S(2)}, u32[]{:S(2)}) collective-permute-start(bf16[528,128]{1,0:T(8,128)(2,1)S(1)} %get-tuple-element.270), channel_id=1, source_target_pairs={{0,8},{1,9},{2,10},{3,11},{4,12},{5,13},{6,14},{7,15},{8,0},{9,1},... | collective-permute-start | bytes 405512 | tf_op jit(solution)/shard_map/ppermute | solution.py:1157
  104.3 8.3 %collective-permute-start.24 = (bf16[528,128]{1,0:T(8,128)(2,1)S(1)}, bf16[528,128]{1,0:T(8,128)(2,1)S(1)}, u32[]{:S(2)}, u32[]{:S(2)}) collective-permute-start(bf16[528,128]{1,0:T(8,128)(2,1)S(1)} %get-tuple-element.271), channel_id=1, source_target_pairs={{0,12},{1,13},{2,14},{3,15},{4,8},{5,9},{6,10},{7,11},{8,4},{9,5},... | collective-permute-start | bytes 405512 | tf_op jit(solution)/shard_map/ppermute | solution.py:1157
  107.6 12.6 %collective-permute-start.25 = (bf16[896,128]{1,0:T(8,128)(2,1)S(1)}, bf16[896,128]{1,0:T(8,128)(2,1)S(1)}, u32[]{:S(2)}, u32[]{:S(2)}) collective-permute-start(bf16[896,128]{1,0:T(8,128)(2,1)S(1)} %get-tuple-element.273.refs_1_), channel_id=1, source_target_pairs={{0,2},{1,3},{2,0},{3,1},{4,6},{5,7},{6,4},{7,5},{8,10},{9,11},{10,... | collective-permute-start | bytes 688136 | tf_op jit(solution)/shard_map/ppermute | solution.py:1157
  108.1 12.0 %collective-permute-start.26 = (bf16[896,128]{1,0:T(8,128)(2,1)S(1)}, bf16[896,128]{1,0:T(8,128)(2,1)S(1)}, u32[]{:S(2)}, u32[]{:S(2)}) collective-permute-start(bf16[896,128]{1,0:T(8,128)(2,1)S(1)} %get-tuple-element.274.refs_3_), channel_id=1, source_target_pairs={{0,1},{1,0},{2,3},{3,2},{4,5},{5,4},{6,7},{7,6},{8,9},{9,8},{10,11... | collective-permute-start | bytes 688136 | tf_op jit(solution)/shard_map/ppermute | solution.py:1157
  112.8 7.6 %collective-permute-start.31 = (bf16[448,128]{1,0:T(8,128)(2,1)S(1)}, bf16[448,128]{1,0:T(8,128)(2,1)S(1)}, u32[]{:S(2)}, u32[]{:S(2)}) collective-permute-start(bf16[448,128]{1,0:T(8,128)(2,1)S(1)} %get-tuple-element.278.refs_1_), channel_id=1, source_target_pairs={{0,12},{1,13},{2,14},{3,15},{4,8},{5,9},{6,10},{7,11},{8,4},{9,5},... | collective-permute-start | bytes 344072 | tf_op jit(solution)/shard_map/ppermute | solution.py:1157
  114.6 13.3 %collective-permute-start.30 = (bf16[448,128]{1,0:T(8,128)(2,1)S(1)}, bf16[448,128]{1,0:T(8,128)(2,1)S(1)}, u32[]{:S(2)}, u32[]{:S(2)}) collective-permute-start(bf16[448,128]{1,0:T(8,128)(2,1)S(1)} %get-tuple-element.278.refs_1_), channel_id=1, source_target_pairs={{0,8},{1,9},{2,10},{3,11},{4,12},{5,13},{6,14},{7,15},{8,0},{9,1},... | collective-permute-start | bytes 344072 | tf_op jit(solution)/shard_map/ppermute | solution.py:1157
  120.1 7.8 %collective-permute-start.29 = (bf16[448,128]{1,0:T(8,128)(2,1)S(1)}, bf16[448,128]{1,0:T(8,128)(2,1)S(1)}, u32[]{:S(2)}, u32[]{:S(2)}) collective-permute-start(bf16[448,128]{1,0:T(8,128)(2,1)S(1)} %get-tuple-element.278.refs_1_), channel_id=1, source_target_pairs={{0,4},{1,5},{2,6},{3,7},{4,0},{5,1},{6,2},{7,3},{8,12},{9,13},{10,... | collective-permute-start | bytes 344072 | tf_op jit(solution)/shard_map/ppermute | solution.py:1157
  120.2 15.6 %collective-permute-start.27 = (bf16[1792,128]{1,0:T(8,128)(2,1)S(1)}, bf16[1792,128]{1,0:T(8,128)(2,1)S(1)}, u32[]{:S(2)}, u32[]{:S(2)}) collective-permute-start(bf16[1792,128]{1,0:T(8,128)(2,1)S(1)} %get-tuple-element.275.refs_1_), channel_id=1, source_target_pairs={{0,1},{1,0},{2,3},{3,2},{4,5},{5,4},{6,7},{7,6},{8,9},{9,8},{10,11... | collective-permute-start | bytes 1376264 | tf_op jit(solution)/shard_map/ppermute | solution.py:1157
  120.3 15.5 %collective-permute-start.28 = (bf16[1792,128]{1,0:T(8,128)(2,1)S(1)}, bf16[1792,128]{1,0:T(8,128)(2,1)S(1)}, u32[]{:S(2)}, u32[]{:S(2)}) collective-permute-start(bf16[1792,128]{1,0:T(8,128)(2,1)S(1)} %get-tuple-element.276.refs_3_), channel_id=1, source_target_pairs={{0,2},{1,3},{2,0},{3,1},{4,6},{5,7},{6,4},{7,5},{8,10},{9,11},{10,... | collective-permute-start | bytes 1376264 | tf_op jit(solution)/shard_map/ppermute | solution.py:1157
  128.0 7.8 %collective-permute-start.32 = (bf16[896,128]{1,0:T(8,128)(2,1)S(1)}, bf16[896,128]{1,0:T(8,128)(2,1)S(1)}, u32[]{:S(2)}, u32[]{:S(2)}) collective-permute-start(bf16[896,128]{1,0:T(8,128)(2,1)S(1)} %get-tuple-element.280.refs_3_), channel_id=1, source_target_pairs={{0,2},{1,3},{2,0},{3,1},{4,6},{5,7},{6,4},{7,5},{8,10},{9,11},{10,... | collective-permute-start | bytes 688136 | tf_op jit(solution)/shard_map/ppermute | solution.py:1157
  128.1 7.8 %collective-permute-start.33 = (bf16[896,128]{1,0:T(8,128)(2,1)S(1)}, bf16[896,128]{1,0:T(8,128)(2,1)S(1)}, u32[]{:S(2)}, u32[]{:S(2)}) collective-permute-start(bf16[896,128]{1,0:T(8,128)(2,1)S(1)} %get-tuple-element.281.refs_5_), channel_id=1, source_target_pairs={{0,1},{1,0},{2,3},{3,2},{4,5},{5,4},{6,7},{7,6},{8,9},{9,8},{10,11... | collective-permute-start | bytes 688136 | tf_op jit(solution)/shard_map/ppermute | solution.py:1157
  135.9 7.4 %collective-permute-start.35 = (f32[2,512,512]{2,1,0:T(8,128)S(1)}, f32[2,512,512]{2,1,0:T(8,128)S(1)}, u32[]{:S(2)}, u32[]{:S(2)}) collective-permute-start(f32[2,512,512]{2,1,0:T(8,128)S(1)} %get-tuple-element.288.refs_1_), channel_id=1, source_target_pairs={{0,16},{16,0},{1,17},{17,1},{2,18},{18,2},{3,19},{19,3},{4,20},{20... | collective-permute-start | bytes 6291464 | tf_op jit(solution)/shard_map/ppermute | solution.py:1152
  138.4 12.1 %collective-permute-start.37 = (bf16[1792,128]{1,0:T(8,128)(2,1)S(1)}, bf16[1792,128]{1,0:T(8,128)(2,1)S(1)}, u32[]{:S(2)}, u32[]{:S(2)}) collective-permute-start(bf16[1792,128]{1,0:T(8,128)(2,1)S(1)} %get-tuple-element.296.refs_1_), channel_id=1, source_target_pairs={{0,1},{1,0},{2,3},{3,2},{4,5},{5,4},{6,7},{7,6},{8,9},{9,8},{10,11... | collective-permute-start | bytes 1376264 | tf_op jit(solution)/shard_map/ppermute | solution.py:1157
  139.8 11.8 %collective-permute-start.38 = (bf16[1792,128]{1,0:T(8,128)(2,1)S(1)}, bf16[1792,128]{1,0:T(8,128)(2,1)S(1)}, u32[]{:S(2)}, u32[]{:S(2)}) collective-permute-start(bf16[1792,128]{1,0:T(8,128)(2,1)S(1)} %get-tuple-element.297.refs_3_), channel_id=1, source_target_pairs={{0,2},{1,3},{2,0},{3,1},{4,6},{5,7},{6,4},{7,5},{8,10},{9,11},{10,... | collective-permute-start | bytes 1376264 | tf_op jit(solution)/shard_map/ppermute | solution.py:1157
  139.9 5.7 %collective-permute-start.36 = (bf16[1024,128]{1,0:T(8,128)(2,1)S(1)}, bf16[1024,128]{1,0:T(8,128)(2,1)S(1)}, u32[]{:S(2)}, u32[]{:S(2)}) collective-permute-start(bf16[1024,128]{1,0:T(8,128)(2,1)S(1)} %get-tuple-element.294.refs_1_), channel_id=1, source_target_pairs={{0,16},{16,0},{1,17},{17,1},{2,18},{18,2},{3,19},{19,3},{4,20},{20... | collective-permute-start | bytes 786440 | tf_op jit(solution)/shard_map/ppermute | solution.py:1152
  140.5 2.1 %collective-permute-start.34 = (f32[80,128]{1,0:T(8,128)S(1)}, f32[80,128]{1,0:T(8,128)S(1)}, u32[]{:S(2)}, u32[]{:S(2)}) collective-permute-start(f32[80,128]{1,0:T(8,128)S(1)} %get-tuple-element.286.refs_1_), channel_id=1, source_target_pairs={{0,16},{16,0},{1,17},{17,1},{2,18},{18,2},{3,19},{19,3},{4,20},{20... | collective-permute-start | bytes 122888 | tf_op jit(solution)/shard_map/ppermute | solution.py:1152
  151.6 3.3 %collective-permute-start.39 = (bf16[1024,128]{1,0:T(8,128)(2,1)S(1)}, bf16[1024,128]{1,0:T(8,128)(2,1)S(1)}, u32[]{:S(2)}, u32[]{:S(2)}) collective-permute-start(bf16[1024,128]{1,0:T(8,128)(2,1)S(1)} %get-tuple-element.307.refs_1_), channel_id=1, source_target_pairs={{0,16},{16,0},{1,17},{17,1},{2,18},{18,2},{3,19},{19,3},{4,20},{20... | collective-permute-start | bytes 786440 | tf_op jit(solution)/shard_map/ppermute | solution.py:1152
